TPU v7x, 32 devices: a whole 2x2x4 slice. The times are simulated.
32 devices in a mesh: freq: 2 (over y), row: 4 (over z), col: 4 (over x, core).
Axes of the slice: x: 2, y: 2, z: 4, core: 2. Of those that a mesh axis runs over, the one named last changes fastest.
Arguments:
- traces: bfloat16 [4, 6144, 6144], P('freq', 'row', 'col'), parts along dimension 0, may hold values from -6 to 6
- recv_live: int32 [12288], P('freq'), parts along dimension 0, may hold values 0 or 1
- missing: int32 [8, 96], P('freq'), parts along dimension 0, may hold values from 0 to 1535, as said below
- wavelet: float32 [4], P('freq'), parts along dimension 0, may hold values from 0.5 to 1.5
Outputs:
- primaries: float32 [4, 6144, 512], P('freq', 'row', 'col'), parts along dimension 0
There are 2 independent parts, one for each index of `freq`. A program takes and returns all parts, laid end to end along the dimension named above; each array names one. Nothing has to cross between parts.
Inputs may be any that keep to these rules, and one draw needn't show every extreme that they name: `missing`: each row lists 96 distinct positions within one block of 1536 shots, the shots of that block that were not recorded; the block's first and last shots are always among them.
All inputs are finite; a program needn't handle non-finite values.
Results may differ from a plain program's by a relative error of at most 0.0003.
Values may be sent and summed in bfloat16 or wider, within the bound.
No kernel may reach another device: no remote copies, remote signals or barrier semaphores. Data moves between devices by JAX's collectives and lax.ppermute only.
A program may use at most 128 MiB of HBM per device.

v0:
```python
import math

import jax
import jax.numpy as jnp
from jax import lax
from jax.sharding import PartitionSpec as P

ORDER = 6144
WIN = 128


def from_behind(block, axis, distance):
    devices = range(lax.axis_size(axis))
    route = [((i - distance) % len(devices), i) for i in devices]
    return lax.ppermute(block, axis, route)


def matmul(first, second):
    return jnp.dot(first, second, preferred_element_type=jnp.float32)


def complex_product(left_tile, right_tile):
    real_part = matmul(left_tile[0], right_tile[0]) - matmul(left_tile[1], right_tile[1])
    imag_part = matmul(left_tile[0], right_tile[1]) + matmul(left_tile[1], right_tile[0])
    return jnp.stack([real_part, imag_part])


def mirror(payload, grid_size, row_index, col_index):
    anti_sum = row_index + col_index
    anchors = jnp.arange(grid_size, dtype=jnp.int32)
    bit_count = grid_size.bit_length() - 1
    for bit_number in range(bit_count):
        stride = 2**bit_number
        carried = from_behind(payload, "row", stride)
        carried = from_behind(carried, "col", grid_size - stride)
        offset = (anti_sum - 2 * anchors) % grid_size
        spot_row = (anchors + offset % stride) % grid_size
        arrive = jnp.any(
            (spot_row == (row_index - stride) % grid_size) & (offset // stride % 2 == 1)
        )
        payload = jnp.where(arrive, carried, payload)
    return payload


def transpose_blocks(payload, grid_size, row_index, col_index):
    anti_sum = row_index + col_index
    anchors = jnp.arange(grid_size, dtype=jnp.int32)
    bit_count = grid_size.bit_length() - 1
    for bit_number in range(bit_count):
        stride = 2**bit_number
        carried = from_behind(payload, "row", stride)
        carried = from_behind(carried, "col", grid_size - stride)
        offset = (anti_sum - 2 * anchors) % grid_size
        spot_row = (anchors + offset % stride) % grid_size
        arrive = jnp.any(
            (spot_row == (row_index - stride) % grid_size) & (offset // stride % 2 == 1)
        )
        payload = jnp.where(arrive, carried, payload)
    return payload


def local(traces, recv_live, missing, wavelet):
    tile_size = traces.shape[1]
    grid_size = lax.axis_size("row")
    row_index = lax.axis_index("row")
    col_index = lax.axis_index("col")
    positions = jnp.arange(tile_size, dtype=jnp.int32)
    miss_row = lax.dynamic_index_in_dim(missing, row_index, 0, keepdims=False)
    miss_col = lax.dynamic_index_in_dim(missing, col_index, 0, keepdims=False)
    dead_row = jnp.any(positions[:, None] == miss_row[None, :], axis=1)
    dead_col = jnp.any(positions[:, None] == miss_col[None, :], axis=1)
    recv_row = lax.dynamic_slice_in_dim(recv_live, row_index * tile_size, tile_size) == 1
    recv_col = lax.dynamic_slice_in_dim(recv_live, col_index * tile_size, tile_size) == 1
    zero_bf = jnp.zeros((), jnp.bfloat16)
    outgoing = jnp.swapaxes(jnp.take(traces, miss_col, axis=2), 1, 2)
    incoming = mirror(outgoing, grid_size, row_index, col_index)
    direct = jnp.where(recv_col[None, None, :], traces, zero_bf)
    direct = jnp.where(dead_row[None, :, None], zero_bf, direct)
    keep_mask = jnp.take(recv_row, miss_row)[:, None] & jnp.logical_not(dead_col)[None, :]
    patched = jnp.where(keep_mask[None], incoming, zero_bf)
    filled = direct.at[:, miss_row, :].set(patched)
    window = filled[:, :, :WIN]
    win_width = window.shape[2]
    running = jnp.zeros((2, tile_size, win_width), jnp.float32)
    swapped = transpose_blocks(window, grid_size, row_index, col_index)
    gathered = lax.all_gather(swapped, "row", axis=2, tiled=True)

    def one_hop(stop_index, total):
        source_block = (col_index - stop_index - 1) % grid_size
        piece = lax.dynamic_slice_in_dim(gathered, source_block * win_width, win_width, 2)
        total = total + complex_product(filled, piece)
        return from_behind(total, "col", 1)

    running = lax.fori_loop(0, grid_size - 1, one_hop, running)
    own_piece = lax.dynamic_slice_in_dim(gathered, col_index * win_width, win_width, 2)
    running = running + complex_product(filled, own_piece)
    norm_scale = 1.0 / math.sqrt(ORDER)
    pred_real = (wavelet[0] * running[0] - wavelet[1] * running[1]) * norm_scale
    pred_imag = (wavelet[0] * running[1] + wavelet[1] * running[0]) * norm_scale
    window_f = window.astype(jnp.float32)
    return jnp.stack([window_f[0] - pred_real, window_f[1] - pred_imag])


def solution(mesh):
    in_specs = (P("freq", "row", "col"), P("freq"), P("freq", None), P("freq"))
    out_specs = P("freq", "row", "col")
    return jax.shard_map(local, mesh=mesh, in_specs=in_specs, out_specs=out_specs, check_vma=False)
```

profile of v0, /device:TPU:1, one launch (start us, length us, event | category | flops | bytes accessed | tf_op | source)
XLA Modules:
  0.0 445.7 jit_solution(11039672735321170451)
XLA Ops:
  8.2 1.3 gather_fusion
  10.2 24.0 %copy.16 = bf16[2,1536,1536]{1,0,2:T(2,128)(2,1)} copy(bf16[2,1536,1536]{2,1,0:T(8,128)(2,1)} %param.6) | data formatting | bytes 18874368 | tf_op args[0]
  34.2 5.5 %gather_fusion.1 = bf16[96,2,1536]{2,1,0:T(2,128)(2,1)S(1)} fusion(bf16[2,1536,1536]{1,0,2:T(2,128)(2,1)} %copy.16, s32[1024]{0:T(1024)S(1)} %get-tuple-element.183), kind=kCustom, calls=%fused_computation.1 | custom fusion | bytes 1180032 | tf_op jit(solution)/shard_map/jit(_take)/gather | solution.py:75
  40.3 2.2 collective-permute-start.1
  42.5 15.0 %collective-permute-done.1 = bf16[2,96,1536]{2,0,1:T(2,128)(2,1)S(1)} collective-permute-done((bf16[2,96,1536]{2,0,1:T(2,128)(2,1)S(1)}, bf16[2,96,1536]{2,0,1:T(2,128)(2,1)S(1)}, u32[]{:S(2)}, u32[]{:S(2)}) %collective-permute-start.1) | collective-permute-done | bytes 589856 | tf_op jit(solution)/shard_map/ppermute | solution.py:15
  57.5 1.2 collective-permute-start.2
  59.4 8.0 %collective-permute-done.2 = bf16[2,96,1536]{2,0,1:T(2,128)(2,1)S(1)} collective-permute-done((bf16[2,96,1536]{2,0,1:T(2,128)(2,1)S(1)}, bf16[2,96,1536]{2,0,1:T(2,128)(2,1)S(1)}, u32[]{:S(2)}, u32[]{:S(2)}) %collective-permute-start.2) | collective-permute-done | bytes 589856 | tf_op jit(solution)/shard_map/ppermute | solution.py:15
  67.5 1.5 broadcast_select_fusion.3
  69.6 26.6 %collective-permute-done.3 = bf16[2,96,1536]{2,0,1:T(2,128)(2,1)S(1)} collective-permute-done((bf16[2,96,1536]{2,0,1:T(2,128)(2,1)S(1)}, bf16[2,96,1536]{2,0,1:T(2,128)(2,1)S(1)}, u32[]{:S(2)}, u32[]{:S(2)}) %collective-permute-start.3) | collective-permute-done | bytes 589856 | tf_op jit(solution)/shard_map/ppermute | solution.py:15
  97.3 42.0 %broadcast_select_fusion = bf16[2,1536,1536]{2,0,1:T(2,128)(2,1)} fusion(pred[1536]{0:T(1024)(128)(4,1)S(1)} %fusion.54, pred[1536]{0:T(1024)(128)(4,1)S(1)} %get-tuple-element.175, bf16[2,1536,1536]{2,1,0:T(8,128)(2,1)} %param.6), kind=kLoop, calls=%fused_computation.26 | loop fusion | flops 9437184 | bytes 18877440 | tf_op jit(solution)/shard_map/jit(_where)/select_n | solution.py:78
  140.2 1.7 fusion.52
  141.9 11.7 %scatter_fusion = bf16[2,1536,1536]{2,0,1:T(2,128)(2,1)} fusion(bf16[2,1536,1536]{2,0,1:T(2,128)(2,1)} %broadcast_select_fusion, s32[96]{0:T(128)S(1)} %get-tuple-element.178, bf16[96,2,1536]{2,1,0:T(2,128)(2,1)S(1)} %fusion.52), kind=kCustom, calls=%fused_computation.2 | custom fusion | bytes 1769856 | tf_op jit(solution)/shard_map/scatter | solution.py:81
  153.6 8.8 %copy.17 = bf16[2,1536,1536]{2,1,0:T(8,128)(2,1)} copy(bf16[2,1536,1536]{2,0,1:T(2,128)(2,1)} %scatter_fusion) | data formatting | bytes 18874368 | tf_op jit(solution)/shard_map/scatter | solution.py:81
  163.7 20.2 %collective-permute-done.5 = bf16[2,1536,128]{2,1,0:T(8,128)(2,1)S(1)} collective-permute-done((bf16[2,1536,128]{2,1,0:T(8,128)(2,1)S(1)}, bf16[2,1536,128]{2,1,0:T(8,128)(2,1)S(1)}, u32[]{:S(2)}, u32[]{:S(2)}) %collective-permute-start.5) | collective-permute-done | bytes 786464 | tf_op jit(solution)/shard_map/ppermute | solution.py:15
  183.9 1.5 collective-permute-start.6
  185.5 9.9 %collective-permute-done.6 = bf16[2,1536,128]{2,1,0:T(8,128)(2,1)S(1)} collective-permute-done((bf16[2,1536,128]{2,1,0:T(8,128)(2,1)S(1)}, bf16[2,1536,128]{2,1,0:T(8,128)(2,1)S(1)}, u32[]{:S(2)}, u32[]{:S(2)}) %collective-permute-start.6) | collective-permute-done | bytes 786464 | tf_op jit(solution)/shard_map/ppermute | solution.py:15
  195.4 3.1 broadcast_select_fusion.6
  198.4 35.3 %collective-permute-done.7 = bf16[2,1536,128]{2,1,0:T(8,128)(2,1)S(1)} collective-permute-done((bf16[2,1536,128]{2,1,0:T(8,128)(2,1)S(1)}, bf16[2,1536,128]{2,1,0:T(8,128)(2,1)S(1)}, u32[]{:S(2)}, u32[]{:S(2)}) %collective-permute-start.7) | collective-permute-done | bytes 786464 | tf_op jit(solution)/shard_map/ppermute | solution.py:15
  234.3 18.2 %collective-permute-done.8 = bf16[2,1536,128]{2,1,0:T(8,128)(2,1)S(1)} collective-permute-done((bf16[2,1536,128]{2,1,0:T(8,128)(2,1)S(1)}, bf16[2,1536,128]{2,1,0:T(8,128)(2,1)S(1)}, u32[]{:S(2)}, u32[]{:S(2)}) %collective-permute-start.8) | collective-permute-done | bytes 786464 | tf_op jit(solution)/shard_map/ppermute | solution.py:15
  252.4 1.5 broadcast_select_fusion.7
  254.6 19.5 %fusion.69 = (bf16[1,1536,1536]{2,0,1:T(2,128)(2,1)}, bf16[1,1536,1536]{2,0,1:T(2,128)(2,1)}) fusion(bf16[2,1536,1536]{2,0,1:T(2,128)(2,1)} %scatter_fusion), kind=kLoop, calls=%fused_computation.104 | loop fusion | bytes 18874368 | tf_op jit(solution)/shard_map/slice | solution.py:23
  274.1 43.5 %all-gather.2.cloned.1.call-done = bf16[2,1536,512]{2,1,0:T(8,128)(2,1)} async-done(((bf16[2,1536,128]{2,1,0:T(8,128)(2,1)}), bf16[2,1536,512]{2,1,0:T(8,128)(2,1)}) %all-gather.2.cloned.1.call-update) | async-done | bytes 3145744 | tf_op jit(solution)/shard_map/all_gather | solution.py:86
  317.9 100.9 %while.15 = (s32[]{:T(128)}, f32[2,1536,128]{1,2,0:T(8,128)S(1)}, s32[]{:T(128)}, bf16[2,1536,512]{2,1,0:T(8,128)(2,1)}, bf16[2,1536,1536]{2,1,0:T(8,128)(2,1)},...) while((s32[]{:T(128)}, f32[2,1536,128]{1,2,0:T(8,128)S(1)}, ...), condition=%wide.region_6.7_spmd, body=%wide.region_5.6_spmd.sunk | while | flops 2417098752 | bytes 73925016 | solution.py:94
  317.9 4.3 fusion.83
  322.2 4.2 fusion.85
  326.4 2.7 fusion.84
  329.1 2.7 fusion.86
  331.9 1.7 collective-permute-start
  333.6 17.4 %collective-permute-done = f32[2,1536,128]{1,2,0:T(8,128)S(1)} collective-permute-done((f32[2,1536,128]{1,2,0:T(8,128)S(1)}, f32[2,1536,128]{1,2,0:T(8,128)S(1)}, u32[]{:S(2)}, u32[]{:S(2)}) %collective-permute-start) | collective-permute-done | bytes 1572896 | tf_op jit(solution)/shard_map/while/body/eval_jaxpr/ppermute | solution.py:15
  351.0 4.3 fusion.83
  355.3 4.2 fusion.85
  359.4 2.7 fusion.84
  362.1 2.7 fusion.86
  365.0 2.5 collective-permute-start
  367.5 17.4 %collective-permute-done = f32[2,1536,128]{1,2,0:T(8,128)S(1)} collective-permute-done((f32[2,1536,128]{1,2,0:T(8,128)S(1)}, f32[2,1536,128]{1,2,0:T(8,128)S(1)}, u32[]{:S(2)}, u32[]{:S(2)}) %collective-permute-start) | collective-permute-done | bytes 1572896 | tf_op jit(solution)/shard_map/while/body/eval_jaxpr/ppermute | solution.py:15
  384.9 4.3 fusion.83
  389.2 4.2 fusion.85
  393.4 2.7 fusion.84
  396.0 2.7 fusion.86
  398.9 2.5 collective-permute-start
  401.4 17.4 %collective-permute-done = f32[2,1536,128]{1,2,0:T(8,128)S(1)} collective-permute-done((f32[2,1536,128]{1,2,0:T(8,128)S(1)}, f32[2,1536,128]{1,2,0:T(8,128)S(1)}, u32[]{:S(2)}, u32[]{:S(2)}) %collective-permute-start) | collective-permute-done | bytes 1572896 | tf_op jit(solution)/shard_map/while/body/eval_jaxpr/ppermute | solution.py:15
  419.3 5.2 %fusion.28 = f32[1536,128]{1,0:T(8,128)S(1)} fusion(bf16[1,1536,1536]{2,0,1:T(2,128)(2,1)} %get-tuple-element.170, bf16[2,1536,512]{2,1,0:T(8,128)(2,1)} %get-tuple-element.269, s32[]{:T(128)S(6)} %select_n.231), kind=kOutput, calls=%fused_computation.28 | convolution fusion | flops 603979776 | bytes 10616836 | tf_op jit(solution)/shard_map/dot_general | solution.py:19
  424.5 5.3 %fusion.30 = f32[1536,128]{1,0:T(8,128)S(1)} fusion(bf16[1,1536,1536]{2,0,1:T(2,128)(2,1)} %get-tuple-element.170, bf16[2,1536,512]{2,1,0:T(8,128)(2,1)} %get-tuple-element.269, s32[]{:T(128)S(6)} %add.229, s32[]{:T(128)S(6)} %select_n.231), kind=kOutput, calls=%fused_computation.30 | convolution fusion | flops 603979776 | bytes 10616840 | tf_op jit(solution)/shard_map/dot_general | solution.py:19
  429.9 2.4 fusion.42
  432.3 2.4 fusion.45
  434.9 1.2 copy-done.1
  436.1 1.5 slice_subtract_fusion.1
  437.6 1.2 pad_maximum_fusion
  (43 shorter events, 10.2 us)
Async XLA Ops:
  6.5 311.2 %all-gather.2.cloned.1.call-start = ((), (), s32[]{:S(2)}) async-start(), calls=%async_computation | async-start | bytes 3932160 | tf_op jit(solution)/shard_map/all_gather | solution.py:86
  40.3 17.2 %collective-permute-start.1 = (bf16[2,96,1536]{2,0,1:T(2,128)(2,1)S(1)}, bf16[2,96,1536]{2,0,1:T(2,128)(2,1)S(1)}, u32[]{:S(2)}, u32[]{:S(2)}) collective-permute-start(bf16[2,96,1536]{2,0,1:T(2,128)(2,1)S(1)} %fusion.53), channel_id=1, source_target_pairs={{12,0},{0,4},{4,8},{8,12},{13,1},{1,5},{5,9},{9,13},{14,2},{2,6},{... | collective-permute-start | bytes 1769480 | tf_op jit(solution)/shard_map/ppermute | solution.py:15
  57.5 9.9 %collective-permute-start.2 = (bf16[2,96,1536]{2,0,1:T(2,128)(2,1)S(1)}, bf16[2,96,1536]{2,0,1:T(2,128)(2,1)S(1)}, u32[]{:S(2)}, u32[]{:S(2)}) collective-permute-start(bf16[2,96,1536]{2,0,1:T(2,128)(2,1)S(1)} %collective-permute-done.1), channel_id=1, source_target_pairs={{1,0},{2,1},{3,2},{0,3},{5,4},{6,5},{7,6},{4,7},{9,8},{10,9},{11,1... | collective-permute-start | bytes 1769480 | tf_op jit(solution)/shard_map/ppermute | solution.py:15
  68.9 27.3 %collective-permute-start.3 = (bf16[2,96,1536]{2,0,1:T(2,128)(2,1)S(1)}, bf16[2,96,1536]{2,0,1:T(2,128)(2,1)S(1)}, u32[]{:S(2)}, u32[]{:S(2)}) collective-permute-start(bf16[2,96,1536]{2,0,1:T(2,128)(2,1)S(1)} %broadcast_select_fusion.3), channel_id=1, source_target_pairs={{8,0},{12,4},{0,8},{4,12},{9,1},{13,5},{1,9},{5,13},{10,2},{14,6},... | collective-permute-start | bytes 1769480 | tf_op jit(solution)/shard_map/ppermute | solution.py:15
  96.2 44.0 %collective-permute-start.4 = (bf16[2,96,1536]{2,0,1:T(2,128)(2,1)S(1)}, bf16[2,96,1536]{2,0,1:T(2,128)(2,1)S(1)}, u32[]{:S(2)}, u32[]{:S(2)}) collective-permute-start(bf16[2,96,1536]{2,0,1:T(2,128)(2,1)S(1)} %collective-permute-done.3), channel_id=1, source_target_pairs={{2,0},{3,1},{0,2},{1,3},{6,4},{7,5},{4,6},{5,7},{10,8},{11,9},{8,1... | collective-permute-start | bytes 1769480 | tf_op jit(solution)/shard_map/ppermute | solution.py:15
  162.4 91.6 %copy-start.2 = (f32[2]{0:T(128)S(1)}, f32[2]{0:T(128)}, u32[]{:S(2)}) copy-start(f32[2]{0:T(128)} %param.9) | copy-start | bytes 28
  163.6 20.3 %collective-permute-start.5 = (bf16[2,1536,128]{2,1,0:T(8,128)(2,1)S(1)}, bf16[2,1536,128]{2,1,0:T(8,128)(2,1)S(1)}, u32[]{:S(2)}, u32[]{:S(2)}) collective-permute-start(bf16[2,1536,128]{2,1,0:T(8,128)(2,1)S(1)} %slice.100), channel_id=1, source_target_pairs={{12,0},{0,4},{4,8},{8,12},{13,1},{1,5},{5,9},{9,13},{14,2},{2,6},{... | collective-permute-start | bytes 2359304 | tf_op jit(solution)/shard_map/ppermute | solution.py:15
  183.9 11.5 %collective-permute-start.6 = (bf16[2,1536,128]{2,1,0:T(8,128)(2,1)S(1)}, bf16[2,1536,128]{2,1,0:T(8,128)(2,1)S(1)}, u32[]{:S(2)}, u32[]{:S(2)}) collective-permute-start(bf16[2,1536,128]{2,1,0:T(8,128)(2,1)S(1)} %collective-permute-done.5), channel_id=1, source_target_pairs={{1,0},{2,1},{3,2},{0,3},{5,4},{6,5},{7,6},{4,7},{9,8},{10,9},{11,1... | collective-permute-start | bytes 2359304 | tf_op jit(solution)/shard_map/ppermute | solution.py:15
  198.4 35.3 %collective-permute-start.7 = (bf16[2,1536,128]{2,1,0:T(8,128)(2,1)S(1)}, bf16[2,1536,128]{2,1,0:T(8,128)(2,1)S(1)}, u32[]{:S(2)}, u32[]{:S(2)}) collective-permute-start(bf16[2,1536,128]{2,1,0:T(8,128)(2,1)S(1)} %get-tuple-element.171), channel_id=1, source_target_pairs={{8,0},{12,4},{0,8},{4,12},{9,1},{13,5},{1,9},{5,13},{10,2},{14,6},... | collective-permute-start | bytes 2359304 | tf_op jit(solution)/shard_map/ppermute | solution.py:15
  233.7 18.7 %collective-permute-start.8 = (bf16[2,1536,128]{2,1,0:T(8,128)(2,1)S(1)}, bf16[2,1536,128]{2,1,0:T(8,128)(2,1)S(1)}, u32[]{:S(2)}, u32[]{:S(2)}) collective-permute-start(bf16[2,1536,128]{2,1,0:T(8,128)(2,1)S(1)} %collective-permute-done.7), channel_id=1, source_target_pairs={{2,0},{3,1},{0,2},{1,3},{6,4},{7,5},{4,6},{5,7},{10,8},{11,9},{8,1... | collective-permute-start | bytes 2359304 | tf_op jit(solution)/shard_map/ppermute | solution.py:15
  317.9 8.5 %copy-start = (bf16[2,1536,1536]{2,1,0:T(8,128)(2,1)S(1)}, bf16[2,1536,1536]{2,1,0:T(8,128)(2,1)}, u32[]{:S(2)}) copy-start(bf16[2,1536,1536]{2,1,0:T(8,128)(2,1)} %get-tuple-element.246) | copy-start | bytes 28311556 | tf_op jit(solution)/shard_map/while
  331.9 19.0 %collective-permute-start = (f32[2,1536,128]{1,2,0:T(8,128)S(1)}, f32[2,1536,128]{1,2,0:T(8,128)S(1)}, u32[]{:S(2)}, u32[]{:S(2)}) collective-permute-start(f32[2,1536,128]{1,2,0:T(8,128)S(1)} %maximum_add_fusion.3), channel_id=1, source_target_pairs={{3,0},{0,1},{1,2},{2,3},{7,4},{4,5},{5,6},{6,7},{11,8},{8,9},{9,10... | collective-permute-start | bytes 4718600 | tf_op jit(solution)/shard_map/while/body/eval_jaxpr/ppermute | solution.py:15
  351.0 8.5 %copy-start = (bf16[2,1536,1536]{2,1,0:T(8,128)(2,1)S(1)}, bf16[2,1536,1536]{2,1,0:T(8,128)(2,1)}, u32[]{:S(2)}) copy-start(bf16[2,1536,1536]{2,1,0:T(8,128)(2,1)} %get-tuple-element.246) | copy-start | bytes 28311556 | tf_op jit(solution)/shard_map/while
  365.0 19.9 %collective-permute-start = (f32[2,1536,128]{1,2,0:T(8,128)S(1)}, f32[2,1536,128]{1,2,0:T(8,128)S(1)}, u32[]{:S(2)}, u32[]{:S(2)}) collective-permute-start(f32[2,1536,128]{1,2,0:T(8,128)S(1)} %maximum_add_fusion.3), channel_id=1, source_target_pairs={{3,0},{0,1},{1,2},{2,3},{7,4},{4,5},{5,6},{6,7},{11,8},{8,9},{9,10... | collective-permute-start | bytes 4718600 | tf_op jit(solution)/shard_map/while/body/eval_jaxpr/ppermute | solution.py:15
  384.9 8.5 %copy-start = (bf16[2,1536,1536]{2,1,0:T(8,128)(2,1)S(1)}, bf16[2,1536,1536]{2,1,0:T(8,128)(2,1)}, u32[]{:S(2)}) copy-start(bf16[2,1536,1536]{2,1,0:T(8,128)(2,1)} %get-tuple-element.246) | copy-start | bytes 28311556 | tf_op jit(solution)/shard_map/while
  398.9 19.9 %collective-permute-start = (f32[2,1536,128]{1,2,0:T(8,128)S(1)}, f32[2,1536,128]{1,2,0:T(8,128)S(1)}, u32[]{:S(2)}, u32[]{:S(2)}) collective-permute-start(f32[2,1536,128]{1,2,0:T(8,128)S(1)} %maximum_add_fusion.3), channel_id=1, source_target_pairs={{3,0},{0,1},{1,2},{2,3},{7,4},{4,5},{5,6},{6,7},{11,8},{8,9},{9,10... | collective-permute-start | bytes 4718600 | tf_op jit(solution)/shard_map/while/body/eval_jaxpr/ppermute | solution.py:15
  419.3 10.6 %slice-start = ((s8[9437184]{0:T(1024)(128)(4,1)}), s8[4194304]{0:T(1024)(128)(4,1)S(1)}, s32[]{:S(2)}) async-start(s8[9437184]{0:T(1024)(128)(4,1)} %bitcast.106), calls=%async_computation.1 | async-start | bytes 8388608
  419.3 10.6 %slice-start.1 = ((s8[9437184]{0:T(1024)(128)(4,1)}), s8[4194304]{0:T(1024)(128)(4,1)S(1)}, s32[]{:S(2)}) async-start(s8[9437184]{0:T(1024)(128)(4,1)} %bitcast.106), calls=%async_computation.2 | async-start | bytes 8388608
  424.5 5.3 %slice-start.2 = ((s8[9437184]{0:T(1024)(128)(4,1)}), s8[1048576]{0:T(1024)(128)(4,1)S(1)}, s32[]{:S(2)}) async-start(s8[9437184]{0:T(1024)(128)(4,1)} %bitcast.106), calls=%async_computation.3 | async-start | bytes 2097152
  434.7 1.4 copy-start.1
Sparse Core Ops, SparseCore 0:
  254.1 63.5 all-gather.1
where the time goes:
time: 449 us; the launch traced here: 446 us
  waiting for transfers between devices  229 us (51%)
  local copies, waits for them, and re-layouts  74.4 us (17%)
  other arithmetic  58 us (13%)
  matrix products  56.7 us (13%)
  starting transfers between devices  13.9 us (3%)
  between operations  13.6 us (3%)
    ppermute x11, waiting for transfers between devices, from_behind(): return lax.ppermute(block, axis, route)  185 us
    dot_general x16, matrix products, matmul(): return jnp.dot(first, second, preferred_element_type=jnp.float32)  56.7 us
    all_gather x1, waiting for transfers between devices, local(): gathered = lax.all_gather(swapped, 'row', axis=2, tiled=True)  43.5 us
    select_n x1, other arithmetic, local(): direct = jnp.where(dead_row[None, :, None], zero_bf, direct)  42 us
    unnamed x11, local copies, waits for them, and re-layouts  25.3 us
    scatter x2, local copies, waits for them, and re-layouts, local(): filled = direct.at[:, miss_row, :].set(patched)  20.5 us
    slice x1, local copies, waits for them, and re-layouts, complex_product(): left_tile[0]  19.5 us
    ppermute x11, starting transfers between devices, from_behind(): return lax.ppermute(block, axis, route)  13.9 us
  transfers between devices with their start and end apart: 12, of which 11 were waited for; matrix products, arithmetic and copies ran while one was open for 14% of the time, Pallas kernels for 0%

commit v1 on v0

v1 whole, which is shorter than its diff:
```python
import functools
import math

import jax
import jax.numpy as jnp
from jax import lax
from jax.experimental import pallas as pl
from jax.experimental.pallas import tpu as pltpu
from jax.sharding import PartitionSpec as P

WIN = 128
LANES = 128
VMEM_LIMIT = 56 * 2**20


def row_block(rows):
    for size in (512, 384, 256, 128):
        if rows % size == 0:
            return size
    return rows


def one_hot(positions_row, rows, dtype):
    lanes = positions_row.shape[1]
    row_ids = lax.broadcasted_iota(jnp.int32, (rows, lanes), 0)
    return jnp.where(row_ids == positions_row, 1.0, 0.0).astype(dtype)


def pick_kernel(traces_ref, miss_ref, recv_ref, live_ref, out_ref, hot_ref):
    @pl.when(pl.program_id(0) == 0)
    def _():
        hot = one_hot(miss_ref[...], hot_ref.shape[0], jnp.bfloat16)
        alive = jnp.dot(recv_ref[...], hot, preferred_element_type=jnp.float32)
        hot_ref[...] = hot * alive[0:1].astype(jnp.bfloat16)

    misses = out_ref.shape[1]
    for part in range(2):
        picked = jnp.dot(traces_ref[part], hot_ref[...], preferred_element_type=jnp.float32)
        turned = picked.T * live_ref[0:1, :]
        out_ref[part] = turned[:misses].astype(jnp.bfloat16)


def pick_columns(traces, miss_lanes, recv8, live8, misses):
    _, rows, cols = traces.shape
    block = row_block(rows)
    return pl.pallas_call(
        pick_kernel,
        grid=(rows // block,),
        in_specs=[
            pl.BlockSpec((2, block, cols), lambda i: (0, i, 0)),
            pl.BlockSpec((1, LANES), lambda i: (0, 0)),
            pl.BlockSpec((8, cols), lambda i: (0, 0)),
            pl.BlockSpec((8, block), lambda i: (0, i)),
        ],
        out_specs=pl.BlockSpec((2, misses, block), lambda i: (0, 0, i)),
        out_shape=jax.ShapeDtypeStruct((2, misses, rows), jnp.bfloat16),
        scratch_shapes=[pltpu.VMEM((cols, LANES), jnp.bfloat16)],
        compiler_params=pltpu.CompilerParams(vmem_limit_bytes=VMEM_LIMIT),
        cost_estimate=pl.CostEstimate(
            flops=4 * rows * cols * LANES, bytes_accessed=4 * rows * cols, transcendentals=0
        ),
        name="pick_columns",
    )(traces, miss_lanes, recv8, live8)


def window_kernel(raw_ref, patch_ref, miss_ref, recv_ref, out_ref):
    rows = raw_ref.shape[1]
    misses = patch_ref.shape[1]
    hot = one_hot(miss_ref[...], rows, jnp.float32)
    dead = jnp.max(hot, axis=1, keepdims=True)
    hot = hot[:, :misses].astype(jnp.bfloat16)
    keep = (1.0 - dead) * recv_ref[0:1, :].astype(jnp.float32)
    for part in range(2):
        patch = jnp.dot(hot, patch_ref[part], preferred_element_type=jnp.float32)
        filled = raw_ref[part].astype(jnp.float32) * keep + patch
        out_ref[:, part * WIN:(part + 1) * WIN] = filled.astype(jnp.bfloat16)


def fill_window(raw, patch, miss_lanes, recv8):
    rows = raw.shape[1]
    return pl.pallas_call(
        window_kernel,
        out_shape=jax.ShapeDtypeStruct((rows, 2 * WIN), jnp.bfloat16),
        compiler_params=pltpu.CompilerParams(vmem_limit_bytes=VMEM_LIMIT),
        cost_estimate=pl.CostEstimate(
            flops=4 * rows * LANES * WIN, bytes_accessed=8 * rows * WIN, transcendentals=0
        ),
        name="fill_window",
    )(raw, patch, miss_lanes, recv8)


def complex_rows(real_rows, imag_rows, right):
    first = jnp.dot(real_rows, right, preferred_element_type=jnp.float32)
    second = jnp.dot(imag_rows, right, preferred_element_type=jnp.float32)
    real_part = first[:, :WIN] - second[:, WIN:]
    imag_part = first[:, WIN:] + second[:, :WIN]
    return real_part, imag_part


def product_kernel(grid_size, col_ref, traces_ref, recv_ref, right_ref, extra_ref, *outs):
    send_ref, keep_ref, send_extra_ref, keep_extra_ref = outs
    recv = recv_ref[0:1, :]
    real_rows = traces_ref[0] * recv
    imag_rows = traces_ref[1] * recv
    for offset in range(grid_size):
        right = right_ref[col_ref[0] ^ offset]
        out_ref = send_ref if offset % 2 else keep_ref
        real_part, imag_part = complex_rows(real_rows, imag_rows, right)
        out_ref[offset // 2, :, :WIN] = real_part
        out_ref[offset // 2, :, WIN:] = imag_part

    @pl.when(pl.program_id(0) == 0)
    def _():
        for offset in range(grid_size):
            right = right_ref[col_ref[0] ^ offset]
            out_ref = send_extra_ref if offset % 2 else keep_extra_ref
            real_part, imag_part = complex_rows(extra_ref[0], extra_ref[1], right)
            out_ref[offset // 2, :, :WIN] = real_part
            out_ref[offset // 2, :, WIN:] = imag_part


def products(col_index, traces, recv8, right, extra):
    _, rows, cols = traces.shape
    grid_size = right.shape[0]
    misses = extra.shape[1]
    block = row_block(rows)
    half = grid_size // 2
    main = pl.BlockSpec((half, block, 2 * WIN), lambda i, c: (0, i, 0))
    tail = pl.BlockSpec((half, misses, 2 * WIN), lambda i, c: (0, 0, 0))
    main_shape = jax.ShapeDtypeStruct((half, rows, 2 * WIN), jnp.float32)
    tail_shape = jax.ShapeDtypeStruct((half, misses, 2 * WIN), jnp.float32)
    return pl.pallas_call(
        functools.partial(product_kernel, grid_size),
        grid_spec=pltpu.PrefetchScalarGridSpec(
            num_scalar_prefetch=1,
            grid=(rows // block,),
            in_specs=[
                pl.BlockSpec((2, block, cols), lambda i, c: (0, i, 0)),
                pl.BlockSpec((8, cols), lambda i, c: (0, 0)),
                pl.BlockSpec((grid_size, cols, 2 * WIN), lambda i, c: (0, 0, 0)),
                pl.BlockSpec((2, misses, cols), lambda i, c: (0, 0, 0)),
            ],
            out_specs=[main, main, tail, tail],
        ),
        out_shape=[main_shape, main_shape, tail_shape, tail_shape],
        compiler_params=pltpu.CompilerParams(vmem_limit_bytes=VMEM_LIMIT),
        cost_estimate=pl.CostEstimate(
            flops=8 * (rows + misses) * cols * WIN * grid_size,
            bytes_accessed=4 * rows * cols + 8 * grid_size * rows * WIN,
            transcendentals=0,
        ),
        name="products",
    )(col_index, traces, recv8, right, extra)


def finish_kernel(miss_ref, wave_ref, raw_ref, recv_ref, extra_ref, *refs):
    sums, extra_sums = refs[:3], refs[3:6]
    out_ref, row_ref = refs[6], refs[7]

    def subtract(window, terms):
        total = terms[0][...] + terms[1][...] + terms[2][...]
        real_part, imag_part = total[:, :WIN], total[:, WIN:]
        pred_real = real_part * wave_ref[0] - imag_part * wave_ref[1]
        pred_imag = imag_part * wave_ref[0] + real_part * wave_ref[1]
        return window[0] - pred_real, window[1] - pred_imag

    recv = recv_ref[0:1, :].astype(jnp.float32)
    window = [raw_ref[part].astype(jnp.float32) * recv for part in range(2)]
    out_ref[0], out_ref[1] = subtract(window, sums)
    window = [extra_ref[part].astype(jnp.float32) for part in range(2)]
    row_ref[0], row_ref[1] = subtract(window, extra_sums)

    def place(m, carry):
        for part in range(2):
            out_ref[part, pl.ds(miss_ref[m], 1), :] = row_ref[part, pl.ds(m, 1), :]
        return carry

    lax.fori_loop(0, row_ref.shape[1], place, 0, unroll=8)


def finish(miss, wave, raw, recv8, extra, sums, extra_sums):
    _, rows, _ = raw.shape
    misses = extra.shape[1]
    vmem = pl.BlockSpec(memory_space=pltpu.VMEM)
    smem = pl.BlockSpec(memory_space=pltpu.SMEM)
    return pl.pallas_call(
        finish_kernel,
        in_specs=[smem, smem] + [vmem] * 9,
        out_specs=vmem,
        out_shape=jax.ShapeDtypeStruct((2, rows, WIN), jnp.float32),
        scratch_shapes=[pltpu.VMEM((2, misses, WIN), jnp.float32)],
        compiler_params=pltpu.CompilerParams(vmem_limit_bytes=VMEM_LIMIT),
        cost_estimate=pl.CostEstimate(
            flops=20 * rows * WIN, bytes_accessed=36 * rows * WIN, transcendentals=0
        ),
        name="finish",
    )(miss, wave, raw, recv8, extra, *sums, *extra_sums)


def local(traces, recv_live, missing, wavelet):
    tile = traces.shape[1]
    grid_size = lax.axis_size("row")
    misses = missing.shape[1]
    order = recv_live.shape[0]
    row_index = lax.axis_index("row")
    col_index = lax.axis_index("col")
    mirror = [
        (a * grid_size + b, b * grid_size + a) for a in range(grid_size) for b in range(grid_size)
    ]

    def transpose(block):
        return lax.ppermute(block, ("row", "col"), mirror)

    raw = traces[:, :, :WIN]
    raw_turned = transpose(raw)

    miss_row = lax.dynamic_index_in_dim(missing, row_index, 0, keepdims=False)
    miss_col = lax.dynamic_index_in_dim(missing, col_index, 0, keepdims=False)
    miss_col_lanes = jnp.pad(miss_col, (0, LANES - misses), constant_values=-1)[None]
    positions = jnp.arange(tile, dtype=jnp.int32)
    live_row = jnp.all(positions[:, None] != miss_row[None, :], axis=1)
    live8 = jnp.broadcast_to(live_row.astype(jnp.float32)[None], (8, tile))
    recv_mask = (recv_live == 1).astype(jnp.bfloat16)
    recv_row = lax.dynamic_slice_in_dim(recv_mask, row_index * tile, WIN)
    recv_row8 = jnp.broadcast_to(recv_row[None], (8, WIN))
    recv_col = lax.dynamic_slice_in_dim(recv_mask, col_index * tile, tile)
    recv_col8 = jnp.broadcast_to(recv_col[None], (8, tile))

    picked = pick_columns(traces, miss_col_lanes, recv_col8, live8, misses)
    extra = transpose(picked)
    window = fill_window(raw_turned, picked[:, :, :WIN], miss_col_lanes, recv_row8)
    right = lax.all_gather(window, "row", axis=0, tiled=False)

    send, keep, send_extra, keep_extra = products(
        col_index[None].astype(jnp.int32), traces, recv_col8, right, extra
    )

    def swap(block, stride):
        pairs = [(i, i ^ stride) for i in range(grid_size)]
        return lax.ppermute(block, "col", pairs)

    def halve_from(kept, got):
        stride = 2
        while kept.shape[0] > 2:
            total = kept + got
            got = swap(total[1::2], stride)
            kept = total[0::2]
            stride *= 2
        last = swap(kept[1] + got[1], stride)
        return (kept[0], got[0], last)

    def scatter_sum(sent, kept):
        return halve_from(kept, swap(sent, 1))

    sums = scatter_sum(send, keep)
    extra_sums = scatter_sum(send_extra, keep_extra)
    wave = wavelet * (1.0 / math.sqrt(order))
    return finish(
        miss_row, wave, raw, recv_col8[:, :WIN], extra[:, :, :WIN], sums, extra_sums
    )


def solution(mesh):
    in_specs = (P("freq", "row", "col"), P("freq"), P("freq", None), P("freq"))
    out_specs = P("freq", "row", "col")
    return jax.shard_map(local, mesh=mesh, in_specs=in_specs, out_specs=out_specs, check_vma=False)
```

time: 449 us -> 212 us (0.47)
  waiting for transfers between devices: 229 us -> 144 us
  local copies, waits for them, and re-layouts: 74.4 us -> 8.14 us
  matrix products: 56.7 us -> 0 us
  other arithmetic: 58 us -> 5.43 us
  Pallas kernels: 0 us -> 29.9 us
  starting transfers between devices: 13.9 us -> 9.15 us
    ppermute x11 -> x6, waiting for transfers between devices: 185 us -> 65.1 us  [the longest x4 38.4 us: swap(): return lax.ppermute(block, 'col', pairs)]
    dot_general x16 -> x0, matrix products: 56.7 us -> none  [matmul(): return jnp.dot(first, second, preferred_element_type=jnp.float32)]
    select_n x7 -> x0, other arithmetic: 51.1 us -> none  [the longest x1 42 us: local(): direct = jnp.where(dead_row[None, :, None], zero_bf, direct)]
    all_gather x1, waiting for transfers between devices: 43.5 us -> 79 us  [local(): right = lax.all_gather(window, 'row', axis=0, tiled=False)]
    pallas_call x0 -> x4, Pallas kernels: none -> 29.9 us  [the longest x1 16 us: products(): pl.pallas_call(functools.partial(product_kernel, grid_size), grid_spec=pl...]
    unnamed x11 -> x24, local copies, waits for them, and re-layouts: 25.3 us -> 0.81 us
    scatter x2 -> x0, local copies, waits for them, and re-layouts: 20.5 us -> none  [local(): filled = direct.at[:, miss_row, :].set(patched)]
    slice x3, local copies, waits for them, and re-layouts: 21.3 us -> 4.1 us  [the longest x1 1.48 us: local(): picked[:, :, :WIN]]
  transfers between devices with their start and end apart: 12 -> 7, of which waited for: 11 -> 6; matrix products, arithmetic and copies ran while one was open for 14% -> 3% of each run, Pallas kernels for 0% -> 3%
where the time goes in v1:
time: 212 us; the launch traced here: 210 us
  waiting for transfers between devices  144 us (68%)
  Pallas kernels  29.9 us (14%)
  between operations  13.5 us (6%)
  starting transfers between devices  9.15 us (4%)
  local copies, waits for them, and re-layouts  8.14 us (4%)
  other arithmetic  5.43 us (3%)
    all_gather x1, waiting for transfers between devices, local(): right = lax.all_gather(window, 'row', axis=0, tiled=False)  79 us
    ppermute x4, waiting for transfers between devices, swap(): return lax.ppermute(block, 'col', pairs)  38.4 us
    ppermute x2, waiting for transfers between devices, transpose(): return lax.ppermute(block, ('row', 'col'), mirror)  26.7 us
    pallas_call x1, Pallas kernels, products(): pl.pallas_call(functools.partial(product_kernel, grid_size), grid_spec=pl...  16 us
    pallas_call x1, Pallas kernels, pick_columns(): pl.pallas_call(pick_kernel, grid=(rows // block,), in_specs=[pl.BlockSpec...  7.02 us
    ppermute x2, starting transfers between devices, transpose(): return lax.ppermute(block, ('row', 'col'), mirror)  6.52 us
    add x2, other arithmetic, halve_from(): last = swap(kept[1] + got[1], stride)  4.68 us
    pallas_call x1, Pallas kernels, finish(): pl.pallas_call(finish_kernel, in_specs=[smem, smem] + [vmem] * 9, out_spe...  4.41 us
  transfers between devices with their start and end apart: 7, of which 6 were waited for; matrix products, arithmetic and copies ran while one was open for 3% of the time, Pallas kernels for 3%

profile of v1, /device:TPU:1, one launch (start us, length us, event | category | flops | bytes accessed | tf_op | source)
XLA Modules:
  0.0 210.2 jit_solution(9857465858168943924)
XLA Ops:
  6.5 0.0 all-gather.3.cloned.1.call-start
  6.5 1.2 slice.38.raw_ref
  7.8 0.0 copy-start
  7.8 4.6 %collective-permute-start.1 = (bf16[2,1536,128]{2,1,0:T(8,128)(2,1)S(1)}, bf16[2,1536,128]{2,1,0:T(8,128)(2,1)S(1)}, u32[]{:S(2)}, u32[]{:S(2)}) collective-permute-start(bf16[2,1536,128]{2,1,0:T(8,128)(2,1)S(1)} %slice.38.raw_ref), channel_id=1, source_target_pairs={{0,0},{1,4},{2,8},{3,12},{4,1},{5,5},{6,9},{7,13},{8,2},{9,6},{10,... | collective-permute-start | bytes 2359304 | tf_op jit(solution)/shard_map/ppermute | solution.py:212
  12.4 0.0 copy-done.9
  12.4 0.0 copy-start.7
  12.4 0.1 fusion.1
  12.6 0.0 copy-done.6
  12.6 0.1 dynamic_slice.14
  12.7 0.5 pad_bitcast_fusion.miss_ref
  13.2 0.6 broadcast_in_dim.14.recv_ref
  13.8 0.6 broadcast_in_dim.15.live_ref
  14.4 7.0 %pick_columns.1 = bf16[2,96,1536]{2,1,0:T(8,128)(2,1)} custom-call(bf16[2,1536,1536]{2,1,0:T(8,128)(2,1)} %traces_ref.3, s32[1,128]{1,0:T(1,128)} %pad_bitcast_fusion.miss_ref, bf16[8,1536]{1,0:T(8,128)(2,1)} %broadcast_in_dim.14.recv_ref, f32[8,1536]{1,0:T(8,128)} %broadcast_in_dim.15.live_ref), custom_call_target="tpu_custom_call" | custom-call | flops 1207959552 | bytes 9437184 | tf_op jit(solution)/shard_map/pick_columns/pallas_call | solution.py:46
  21.4 0.0 copy-done
  21.4 0.0 copy-done.7
  21.5 0.0 copy-start.3
  21.5 1.5 slice.51.patch_ref
  22.9 0.1 fusion.3
  23.0 4.8 %collective-permute-done.1.raw_ref = bf16[2,1536,128]{2,1,0:T(8,128)(2,1)S(1)} collective-permute-done((bf16[2,1536,128]{2,1,0:T(8,128)(2,1)S(1)}, bf16[2,1536,128]{2,1,0:T(8,128)(2,1)S(1)}, u32[]{:S(2)}, u32[]{:S(2)}) %collective-permute-start.1) | collective-permute-done | bytes 786464 | tf_op jit(solution)/shard_map/ppermute | solution.py:212
  27.8 0.6 broadcast_in_dim.33.recv_ref
  28.5 0.2 copy-done.2
  28.7 2.5 %fill_window.1 = bf16[1536,256]{1,0:T(8,128)(2,1)} custom-call(bf16[2,1536,128]{2,1,0:T(8,128)(2,1)} %copy-done.2, bf16[2,96,128]{2,1,0:T(8,128)(2,1)} %slice.51.patch_ref, s32[1,128]{1,0:T(1,128)} %pad_bitcast_fusion.miss_ref, bf16[8,128]{1,0:T(8,128)(2,1)} %broadcast_in_dim.33.recv_ref), custom_call_target="tpu_custom_call" | custom-call | flops 100663296 | bytes 1572864 | tf_op jit(solution)/shard_map/fill_window/pallas_call | solution.py:81
  31.2 0.0 all-gather.3.cloned.1.call-update
  31.2 0.0 copy-done.3
  31.2 1.9 collective-permute-start
  33.1 21.9 %collective-permute-done.extra_ref = bf16[2,96,1536]{2,1,0:T(8,128)(2,1)S(1)} collective-permute-done((bf16[2,96,1536]{2,1,0:T(8,128)(2,1)S(1)}, bf16[2,96,1536]{2,1,0:T(8,128)(2,1)S(1)}, u32[]{:S(2)}, u32[]{:S(2)}) %collective-permute-start) | collective-permute-done | bytes 589856 | tf_op jit(solution)/shard_map/ppermute | solution.py:212
  55.0 79.0 %all-gather.3.cloned.1.call-done = bf16[6144,256]{1,0:T(8,128)(2,1)} async-done(((bf16[1536,256]{1,0:T(8,128)(2,1)}), bf16[6144,256]{1,0:T(8,128)(2,1)}) %all-gather.3.cloned.1.call-update) | async-done | bytes 3145744 | tf_op jit(solution)/shard_map/all_gather | solution.py:232
  134.0 0.0 copy-done.8
  134.0 16.0 %products.1 = (f32[2,1536,256]{2,1,0:T(8,128)}, f32[2,1536,256]{2,1,0:T(8,128)}, f32[2,96,256]{2,1,0:T(8,128)}, f32[2,96,256]{2,1,0:T(8,128)}) custom-call(s32[1]{0:T(128)} %bitcast.3.col_ref, bf16[2,1536,1536]{2,1,0:T(8,128)(2,1)} %traces_ref.3, bf16[8,1536]{1,0:T(8,128)(2,1)} %broadcast_in_dim.14.recv_ref, bf16[4,1536,256]{2,1,0:T(8,128)(2,1)} %bitcast.20, ...), custom_call_target="tpu_custom_call" | custom-call | flops 10267656192 | bytes 15728640 | tf_op jit(solution)/shard_map/products/pallas_call | solution.py:132
  150.0 0.5 collective-permute-start.2
  150.5 5.5 %collective-permute-done.2 = f32[2,1536,256]{2,1,0:T(8,128)S(1)} collective-permute-done((f32[2,1536,256]{2,1,0:T(8,128)}, f32[2,1536,256]{2,1,0:T(8,128)S(1)}, u32[]{:S(2)}, u32[]{:S(2)}) %collective-permute-start.2) | collective-permute-done | bytes 3145760 | tf_op jit(solution)/shard_map/ppermute | solution.py:240
  156.0 4.0 %fusion = (f32[1536,256]{1,0:T(8,128)S(1)}, f32[1536,256]{1,0:T(8,128)}, f32[1536,256]{1,0:T(8,128)}) fusion(f32[2,1536,256]{2,1,0:T(8,128)S(1)} %collective-permute-done.2, f32[2,1536,256]{2,1,0:T(8,128)} %get-tuple-element.9), kind=kLoop, calls=%fused_computation.1 | loop fusion | flops 393216 | bytes 11010048 | tf_op jit(solution)/shard_map/add | solution.py:249
  160.0 0.0 collective-permute-start.3
  160.0 0.0 copy-done.10
  160.0 0.4 collective-permute-start.4
  160.4 1.1 collective-permute-done.4
  161.4 0.0 copy-done.4
  161.4 0.7 fusion.2
  162.1 1.7 collective-permute-start.5
  163.9 0.0 copy-done.11
  163.9 0.6 broadcast_multiply_fusion.wave_ref
  164.5 1.4 slice.50.extra_ref
  165.9 31.8 %collective-permute-done.5.refs_5_ = f32[96,256]{1,0:T(8,128)S(1)} collective-permute-done((f32[96,256]{1,0:T(8,128)S(1)}, f32[96,256]{1,0:T(8,128)S(1)}, u32[]{:S(2)}, u32[]{:S(2)}) %collective-permute-start.5) | collective-permute-done | bytes 98336 | tf_op jit(solution)/shard_map/ppermute | solution.py:240
  197.7 0.0 collective-permute-done.3.refs_2_
  197.7 0.6 broadcast_in_dim.12.recv_ref
  198.4 0.0 copy-done.5
  198.4 0.5 copy-done.1
  198.9 4.4 %finish.1 = f32[2,1536,128]{2,1,0:T(8,128)} custom-call(s32[96]{0:T(128)} %copy-done.7, f32[2]{0:T(128)} %broadcast_multiply_fusion.wave_ref, bf16[2,1536,128]{2,1,0:T(8,128)(2,1)} %copy-done, bf16[8,128]{1,0:T(8,128)(2,1)} %broadcast_in_dim.12.recv_ref, bf16[2,96,128]{2,1,0:T(8,128)(2,1)} %slice.50.extra_ref, f32[1536,256]{1,0:T(8,128)} %get-tuple-element.14.refs_0_, ...), custom_call_target="tpu_custom_call" | custom-call | flops 3932160 | bytes 7077888 | tf_op jit(solution)/shard_map/finish/pallas_call | solution.py:186
  (12 shorter events, 0.0 us)
Async XLA Ops:
  6.5 5.8 %copy-start.9 = (s32[4,96]{1,0:T(4,128)S(1)}, s32[4,96]{1,0:T(4,128)}, u32[]{:S(2)}) copy-start(s32[4,96]{1,0:T(4,128)} %param.6) | copy-start | bytes 4612
  6.5 6.0 %copy-start.6 = (s32[6144]{0:T(1024)S(1)}, s32[6144]{0:T(1024)}, u32[]{:S(2)}) copy-start(s32[6144]{0:T(1024)} %param.5) | copy-start | bytes 73732
  6.5 127.5 %all-gather.3.cloned.1.call-start = ((), (), s32[]{:S(2)}) async-start(), calls=%async_computation | async-start | bytes 3932160 | tf_op jit(solution)/shard_map/all_gather | solution.py:232
  7.8 13.7 %copy-start = (bf16[2,1536,128]{2,1,0:T(8,128)(2,1)}, bf16[2,1536,128]{2,1,0:T(8,128)(2,1)S(1)}, u32[]{:S(2)}) copy-start(bf16[2,1536,128]{2,1,0:T(8,128)(2,1)S(1)} %slice.38.raw_ref) | copy-start | bytes 2359300
  7.8 20.1 %collective-permute-start.1 = (bf16[2,1536,128]{2,1,0:T(8,128)(2,1)S(1)}, bf16[2,1536,128]{2,1,0:T(8,128)(2,1)S(1)}, u32[]{:S(2)}, u32[]{:S(2)}) collective-permute-start(bf16[2,1536,128]{2,1,0:T(8,128)(2,1)S(1)} %slice.38.raw_ref), channel_id=1, source_target_pairs={{0,0},{1,4},{2,8},{3,12},{4,1},{5,5},{6,9},{7,13},{8,2},{9,6},{10,... | collective-permute-start | bytes 2359304 | tf_op jit(solution)/shard_map/ppermute | solution.py:212
  12.4 9.0 %copy-start.7 = (s32[96]{0:T(128)}, s32[96]{0:T(128)S(1)}, u32[]{:S(2)}) copy-start(s32[96]{0:T(128)S(1)} %get-tuple-element.22.miss_ref) | copy-start | bytes 1156
  21.5 9.7 %copy-start.3 = (bf16[2,96,1536]{2,1,0:T(8,128)(2,1)S(1)}, bf16[2,96,1536]{2,1,0:T(8,128)(2,1)}, u32[]{:S(2)}) copy-start(bf16[2,96,1536]{2,1,0:T(8,128)(2,1)} %pick_columns.1) | copy-start | bytes 1769476
  27.8 0.9 copy-start.2
  31.2 23.8 %collective-permute-start = (bf16[2,96,1536]{2,1,0:T(8,128)(2,1)S(1)}, bf16[2,96,1536]{2,1,0:T(8,128)(2,1)S(1)}, u32[]{:S(2)}, u32[]{:S(2)}) collective-permute-start(bf16[2,96,1536]{2,1,0:T(8,128)(2,1)S(1)} %copy-done.3), channel_id=1, source_target_pairs={{0,0},{1,4},{2,8},{3,12},{4,1},{5,5},{6,9},{7,13},{8,2},{9,6},{10,... | collective-permute-start | bytes 1769480 | tf_op jit(solution)/shard_map/ppermute | solution.py:212
  55.0 79.0 %copy-start.8 = (bf16[2,96,1536]{2,1,0:T(8,128)(2,1)}, bf16[2,96,1536]{2,1,0:T(8,128)(2,1)S(1)}, u32[]{:S(2)}) copy-start(bf16[2,96,1536]{2,1,0:T(8,128)(2,1)S(1)} %collective-permute-done.extra_ref) | copy-start | bytes 1769476
  150.0 6.0 %collective-permute-start.2 = (f32[2,1536,256]{2,1,0:T(8,128)}, f32[2,1536,256]{2,1,0:T(8,128)S(1)}, u32[]{:S(2)}, u32[]{:S(2)}) collective-permute-start(f32[2,1536,256]{2,1,0:T(8,128)} %get-tuple-element.10), channel_id=1, source_target_pairs={{0,1},{1,0},{2,3},{3,2},{4,5},{5,4},{6,7},{7,6},{8,9},{9,8},{10,11... | collective-permute-start | bytes 9437192 | tf_op jit(solution)/shard_map/ppermute | solution.py:240
  156.0 4.0 %copy-start.10 = (f32[2,96,256]{2,1,0:T(8,128)S(1)}, f32[2,96,256]{2,1,0:T(8,128)}, u32[]{:S(2)}) copy-start(f32[2,96,256]{2,1,0:T(8,128)} %get-tuple-element.12) | copy-start | bytes 589828
  156.0 5.4 %copy-start.4 = (f32[2,96,256]{2,1,0:T(8,128)S(1)}, f32[2,96,256]{2,1,0:T(8,128)}, u32[]{:S(2)}) copy-start(f32[2,96,256]{2,1,0:T(8,128)} %get-tuple-element.11) | copy-start | bytes 589828
  156.0 7.9 %copy-start.11 = (f32[2]{0:T(128)S(1)}, f32[2]{0:T(128)}, u32[]{:S(2)}) copy-start(f32[2]{0:T(128)} %param.7) | copy-start | bytes 28
  160.0 37.7 %collective-permute-start.3 = (f32[1536,256]{1,0:T(8,128)S(1)}, f32[1536,256]{1,0:T(8,128)S(1)}, u32[]{:S(2)}, u32[]{:S(2)}) collective-permute-start(f32[1536,256]{1,0:T(8,128)S(1)} %get-tuple-element.13), channel_id=1, source_target_pairs={{0,2},{1,3},{2,0},{3,1},{4,6},{5,7},{6,4},{7,5},{8,10},{9,11},{10,... | collective-permute-start | bytes 4718600 | tf_op jit(solution)/shard_map/ppermute | solution.py:240
  160.0 1.4 collective-permute-start.4
  162.1 35.6 %collective-permute-start.5 = (f32[96,256]{1,0:T(8,128)S(1)}, f32[96,256]{1,0:T(8,128)S(1)}, u32[]{:S(2)}, u32[]{:S(2)}) collective-permute-start(f32[96,256]{1,0:T(8,128)S(1)} %get-tuple-element.16), channel_id=1, source_target_pairs={{0,2},{1,3},{2,0},{3,1},{4,6},{5,7},{6,4},{7,5},{8,10},{9,11},{10,... | collective-permute-start | bytes 294920 | tf_op jit(solution)/shard_map/ppermute | solution.py:240
  197.7 0.7 copy-start.5
  197.7 1.2 copy-start.1
Sparse Core Ops, SparseCore 0:
  31.3 102.6 all-gather.2

commit v2 on v1

v2 whole, which is shorter than its diff:
```python
import functools
import math

import jax
import jax.numpy as jnp
from jax import lax
from jax.experimental import pallas as pl
from jax.experimental.pallas import tpu as pltpu
from jax.sharding import PartitionSpec as P

WIN = 128
LANES = 128
CHUNKS = 1
WIDTH = WIN // CHUNKS
VMEM_LIMIT = 48 * 2**20
VMEM = pl.BlockSpec(memory_space=pltpu.VMEM)
SMEM = pl.BlockSpec(memory_space=pltpu.SMEM)


def params():
    return pltpu.CompilerParams(vmem_limit_bytes=VMEM_LIMIT)


def cost(flops, accessed):
    return pl.CostEstimate(flops=int(flops), bytes_accessed=int(accessed), transcendentals=0)


def row_block(rows):
    for size in (512, 384, 256, 128):
        if rows % size == 0:
            return size
    return rows


def one_hot(positions_row, rows, dtype):
    lanes = positions_row.shape[1]
    row_ids = lax.broadcasted_iota(jnp.int32, (rows, lanes), 0)
    return jnp.where(row_ids == positions_row, 1.0, 0.0).astype(dtype)


def pack(real_part, imag_part):
    if CHUNKS == 1:
        return [jnp.concatenate([real_part, imag_part], axis=1)]
    first = lax.broadcasted_iota(jnp.int32, real_part.shape, 1) < WIDTH
    low = jnp.where(first, real_part, pltpu.roll(imag_part, WIDTH, 1))
    high = jnp.where(first, pltpu.roll(real_part, WIDTH, 1), imag_part)
    return [low, high]


def unpack(chunks):
    if CHUNKS == 1:
        return chunks[0][:, :WIN], chunks[0][:, WIN:]
    low, high = chunks
    first = lax.broadcasted_iota(jnp.int32, low.shape, 1) < WIDTH
    real_part = jnp.where(first, low, pltpu.roll(high, WIDTH, 1))
    imag_part = jnp.where(first, pltpu.roll(low, WIDTH, 1), high)
    return real_part, imag_part


def cut_kernel(traces_ref, *out_refs):
    chunks = pack(traces_ref[0].astype(jnp.float32), traces_ref[1].astype(jnp.float32))
    for out_ref, chunk in zip(out_refs, chunks):
        out_ref[...] = chunk.astype(jnp.bfloat16)


def cut_window(traces):
    rows = traces.shape[1]
    return pl.pallas_call(
        cut_kernel,
        grid=(1,),
        in_specs=[pl.BlockSpec((2, rows, WIN), lambda i: (0, 0, 0))],
        out_specs=[pl.BlockSpec((rows, 2 * WIDTH), lambda i: (0, 0))] * CHUNKS,
        out_shape=[jax.ShapeDtypeStruct((rows, 2 * WIDTH), jnp.bfloat16)] * CHUNKS,
        compiler_params=params(),
        cost_estimate=cost(rows * WIN, 8 * rows * WIN),
        name="cut_window",
    )(traces)


def pick_kernel(traces_ref, miss_ref, recv_ref, live_ref, out_ref, hot_ref):
    @pl.when(pl.program_id(0) == 0)
    def _():
        hot = one_hot(miss_ref[...], hot_ref.shape[0], jnp.bfloat16)
        alive = jnp.dot(recv_ref[...], hot, preferred_element_type=jnp.float32)
        hot_ref[...] = hot * alive[0:1].astype(jnp.bfloat16)

    misses = out_ref.shape[1]
    for part in range(2):
        picked = jnp.dot(traces_ref[part], hot_ref[...], preferred_element_type=jnp.float32)
        turned = picked.T * live_ref[0:1, :]
        out_ref[part] = turned[:misses].astype(jnp.bfloat16)


def pick_columns(traces, miss_lanes, recv8, live8, misses):
    _, rows, cols = traces.shape
    block = row_block(rows)
    return pl.pallas_call(
        pick_kernel,
        grid=(rows // block,),
        in_specs=[
            pl.BlockSpec((2, block, cols), lambda i: (0, i, 0)),
            pl.BlockSpec((1, LANES), lambda i: (0, 0)),
            pl.BlockSpec((8, cols), lambda i: (0, 0)),
            pl.BlockSpec((8, block), lambda i: (0, i)),
        ],
        out_specs=pl.BlockSpec((2, misses, block), lambda i: (0, 0, i)),
        out_shape=jax.ShapeDtypeStruct((2, misses, rows), jnp.bfloat16),
        scratch_shapes=[pltpu.VMEM((cols, LANES), jnp.bfloat16)],
        compiler_params=params(),
        cost_estimate=cost(4 * rows * cols * 2 * LANES, 4 * rows * cols),
        name="pick_columns",
    )(traces, miss_lanes, recv8, live8)


def fill_kernel(chunk, raw_ref, patch_ref, miss_ref, recv_ref, out_ref):
    rows = raw_ref.shape[0]
    misses = patch_ref.shape[1]
    hot = one_hot(miss_ref[...], rows, jnp.float32)
    dead = jnp.max(hot, axis=1, keepdims=True)
    hot = hot[:, :misses].astype(jnp.bfloat16)
    patch = pack(patch_ref[0].astype(jnp.float32), patch_ref[1].astype(jnp.float32))[chunk]
    mask = recv_ref[...].astype(jnp.float32)
    mask = pack(mask, mask)[chunk][0:1, :]
    moved = jnp.dot(hot, patch.astype(jnp.bfloat16), preferred_element_type=jnp.float32)
    filled = raw_ref[...].astype(jnp.float32) * ((1.0 - dead) * mask) + moved
    out_ref[...] = filled.astype(jnp.bfloat16)


def fill_window(chunk, raw, picked, miss_lanes, recv8):
    rows, lanes = raw.shape
    misses = picked.shape[1]
    return pl.pallas_call(
        functools.partial(fill_kernel, chunk),
        grid=(1,),
        in_specs=[
            pl.BlockSpec((rows, lanes), lambda i: (0, 0)),
            pl.BlockSpec((2, misses, WIN), lambda i: (0, 0, 0)),
            pl.BlockSpec((1, LANES), lambda i: (0, 0)),
            pl.BlockSpec((8, WIN), lambda i: (0, 0)),
        ],
        out_specs=pl.BlockSpec((rows, lanes), lambda i: (0, 0)),
        out_shape=jax.ShapeDtypeStruct((rows, lanes), jnp.bfloat16),
        compiler_params=params(),
        cost_estimate=cost(4 * rows * LANES * lanes, 8 * rows * lanes),
        name="fill_window",
    )(raw, picked, miss_lanes, recv8)


def complex_rows(real_rows, imag_rows, right):
    first = jnp.dot(real_rows, right, preferred_element_type=jnp.float32)
    second = jnp.dot(imag_rows, right, preferred_element_type=jnp.float32)
    if CHUNKS == 1:
        real_part = first[:, :WIN] - second[:, WIN:]
        imag_part = first[:, WIN:] + second[:, :WIN]
        return jnp.concatenate([real_part, imag_part], axis=1)
    turned = pltpu.roll(second, WIDTH, 1)
    low = lax.broadcasted_iota(jnp.int32, first.shape, 1) < WIDTH
    return first + jnp.where(low, -turned, turned)


def product_kernel(block, miss_ref, traces_ref, recv_ref, right_ref, extra_ref, out_ref, extra_out):
    step = pl.program_id(0)
    recv = recv_ref[0:1, :]
    right = right_ref[...]
    start = pl.multiple_of(step * block, block)
    out_ref[pl.ds(start, block), :] = complex_rows(
        traces_ref[0] * recv, traces_ref[1] * recv, right
    )

    @pl.when(step == pl.num_programs(0) - 1)
    def _():
        extra_out[...] = complex_rows(extra_ref[0], extra_ref[1], right)

        def place(m, carry):
            out_ref[pl.ds(miss_ref[m], 1), :] = extra_out[pl.ds(m, 1), :]
            return carry

        lax.fori_loop(0, extra_out.shape[0], place, 0, unroll=8)


def product(miss, traces, recv8, right, extra):
    _, rows, cols = traces.shape
    lanes = right.shape[1]
    misses = extra.shape[1]
    block = row_block(rows)
    return pl.pallas_call(
        functools.partial(product_kernel, block),
        grid_spec=pltpu.PrefetchScalarGridSpec(
            num_scalar_prefetch=1,
            grid=(rows // block,),
            in_specs=[
                pl.BlockSpec((2, block, cols), lambda i, m: (0, i, 0)),
                pl.BlockSpec((8, cols), lambda i, m: (0, 0)),
                pl.BlockSpec((cols, lanes), lambda i, m: (0, 0)),
                pl.BlockSpec((2, misses, cols), lambda i, m: (0, 0, 0)),
            ],
            out_specs=pl.BlockSpec((rows, lanes), lambda i, m: (0, 0)),
            scratch_shapes=[pltpu.VMEM((misses, lanes), jnp.float32)],
        ),
        out_shape=jax.ShapeDtypeStruct((rows, lanes), jnp.float32),
        compiler_params=params(),
        cost_estimate=cost(8 * rows * cols * WIN, 4 * rows * cols + 4 * rows * lanes),
        name="product",
    )(miss, traces, recv8, right, extra)


def own_kernel(miss_ref, traces_ref, recv_ref, extra_ref, out_ref, row_ref):
    recv = recv_ref[0:1, :].astype(jnp.float32)
    for part in range(2):
        out_ref[part] = traces_ref[part].astype(jnp.float32) * recv
        row_ref[part] = extra_ref[part].astype(jnp.float32)

    def place(m, carry):
        for part in range(2):
            out_ref[part, pl.ds(miss_ref[m], 1), :] = row_ref[part, pl.ds(m, 1), :]
        return carry

    lax.fori_loop(0, row_ref.shape[1], place, 0, unroll=8)


def own_window(miss, traces, recv8, extra):
    rows = traces.shape[1]
    misses = extra.shape[1]
    return pl.pallas_call(
        own_kernel,
        grid_spec=pltpu.PrefetchScalarGridSpec(
            num_scalar_prefetch=1,
            grid=(1,),
            in_specs=[
                pl.BlockSpec((2, rows, WIN), lambda i, m: (0, 0, 0)),
                pl.BlockSpec((8, WIN), lambda i, m: (0, 0)),
                pl.BlockSpec((2, misses, WIN), lambda i, m: (0, 0, 0)),
            ],
            out_specs=pl.BlockSpec((2, rows, WIN), lambda i, m: (0, 0, 0)),
            scratch_shapes=[pltpu.VMEM((2, misses, WIN), jnp.float32)],
        ),
        out_shape=jax.ShapeDtypeStruct((2, rows, WIN), jnp.float32),
        compiler_params=params(),
        cost_estimate=cost(4 * rows * WIN, 12 * rows * WIN),
        name="own_window",
    )(miss, traces, recv8, extra)


def finish_kernel(wave_ref, flag_ref, window_ref, *refs):
    out_ref = refs[-1]
    totals = []
    for chunk in range(CHUNKS):
        early_ref, last_ref, got_ref = refs[3 * chunk:3 * chunk + 3]
        totals.append(early_ref[...] + last_ref[...] * flag_ref[0] + got_ref[...])
    real_part, imag_part = unpack(totals)
    out_ref[0] = window_ref[0] - (real_part * wave_ref[0] - imag_part * wave_ref[1])
    out_ref[1] = window_ref[1] - (imag_part * wave_ref[0] + real_part * wave_ref[1])


def finish(wave, flag, window, terms):
    _, rows, _ = window.shape
    flat = [term for chunk in terms for term in chunk]
    return pl.pallas_call(
        finish_kernel,
        in_specs=[SMEM, SMEM] + [VMEM] * (1 + len(flat)),
        out_specs=VMEM,
        out_shape=jax.ShapeDtypeStruct(window.shape, jnp.float32),
        compiler_params=params(),
        cost_estimate=cost(20 * rows * WIN, 40 * rows * WIN),
        name="finish",
    )(wave, flag, window, *flat)


def spread(block, grid_size, row_index):
    up, down = [block], [block]
    for hop in range(1, grid_size):
        up.append(lax.ppermute(up[-1], "row", [(i, i + 1) for i in range(hop - 1, grid_size - 1)]))
        down.append(lax.ppermute(down[-1], "row", [(i + 1, i) for i in range(grid_size - hop)]))
    slots = [block]
    for offset in range(1, grid_size):
        chosen = None
        for row in range(grid_size):
            other = row ^ offset
            source = up[row - other] if other < row else down[other - row]
            chosen = source if chosen is None else jnp.where(row_index == row, source, chosen)
        slots.append(chosen)
    return slots


def sum_to_column(partial_sum, offset, grid_size):
    stride = 1
    while True:
        pairs = []
        for row in range(grid_size):
            for col in range(grid_size):
                apart = col ^ row ^ offset
                if apart % (2 * stride) == stride:
                    pairs.append((row * grid_size + col, row * grid_size + (col ^ stride)))
        got = lax.ppermute(partial_sum, ("row", "col"), pairs)
        stride *= 2
        if stride >= grid_size:
            return partial_sum, got
        partial_sum = partial_sum + got


def local(traces, recv_live, missing, wavelet):
    tile = traces.shape[1]
    grid_size = lax.axis_size("row")
    misses = missing.shape[1]
    order = recv_live.shape[0]
    row_index = lax.axis_index("row")
    col_index = lax.axis_index("col")
    mirror = [
        (a * grid_size + b, b * grid_size + a) for a in range(grid_size) for b in range(grid_size)
    ]

    def transpose(block):
        return lax.ppermute(block, ("row", "col"), mirror)

    turned = [transpose(chunk) for chunk in cut_window(traces)]

    miss_row = lax.dynamic_index_in_dim(missing, row_index, 0, keepdims=False)
    miss_col = lax.dynamic_index_in_dim(missing, col_index, 0, keepdims=False)
    miss_col_lanes = jnp.pad(miss_col, (0, LANES - misses), constant_values=-1)[None]
    positions = jnp.arange(tile, dtype=jnp.int32)
    live_row = jnp.all(positions[:, None] != miss_row[None, :], axis=1)
    live8 = jnp.broadcast_to(live_row.astype(jnp.float32)[None], (8, tile))
    recv_mask = (recv_live == 1).astype(jnp.bfloat16)
    recv_row = lax.dynamic_slice_in_dim(recv_mask, row_index * tile, WIN)
    recv_row8 = jnp.broadcast_to(recv_row[None], (8, WIN))
    recv_col = lax.dynamic_slice_in_dim(recv_mask, col_index * tile, tile)
    recv_col8 = jnp.broadcast_to(recv_col[None], (8, tile))

    picked = pick_columns(traces, miss_col_lanes, recv_col8, live8, misses)
    extra = transpose(picked)
    mine = row_index ^ col_index
    terms = []
    for chunk in range(CHUNKS):
        window = fill_window(chunk, turned[chunk], picked, miss_col_lanes, recv_row8)
        slots = spread(window, grid_size, row_index)
        early = None
        for offset in range(grid_size):
            partial_sum = product(miss_row, traces, recv_col8, slots[offset], extra)
            there, got = sum_to_column(partial_sum, offset, grid_size)
            if offset == grid_size - 1:
                terms.append((early, there, got))
                continue
            total = jnp.where(mine == offset, there, 0.0) + got
            early = total if early is None else early + total
    window = own_window(miss_row, traces, recv_col8, extra)
    wave = wavelet * (1.0 / math.sqrt(order))
    flag = (mine == grid_size - 1).astype(jnp.float32)[None]
    return finish(wave, flag, window, terms)


def solution(mesh):
    in_specs = (P("freq", "row", "col"), P("freq"), P("freq", None), P("freq"))
    out_specs = P("freq", "row", "col")
    return jax.shard_map(local, mesh=mesh, in_specs=in_specs, out_specs=out_specs, check_vma=False)
```

time: 212 us -> 201 us (0.948)
  waiting for transfers between devices: 144 us -> 106 us
  starting transfers between devices: 9.15 us -> 40.8 us
  between operations: 13.5 us -> 0.29 us
  Pallas kernels: 29.9 us -> 40.9 us
  local copies, waits for them, and re-layouts: 8.14 us -> 0.21 us
  other arithmetic: 5.43 us -> 12.1 us
    all_gather x1 -> x0, waiting for transfers between devices: 79 us -> none  [local(): right = lax.all_gather(window, 'row', axis=0, tiled=False)]
    ppermute x4 -> x14, waiting for transfers between devices: 38.4 us -> 91.6 us  [the longest x3 53.5 us: spread(): lax.ppermute(down[-1], 'row', [(i + 1, i) for i in range(grid_size - hop)])]
    ppermute x4 -> x14, starting transfers between devices: 2.63 us -> 31.6 us  [the longest x8 24.2 us: sum_to_column(): got = lax.ppermute(partial_sum, ('row', 'col'), pairs)]
    ppermute x2, waiting for transfers between devices: 26.7 us -> 13.9 us  [transpose(): return lax.ppermute(block, ('row', 'col'), mirror)]
    pallas_call x3 -> x8, Pallas kernels: 22.8 us -> 34.6 us  [the longest x4 28 us: product(): pl.pallas_call(functools.partial(product_kernel, block), grid_spec=pltpu....]
    add x2 -> x5, other arithmetic: 4.68 us -> 9.11 us  [the longest x4 5.67 us: sum_to_column(): partial_sum = partial_sum + got]
    slice x3 -> x0, local copies, waits for them, and re-layouts: 4.1 us -> none  [the longest x1 1.48 us: local(): picked[:, :, :WIN]]
    select_n x0 -> x2, other arithmetic: none -> 2.79 us  [spread(): jnp.where(row_index == row, source, chosen)]
  transfers between devices with their start and end apart: 7 -> 16, of which waited for: 6 -> 8; matrix products, arithmetic and copies ran while one was open for 3% -> 6% of each run, Pallas kernels for 3% -> 18%
where the time goes in v2:
time: 201 us; the launch traced here: 200 us
  waiting for transfers between devices  106 us (53%)
  Pallas kernels  40.9 us (20%)
  starting transfers between devices  40.8 us (20%)
  other arithmetic  12.1 us (6%)
    ppermute x3, waiting for transfers between devices, spread(): lax.ppermute(down[-1], 'row', [(i + 1, i) for i in range(grid_size - hop)])  53.5 us
    pallas_call x4, Pallas kernels, product(): pl.pallas_call(functools.partial(product_kernel, block), grid_spec=pltpu....  28 us
    ppermute x8, starting transfers between devices, sum_to_column(): got = lax.ppermute(partial_sum, ('row', 'col'), pairs)  24.2 us
    ppermute x8, waiting for transfers between devices, sum_to_column(): got = lax.ppermute(partial_sum, ('row', 'col'), pairs)  23.8 us
    ppermute x3, waiting for transfers between devices, spread(): lax.ppermute(up[-1], 'row', [(i, i + 1) for i in range(hop - 1, grid_size...  14.3 us
    ppermute x2, waiting for transfers between devices, transpose(): return lax.ppermute(block, ('row', 'col'), mirror)  13.9 us
    ppermute x2, starting transfers between devices, transpose(): return lax.ppermute(block, ('row', 'col'), mirror)  9.18 us
    pallas_call x1, Pallas kernels, pick_columns(): pl.pallas_call(pick_kernel, grid=(rows // block,), in_specs=[pl.BlockSpec...  6.27 us
  transfers between devices with their start and end apart: 16, of which 8 were waited for; matrix products, arithmetic and copies ran while one was open for 6% of the time, Pallas kernels for 18%

profile of v2, /device:TPU:1, one launch (start us, length us, event | category | flops | bytes accessed | tf_op | source)
XLA Modules:
  0.0 199.8 jit_solution(13467317022747690982)
XLA Ops:
  0.0 1.3 cut_window.1
  1.3 4.6 %collective-permute-start.1 = (bf16[1536,256]{1,0:T(8,128)(2,1)S(1)}, bf16[1536,256]{1,0:T(8,128)(2,1)S(1)}, u32[]{:S(2)}, u32[]{:S(2)}) collective-permute-start(bf16[1536,256]{1,0:T(8,128)(2,1)S(1)} %cut_window.1), channel_id=1, source_target_pairs={{0,0},{1,4},{2,8},{3,12},{4,1},{5,5},{6,9},{7,13},{8,2},{9,6},{10,... | collective-permute-start | bytes 2359304 | tf_op jit(solution)/shard_map/ppermute | solution.py:313
  5.9 0.1 fusion.1
  6.1 0.1 dynamic_slice.14
  6.2 0.1 dynamic_slice.16
  6.3 6.3 %pick_columns.1.patch_ref = bf16[2,96,1536]{2,1,0:T(8,128)(2,1)S(1)} custom-call(bf16[2,1536,1536]{2,1,0:T(8,128)(2,1)} %traces_ref.13, s32[1,128]{1,0:T(1,128)S(1)} %pad_bitcast_fusion.miss_ref, bf16[8,1536]{1,0:T(8,128)(2,1)S(1)} %broadcast_in_dim.36.recv_ref, f32[8,1536]{1,0:T(8,128)S(1)} %broadcast_in_dim.38.live_ref), custom_call_target="tpu_custom_call" | custom-call | flops 2415919104 | bytes 9437184 | tf_op jit(solution)/shard_map/pick_columns/pallas_call | solution.py:97
  12.6 8.8 %collective-permute-done.1.raw_ref = bf16[1536,256]{1,0:T(8,128)(2,1)S(1)} collective-permute-done((bf16[1536,256]{1,0:T(8,128)(2,1)S(1)}, bf16[1536,256]{1,0:T(8,128)(2,1)S(1)}, u32[]{:S(2)}, u32[]{:S(2)}) %collective-permute-start.1) | collective-permute-done | bytes 786464 | tf_op jit(solution)/shard_map/ppermute | solution.py:313
  21.3 0.4 fill_window.1.right_ref
  21.7 2.2 %collective-permute-start.4 = (bf16[1536,256]{1,0:T(8,128)(2,1)S(1)}, bf16[1536,256]{1,0:T(8,128)(2,1)}, u32[]{:S(2)}, u32[]{:S(2)}) collective-permute-start(bf16[1536,256]{1,0:T(8,128)(2,1)S(1)} %fill_window.1.right_ref), channel_id=1, source_target_pairs={{0,4},{4,8},{8,12},{1,5},{5,9},{9,13},{2,6},{6,10},{10,14},{3,7},{... | collective-permute-start | bytes 2359304 | tf_op jit(solution)/shard_map/ppermute | solution.py:272
  23.9 1.3 collective-permute-start.5
  25.2 14.3 %collective-permute-done.4 = bf16[1536,256]{1,0:T(8,128)(2,1)} collective-permute-done((bf16[1536,256]{1,0:T(8,128)(2,1)S(1)}, bf16[1536,256]{1,0:T(8,128)(2,1)}, u32[]{:S(2)}, u32[]{:S(2)}) %collective-permute-start.4) | collective-permute-done | bytes 786464 | tf_op jit(solution)/shard_map/ppermute | solution.py:272
  39.5 0.7 collective-permute-start.8
  40.2 25.2 %collective-permute-done.5 = bf16[1536,256]{1,0:T(8,128)(2,1)} collective-permute-done((bf16[1536,256]{1,0:T(8,128)(2,1)S(1)}, bf16[1536,256]{1,0:T(8,128)(2,1)}, u32[]{:S(2)}, u32[]{:S(2)}) %collective-permute-start.5) | collective-permute-done | bytes 786464 | tf_op jit(solution)/shard_map/ppermute | solution.py:273
  65.4 1.3 collective-permute-start.9
  66.7 4.6 %collective-permute-start = (bf16[2,96,1536]{2,1,0:T(8,128)(2,1)S(1)}, bf16[2,96,1536]{2,1,0:T(8,128)(2,1)S(1)}, u32[]{:S(2)}, u32[]{:S(2)}) collective-permute-start(bf16[2,96,1536]{2,1,0:T(8,128)(2,1)S(1)} %pick_columns.1.patch_ref), channel_id=1, source_target_pairs={{0,0},{1,4},{2,8},{3,12},{4,1},{5,5},{6,9},{7,13},{8,2},{9,6},{10,... | collective-permute-start | bytes 1769480 | tf_op jit(solution)/shard_map/ppermute | solution.py:313
  71.3 0.0 collective-permute-done.8
  71.3 0.7 collective-permute-start.12
  72.1 21.3 %collective-permute-done.9 = bf16[1536,256]{1,0:T(8,128)(2,1)} collective-permute-done((bf16[1536,256]{1,0:T(8,128)(2,1)}, bf16[1536,256]{1,0:T(8,128)(2,1)}, u32[]{:S(2)}, u32[]{:S(2)}) %collective-permute-start.9) | collective-permute-done | bytes 786464 | tf_op jit(solution)/shard_map/ppermute | solution.py:273
  93.3 1.3 collective-permute-start.13
  94.6 5.1 %collective-permute-done.extra_ref = bf16[2,96,1536]{2,1,0:T(8,128)(2,1)S(1)} collective-permute-done((bf16[2,96,1536]{2,1,0:T(8,128)(2,1)S(1)}, bf16[2,96,1536]{2,1,0:T(8,128)(2,1)S(1)}, u32[]{:S(2)}, u32[]{:S(2)}) %collective-permute-start) | collective-permute-done | bytes 589856 | tf_op jit(solution)/shard_map/ppermute | solution.py:313
  99.8 7.0 %product.4 = f32[1536,256]{1,0:T(8,128)S(1)} custom-call(s32[96]{0:T(128)S(1)} %get-tuple-element.8.miss_ref, bf16[2,1536,1536]{2,1,0:T(8,128)(2,1)} %traces_ref.13, bf16[8,1536]{1,0:T(8,128)(2,1)S(1)} %broadcast_in_dim.36.recv_ref, bf16[1536,256]{1,0:T(8,128)(2,1)S(1)} %fill_window.1.right_ref, bf16[2,96,1536]{2,1,0:T(8,128)(2,1)S(1)} %collective-permute-done.extra_ref), custom_call_target="tpu_custom_call" | custom-call | flops 2415919104 | bytes 11010048 | tf_op jit(solution)/shard_map/product/pallas_call | solution.py:186
  106.8 1.4 collective-permute-start.2
  108.1 1.2 select_select_fusion.right_ref
  109.4 7.0 %product.6 = f32[1536,256]{1,0:T(8,128)S(1)} custom-call(s32[96]{0:T(128)S(1)} %get-tuple-element.8.miss_ref, bf16[2,1536,1536]{2,1,0:T(8,128)(2,1)} %traces_ref.13, bf16[8,1536]{1,0:T(8,128)(2,1)S(1)} %broadcast_in_dim.36.recv_ref, bf16[1536,256]{1,0:T(8,128)(2,1)S(1)} %select_select_fusion.right_ref, bf16[2,96,1536]{2,1,0:T(8,128)(2,1)S(1)} %collective-permute-done.extra_ref), custom_call_target="tpu_custom_call" | custom-call | flops 2415919104 | bytes 11010048 | tf_op jit(solution)/shard_map/product/pallas_call | solution.py:186
  116.4 1.4 collective-permute-start.10
  117.8 7.0 %collective-permute-done.13 = bf16[1536,256]{1,0:T(8,128)(2,1)S(1)} collective-permute-done((bf16[1536,256]{1,0:T(8,128)(2,1)}, bf16[1536,256]{1,0:T(8,128)(2,1)S(1)}, u32[]{:S(2)}, u32[]{:S(2)}) %collective-permute-start.13) | collective-permute-done | bytes 786464 | tf_op jit(solution)/shard_map/ppermute | solution.py:273
  124.8 1.5 select_select_fusion.2
  126.3 7.0 %product.5 = f32[1536,256]{1,0:T(8,128)S(1)} custom-call(s32[96]{0:T(128)S(1)} %get-tuple-element.8.miss_ref, bf16[2,1536,1536]{2,1,0:T(8,128)(2,1)} %traces_ref.13, bf16[8,1536]{1,0:T(8,128)(2,1)S(1)} %broadcast_in_dim.36.recv_ref, bf16[1536,256]{1,0:T(8,128)(2,1)S(1)} %get-tuple-element.6.right_ref, bf16[2,96,1536]{2,1,0:T(8,128)(2,1)S(1)} %collective-permute-done.extra_ref), custom_call_target="tpu_custom_call" | custom-call | flops 2415919104 | bytes 11010048 | tf_op jit(solution)/shard_map/product/pallas_call | solution.py:186
  133.3 1.3 collective-permute-start.6
  134.6 7.0 %product.7 = f32[1536,256]{1,0:T(8,128)S(1)} custom-call(s32[96]{0:T(128)S(1)} %get-tuple-element.8.miss_ref, bf16[2,1536,1536]{2,1,0:T(8,128)(2,1)} %traces_ref.13, bf16[8,1536]{1,0:T(8,128)(2,1)S(1)} %broadcast_in_dim.36.recv_ref, bf16[1536,256]{1,0:T(8,128)(2,1)S(1)} %get-tuple-element.5.right_ref, bf16[2,96,1536]{2,1,0:T(8,128)(2,1)S(1)} %collective-permute-done.extra_ref), custom_call_target="tpu_custom_call" | custom-call | flops 2415919104 | bytes 11010048 | tf_op jit(solution)/shard_map/product/pallas_call | solution.py:186
  141.6 1.3 collective-permute-start.14
  142.9 1.4 add.46
  144.3 1.9 collective-permute-start.3
  146.2 0.0 collective-permute-done.10
  146.2 1.3 add.51
  147.5 1.8 collective-permute-start.11
  149.3 0.0 collective-permute-done.6
  149.3 2.7 %add.48 = f32[1536,256]{1,0:T(8,128)} add(f32[1536,256]{1,0:T(8,128)S(1)} %product.5, f32[1536,256]{1,0:T(8,128)} %collective-permute-done.6) | non-fusion elementwise | flops 393216 | bytes 4718592 | tf_op jit(solution)/shard_map/add | solution.py:298
  152.1 1.4 collective-permute-start.7
  153.5 0.0 collective-permute-done.14
  153.5 0.2 add.54.refs_1_
  153.7 13.7 %collective-permute-start.15 = (f32[1536,256]{1,0:T(8,128)S(1)}, f32[1536,256]{1,0:T(8,128)}, u32[]{:S(2)}, u32[]{:S(2)}) collective-permute-start(f32[1536,256]{1,0:T(8,128)S(1)} %add.54.refs_1_), channel_id=1, source_target_pairs={{1,3},{4,6},{11,9},{14,12},{17,19},{20,22},{27,25},{30,28}} | collective-permute-start | bytes 4718600 | tf_op jit(solution)/shard_map/ppermute | solution.py:294
  167.5 2.0 own_window.1.window_ref
  169.5 0.0 collective-permute-done.11
  169.5 23.1 %collective-permute-done.7 = f32[1536,256]{1,0:T(8,128)} collective-permute-done((f32[1536,256]{1,0:T(8,128)}, f32[1536,256]{1,0:T(8,128)}, u32[]{:S(2)}, u32[]{:S(2)}) %collective-permute-start.7) | collective-permute-done | bytes 1572896 | tf_op jit(solution)/shard_map/ppermute | solution.py:294
  192.5 3.4 %add_add_fusion.refs_0_ = f32[1536,256]{1,0:T(8,128)S(1)} fusion(f32[1536,256]{1,0:T(8,128)} %collective-permute-done.11, f32[1536,256]{1,0:T(8,128)} %add.51, f32[1536,256]{1,0:T(8,128)} %collective-permute-done.7, f32[1536,256]{1,0:T(8,128)} %add.48, f32[1536,256]{1,0:T(8,128)} %collective-permute-done.3, f32[1536,256]{1,0:T(8,128)} %add.46, pred[]{:T(512)S(6)} %eq.41, ...), kind=kLoop, calls=%fused_computation | loop fusion | flops 3145728 | bytes 11010051 | tf_op jit(solution)/shard_map/add | solution.py:344
  196.0 0.7 collective-permute-done.15.refs_2_
  196.7 3.0 %finish.1 = f32[2,1536,128]{2,1,0:T(8,128)} custom-call(f32[2]{0:T(128)S(1)} %broadcast_multiply_fusion.wave_ref, f32[1]{0:T(128)} %bitcast.flag_ref, f32[2,1536,128]{2,1,0:T(8,128)S(1)} %own_window.1.window_ref, f32[1536,256]{1,0:T(8,128)S(1)} %add_add_fusion.refs_0_, f32[1536,256]{1,0:T(8,128)S(1)} %add.54.refs_1_, f32[1536,256]{1,0:T(8,128)} %collective-permute-done.15.refs_2_), custom_call_target="tpu_custom_call" | custom-call | flops 3932160 | bytes 7864320 | tf_op jit(solution)/shard_map/finish/pallas_call | solution.py:258
  (17 shorter events, 0.1 us)
Async XLA Ops:
  0.0 5.9 %copy-start.1 = (s32[4,96]{1,0:T(4,128)S(1)}, s32[4,96]{1,0:T(4,128)}, u32[]{:S(2)}) copy-start(s32[4,96]{1,0:T(4,128)} %param.6) | copy-start | bytes 4612
  0.0 6.1 %copy-start = (s32[6144]{0:T(1024)S(1)}, s32[6144]{0:T(1024)}, u32[]{:S(2)}) copy-start(s32[6144]{0:T(1024)} %param.5) | copy-start | bytes 73732
  1.3 20.1 %collective-permute-start.1 = (bf16[1536,256]{1,0:T(8,128)(2,1)S(1)}, bf16[1536,256]{1,0:T(8,128)(2,1)S(1)}, u32[]{:S(2)}, u32[]{:S(2)}) collective-permute-start(bf16[1536,256]{1,0:T(8,128)(2,1)S(1)} %cut_window.1), channel_id=1, source_target_pairs={{0,0},{1,4},{2,8},{3,12},{4,1},{5,5},{6,9},{7,13},{8,2},{9,6},{10,... | collective-permute-start | bytes 2359304 | tf_op jit(solution)/shard_map/ppermute | solution.py:313
  21.7 17.8 %collective-permute-start.4 = (bf16[1536,256]{1,0:T(8,128)(2,1)S(1)}, bf16[1536,256]{1,0:T(8,128)(2,1)}, u32[]{:S(2)}, u32[]{:S(2)}) collective-permute-start(bf16[1536,256]{1,0:T(8,128)(2,1)S(1)} %fill_window.1.right_ref), channel_id=1, source_target_pairs={{0,4},{4,8},{8,12},{1,5},{5,9},{9,13},{2,6},{6,10},{10,14},{3,7},{... | collective-permute-start | bytes 2359304 | tf_op jit(solution)/shard_map/ppermute | solution.py:272
  23.9 41.5 %collective-permute-start.5 = (bf16[1536,256]{1,0:T(8,128)(2,1)S(1)}, bf16[1536,256]{1,0:T(8,128)(2,1)}, u32[]{:S(2)}, u32[]{:S(2)}) collective-permute-start(bf16[1536,256]{1,0:T(8,128)(2,1)S(1)} %fill_window.1.right_ref), channel_id=1, source_target_pairs={{4,0},{8,4},{12,8},{5,1},{9,5},{13,9},{6,2},{10,6},{14,10},{7,3},{... | collective-permute-start | bytes 2359304 | tf_op jit(solution)/shard_map/ppermute | solution.py:273
  39.5 31.8 %collective-permute-start.8 = (bf16[1536,256]{1,0:T(8,128)(2,1)}, bf16[1536,256]{1,0:T(8,128)(2,1)S(1)}, u32[]{:S(2)}, u32[]{:S(2)}) collective-permute-start(bf16[1536,256]{1,0:T(8,128)(2,1)} %collective-permute-done.4), channel_id=1, source_target_pairs={{4,8},{8,12},{5,9},{9,13},{6,10},{10,14},{7,11},{11,15},{20,24},{2... | collective-permute-start | bytes 2359304 | tf_op jit(solution)/shard_map/ppermute | solution.py:272
  65.4 27.9 %collective-permute-start.9 = (bf16[1536,256]{1,0:T(8,128)(2,1)}, bf16[1536,256]{1,0:T(8,128)(2,1)}, u32[]{:S(2)}, u32[]{:S(2)}) collective-permute-start(bf16[1536,256]{1,0:T(8,128)(2,1)} %collective-permute-done.5), channel_id=1, source_target_pairs={{4,0},{8,4},{5,1},{9,5},{6,2},{10,6},{7,3},{11,7},{20,16},{24,20},... | collective-permute-start | bytes 2359304 | tf_op jit(solution)/shard_map/ppermute | solution.py:273
  66.7 33.0 %collective-permute-start = (bf16[2,96,1536]{2,1,0:T(8,128)(2,1)S(1)}, bf16[2,96,1536]{2,1,0:T(8,128)(2,1)S(1)}, u32[]{:S(2)}, u32[]{:S(2)}) collective-permute-start(bf16[2,96,1536]{2,1,0:T(8,128)(2,1)S(1)} %pick_columns.1.patch_ref), channel_id=1, source_target_pairs={{0,0},{1,4},{2,8},{3,12},{4,1},{5,5},{6,9},{7,13},{8,2},{9,6},{10,... | collective-permute-start | bytes 1769480 | tf_op jit(solution)/shard_map/ppermute | solution.py:313
  71.3 46.5 %collective-permute-start.12 = (bf16[1536,256]{1,0:T(8,128)(2,1)S(1)}, bf16[1536,256]{1,0:T(8,128)(2,1)S(1)}, u32[]{:S(2)}, u32[]{:S(2)}) collective-permute-start(bf16[1536,256]{1,0:T(8,128)(2,1)S(1)} %collective-permute-done.8), channel_id=1, source_target_pairs={{8,12},{9,13},{10,14},{11,15},{24,28},{25,29},{26,30},{27,31}} | collective-permute-start | bytes 2359304 | tf_op jit(solution)/shard_map/ppermute | solution.py:272
  93.3 31.4 %collective-permute-start.13 = (bf16[1536,256]{1,0:T(8,128)(2,1)}, bf16[1536,256]{1,0:T(8,128)(2,1)S(1)}, u32[]{:S(2)}, u32[]{:S(2)}) collective-permute-start(bf16[1536,256]{1,0:T(8,128)(2,1)} %collective-permute-done.9), channel_id=1, source_target_pairs={{4,0},{5,1},{6,2},{7,3},{20,16},{21,17},{22,18},{23,19}} | collective-permute-start | bytes 2359304 | tf_op jit(solution)/shard_map/ppermute | solution.py:273
  106.8 36.2 %collective-permute-start.2 = (f32[1536,256]{1,0:T(8,128)S(1)}, f32[1536,256]{1,0:T(8,128)S(1)}, u32[]{:S(2)}, u32[]{:S(2)}) collective-permute-start(f32[1536,256]{1,0:T(8,128)S(1)} %product.4), channel_id=1, source_target_pairs={{1,0},{3,2},{4,5},{6,7},{9,8},{11,10},{12,13},{14,15},{17,16},{19,... | collective-permute-start | bytes 4718600 | tf_op jit(solution)/shard_map/ppermute | solution.py:294
  116.4 29.8 %collective-permute-start.10 = (f32[1536,256]{1,0:T(8,128)S(1)}, f32[1536,256]{1,0:T(8,128)S(1)}, u32[]{:S(2)}, u32[]{:S(2)}) collective-permute-start(f32[1536,256]{1,0:T(8,128)S(1)} %product.6), channel_id=1, source_target_pairs={{1,0},{3,2},{4,5},{6,7},{9,8},{11,10},{12,13},{14,15},{17,16},{19,... | collective-permute-start | bytes 4718600 | tf_op jit(solution)/shard_map/ppermute | solution.py:294
  133.3 16.0 %collective-permute-start.6 = (f32[1536,256]{1,0:T(8,128)S(1)}, f32[1536,256]{1,0:T(8,128)}, u32[]{:S(2)}, u32[]{:S(2)}) collective-permute-start(f32[1536,256]{1,0:T(8,128)S(1)} %product.5), channel_id=1, source_target_pairs={{0,1},{2,3},{5,4},{7,6},{8,9},{10,11},{13,12},{15,14},{16,17},{18,... | collective-permute-start | bytes 4718600 | tf_op jit(solution)/shard_map/ppermute | solution.py:294
  141.6 11.9 %collective-permute-start.14 = (f32[1536,256]{1,0:T(8,128)S(1)}, f32[1536,256]{1,0:T(8,128)S(1)}, u32[]{:S(2)}, u32[]{:S(2)}) collective-permute-start(f32[1536,256]{1,0:T(8,128)S(1)} %product.7), channel_id=1, source_target_pairs={{0,1},{2,3},{5,4},{7,6},{8,9},{10,11},{13,12},{15,14},{16,17},{18,... | collective-permute-start | bytes 4718600 | tf_op jit(solution)/shard_map/ppermute | solution.py:294
  144.3 25.2 %collective-permute-start.3 = (f32[1536,256]{1,0:T(8,128)}, f32[1536,256]{1,0:T(8,128)}, u32[]{:S(2)}, u32[]{:S(2)}) collective-permute-start(f32[1536,256]{1,0:T(8,128)} %add.46), channel_id=1, source_target_pairs={{2,0},{7,5},{8,10},{13,15},{18,16},{23,21},{24,26},{29,31}} | collective-permute-start | bytes 4718600 | tf_op jit(solution)/shard_map/ppermute | solution.py:294
  147.5 22.0 %collective-permute-start.11 = (f32[1536,256]{1,0:T(8,128)}, f32[1536,256]{1,0:T(8,128)}, u32[]{:S(2)}, u32[]{:S(2)}) collective-permute-start(f32[1536,256]{1,0:T(8,128)} %add.51), channel_id=1, source_target_pairs={{0,2},{5,7},{10,8},{15,13},{16,18},{21,23},{26,24},{31,29}} | collective-permute-start | bytes 4718600 | tf_op jit(solution)/shard_map/ppermute | solution.py:294
  152.1 15.4 %copy-start.2 = (f32[2]{0:T(128)S(1)}, f32[2]{0:T(128)}, u32[]{:S(2)}) copy-start(f32[2]{0:T(128)} %param.7) | copy-start | bytes 28
  152.1 40.4 %collective-permute-start.7 = (f32[1536,256]{1,0:T(8,128)}, f32[1536,256]{1,0:T(8,128)}, u32[]{:S(2)}, u32[]{:S(2)}) collective-permute-start(f32[1536,256]{1,0:T(8,128)} %add.48), channel_id=1, source_target_pairs={{3,1},{6,4},{9,11},{12,14},{19,17},{22,20},{25,27},{28,30}} | collective-permute-start | bytes 4718600 | tf_op jit(solution)/shard_map/ppermute | solution.py:294
  153.7 43.0 %collective-permute-start.15 = (f32[1536,256]{1,0:T(8,128)S(1)}, f32[1536,256]{1,0:T(8,128)}, u32[]{:S(2)}, u32[]{:S(2)}) collective-permute-start(f32[1536,256]{1,0:T(8,128)S(1)} %add.54.refs_1_), channel_id=1, source_target_pairs={{1,3},{4,6},{11,9},{14,12},{17,19},{20,22},{27,25},{30,28}} | collective-permute-start | bytes 4718600 | tf_op jit(solution)/shard_map/ppermute | solution.py:294

commit v3 on v2

v3 whole, which is shorter than its diff:
```python
import functools
import math

import jax
import jax.numpy as jnp
from jax import lax
from jax.experimental import pallas as pl
from jax.experimental.pallas import tpu as pltpu
from jax.sharding import PartitionSpec as P

WIN = 128
LANES = 128
CHUNKS = 1
WIDTH = WIN // CHUNKS
VMEM_LIMIT = 32 * 2**20
VMEM = pl.BlockSpec(memory_space=pltpu.VMEM)
SMEM = pl.BlockSpec(memory_space=pltpu.SMEM)


def params():
    return pltpu.CompilerParams(vmem_limit_bytes=VMEM_LIMIT)


def cost(flops, accessed):
    return pl.CostEstimate(
        flops=int(flops) // 64, bytes_accessed=int(accessed) // 64, transcendentals=0
    )


def row_block(rows):
    for size in (512, 384, 256, 128):
        if rows % size == 0:
            return size
    return rows


def one_hot(positions_row, rows, dtype):
    lanes = positions_row.shape[1]
    row_ids = lax.broadcasted_iota(jnp.int32, (rows, lanes), 0)
    return jnp.where(row_ids == positions_row, 1.0, 0.0).astype(dtype)


def pack(real_part, imag_part):
    if CHUNKS == 1:
        return [jnp.concatenate([real_part, imag_part], axis=1)]
    first = lax.broadcasted_iota(jnp.int32, real_part.shape, 1) < WIDTH
    low = jnp.where(first, real_part, pltpu.roll(imag_part, WIDTH, 1))
    high = jnp.where(first, pltpu.roll(real_part, WIDTH, 1), imag_part)
    return [low, high]


def unpack(chunks):
    if CHUNKS == 1:
        return chunks[0][:, :WIN], chunks[0][:, WIN:]
    low, high = chunks
    first = lax.broadcasted_iota(jnp.int32, low.shape, 1) < WIDTH
    real_part = jnp.where(first, low, pltpu.roll(high, WIDTH, 1))
    imag_part = jnp.where(first, pltpu.roll(low, WIDTH, 1), high)
    return real_part, imag_part


def halves(real_part, imag_part):
    return [real_part, imag_part] if CHUNKS == 1 else pack(real_part, imag_part)


def cut_kernel(traces_ref, *out_refs):
    parts = halves(traces_ref[0].astype(jnp.float32), traces_ref[1].astype(jnp.float32))
    for out_ref, part in zip(out_refs, parts):
        out_ref[...] = part.astype(jnp.bfloat16)


def cut_window(traces):
    rows = traces.shape[1]
    return pl.pallas_call(
        cut_kernel,
        grid=(1,),
        in_specs=[pl.BlockSpec((2, rows, WIN), lambda i: (0, 0, 0))],
        out_specs=[pl.BlockSpec((rows, WIN), lambda i: (0, 0))] * 2,
        out_shape=[jax.ShapeDtypeStruct((rows, WIN), jnp.bfloat16)] * 2,
        compiler_params=params(),
        cost_estimate=cost(rows * WIN, 8 * rows * WIN),
        name="cut_window",
    )(traces)


def pick_kernel(traces_ref, miss_ref, recv_ref, live_ref, out_ref, tile_ref, hot_ref):
    @pl.when(pl.program_id(0) == 0)
    def _():
        hot = one_hot(miss_ref[...], hot_ref.shape[0], jnp.bfloat16)
        alive = jnp.dot(recv_ref[...], hot, preferred_element_type=jnp.float32)
        hot_ref[...] = hot * alive[0:1].astype(jnp.bfloat16)

    misses = out_ref.shape[1]
    for part in range(2):
        picked = jnp.dot(traces_ref[part], hot_ref[...], preferred_element_type=jnp.float32)
        turned = picked.T * live_ref[0:1, :]
        out_ref[part] = turned[:misses].astype(jnp.bfloat16)
        tile_ref[part] = traces_ref[part] * recv_ref[0:1, :]


def pick_columns(traces, miss_lanes, recv8, live8, misses):
    _, rows, cols = traces.shape
    block = row_block(rows)
    return pl.pallas_call(
        pick_kernel,
        grid=(rows // block,),
        in_specs=[
            pl.BlockSpec((2, block, cols), lambda i: (0, i, 0)),
            pl.BlockSpec((1, LANES), lambda i: (0, 0)),
            pl.BlockSpec((8, cols), lambda i: (0, 0)),
            pl.BlockSpec((8, block), lambda i: (0, i)),
        ],
        out_specs=[
            pl.BlockSpec((2, misses, block), lambda i: (0, 0, i)),
            pl.BlockSpec((2, block, cols), lambda i: (0, i, 0)),
        ],
        out_shape=[
            jax.ShapeDtypeStruct((2, misses, rows), jnp.bfloat16),
            jax.ShapeDtypeStruct(traces.shape, jnp.bfloat16),
        ],
        scratch_shapes=[pltpu.VMEM((cols, LANES), jnp.bfloat16)],
        compiler_params=params(),
        cost_estimate=cost(4 * rows * cols * 2 * LANES, 4 * rows * cols),
        name="pick_columns",
    )(traces, miss_lanes, recv8, live8)


def fill_kernel(counts, first_half, patch_ref, miss_ref, recv_ref, *refs):
    out_ref = refs[-1]
    rows = out_ref.shape[0]
    misses = patch_ref.shape[1]
    hot = one_hot(miss_ref[...], rows, jnp.float32)
    dead = jnp.max(hot, axis=1, keepdims=True)
    hot = hot[:, :misses].astype(jnp.bfloat16)
    patches = halves(patch_ref[0].astype(jnp.float32), patch_ref[1].astype(jnp.float32))
    mask = recv_ref[...].astype(jnp.float32)
    mask = halves(mask, mask)[0][0:1, :]
    used = 0
    for index, count in enumerate(counts):
        arrived = refs[used][...].astype(jnp.float32)
        for more in refs[used + 1:used + count]:
            arrived = arrived + more[...].astype(jnp.float32)
        used += count
        patch = patches[first_half + index].astype(jnp.bfloat16)
        moved = jnp.dot(hot, patch, preferred_element_type=jnp.float32)
        filled = arrived * ((1.0 - dead) * mask) + moved
        out_ref[:, index * WIN:(index + 1) * WIN] = filled.astype(jnp.bfloat16)


def fill_window(first_half, arrived, picked, miss_lanes, recv8):
    rows = arrived[0][0].shape[0]
    misses = picked.shape[1]
    counts = tuple(len(group) for group in arrived)
    flat = [part for group in arrived for part in group]
    lanes = len(counts) * WIN
    whole = pl.BlockSpec((rows, WIN), lambda i: (0, 0))
    return pl.pallas_call(
        functools.partial(fill_kernel, counts, first_half),
        grid=(1,),
        in_specs=[
            pl.BlockSpec((2, misses, WIN), lambda i: (0, 0, 0)),
            pl.BlockSpec((1, LANES), lambda i: (0, 0)),
            pl.BlockSpec((8, WIN), lambda i: (0, 0)),
        ]
        + [whole] * len(flat),
        out_specs=pl.BlockSpec((rows, lanes), lambda i: (0, 0)),
        out_shape=jax.ShapeDtypeStruct((rows, lanes), jnp.bfloat16),
        compiler_params=params(),
        cost_estimate=cost(4 * rows * LANES * lanes, 8 * rows * lanes),
        name="fill_window",
    )(picked, miss_lanes, recv8, *flat)


def complex_rows(real_rows, imag_rows, right):
    first = jnp.dot(real_rows, right, preferred_element_type=jnp.float32)
    second = jnp.dot(imag_rows, right, preferred_element_type=jnp.float32)
    if CHUNKS == 1:
        real_part = first[:, :WIN] - second[:, WIN:]
        imag_part = first[:, WIN:] + second[:, :WIN]
        return jnp.concatenate([real_part, imag_part], axis=1)
    turned = pltpu.roll(second, WIDTH, 1)
    low = lax.broadcasted_iota(jnp.int32, first.shape, 1) < WIDTH
    return first + jnp.where(low, -turned, turned)


def choose(out_ref, pick, refs):
    for index, ref in enumerate(refs):

        @pl.when(pick == index)
        def _():
            out_ref[...] = ref[...]


def product_kernel(block, counts, pick_ref, tile_ref, *refs):
    total = sum(counts)
    out_refs, right_ref = refs[total:-1], refs[-1]
    used = 0
    for place, (count, out_ref) in enumerate(zip(counts, out_refs)):
        choose(right_ref, pick_ref[place], refs[used:used + count])
        used += count
        for start in range(0, out_ref.shape[0], block):
            rows = pl.ds(start, block)
            out_ref[rows, :] = complex_rows(
                tile_ref[0, rows, :], tile_ref[1, rows, :], right_ref[...]
            )


def products(tile, groups):
    _, rows, cols = tile.shape
    lanes = groups[0][1][0].shape[1]
    counts = tuple(len(sources) for _, sources in groups)
    flat = [source for _, sources in groups for source in sources]
    picks = jnp.stack([pick for pick, _ in groups]).astype(jnp.int32)
    return pl.pallas_call(
        functools.partial(product_kernel, row_block(rows), counts),
        in_specs=[SMEM] + [VMEM] * (1 + len(flat)),
        out_specs=[VMEM] * len(groups),
        out_shape=[jax.ShapeDtypeStruct((rows, lanes), jnp.float32)] * len(groups),
        scratch_shapes=[pltpu.VMEM((cols, lanes), jnp.bfloat16)],
        compiler_params=params(),
        cost_estimate=cost(8 * rows * cols * lanes * len(groups), 4 * rows * lanes),
        name="products",
    )(picks, tile, *flat)


def extra_kernel(counts, pick_ref, rows_ref, *refs):
    out_ref, right_ref = refs[-2:]
    used = 0
    for place, count in enumerate(counts):
        choose(right_ref, pick_ref[2 * place], refs[used:used + count])
        used += count
        out_ref[pick_ref[2 * place + 1]] = complex_rows(rows_ref[0], rows_ref[1], right_ref[...])


def extra_products(rows, groups):
    _, misses, cols = rows.shape
    lanes = groups[0][2][0].shape[1]
    counts = tuple(len(sources) for _, _, sources in groups)
    flat = [source for _, _, sources in groups for source in sources]
    picks = jnp.stack([x for pick, place, _ in groups for x in (pick, place)]).astype(jnp.int32)
    return pl.pallas_call(
        functools.partial(extra_kernel, counts),
        in_specs=[SMEM] + [VMEM] * (1 + len(flat)),
        out_specs=VMEM,
        out_shape=jax.ShapeDtypeStruct((len(groups), misses, lanes), jnp.float32),
        scratch_shapes=[pltpu.VMEM((cols, lanes), jnp.bfloat16)],
        compiler_params=params(),
        cost_estimate=cost(8 * misses * cols * lanes * len(groups), 4 * cols * lanes),
        name="extra_products",
    )(picks, rows, *flat)


def finish_kernel(counts, wave_ref, flag_ref, miss_ref, tile_ref, extra_ref, *refs):
    out_ref, row_ref = refs[-2:]
    totals = []
    used = 0
    for count in counts:
        total = refs[used][...]
        if count > 1:
            total = total * flag_ref[0]
        for ref in refs[used + 1:used + count]:
            total = total + ref[...]
        used += count
        totals.append(total)

    def write(target, window_ref, chunks):
        real_part, imag_part = unpack(chunks)
        real_pred = real_part * wave_ref[0] - imag_part * wave_ref[1]
        imag_pred = imag_part * wave_ref[0] + real_part * wave_ref[1]
        target[0] = window_ref[0].astype(jnp.float32) - real_pred
        target[1] = window_ref[1].astype(jnp.float32) - imag_pred

    write(out_ref, tile_ref, totals[:CHUNKS])
    write(row_ref, extra_ref, totals[CHUNKS:])

    def place(m, carry):
        for part in range(2):
            out_ref[part, pl.ds(miss_ref[m], 1), :] = row_ref[part, pl.ds(m, 1), :]
        return carry

    lax.fori_loop(0, row_ref.shape[1], place, 0, unroll=8)


def finish(wave, flag, miss, tile, extra, terms):
    _, rows, _ = tile.shape
    misses = extra.shape[1]
    counts = tuple(len(group) for group in terms)
    flat = [term for group in terms for term in group]
    window = lambda size: pl.BlockSpec((2, size, WIN), lambda i: (0, 0, 0))
    return pl.pallas_call(
        functools.partial(finish_kernel, counts),
        grid=(1,),
        in_specs=[SMEM, SMEM, SMEM, window(rows), window(misses)] + [VMEM] * len(flat),
        out_specs=window(rows),
        out_shape=jax.ShapeDtypeStruct((2, rows, WIN), jnp.float32),
        scratch_shapes=[pltpu.VMEM((2, misses, WIN), jnp.float32)],
        compiler_params=params(),
        cost_estimate=cost(20 * rows * WIN, 40 * rows * WIN),
        name="finish",
    )(wave, flag, miss, tile, extra, *flat)


def mirror_routes(grid_size):
    cells = [(a, b) for a in range(grid_size) for b in range(grid_size)]
    index = lambda row, col: row * grid_size + col
    whole = [(index(a, b), index(b, a)) for a, b in cells]
    near = [(index(a, b), index(b, a)) for a, b in cells if a // 2 == b // 2]
    far = [(a, b) for a, b in cells if a // 2 != b // 2]
    hop = lambda a, b: index(b, b // 2 * 2 + a % 2)
    first = [(index(a, b), hop(a, b)) for a, b in far]
    second = [(hop(a, b), index(b, a)) for a, b in far]
    if len({target for _, target in first}) < len(first):
        return whole, None
    return whole, (near, first, second)


def sources_of(up, down, offset, grid_size, row_index):
    places, sources = [], []
    for row in range(grid_size):
        other = row ^ offset
        source = up[row - other] if other < row else down[other - row]
        known = [index for index, seen in enumerate(sources) if seen is source]
        places.append(known[0] if known else len(sources))
        if not known:
            sources.append(source)
    pick = jnp.zeros((), jnp.int32)
    for row, place in enumerate(places):
        pick = jnp.where(row_index == row, place, pick)
    return pick, sources


def sum_route(offset, grid_size, stride, skip):
    route = []
    for row in range(grid_size):
        for col in range(grid_size):
            if ((col ^ row ^ offset) & ~skip) % (2 * stride) == stride:
                route.append((row * grid_size + col, row * grid_size + (col ^ stride)))
    return route


def local(traces, recv_live, missing, wavelet):
    tile = traces.shape[1]
    grid_size = lax.axis_size("row")
    misses = missing.shape[1]
    order = recv_live.shape[0]
    row_index = lax.axis_index("row")
    col_index = lax.axis_index("col")
    whole, hops = mirror_routes(grid_size)

    def move(block, route):
        return lax.ppermute(block, ("row", "col"), route)

    def transpose(block):
        return move(block, whole)

    def transpose_round(block):
        if hops is None:
            return [move(block, whole)]
        near, first, second = hops
        return [move(move(block, first), second), move(block, near)]

    direct, round_about = cut_window(traces)
    arrived = [[transpose(direct)], transpose_round(round_about)]
    if CHUNKS == 1:
        arrived = [arrived]
    else:
        arrived = [arrived[:1], arrived[1:]]

    miss_row = lax.dynamic_index_in_dim(missing, row_index, 0, keepdims=False)
    miss_col = lax.dynamic_index_in_dim(missing, col_index, 0, keepdims=False)
    as_lanes = lambda m: jnp.pad(m, (0, LANES - misses), constant_values=-1)[None]
    miss_col_lanes = as_lanes(miss_col)
    positions = jnp.arange(tile, dtype=jnp.int32)
    live_row = jnp.all(positions[:, None] != miss_row[None, :], axis=1)
    live8 = jnp.broadcast_to(live_row.astype(jnp.float32)[None], (8, tile))
    recv_mask = (recv_live == 1).astype(jnp.bfloat16)
    recv_row = lax.dynamic_slice_in_dim(recv_mask, row_index * tile, WIN)
    recv_row8 = jnp.broadcast_to(recv_row[None], (8, WIN))
    recv_col = lax.dynamic_slice_in_dim(recv_mask, col_index * tile, tile)
    recv_col8 = jnp.broadcast_to(recv_col[None], (8, tile))

    picked, tile_masked = pick_columns(traces, miss_col_lanes, recv_col8, live8, misses)
    extra = transpose(picked)
    apart = row_index ^ col_index
    strides = [2**bit for bit in range(grid_size.bit_length() - 1)]
    terms, extra_terms = [], []
    for chunk in range(CHUNKS):
        window = fill_window(chunk, arrived[chunk], picked, miss_col_lanes, recv_row8)
        up, down = [window], [window]
        sums = []

        def hop(distance):
            ends = [(i, i + 1) for i in range(distance - 1, grid_size - 1)]
            back = [(i + 1, i) for i in range(grid_size - distance)]
            up.append(lax.ppermute(up[-1], "row", ends))
            down.append(lax.ppermute(down[-1], "row", back))

        def add_up(total, offset, strides, skip):
            for stride in strides:
                total = total + move(total, sum_route(offset, grid_size, stride, skip))
            return total

        def last(total, offset, skip):
            return move(total, sum_route(offset, grid_size, strides[-1], skip))

        def options(offset):
            return sources_of(up, down, offset, grid_size, row_index)

        hop(1)
        hop(2)
        _, (block0,) = options(0)
        pick1, sources1 = options(1)
        odd = apart & 1
        everything = [block0] + sources1
        keep, sent = products(
            tile_masked,
            [
                (jnp.where(odd == 1, 1 + pick1, 0), everything),
                (jnp.where(odd == 1, 0, 1 + pick1), everything),
            ],
        )
        other_core = [(i, i ^ 1) for i in range(grid_size)]
        total = add_up(keep + lax.ppermute(sent, "col", other_core), 0, strides[1:-1], 1)
        up[-1], down[-1], total = lax.optimization_barrier((up[-1], down[-1], total))
        for distance in range(3, grid_size):
            hop(distance)
        got = last(total, 0, 1)
        tile, extra = lax.optimization_barrier((tile_masked, extra))
        early = None
        for offset in range(2, grid_size):
            mine = apart // 2 == 0 if offset == 2 else apart == offset - 1
            (new,) = products(tile, [options(offset)])
            new = add_up(new, offset, strides[:-1], 0)
            if offset < grid_size - 1:
                tile, got, new = lax.optimization_barrier((tile, got, new))
            term = jnp.where(mine, total, 0.0) + got
            early = term if early is None else early + term
            total, got = new, last(new, offset, 0)
        terms.append((total, early, got))
        group = [(pick, apart ^ offset, sources) for offset in range(grid_size)
                 for pick, sources in [options(offset)]]
        rest = extra_products(extra, group)
        for stride in strides:
            pairs = [(i, i ^ stride) for i in range(grid_size)]
            arrive = lax.ppermute(rest[1::2], "col", pairs)
            rest = rest[0::2] + arrive
        extra_terms.append((rest[0],))
    wave = wavelet * (1.0 / math.sqrt(order))
    flag = (apart == grid_size - 1).astype(jnp.float32)[None]
    return finish(wave, flag, miss_row, tile_masked, extra, terms + extra_terms)


def solution(mesh):
    in_specs = (P("freq", "row", "col"), P("freq"), P("freq", None), P("freq"))
    out_specs = P("freq", "row", "col")
    return jax.shard_map(local, mesh=mesh, in_specs=in_specs, out_specs=out_specs, check_vma=False)
```

time: 201 us -> 248 us (1.23)
  local copies, waits for them, and re-layouts: 0.21 us -> 27.2 us
  starting transfers between devices: 40.8 us -> 57.2 us
  waiting for transfers between devices: 106 us -> 120 us
  Pallas kernels: 40.9 us -> 30.3 us
    unnamed x6 -> x22, local copies, waits for them, and re-layouts: 0.01 us -> 26.9 us
    ppermute x16 -> x19, starting transfers between devices: 40.8 us -> 57.2 us  [the longest x10 26.9 us: move(): return lax.ppermute(block, ('row', 'col'), route)]
    ppermute x16 -> x19, waiting for transfers between devices: 106 us -> 120 us  [the longest x10 75.3 us: move(): return lax.ppermute(block, ('row', 'col'), route)]
    pallas_call x7 -> x6, Pallas kernels: 33.4 us -> 24.5 us  [the longest x3 17.1 us: products(): pl.pallas_call(functools.partial(product_kernel, row_block(rows), counts)...]
    select_n x2 -> x0, other arithmetic: 2.79 us -> none  [spread(): jnp.where(row_index == row, source, chosen)]
  transfers between devices with their start and end apart: 16 -> 19, of which waited for: 8 -> 6; matrix products, arithmetic and copies ran while one was open for 6% -> 5% of each run, Pallas kernels for 18% -> 4%
where the time goes in v3:
time: 248 us; the launch traced here: 247 us
  waiting for transfers between devices  120 us (48%)
  starting transfers between devices  57.2 us (23%)
  Pallas kernels  30.3 us (12%)
  local copies, waits for them, and re-layouts  27.2 us (11%)
  other arithmetic  11.6 us (5%)
    ppermute x10, waiting for transfers between devices, move(): return lax.ppermute(block, ('row', 'col'), route)  75.3 us
    ppermute x2, waiting for transfers between devices, local(): arrive = lax.ppermute(rest[1::2], 'col', pairs)  28.1 us
    unnamed x22, local copies, waits for them, and re-layouts  26.9 us
    ppermute x10, starting transfers between devices, move(): return lax.ppermute(block, ('row', 'col'), route)  26.9 us
    ppermute x3, starting transfers between devices, hop(): up.append(lax.ppermute(up[-1], 'row', ends))  22.3 us
    pallas_call x3, Pallas kernels, products(): pl.pallas_call(functools.partial(product_kernel, row_block(rows), counts)...  17.1 us
    ppermute x3, waiting for transfers between devices, hop(): down.append(lax.ppermute(down[-1], 'row', back))  15.9 us
    pallas_call x1, Pallas kernels, pick_columns(): pl.pallas_call(pick_kernel, grid=(rows // block,), in_specs=[pl.BlockSpec...  5.51 us
  transfers between devices with their start and end apart: 19, of which 6 were waited for; matrix products, arithmetic and copies ran while one was open for 5% of the time, Pallas kernels for 4%

profile of v3, /device:TPU:1, one launch (start us, length us, event | category | flops | bytes accessed | tf_op | source)
XLA Modules:
  0.0 247.0 jit_solution(590530359652230278)
XLA Ops:
  0.0 3.7 %copy-done.5 = bf16[2,1536,1536]{2,1,0:T(8,128)(2,1)S(1)} copy-done((bf16[2,1536,1536]{2,1,0:T(8,128)(2,1)S(1)}, bf16[2,1536,1536]{2,1,0:T(8,128)(2,1)}, u32[]{:S(2)}) %copy-start.5) | copy-done | bytes 9437208
  3.7 0.3 cut_window.1
  4.0 1.3 collective-permute-start.2
  5.3 4.6 %collective-permute-start.4 = (bf16[1536,128]{1,0:T(8,128)(2,1)S(1)}, bf16[1536,128]{1,0:T(8,128)(2,1)S(1)}, u32[]{:S(2)}, u32[]{:S(2)}) collective-permute-start(bf16[1536,128]{1,0:T(8,128)(2,1)S(1)} %get-tuple-element.24), channel_id=1, source_target_pairs={{0,0},{1,4},{4,1},{5,5},{10,10},{11,14},{14,11},{15,15},{16,16},{1... | collective-permute-start | bytes 1179656 | tf_op jit(solution)/shard_map/ppermute | solution.py:351
  9.9 1.9 collective-permute-start.1
  11.8 7.9 %collective-permute-done.2 = bf16[1536,128]{1,0:T(8,128)(2,1)S(1)} collective-permute-done((bf16[1536,128]{1,0:T(8,128)(2,1)S(1)}, bf16[1536,128]{1,0:T(8,128)(2,1)S(1)}, u32[]{:S(2)}, u32[]{:S(2)}) %collective-permute-start.2) | collective-permute-done | bytes 393248 | tf_op jit(solution)/shard_map/ppermute | solution.py:351
  19.7 2.9 %collective-permute-start.3 = (bf16[1536,128]{1,0:T(8,128)(2,1)S(1)}, bf16[1536,128]{1,0:T(8,128)(2,1)S(1)}, u32[]{:S(2)}, u32[]{:S(2)}) collective-permute-start(bf16[1536,128]{1,0:T(8,128)(2,1)S(1)} %collective-permute-done.2), channel_id=1, source_target_pairs={{10,8},{14,12},{11,9},{15,13},{0,2},{4,6},{1,3},{5,7},{26,24},{30,... | collective-permute-start | bytes 1179656 | tf_op jit(solution)/shard_map/ppermute | solution.py:351
  22.6 0.1 fusion
  22.8 0.1 dynamic_slice.16
  22.9 0.1 dynamic_slice.15
  23.0 3.7 %copy-done.6 = bf16[2,1536,1536]{2,1,0:T(8,128)(2,1)S(1)} copy-done((bf16[2,1536,1536]{2,1,0:T(8,128)(2,1)S(1)}, bf16[2,1536,1536]{2,1,0:T(8,128)(2,1)}, u32[]{:S(2)}) %copy-start.6) | copy-done | bytes 9437208
  26.6 5.5 %pick_columns.1 = (bf16[2,96,1536]{2,1,0:T(8,128)(2,1)}, bf16[2,1536,1536]{2,1,0:T(8,128)(2,1)S(1)}) custom-call(bf16[2,1536,1536]{2,1,0:T(8,128)(2,1)S(1)} %copy-done.6, s32[1,128]{1,0:T(1,128)S(1)} %pad_bitcast_fusion.miss_ref, bf16[8,1536]{1,0:T(8,128)(2,1)S(1)} %broadcast_in_dim.36.recv_ref, f32[8,1536]{1,0:T(8,128)S(1)} %broadcast_in_dim.37.live_ref), custom_call_target="tpu_custom_call" | custom-call | flops 37748736 | bytes 147456 | tf_op jit(solution)/shard_map/pick_columns/pallas_call | solution.py:104
  32.2 3.6 %copy-done = bf16[2,1536,1536]{2,1,0:T(8,128)(2,1)} copy-done((bf16[2,1536,1536]{2,1,0:T(8,128)(2,1)}, bf16[2,1536,1536]{2,1,0:T(8,128)(2,1)S(1)}, u32[]{:S(2)}) %copy-start) | copy-done | bytes 9437208
  35.8 1.2 fill_window.1.refs_0_.refs_3_
  37.1 1.3 collective-permute-start.7
  38.4 19.1 %collective-permute-start.5 = (bf16[1536,256]{1,0:T(8,128)(2,1)S(1)}, bf16[1536,256]{1,0:T(8,128)(2,1)S(1)}, u32[]{:S(2)}, u32[]{:S(2)}) collective-permute-start(bf16[1536,256]{1,0:T(8,128)(2,1)S(1)} %fill_window.1.refs_0_.refs_3_), channel_id=1, source_target_pairs={{0,4},{4,8},{8,12},{1,5},{5,9},{9,13},{2,6},{6,10},{10,14},{3,7},{... | collective-permute-start | bytes 2359304 | tf_op jit(solution)/shard_map/ppermute | solution.py:395
  57.6 15.9 %collective-permute-done.7.refs_1_.refs_4_.refs_6_ = bf16[1536,256]{1,0:T(8,128)(2,1)S(1)} collective-permute-done((bf16[1536,256]{1,0:T(8,128)(2,1)S(1)}, bf16[1536,256]{1,0:T(8,128)(2,1)S(1)}, u32[]{:S(2)}, u32[]{:S(2)}) %collective-permute-start.7) | collective-permute-done | bytes 786464 | tf_op jit(solution)/shard_map/ppermute | solution.py:396
  73.5 1.0 collective-permute-done.5.refs_2_.refs_5_.refs_7_
  74.4 3.7 %copy-done.1 = bf16[2,1536,1536]{2,1,0:T(8,128)(2,1)S(1)} copy-done((bf16[2,1536,1536]{2,1,0:T(8,128)(2,1)S(1)}, bf16[2,1536,1536]{2,1,0:T(8,128)(2,1)}, u32[]{:S(2)}) %copy-start.1) | copy-done | bytes 9437208
  78.1 7.0 %products.3 = (f32[1536,256]{1,0:T(8,128)S(1)}, f32[1536,256]{1,0:T(8,128)}) custom-call(s32[2]{0:T(128)S(1)} %pad_add_fusion.pick_ref, bf16[2,1536,1536]{2,1,0:T(8,128)(2,1)S(1)} %copy-done.1, bf16[1536,256]{1,0:T(8,128)(2,1)S(1)} %fill_window.1.refs_0_.refs_3_, bf16[1536,256]{1,0:T(8,128)(2,1)S(1)} %collective-permute-done.7.refs_1_.refs_4_.refs_6_, ...), custom_call_target="tpu_custom_call" | custom-call | flops 150994944 | bytes 24576 | tf_op jit(solution)/shard_map/products/pallas_call | solution.py:214
  85.1 1.2 copy-done.7
  86.3 0.8 collective-permute-start.9
  87.1 1.3 collective-permute-start.8
  88.3 1.6 collective-permute-start.6
  89.9 7.9 %collective-permute-start = (bf16[2,96,1536]{2,1,0:T(8,128)(2,1)}, bf16[2,96,1536]{2,1,0:T(8,128)(2,1)}, u32[]{:S(2)}, u32[]{:S(2)}) collective-permute-start(bf16[2,96,1536]{2,1,0:T(8,128)(2,1)} %get-tuple-element.20.patch_ref), channel_id=1, source_target_pairs={{0,0},{1,4},{2,8},{3,12},{4,1},{5,5},{6,9},{7,13},{8,2},{9,6},{10,... | collective-permute-start | bytes 1769480 | tf_op jit(solution)/shard_map/ppermute | solution.py:351
  97.9 23.8 %collective-permute-done.rows_ref.extra_ref = bf16[2,96,1536]{2,1,0:T(8,128)(2,1)} collective-permute-done((bf16[2,96,1536]{2,1,0:T(8,128)(2,1)}, bf16[2,96,1536]{2,1,0:T(8,128)(2,1)}, u32[]{:S(2)}, u32[]{:S(2)}) %collective-permute-start) | collective-permute-done | bytes 589856 | tf_op jit(solution)/shard_map/ppermute | solution.py:351
  121.7 3.2 %add.49 = f32[1536,256]{1,0:T(8,128)} add(f32[1536,256]{1,0:T(8,128)} %copy-done.7, f32[1536,256]{1,0:T(8,128)} %collective-permute-done.9) | non-fusion elementwise | flops 393216 | bytes 4718592 | tf_op jit(solution)/shard_map/add | solution.py:423
  124.9 3.7 %copy-done.2 = bf16[2,1536,1536]{2,1,0:T(8,128)(2,1)S(1)} copy-done((bf16[2,1536,1536]{2,1,0:T(8,128)(2,1)S(1)}, bf16[2,1536,1536]{2,1,0:T(8,128)(2,1)}, u32[]{:S(2)}) %copy-start.2) | copy-done | bytes 9437208
  128.6 4.9 %products.4 = f32[1536,256]{1,0:T(8,128)} custom-call(s32[1]{0:T(128)} %bitcast.7.pick_ref, bf16[2,1536,1536]{2,1,0:T(8,128)(2,1)S(1)} %copy-done.2, bf16[1536,256]{1,0:T(8,128)(2,1)S(1)} %collective-permute-done.8.refs_0_.refs_3_, bf16[1536,256]{1,0:T(8,128)(2,1)} %collective-permute-done.6.refs_1_.refs_4_), custom_call_target="tpu_custom_call" | custom-call | flops 75497472 | bytes 24576 | tf_op jit(solution)/shard_map/products/pallas_call | solution.py:214
  133.5 2.5 collective-permute-start.11
  136.0 1.3 collective-permute-start.10
  137.3 1.3 collective-permute-start.12
  138.6 1.6 collective-permute-start.13
  140.2 3.2 %add.50 = f32[1536,256]{1,0:T(8,128)} add(f32[1536,256]{1,0:T(8,128)} %products.4, f32[1536,256]{1,0:T(8,128)} %collective-permute-done.11) | non-fusion elementwise | flops 393216 | bytes 4718592 | tf_op jit(solution)/shard_map/add | solution.py:400
  143.4 43.5 %collective-permute-done.10 = f32[1536,256]{1,0:T(8,128)} collective-permute-done((f32[1536,256]{1,0:T(8,128)}, f32[1536,256]{1,0:T(8,128)}, u32[]{:S(2)}, u32[]{:S(2)}) %collective-permute-start.10) | collective-permute-done | bytes 1572896 | tf_op jit(solution)/shard_map/ppermute | solution.py:351
  186.9 3.7 %copy-done.3 = bf16[2,1536,1536]{2,1,0:T(8,128)(2,1)S(1)} copy-done((bf16[2,1536,1536]{2,1,0:T(8,128)(2,1)S(1)}, bf16[2,1536,1536]{2,1,0:T(8,128)(2,1)}, u32[]{:S(2)}) %copy-start.3) | copy-done | bytes 9437208
  190.6 5.2 %products.5 = f32[1536,256]{1,0:T(8,128)} custom-call(s32[1]{0:T(128)} %bitcast.4.pick_ref, bf16[2,1536,1536]{2,1,0:T(8,128)(2,1)S(1)} %copy-done.3, bf16[1536,256]{1,0:T(8,128)(2,1)} %collective-permute-done.12.refs_0_.refs_5_, bf16[1536,256]{1,0:T(8,128)(2,1)S(1)} %collective-permute-done.7.refs_1_.refs_4_.refs_6_, ...), custom_call_target="tpu_custom_call" | custom-call | flops 75497472 | bytes 24576 | tf_op jit(solution)/shard_map/products/pallas_call | solution.py:214
  195.8 1.3 collective-permute-start.14
  197.1 1.8 collective-permute-start.15
  198.9 0.1 stack.46.pick_ref
  199.0 3.5 %extra_products.1 = f32[4,96,256]{2,1,0:T(8,128)S(1)} custom-call(s32[8]{0:T(128)S(1)} %stack.46.pick_ref, bf16[2,96,1536]{2,1,0:T(8,128)(2,1)} %collective-permute-done.rows_ref.extra_ref, bf16[1536,256]{1,0:T(8,128)(2,1)S(1)} %fill_window.1.refs_0_.refs_3_, bf16[1536,256]{1,0:T(8,128)(2,1)S(1)} %collective-permute-done.7.refs_1_.refs_4_.refs_6_, ...), custom_call_target="tpu_custom_call" | custom-call | flops 18874368 | bytes 24576 | tf_op jit(solution)/shard_map/extra_products/pallas_call | solution.py:241
  202.6 3.4 %collective-permute-start.17 = (f32[2,96,256]{2,1,0:T(8,128)S(1)}, f32[2,96,256]{2,1,0:T(8,128)S(1)}, u32[]{:S(2)}, u32[]{:S(2)}) collective-permute-start(f32[2,96,256]{2,1,0:T(8,128)S(1)} %slice.15), channel_id=1, source_target_pairs={{0,1},{1,0},{2,3},{3,2},{4,5},{5,4},{6,7},{7,6},{8,9},{9,8},{10,11... | collective-permute-start | bytes 589832 | tf_op jit(solution)/shard_map/ppermute | solution.py:445
  206.0 2.1 add.51.refs_0_
  208.1 1.4 collective-permute-start.16
  209.7 28.1 %collective-permute-done.18 = f32[1,96,256]{2,1,0:T(8,128)S(1)} collective-permute-done((f32[1,96,256]{2,1,0:T(8,128)S(1)}, f32[1,96,256]{2,1,0:T(8,128)S(1)}, u32[]{:S(2)}, u32[]{:S(2)}) %collective-permute-start.18) | collective-permute-done | bytes 98336 | tf_op jit(solution)/shard_map/ppermute | solution.py:445
  237.8 2.8 %add_add_fusion.refs_1_ = f32[1536,256]{1,0:T(8,128)S(1)} fusion(f32[1536,256]{1,0:T(8,128)} %collective-permute-done.15, f32[1536,256]{1,0:T(8,128)} %add.50, f32[1536,256]{1,0:T(8,128)} %collective-permute-done.10, f32[1536,256]{1,0:T(8,128)} %add.49, pred[]{:T(512)S(6)} %eq.26, pred[]{:T(512)S(6)} %eq.25), kind=kLoop, calls=%fused_computation | loop fusion | flops 1966080 | bytes 7864322 | tf_op jit(solution)/shard_map/add | solution.py:437
  240.6 3.7 %copy-done.4 = bf16[2,1536,1536]{2,1,0:T(8,128)(2,1)S(1)} copy-done((bf16[2,1536,1536]{2,1,0:T(8,128)(2,1)S(1)}, bf16[2,1536,1536]{2,1,0:T(8,128)(2,1)}, u32[]{:S(2)}) %copy-start.4) | copy-done | bytes 9437208
  244.3 2.7 %finish.1 = f32[2,1536,128]{2,1,0:T(8,128)} custom-call(f32[2]{0:T(128)S(1)} %broadcast_multiply_fusion.wave_ref, f32[1]{0:T(128)} %bitcast.flag_ref, s32[96]{0:T(128)S(1)} %get-tuple-element.34.miss_ref, bf16[2,1536,1536]{2,1,0:T(8,128)(2,1)S(1)} %copy-done.4, bf16[2,96,1536]{2,1,0:T(8,128)(2,1)} %collective-permute-done.rows_ref.extra_ref, ...), custom_call_target="tpu_custom_call" | custom-call | flops 61440 | bytes 122880 | tf_op jit(solution)/shard_map/finish/pallas_call | solution.py:290
  (41 shorter events, 0.3 us)
Async XLA Ops:
  0.0 3.7 %copy-start.5 = (bf16[2,1536,1536]{2,1,0:T(8,128)(2,1)S(1)}, bf16[2,1536,1536]{2,1,0:T(8,128)(2,1)}, u32[]{:S(2)}) copy-start(bf16[2,1536,1536]{2,1,0:T(8,128)(2,1)} %traces_ref.3) | copy-start | bytes 28311556
  3.7 8.1 %copy-start.9 = (s32[4,96]{1,0:T(4,128)S(1)}, s32[4,96]{1,0:T(4,128)}, u32[]{:S(2)}) copy-start(s32[4,96]{1,0:T(4,128)} %param.6) | copy-start | bytes 4612
  3.7 19.1 %copy-start.8 = (s32[6144]{0:T(1024)S(1)}, s32[6144]{0:T(1024)}, u32[]{:S(2)}) copy-start(s32[6144]{0:T(1024)} %param.5) | copy-start | bytes 73732
  4.0 15.8 %collective-permute-start.2 = (bf16[1536,128]{1,0:T(8,128)(2,1)S(1)}, bf16[1536,128]{1,0:T(8,128)(2,1)S(1)}, u32[]{:S(2)}, u32[]{:S(2)}) collective-permute-start(bf16[1536,128]{1,0:T(8,128)(2,1)S(1)} %get-tuple-element.24), channel_id=1, source_target_pairs={{2,10},{3,14},{6,11},{7,15},{8,0},{9,4},{12,1},{13,5},{18,26},{19,... | collective-permute-start | bytes 1179656 | tf_op jit(solution)/shard_map/ppermute | solution.py:351
  5.3 30.6 %collective-permute-start.4 = (bf16[1536,128]{1,0:T(8,128)(2,1)S(1)}, bf16[1536,128]{1,0:T(8,128)(2,1)S(1)}, u32[]{:S(2)}, u32[]{:S(2)}) collective-permute-start(bf16[1536,128]{1,0:T(8,128)(2,1)S(1)} %get-tuple-element.24), channel_id=1, source_target_pairs={{0,0},{1,4},{4,1},{5,5},{10,10},{11,14},{14,11},{15,15},{16,16},{1... | collective-permute-start | bytes 1179656 | tf_op jit(solution)/shard_map/ppermute | solution.py:351
  9.9 25.9 %collective-permute-start.1 = (bf16[1536,128]{1,0:T(8,128)(2,1)S(1)}, bf16[1536,128]{1,0:T(8,128)(2,1)S(1)}, u32[]{:S(2)}, u32[]{:S(2)}) collective-permute-start(bf16[1536,128]{1,0:T(8,128)(2,1)S(1)} %get-tuple-element.23), channel_id=1, source_target_pairs={{0,0},{1,4},{2,8},{3,12},{4,1},{5,5},{6,9},{7,13},{8,2},{9,6},{10,... | collective-permute-start | bytes 1179656 | tf_op jit(solution)/shard_map/ppermute | solution.py:351
  19.7 16.1 %collective-permute-start.3 = (bf16[1536,128]{1,0:T(8,128)(2,1)S(1)}, bf16[1536,128]{1,0:T(8,128)(2,1)S(1)}, u32[]{:S(2)}, u32[]{:S(2)}) collective-permute-start(bf16[1536,128]{1,0:T(8,128)(2,1)S(1)} %collective-permute-done.2), channel_id=1, source_target_pairs={{10,8},{14,12},{11,9},{15,13},{0,2},{4,6},{1,3},{5,7},{26,24},{30,... | collective-permute-start | bytes 1179656 | tf_op jit(solution)/shard_map/ppermute | solution.py:351
  23.0 3.7 %copy-start.6 = (bf16[2,1536,1536]{2,1,0:T(8,128)(2,1)S(1)}, bf16[2,1536,1536]{2,1,0:T(8,128)(2,1)}, u32[]{:S(2)}) copy-start(bf16[2,1536,1536]{2,1,0:T(8,128)(2,1)} %traces_ref.3) | copy-start | bytes 28311556
  32.2 3.6 %copy-start = (bf16[2,1536,1536]{2,1,0:T(8,128)(2,1)}, bf16[2,1536,1536]{2,1,0:T(8,128)(2,1)S(1)}, u32[]{:S(2)}) copy-start(bf16[2,1536,1536]{2,1,0:T(8,128)(2,1)S(1)} %get-tuple-element.30.tile_ref) | copy-start | bytes 28311556
  37.1 36.4 %collective-permute-start.7 = (bf16[1536,256]{1,0:T(8,128)(2,1)S(1)}, bf16[1536,256]{1,0:T(8,128)(2,1)S(1)}, u32[]{:S(2)}, u32[]{:S(2)}) collective-permute-start(bf16[1536,256]{1,0:T(8,128)(2,1)S(1)} %fill_window.1.refs_0_.refs_3_), channel_id=1, source_target_pairs={{4,0},{8,4},{12,8},{5,1},{9,5},{13,9},{6,2},{10,6},{14,10},{7,3},{... | collective-permute-start | bytes 2359304 | tf_op jit(solution)/shard_map/ppermute | solution.py:396
  38.4 36.1 %collective-permute-start.5 = (bf16[1536,256]{1,0:T(8,128)(2,1)S(1)}, bf16[1536,256]{1,0:T(8,128)(2,1)S(1)}, u32[]{:S(2)}, u32[]{:S(2)}) collective-permute-start(bf16[1536,256]{1,0:T(8,128)(2,1)S(1)} %fill_window.1.refs_0_.refs_3_), channel_id=1, source_target_pairs={{0,4},{4,8},{8,12},{1,5},{5,9},{9,13},{2,6},{6,10},{10,14},{3,7},{... | collective-permute-start | bytes 2359304 | tf_op jit(solution)/shard_map/ppermute | solution.py:395
  74.4 3.7 %copy-start.1 = (bf16[2,1536,1536]{2,1,0:T(8,128)(2,1)S(1)}, bf16[2,1536,1536]{2,1,0:T(8,128)(2,1)}, u32[]{:S(2)}) copy-start(bf16[2,1536,1536]{2,1,0:T(8,128)(2,1)} %copy-done) | copy-start | bytes 28311556
  85.1 1.2 copy-start.7
  86.3 35.4 %collective-permute-start.9 = (f32[1536,256]{1,0:T(8,128)}, f32[1536,256]{1,0:T(8,128)}, u32[]{:S(2)}, u32[]{:S(2)}) collective-permute-start(f32[1536,256]{1,0:T(8,128)} %get-tuple-element.26), channel_id=1, source_target_pairs={{0,1},{1,0},{2,3},{3,2},{4,5},{5,4},{6,7},{7,6},{8,9},{9,8},{10,11... | collective-permute-start | bytes 4718600 | tf_op jit(solution)/shard_map/ppermute | solution.py:423
  87.1 37.9 %collective-permute-start.8 = (bf16[1536,256]{1,0:T(8,128)(2,1)S(1)}, bf16[1536,256]{1,0:T(8,128)(2,1)S(1)}, u32[]{:S(2)}, u32[]{:S(2)}) collective-permute-start(bf16[1536,256]{1,0:T(8,128)(2,1)S(1)} %collective-permute-done.7.refs_1_.refs_4_.refs_6_), channel_id=1, source_target_pairs={{4,0},{8,4},{5,1},{9,5},{6,2},{10,6},{7,3},{11,7},{20,16},{24,20},... | collective-permute-start | bytes 2359304 | tf_op jit(solution)/shard_map/ppermute | solution.py:396
  88.3 36.6 %collective-permute-start.6 = (bf16[1536,256]{1,0:T(8,128)(2,1)S(1)}, bf16[1536,256]{1,0:T(8,128)(2,1)}, u32[]{:S(2)}, u32[]{:S(2)}) collective-permute-start(bf16[1536,256]{1,0:T(8,128)(2,1)S(1)} %collective-permute-done.5.refs_2_.refs_5_.refs_7_), channel_id=1, source_target_pairs={{4,8},{8,12},{5,9},{9,13},{6,10},{10,14},{7,11},{11,15},{20,24},{2... | collective-permute-start | bytes 2359304 | tf_op jit(solution)/shard_map/ppermute | solution.py:395
  89.9 31.7 %collective-permute-start = (bf16[2,96,1536]{2,1,0:T(8,128)(2,1)}, bf16[2,96,1536]{2,1,0:T(8,128)(2,1)}, u32[]{:S(2)}, u32[]{:S(2)}) collective-permute-start(bf16[2,96,1536]{2,1,0:T(8,128)(2,1)} %get-tuple-element.20.patch_ref), channel_id=1, source_target_pairs={{0,0},{1,4},{2,8},{3,12},{4,1},{5,5},{6,9},{7,13},{8,2},{9,6},{10,... | collective-permute-start | bytes 1769480 | tf_op jit(solution)/shard_map/ppermute | solution.py:351
  124.9 3.7 %copy-start.2 = (bf16[2,1536,1536]{2,1,0:T(8,128)(2,1)S(1)}, bf16[2,1536,1536]{2,1,0:T(8,128)(2,1)}, u32[]{:S(2)}) copy-start(bf16[2,1536,1536]{2,1,0:T(8,128)(2,1)} %copy-done) | copy-start | bytes 28311556
  133.5 6.6 %collective-permute-start.11 = (f32[1536,256]{1,0:T(8,128)}, f32[1536,256]{1,0:T(8,128)}, u32[]{:S(2)}, u32[]{:S(2)}) collective-permute-start(f32[1536,256]{1,0:T(8,128)} %products.4), channel_id=1, source_target_pairs={{1,0},{3,2},{4,5},{6,7},{9,8},{11,10},{12,13},{14,15},{17,16},{19,... | collective-permute-start | bytes 4718600 | tf_op jit(solution)/shard_map/ppermute | solution.py:351
  136.0 50.9 %collective-permute-start.10 = (f32[1536,256]{1,0:T(8,128)}, f32[1536,256]{1,0:T(8,128)}, u32[]{:S(2)}, u32[]{:S(2)}) collective-permute-start(f32[1536,256]{1,0:T(8,128)} %add.49), channel_id=1, source_target_pairs={{2,0},{3,1},{6,4},{7,5},{8,10},{9,11},{12,14},{13,15},{18,16},{19,... | collective-permute-start | bytes 4718600 | tf_op jit(solution)/shard_map/ppermute | solution.py:351
  137.3 49.6 %collective-permute-start.12 = (bf16[1536,256]{1,0:T(8,128)(2,1)S(1)}, bf16[1536,256]{1,0:T(8,128)(2,1)}, u32[]{:S(2)}, u32[]{:S(2)}) collective-permute-start(bf16[1536,256]{1,0:T(8,128)(2,1)S(1)} %collective-permute-done.8.refs_0_.refs_3_), channel_id=1, source_target_pairs={{4,0},{5,1},{6,2},{7,3},{20,16},{21,17},{22,18},{23,19}} | collective-permute-start | bytes 2359304 | tf_op jit(solution)/shard_map/ppermute | solution.py:396
  138.6 48.4 %collective-permute-start.13 = (bf16[1536,256]{1,0:T(8,128)(2,1)}, bf16[1536,256]{1,0:T(8,128)(2,1)}, u32[]{:S(2)}, u32[]{:S(2)}) collective-permute-start(bf16[1536,256]{1,0:T(8,128)(2,1)} %collective-permute-done.6.refs_1_.refs_4_), channel_id=1, source_target_pairs={{8,12},{9,13},{10,14},{11,15},{24,28},{25,29},{26,30},{27,31}} | collective-permute-start | bytes 2359304 | tf_op jit(solution)/shard_map/ppermute | solution.py:395
  186.9 3.7 %copy-start.3 = (bf16[2,1536,1536]{2,1,0:T(8,128)(2,1)S(1)}, bf16[2,1536,1536]{2,1,0:T(8,128)(2,1)}, u32[]{:S(2)}) copy-start(bf16[2,1536,1536]{2,1,0:T(8,128)(2,1)} %copy-done) | copy-start | bytes 28311556
  195.8 10.2 %collective-permute-start.14 = (f32[1536,256]{1,0:T(8,128)}, f32[1536,256]{1,0:T(8,128)}, u32[]{:S(2)}, u32[]{:S(2)}) collective-permute-start(f32[1536,256]{1,0:T(8,128)} %products.5), channel_id=1, source_target_pairs={{0,1},{2,3},{5,4},{7,6},{8,9},{10,11},{13,12},{15,14},{16,17},{18,... | collective-permute-start | bytes 4718600 | tf_op jit(solution)/shard_map/ppermute | solution.py:351
  197.1 40.7 %collective-permute-start.15 = (f32[1536,256]{1,0:T(8,128)}, f32[1536,256]{1,0:T(8,128)}, u32[]{:S(2)}, u32[]{:S(2)}) collective-permute-start(f32[1536,256]{1,0:T(8,128)} %add.50), channel_id=1, source_target_pairs={{0,2},{5,7},{10,8},{15,13},{16,18},{21,23},{26,24},{31,29}} | collective-permute-start | bytes 4718600 | tf_op jit(solution)/shard_map/ppermute | solution.py:351
  202.6 7.1 %copy-start.10 = (f32[2]{0:T(128)S(1)}, f32[2]{0:T(128)}, u32[]{:S(2)}) copy-start(f32[2]{0:T(128)} %param.7) | copy-start | bytes 28
  202.6 6.9 %collective-permute-start.17 = (f32[2,96,256]{2,1,0:T(8,128)S(1)}, f32[2,96,256]{2,1,0:T(8,128)S(1)}, u32[]{:S(2)}, u32[]{:S(2)}) collective-permute-start(f32[2,96,256]{2,1,0:T(8,128)S(1)} %slice.15), channel_id=1, source_target_pairs={{0,1},{1,0},{2,3},{3,2},{4,5},{5,4},{6,7},{7,6},{8,9},{9,8},{10,11... | collective-permute-start | bytes 589832 | tf_op jit(solution)/shard_map/ppermute | solution.py:445
  208.1 32.5 %collective-permute-start.16 = (f32[1536,256]{1,0:T(8,128)S(1)}, f32[1536,256]{1,0:T(8,128)S(1)}, u32[]{:S(2)}, u32[]{:S(2)}) collective-permute-start(f32[1536,256]{1,0:T(8,128)S(1)} %add.51.refs_0_), channel_id=1, source_target_pairs={{1,3},{4,6},{11,9},{14,12},{17,19},{20,22},{27,25},{30,28}} | collective-permute-start | bytes 4718600 | tf_op jit(solution)/shard_map/ppermute | solution.py:351
  209.5 28.3 %collective-permute-start.18 = (f32[1,96,256]{2,1,0:T(8,128)S(1)}, f32[1,96,256]{2,1,0:T(8,128)S(1)}, u32[]{:S(2)}, u32[]{:S(2)}) collective-permute-start(f32[1,96,256]{2,1,0:T(8,128)S(1)} %slice.19), channel_id=1, source_target_pairs={{0,2},{1,3},{2,0},{3,1},{4,6},{5,7},{6,4},{7,5},{8,10},{9,11},{10,... | collective-permute-start | bytes 294920 | tf_op jit(solution)/shard_map/ppermute | solution.py:445
  240.6 3.7 %copy-start.4 = (bf16[2,1536,1536]{2,1,0:T(8,128)(2,1)S(1)}, bf16[2,1536,1536]{2,1,0:T(8,128)(2,1)}, u32[]{:S(2)}) copy-start(bf16[2,1536,1536]{2,1,0:T(8,128)(2,1)} %copy-done) | copy-start | bytes 28311556

commit v4 on v3

--- a/solution.py
+++ b/solution.py
@@ -12,7 +12,7 @@
 LANES = 128
 CHUNKS = 1
 WIDTH = WIN // CHUNKS
-VMEM_LIMIT = 32 * 2**20
+VMEM_LIMIT = 48 * 2**20
 VMEM = pl.BlockSpec(memory_space=pltpu.VMEM)
 SMEM = pl.BlockSpec(memory_space=pltpu.SMEM)
 
@@ -83,19 +83,18 @@
     )(traces)
 
 
-def pick_kernel(traces_ref, miss_ref, recv_ref, live_ref, out_ref, tile_ref, hot_ref):
+def pick_kernel(traces_ref, miss_ref, recv_ref, live_ref, real_ref, imag_ref, hot_ref):
     @pl.when(pl.program_id(0) == 0)
     def _():
         hot = one_hot(miss_ref[...], hot_ref.shape[0], jnp.bfloat16)
         alive = jnp.dot(recv_ref[...], hot, preferred_element_type=jnp.float32)
         hot_ref[...] = hot * alive[0:1].astype(jnp.bfloat16)
 
-    misses = out_ref.shape[1]
-    for part in range(2):
+    misses = real_ref.shape[0]
+    for part, out_ref in enumerate((real_ref, imag_ref)):
         picked = jnp.dot(traces_ref[part], hot_ref[...], preferred_element_type=jnp.float32)
         turned = picked.T * live_ref[0:1, :]
-        out_ref[part] = turned[:misses].astype(jnp.bfloat16)
-        tile_ref[part] = traces_ref[part] * recv_ref[0:1, :]
+        out_ref[...] = turned[:misses].astype(jnp.bfloat16)
 
 
 def pick_columns(traces, miss_lanes, recv8, live8, misses):
@@ -110,14 +109,8 @@
             pl.BlockSpec((8, cols), lambda i: (0, 0)),
             pl.BlockSpec((8, block), lambda i: (0, i)),
         ],
-        out_specs=[
-            pl.BlockSpec((2, misses, block), lambda i: (0, 0, i)),
-            pl.BlockSpec((2, block, cols), lambda i: (0, i, 0)),
-        ],
-        out_shape=[
-            jax.ShapeDtypeStruct((2, misses, rows), jnp.bfloat16),
-            jax.ShapeDtypeStruct(traces.shape, jnp.bfloat16),
-        ],
+        out_specs=[pl.BlockSpec((misses, block), lambda i: (0, i))] * 2,
+        out_shape=[jax.ShapeDtypeStruct((misses, rows), jnp.bfloat16)] * 2,
         scratch_shapes=[pltpu.VMEM((cols, LANES), jnp.bfloat16)],
         compiler_params=params(),
         cost_estimate=cost(4 * rows * cols * 2 * LANES, 4 * rows * cols),
@@ -125,14 +118,14 @@
     )(traces, miss_lanes, recv8, live8)
 
 
-def fill_kernel(counts, first_half, patch_ref, miss_ref, recv_ref, *refs):
+def fill_kernel(counts, first_half, real_ref, imag_ref, miss_ref, recv_ref, *refs):
     out_ref = refs[-1]
     rows = out_ref.shape[0]
-    misses = patch_ref.shape[1]
+    misses = real_ref.shape[0]
     hot = one_hot(miss_ref[...], rows, jnp.float32)
     dead = jnp.max(hot, axis=1, keepdims=True)
     hot = hot[:, :misses].astype(jnp.bfloat16)
-    patches = halves(patch_ref[0].astype(jnp.float32), patch_ref[1].astype(jnp.float32))
+    patches = halves(real_ref[...].astype(jnp.float32), imag_ref[...].astype(jnp.float32))
     mask = recv_ref[...].astype(jnp.float32)
     mask = halves(mask, mask)[0][0:1, :]
     used = 0
@@ -149,7 +142,7 @@
 
 def fill_window(first_half, arrived, picked, miss_lanes, recv8):
     rows = arrived[0][0].shape[0]
-    misses = picked.shape[1]
+    misses = picked[0].shape[0]
     counts = tuple(len(group) for group in arrived)
     flat = [part for group in arrived for part in group]
     lanes = len(counts) * WIN
@@ -158,7 +151,8 @@
         functools.partial(fill_kernel, counts, first_half),
         grid=(1,),
         in_specs=[
-            pl.BlockSpec((2, misses, WIN), lambda i: (0, 0, 0)),
+            pl.BlockSpec((misses, WIN), lambda i: (0, 0)),
+            pl.BlockSpec((misses, WIN), lambda i: (0, 0)),
             pl.BlockSpec((1, LANES), lambda i: (0, 0)),
             pl.BlockSpec((8, WIN), lambda i: (0, 0)),
         ]
@@ -168,7 +162,7 @@
         compiler_params=params(),
         cost_estimate=cost(4 * rows * LANES * lanes, 8 * rows * lanes),
         name="fill_window",
-    )(picked, miss_lanes, recv8, *flat)
+    )(*picked, miss_lanes, recv8, *flat)
 
 
 def complex_rows(real_rows, imag_rows, right):
@@ -191,66 +185,76 @@
             out_ref[...] = ref[...]
 
 
-def product_kernel(block, counts, pick_ref, tile_ref, *refs):
-    total = sum(counts)
-    out_refs, right_ref = refs[total:-1], refs[-1]
-    used = 0
-    for place, (count, out_ref) in enumerate(zip(counts, out_refs)):
-        choose(right_ref, pick_ref[place], refs[used:used + count])
-        used += count
-        for start in range(0, out_ref.shape[0], block):
-            rows = pl.ds(start, block)
-            out_ref[rows, :] = complex_rows(
-                tile_ref[0, rows, :], tile_ref[1, rows, :], right_ref[...]
-            )
-
-
-def products(tile, groups):
-    _, rows, cols = tile.shape
+def product_kernel(counts, pick_ref, traces_ref, recv_ref, *refs):
+    total, places = sum(counts), len(counts)
+    out_refs, right_refs = refs[total:total + places], refs[total + places:]
+
+    @pl.when(pl.program_id(0) == 0)
+    def _():
+        used = 0
+        for place, count in enumerate(counts):
+            choose(right_refs[place], pick_ref[place], refs[used:used + count])
+            used += count
+
+    recv = recv_ref[0:1, :]
+    real_rows, imag_rows = traces_ref[0] * recv, traces_ref[1] * recv
+    for out_ref, right_ref in zip(out_refs, right_refs):
+        out_ref[...] = complex_rows(real_rows, imag_rows, right_ref[...])
+
+
+def products(traces, recv8, groups):
+    _, rows, cols = traces.shape
     lanes = groups[0][1][0].shape[1]
     counts = tuple(len(sources) for _, sources in groups)
     flat = [source for _, sources in groups for source in sources]
     picks = jnp.stack([pick for pick, _ in groups]).astype(jnp.int32)
-    return pl.pallas_call(
-        functools.partial(product_kernel, row_block(rows), counts),
-        in_specs=[SMEM] + [VMEM] * (1 + len(flat)),
-        out_specs=[VMEM] * len(groups),
+    block = row_block(rows) // 2
+    return pl.pallas_call(
+        functools.partial(product_kernel, counts),
+        grid=(rows // block,),
+        in_specs=[
+            SMEM,
+            pl.BlockSpec((2, block, cols), lambda i: (0, i, 0)),
+            pl.BlockSpec((8, cols), lambda i: (0, 0)),
+        ]
+        + [pl.BlockSpec((cols, lanes), lambda i: (0, 0))] * len(flat),
+        out_specs=[pl.BlockSpec((block, lanes), lambda i: (i, 0))] * len(groups),
         out_shape=[jax.ShapeDtypeStruct((rows, lanes), jnp.float32)] * len(groups),
-        scratch_shapes=[pltpu.VMEM((cols, lanes), jnp.bfloat16)],
+        scratch_shapes=[pltpu.VMEM((cols, lanes), jnp.bfloat16)] * len(groups),
         compiler_params=params(),
         cost_estimate=cost(8 * rows * cols * lanes * len(groups), 4 * rows * lanes),
         name="products",
-    )(picks, tile, *flat)
-
-
-def extra_kernel(counts, pick_ref, rows_ref, *refs):
+    )(picks, traces, recv8, *flat)
+
+
+def extra_kernel(counts, pick_ref, real_ref, imag_ref, *refs):
     out_ref, right_ref = refs[-2:]
     used = 0
     for place, count in enumerate(counts):
         choose(right_ref, pick_ref[2 * place], refs[used:used + count])
         used += count
-        out_ref[pick_ref[2 * place + 1]] = complex_rows(rows_ref[0], rows_ref[1], right_ref[...])
+        out_ref[pick_ref[2 * place + 1]] = complex_rows(real_ref[...], imag_ref[...], right_ref[...])
 
 
 def extra_products(rows, groups):
-    _, misses, cols = rows.shape
+    misses, cols = rows[0].shape
     lanes = groups[0][2][0].shape[1]
     counts = tuple(len(sources) for _, _, sources in groups)
     flat = [source for _, _, sources in groups for source in sources]
     picks = jnp.stack([x for pick, place, _ in groups for x in (pick, place)]).astype(jnp.int32)
     return pl.pallas_call(
         functools.partial(extra_kernel, counts),
-        in_specs=[SMEM] + [VMEM] * (1 + len(flat)),
+        in_specs=[SMEM] + [VMEM] * (2 + len(flat)),
         out_specs=VMEM,
         out_shape=jax.ShapeDtypeStruct((len(groups), misses, lanes), jnp.float32),
         scratch_shapes=[pltpu.VMEM((cols, lanes), jnp.bfloat16)],
         compiler_params=params(),
         cost_estimate=cost(8 * misses * cols * lanes * len(groups), 4 * cols * lanes),
         name="extra_products",
-    )(picks, rows, *flat)
-
-
-def finish_kernel(counts, wave_ref, flag_ref, miss_ref, tile_ref, extra_ref, *refs):
+    )(picks, *rows, *flat)
+
+
+def finish_kernel(counts, wave_ref, flag_ref, miss_ref, recv_ref, tile_ref, real_ref, imag_ref, *refs):
     out_ref, row_ref = refs[-2:]
     totals = []
     used = 0
@@ -263,15 +267,16 @@
         used += count
         totals.append(total)
 
-    def write(target, window_ref, chunks):
+    def write(target, window, chunks):
         real_part, imag_part = unpack(chunks)
         real_pred = real_part * wave_ref[0] - imag_part * wave_ref[1]
         imag_pred = imag_part * wave_ref[0] + real_part * wave_ref[1]
-        target[0] = window_ref[0].astype(jnp.float32) - real_pred
-        target[1] = window_ref[1].astype(jnp.float32) - imag_pred
-
-    write(out_ref, tile_ref, totals[:CHUNKS])
-    write(row_ref, extra_ref, totals[CHUNKS:])
+        target[0] = window[0] - real_pred
+        target[1] = window[1] - imag_pred
+
+    recv = recv_ref[0:1, :].astype(jnp.float32)
+    write(out_ref, [tile_ref[part].astype(jnp.float32) * recv for part in range(2)], totals[:CHUNKS])
+    write(row_ref, [ref[...].astype(jnp.float32) for ref in (real_ref, imag_ref)], totals[CHUNKS:])
 
     def place(m, carry):
         for part in range(2):
@@ -281,23 +286,25 @@
     lax.fori_loop(0, row_ref.shape[1], place, 0, unroll=8)
 
 
-def finish(wave, flag, miss, tile, extra, terms):
-    _, rows, _ = tile.shape
-    misses = extra.shape[1]
+def finish(wave, flag, miss, recv8, traces, extra, terms):
+    _, rows, _ = traces.shape
+    misses = extra[0].shape[0]
     counts = tuple(len(group) for group in terms)
     flat = [term for group in terms for term in group]
     window = lambda size: pl.BlockSpec((2, size, WIN), lambda i: (0, 0, 0))
     return pl.pallas_call(
         functools.partial(finish_kernel, counts),
         grid=(1,),
-        in_specs=[SMEM, SMEM, SMEM, window(rows), window(misses)] + [VMEM] * len(flat),
+        in_specs=[SMEM, SMEM, SMEM, pl.BlockSpec((8, WIN), lambda i: (0, 0)), window(rows)]
+        + [pl.BlockSpec((misses, WIN), lambda i: (0, 0))] * 2
+        + [VMEM] * len(flat),
         out_specs=window(rows),
         out_shape=jax.ShapeDtypeStruct((2, rows, WIN), jnp.float32),
         scratch_shapes=[pltpu.VMEM((2, misses, WIN), jnp.float32)],
         compiler_params=params(),
         cost_estimate=cost(20 * rows * WIN, 40 * rows * WIN),
         name="finish",
-    )(wave, flag, miss, tile, extra, *flat)
+    )(wave, flag, miss, recv8, traces, *extra, *flat)
 
 
 def mirror_routes(grid_size):
@@ -306,7 +313,7 @@
     whole = [(index(a, b), index(b, a)) for a, b in cells]
     near = [(index(a, b), index(b, a)) for a, b in cells if a // 2 == b // 2]
     far = [(a, b) for a, b in cells if a // 2 != b // 2]
-    hop = lambda a, b: index(b, b // 2 * 2 + a % 2)
+    hop = lambda a, b: index(a, a // 2 * 2 + b % 2)
     first = [(index(a, b), hop(a, b)) for a, b in far]
     second = [(hop(a, b), index(b, a)) for a, b in far]
     if len({target for _, target in first}) < len(first):
@@ -379,8 +386,9 @@
     recv_col = lax.dynamic_slice_in_dim(recv_mask, col_index * tile, tile)
     recv_col8 = jnp.broadcast_to(recv_col[None], (8, tile))
 
-    picked, tile_masked = pick_columns(traces, miss_col_lanes, recv_col8, live8, misses)
-    extra = transpose(picked)
+    picked = pick_columns(traces, miss_col_lanes, recv_col8, live8, misses)
+    extra = [transpose(picked[0]), functools.reduce(jnp.add, transpose_round(picked[1]))]
+    picked, extra = lax.optimization_barrier((picked, extra))
     apart = row_index ^ col_index
     strides = [2**bit for bit in range(grid_size.bit_length() - 1)]
     terms, extra_terms = [], []
@@ -413,7 +421,8 @@
         odd = apart & 1
         everything = [block0] + sources1
         keep, sent = products(
-            tile_masked,
+            traces,
+            recv_col8,
             [
                 (jnp.where(odd == 1, 1 + pick1, 0), everything),
                 (jnp.where(odd == 1, 0, 1 + pick1), everything),
@@ -421,22 +430,24 @@
         )
         other_core = [(i, i ^ 1) for i in range(grid_size)]
         total = add_up(keep + lax.ppermute(sent, "col", other_core), 0, strides[1:-1], 1)
-        up[-1], down[-1], total = lax.optimization_barrier((up[-1], down[-1], total))
         for distance in range(3, grid_size):
             hop(distance)
-        got = last(total, 0, 1)
-        tile, extra = lax.optimization_barrier((tile_masked, extra))
+        sums = [(0, 1, apart // 2 == 0, total)]
+        mask = recv_col8
+        for offset in range(2, grid_size):
+            if offset == grid_size - 1:
+                totals = [total for *_, total in sums]
+                mask, totals = lax.optimization_barrier((mask, totals))
+                sums = [(*rest, total) for (*rest, _), total in zip(sums, totals)]
+            (total,) = products(traces, mask, [options(offset)])
+            total = add_up(total, offset, strides[:-1], 0)
+            sums.append((offset, 0, apart == offset, total))
         early = None
-        for offset in range(2, grid_size):
-            mine = apart // 2 == 0 if offset == 2 else apart == offset - 1
-            (new,) = products(tile, [options(offset)])
-            new = add_up(new, offset, strides[:-1], 0)
-            if offset < grid_size - 1:
-                tile, got, new = lax.optimization_barrier((tile, got, new))
-            term = jnp.where(mine, total, 0.0) + got
+        for offset, skip, mine, total in sums[:-1]:
+            term = jnp.where(mine, total, 0.0) + last(total, offset, skip)
             early = term if early is None else early + term
-            total, got = new, last(new, offset, 0)
-        terms.append((total, early, got))
+        total = sums[-1][-1]
+        terms.append((total, early, last(total, grid_size - 1, 0)))
         group = [(pick, apart ^ offset, sources) for offset in range(grid_size)
                  for pick, sources in [options(offset)]]
         rest = extra_products(extra, group)
@@ -447,7 +458,7 @@
         extra_terms.append((rest[0],))
     wave = wavelet * (1.0 / math.sqrt(order))
     flag = (apart == grid_size - 1).astype(jnp.float32)[None]
-    return finish(wave, flag, miss_row, tile_masked, extra, terms + extra_terms)
+    return finish(wave, flag, miss_row, recv_col8, traces, extra, terms + extra_terms)
 
 
 def solution(mesh):

time: 248 us -> 197 us (0.79)
  waiting for transfers between devices: 120 us -> 81 us
  local copies, waits for them, and re-layouts: 27.2 us -> 3.87 us
  Pallas kernels: 30.3 us -> 40.1 us
    ppermute x10 -> x13, waiting for transfers between devices: 75.3 us -> 15.2 us  [move(): return lax.ppermute(block, ('row', 'col'), route)]
    unnamed x22 -> x16, local copies, waits for them, and re-layouts: 26.9 us -> 2.89 us
    ppermute x3, waiting for transfers between devices: 0.99 us -> 14.7 us  [hop(): up.append(lax.ppermute(up[-1], 'row', ends))]
    ppermute x3, starting transfers between devices: 22.3 us -> 13.4 us  [hop(): up.append(lax.ppermute(up[-1], 'row', ends))]
    pallas_call x3, Pallas kernels: 17.1 us -> 25.7 us  [products(): pl.pallas_call(functools.partial(product_kernel, counts), grid=(rows // b...]
    ppermute x3, waiting for transfers between devices: 15.9 us -> 24.3 us  [hop(): down.append(lax.ppermute(down[-1], 'row', back))]
    ppermute x10 -> x13, starting transfers between devices: 26.9 us -> 31.8 us  [move(): return lax.ppermute(block, ('row', 'col'), route)]
    ppermute x2, starting transfers between devices: 3.49 us -> 7.4 us  [local(): arrive = lax.ppermute(rest[1::2], 'col', pairs)]
  transfers between devices with their start and end apart: 19 -> 22, of which waited for: 6 -> 7; matrix products, arithmetic and copies ran while one was open for 5% -> 7% of each run, Pallas kernels for 4% -> 14%
where the time goes in v4:
time: 197 us; the launch traced here: 196 us
  waiting for transfers between devices  81 us (41%)
  starting transfers between devices  57.5 us (29%)
  Pallas kernels  40.1 us (20%)
  other arithmetic  13.6 us (7%)
  local copies, waits for them, and re-layouts  3.87 us (2%)
    ppermute x13, starting transfers between devices, move(): return lax.ppermute(block, ('row', 'col'), route)  31.8 us
    ppermute x2, waiting for transfers between devices, local(): arrive = lax.ppermute(rest[1::2], 'col', pairs)  26.8 us
    pallas_call x3, Pallas kernels, products(): pl.pallas_call(functools.partial(product_kernel, counts), grid=(rows // b...  25.7 us
    ppermute x3, waiting for transfers between devices, hop(): down.append(lax.ppermute(down[-1], 'row', back))  24.3 us
    ppermute x13, waiting for transfers between devices, move(): return lax.ppermute(block, ('row', 'col'), route)  15.2 us
    ppermute x3, waiting for transfers between devices, hop(): up.append(lax.ppermute(up[-1], 'row', ends))  14.7 us
    ppermute x3, starting transfers between devices, hop(): up.append(lax.ppermute(up[-1], 'row', ends))  13.4 us
    ppermute x2, starting transfers between devices, local(): arrive = lax.ppermute(rest[1::2], 'col', pairs)  7.4 us
  transfers between devices with their start and end apart: 22, of which 7 were waited for; matrix products, arithmetic and copies ran while one was open for 7% of the time, Pallas kernels for 14%

profile of v4, /device:TPU:1, one launch (start us, length us, event | category | flops | bytes accessed | tf_op | source)
XLA Modules:
  0.0 196.5 jit_solution(5081307829666393556)
XLA Ops:
  0.0 1.3 cut_window.1
  1.3 1.3 collective-permute-start.5
  2.6 0.1 fusion
  2.8 0.1 dynamic_slice.14
  2.9 6.3 %pick_columns.1 = (bf16[96,1536]{1,0:T(8,128)(2,1)S(1)}, bf16[96,1536]{1,0:T(8,128)(2,1)S(1)}) custom-call(bf16[2,1536,1536]{2,1,0:T(8,128)(2,1)} %tile_ref.1, s32[1,128]{1,0:T(1,128)S(1)} %pad_bitcast_fusion.miss_ref, bf16[8,1536]{1,0:T(8,128)(2,1)S(1)} %broadcast_in_dim.35.recv_ref, f32[8,1536]{1,0:T(8,128)S(1)} %broadcast_in_dim.37.live_ref), custom_call_target="tpu_custom_call" | custom-call | flops 37748736 | bytes 147456 | tf_op jit(solution)/shard_map/pick_columns/pallas_call | solution.py:103
  9.2 1.3 collective-permute-start.1
  10.5 4.6 %collective-permute-start.3 = (bf16[96,1536]{1,0:T(8,128)(2,1)S(1)}, bf16[96,1536]{1,0:T(8,128)(2,1)S(1)}, u32[]{:S(2)}, u32[]{:S(2)}) collective-permute-start(bf16[96,1536]{1,0:T(8,128)(2,1)S(1)} %get-tuple-element.23.imag_ref), channel_id=1, source_target_pairs={{0,0},{1,4},{4,1},{5,5},{10,10},{11,14},{14,11},{15,15},{16,16},{1... | collective-permute-start | bytes 884744 | tf_op jit(solution)/shard_map/ppermute | solution.py:358
  15.1 1.9 collective-permute-start.7
  17.0 3.6 %collective-permute-start.4 = (bf16[1536,128]{1,0:T(8,128)(2,1)S(1)}, bf16[1536,128]{1,0:T(8,128)(2,1)S(1)}, u32[]{:S(2)}, u32[]{:S(2)}) collective-permute-start(bf16[1536,128]{1,0:T(8,128)(2,1)S(1)} %get-tuple-element.24), channel_id=1, source_target_pairs={{0,0},{1,4},{2,8},{3,12},{4,1},{5,5},{6,9},{7,13},{8,2},{9,6},{10,... | collective-permute-start | bytes 1179656 | tf_op jit(solution)/shard_map/ppermute | solution.py:358
  20.7 3.3 %collective-permute-start.6 = (bf16[1536,128]{1,0:T(8,128)(2,1)}, bf16[1536,128]{1,0:T(8,128)(2,1)S(1)}, u32[]{:S(2)}, u32[]{:S(2)}) collective-permute-start(bf16[1536,128]{1,0:T(8,128)(2,1)} %collective-permute-done.5), channel_id=1, source_target_pairs={{0,8},{1,12},{4,9},{5,13},{10,2},{11,6},{14,3},{15,7},{16,24},{17,... | collective-permute-start | bytes 1179656 | tf_op jit(solution)/shard_map/ppermute | solution.py:358
  24.0 2.9 %collective-permute-start.2 = (bf16[96,1536]{1,0:T(8,128)(2,1)}, bf16[96,1536]{1,0:T(8,128)(2,1)}, u32[]{:S(2)}, u32[]{:S(2)}) collective-permute-start(bf16[96,1536]{1,0:T(8,128)(2,1)} %collective-permute-done.1), channel_id=1, source_target_pairs={{0,8},{1,12},{4,9},{5,13},{10,2},{11,6},{14,3},{15,7},{16,24},{17,... | collective-permute-start | bytes 884744 | tf_op jit(solution)/shard_map/ppermute | solution.py:358
  26.9 1.9 collective-permute-start
  28.9 13.1 %collective-permute-done.2 = bf16[96,1536]{1,0:T(8,128)(2,1)} collective-permute-done((bf16[96,1536]{1,0:T(8,128)(2,1)}, bf16[96,1536]{1,0:T(8,128)(2,1)}, u32[]{:S(2)}, u32[]{:S(2)}) %collective-permute-start.2) | collective-permute-done | bytes 294944 | tf_op jit(solution)/shard_map/ppermute | solution.py:358
  42.1 1.0 add.50.imag_ref
  43.1 2.0 %collective-permute-done.real_ref = bf16[96,1536]{1,0:T(8,128)(2,1)S(1)} collective-permute-done((bf16[96,1536]{1,0:T(8,128)(2,1)S(1)}, bf16[96,1536]{1,0:T(8,128)(2,1)S(1)}, u32[]{:S(2)}, u32[]{:S(2)}) %collective-permute-start) | collective-permute-done | bytes 294944 | tf_op jit(solution)/shard_map/ppermute | solution.py:358
  45.1 0.7 copy-done.1
  45.9 0.5 fill_window.1.refs_0_.refs_3_
  46.4 11.2 %collective-permute-start.9 = (bf16[1536,256]{1,0:T(8,128)(2,1)S(1)}, bf16[1536,256]{1,0:T(8,128)(2,1)S(1)}, u32[]{:S(2)}, u32[]{:S(2)}) collective-permute-start(bf16[1536,256]{1,0:T(8,128)(2,1)S(1)} %fill_window.1.refs_0_.refs_3_), channel_id=1, source_target_pairs={{0,4},{4,8},{8,12},{1,5},{5,9},{9,13},{2,6},{6,10},{10,14},{3,7},{... | collective-permute-start | bytes 2359304 | tf_op jit(solution)/shard_map/ppermute | solution.py:403
  57.5 1.3 collective-permute-start.8
  58.8 14.7 %collective-permute-done.9.refs_2_.refs_5_.refs_7_ = bf16[1536,256]{1,0:T(8,128)(2,1)S(1)} collective-permute-done((bf16[1536,256]{1,0:T(8,128)(2,1)S(1)}, bf16[1536,256]{1,0:T(8,128)(2,1)S(1)}, u32[]{:S(2)}, u32[]{:S(2)}) %collective-permute-start.9) | collective-permute-done | bytes 786464 | tf_op jit(solution)/shard_map/ppermute | solution.py:403
  73.5 0.7 collective-permute-start.12
  74.2 5.0 %collective-permute-done.8.refs_1_.refs_4_.refs_6_ = bf16[1536,256]{1,0:T(8,128)(2,1)S(1)} collective-permute-done((bf16[1536,256]{1,0:T(8,128)(2,1)S(1)}, bf16[1536,256]{1,0:T(8,128)(2,1)S(1)}, u32[]{:S(2)}, u32[]{:S(2)}) %collective-permute-start.8) | collective-permute-done | bytes 786464 | tf_op jit(solution)/shard_map/ppermute | solution.py:404
  79.1 1.3 collective-permute-start.11
  80.5 9.6 %products.3 = (f32[1536,256]{1,0:T(8,128)S(1)}, f32[1536,256]{1,0:T(8,128)}) custom-call(s32[2]{0:T(128)S(1)} %pad_add_fusion.pick_ref, bf16[2,1536,1536]{2,1,0:T(8,128)(2,1)} %tile_ref.1, bf16[8,1536]{1,0:T(8,128)(2,1)S(1)} %broadcast_in_dim.35.recv_ref, bf16[1536,256]{1,0:T(8,128)(2,1)S(1)} %fill_window.1.refs_0_.refs_3_, ...), custom_call_target="tpu_custom_call" | custom-call | flops 150994944 | bytes 24576 | tf_op jit(solution)/shard_map/products/pallas_call | solution.py:212
  90.1 1.1 copy-done
  91.2 1.1 collective-permute-start.10
  92.3 6.7 %collective-permute-done.11.refs_0_.refs_3_ = bf16[1536,256]{1,0:T(8,128)(2,1)} collective-permute-done((bf16[1536,256]{1,0:T(8,128)(2,1)S(1)}, bf16[1536,256]{1,0:T(8,128)(2,1)}, u32[]{:S(2)}, u32[]{:S(2)}) %collective-permute-start.11) | collective-permute-done | bytes 786464 | tf_op jit(solution)/shard_map/ppermute | solution.py:404
  99.1 8.0 %products.4 = f32[1536,256]{1,0:T(8,128)} custom-call(s32[1]{0:T(128)} %bitcast.7.pick_ref, bf16[2,1536,1536]{2,1,0:T(8,128)(2,1)} %tile_ref.1, bf16[8,1536]{1,0:T(8,128)(2,1)S(1)} %broadcast_in_dim.35.recv_ref, bf16[1536,256]{1,0:T(8,128)(2,1)} %collective-permute-done.11.refs_0_.refs_3_, bf16[1536,256]{1,0:T(8,128)(2,1)S(1)} %collective-permute-done.12.refs_1_.refs_4_), custom_call_target="tpu_custom_call" | custom-call | flops 75497472 | bytes 24576 | tf_op jit(solution)/shard_map/products/pallas_call | solution.py:212
  107.0 5.1 %collective-permute-start.13 = (f32[1536,256]{1,0:T(8,128)}, f32[1536,256]{1,0:T(8,128)}, u32[]{:S(2)}, u32[]{:S(2)}) collective-permute-start(f32[1536,256]{1,0:T(8,128)} %products.4), channel_id=1, source_target_pairs={{1,0},{3,2},{4,5},{6,7},{9,8},{11,10},{12,13},{14,15},{17,16},{19,... | collective-permute-start | bytes 4718600 | tf_op jit(solution)/shard_map/ppermute | solution.py:358
  112.1 1.5 collective-permute-start.15
  113.7 1.3 collective-permute-start.14
  115.0 3.3 %add.53 = f32[1536,256]{1,0:T(8,128)} add(f32[1536,256]{1,0:T(8,128)} %copy-done, f32[1536,256]{1,0:T(8,128)} %collective-permute-done.10) | non-fusion elementwise | flops 393216 | bytes 4718592 | tf_op jit(solution)/shard_map/add | solution.py:432
  118.3 3.2 %add.54 = f32[1536,256]{1,0:T(8,128)} add(f32[1536,256]{1,0:T(8,128)} %products.4, f32[1536,256]{1,0:T(8,128)} %collective-permute-done.13) | non-fusion elementwise | flops 393216 | bytes 4718592 | tf_op jit(solution)/shard_map/add | solution.py:408
  121.5 12.6 %collective-permute-done.14.refs_0_.refs_5_ = bf16[1536,256]{1,0:T(8,128)(2,1)} collective-permute-done((bf16[1536,256]{1,0:T(8,128)(2,1)}, bf16[1536,256]{1,0:T(8,128)(2,1)}, u32[]{:S(2)}, u32[]{:S(2)}) %collective-permute-start.14) | collective-permute-done | bytes 786464 | tf_op jit(solution)/shard_map/ppermute | solution.py:404
  134.1 8.2 %products.5 = f32[1536,256]{1,0:T(8,128)} custom-call(s32[1]{0:T(128)} %bitcast.4.pick_ref, bf16[2,1536,1536]{2,1,0:T(8,128)(2,1)} %tile_ref.1, bf16[8,1536]{1,0:T(8,128)(2,1)S(1)} %broadcast_in_dim.35.recv_ref, bf16[1536,256]{1,0:T(8,128)(2,1)} %collective-permute-done.14.refs_0_.refs_5_, ...), custom_call_target="tpu_custom_call" | custom-call | flops 75497472 | bytes 24576 | tf_op jit(solution)/shard_map/products/pallas_call | solution.py:212
  142.3 1.3 collective-permute-start.16
  143.6 1.3 collective-permute-start.17
  144.9 1.8 collective-permute-start.18
  146.8 1.0 copy-done.2
  147.8 3.3 %extra_products.1 = f32[4,96,256]{2,1,0:T(8,128)S(1)} custom-call(s32[8]{0:T(128)S(1)} %stack.46.pick_ref, bf16[96,1536]{1,0:T(8,128)(2,1)S(1)} %copy-done.2, bf16[96,1536]{1,0:T(8,128)(2,1)S(1)} %add.50.imag_ref, bf16[1536,256]{1,0:T(8,128)(2,1)S(1)} %fill_window.1.refs_0_.refs_3_, bf16[1536,256]{1,0:T(8,128)(2,1)S(1)} %collective-permute-done.8.refs_1_.refs_4_.refs_6_, ...), custom_call_target="tpu_custom_call" | custom-call | flops 18874368 | bytes 24576 | tf_op jit(solution)/shard_map/extra_products/pallas_call | solution.py:245
  151.2 7.4 %collective-permute-start.20 = (f32[2,96,256]{2,1,0:T(8,128)S(1)}, f32[2,96,256]{2,1,0:T(8,128)S(1)}, u32[]{:S(2)}, u32[]{:S(2)}) collective-permute-start(f32[2,96,256]{2,1,0:T(8,128)S(1)} %slice.15), channel_id=1, source_target_pairs={{0,1},{1,0},{2,3},{3,2},{4,5},{5,4},{6,7},{7,6},{8,9},{9,8},{10,11... | collective-permute-start | bytes 589832 | tf_op jit(solution)/shard_map/ppermute | solution.py:456
  158.6 2.1 %add.55.refs_0_ = f32[1536,256]{1,0:T(8,128)S(1)} add(f32[1536,256]{1,0:T(8,128)} %products.5, f32[1536,256]{1,0:T(8,128)} %collective-permute-done.16) | non-fusion elementwise | flops 393216 | bytes 4718592 | tf_op jit(solution)/shard_map/add | solution.py:408
  160.6 1.4 collective-permute-start.19
  162.1 0.7 slice.19
  162.8 26.8 %collective-permute-done.21 = f32[1,96,256]{2,1,0:T(8,128)} collective-permute-done((f32[1,96,256]{2,1,0:T(8,128)}, f32[1,96,256]{2,1,0:T(8,128)}, u32[]{:S(2)}, u32[]{:S(2)}) %collective-permute-start.21) | collective-permute-done | bytes 98336 | tf_op jit(solution)/shard_map/ppermute | solution.py:456
  189.7 1.0 fusion.1.refs_3_
  190.7 2.8 %add_add_fusion.refs_1_ = f32[1536,256]{1,0:T(8,128)S(1)} fusion(f32[1536,256]{1,0:T(8,128)} %collective-permute-done.18, f32[1536,256]{1,0:T(8,128)} %add.54, f32[1536,256]{1,0:T(8,128)} %collective-permute-done.17, f32[1536,256]{1,0:T(8,128)} %add.53, pred[]{:T(512)S(6)} %eq.26, pred[]{:T(512)S(6)} %eq.25), kind=kLoop, calls=%fused_computation | loop fusion | flops 1966080 | bytes 7864322 | tf_op jit(solution)/shard_map/add | solution.py:448
  193.5 3.0 %finish.1 = f32[2,1536,128]{2,1,0:T(8,128)} custom-call(f32[2]{0:T(128)S(1)} %broadcast_multiply_fusion.wave_ref, f32[1]{0:T(128)} %bitcast.flag_ref, s32[96]{0:T(128)S(1)} %get-tuple-element.32.miss_ref, bf16[8,1536]{1,0:T(8,128)(2,1)S(1)} %broadcast_in_dim.35.recv_ref, bf16[2,1536,1536]{2,1,0:T(8,128)(2,1)} %tile_ref.1, bf16[96,1536]{1,0:T(8,128)(2,1)S(1)} %copy-done.3, ...), custom_call_target="tpu_custom_call" | custom-call | flops 61440 | bytes 122880 | tf_op jit(solution)/shard_map/finish/pallas_call | solution.py:295
  (42 shorter events, 0.4 us)
Async XLA Ops:
  0.0 2.6 %copy-start.5 = (s32[6144]{0:T(1024)S(1)}, s32[6144]{0:T(1024)}, u32[]{:S(2)}) copy-start(s32[6144]{0:T(1024)} %param.5) | copy-start | bytes 73732
  0.0 2.6 %copy-start.6 = (s32[4,96]{1,0:T(4,128)S(1)}, s32[4,96]{1,0:T(4,128)}, u32[]{:S(2)}) copy-start(s32[4,96]{1,0:T(4,128)} %param.6) | copy-start | bytes 4612
  1.3 19.4 %collective-permute-start.5 = (bf16[1536,128]{1,0:T(8,128)(2,1)S(1)}, bf16[1536,128]{1,0:T(8,128)(2,1)}, u32[]{:S(2)}, u32[]{:S(2)}) collective-permute-start(bf16[1536,128]{1,0:T(8,128)(2,1)S(1)} %get-tuple-element.25), channel_id=1, source_target_pairs={{2,0},{3,1},{6,4},{7,5},{8,10},{9,11},{12,14},{13,15},{18,16},{19,... | collective-permute-start | bytes 1179656 | tf_op jit(solution)/shard_map/ppermute | solution.py:358
  9.2 14.8 %collective-permute-start.1 = (bf16[96,1536]{1,0:T(8,128)(2,1)S(1)}, bf16[96,1536]{1,0:T(8,128)(2,1)}, u32[]{:S(2)}, u32[]{:S(2)}) collective-permute-start(bf16[96,1536]{1,0:T(8,128)(2,1)S(1)} %get-tuple-element.23.imag_ref), channel_id=1, source_target_pairs={{2,0},{3,1},{6,4},{7,5},{8,10},{9,11},{12,14},{13,15},{18,16},{19,... | collective-permute-start | bytes 884744 | tf_op jit(solution)/shard_map/ppermute | solution.py:358
  10.5 16.4 %collective-permute-start.3 = (bf16[96,1536]{1,0:T(8,128)(2,1)S(1)}, bf16[96,1536]{1,0:T(8,128)(2,1)S(1)}, u32[]{:S(2)}, u32[]{:S(2)}) collective-permute-start(bf16[96,1536]{1,0:T(8,128)(2,1)S(1)} %get-tuple-element.23.imag_ref), channel_id=1, source_target_pairs={{0,0},{1,4},{4,1},{5,5},{10,10},{11,14},{14,11},{15,15},{16,16},{1... | collective-permute-start | bytes 884744 | tf_op jit(solution)/shard_map/ppermute | solution.py:358
  15.1 30.8 %collective-permute-start.7 = (bf16[1536,128]{1,0:T(8,128)(2,1)S(1)}, bf16[1536,128]{1,0:T(8,128)(2,1)S(1)}, u32[]{:S(2)}, u32[]{:S(2)}) collective-permute-start(bf16[1536,128]{1,0:T(8,128)(2,1)S(1)} %get-tuple-element.25), channel_id=1, source_target_pairs={{0,0},{1,4},{4,1},{5,5},{10,10},{11,14},{14,11},{15,15},{16,16},{1... | collective-permute-start | bytes 1179656 | tf_op jit(solution)/shard_map/ppermute | solution.py:358
  17.0 28.8 %collective-permute-start.4 = (bf16[1536,128]{1,0:T(8,128)(2,1)S(1)}, bf16[1536,128]{1,0:T(8,128)(2,1)S(1)}, u32[]{:S(2)}, u32[]{:S(2)}) collective-permute-start(bf16[1536,128]{1,0:T(8,128)(2,1)S(1)} %get-tuple-element.24), channel_id=1, source_target_pairs={{0,0},{1,4},{2,8},{3,12},{4,1},{5,5},{6,9},{7,13},{8,2},{9,6},{10,... | collective-permute-start | bytes 1179656 | tf_op jit(solution)/shard_map/ppermute | solution.py:358
  20.7 25.2 %collective-permute-start.6 = (bf16[1536,128]{1,0:T(8,128)(2,1)}, bf16[1536,128]{1,0:T(8,128)(2,1)S(1)}, u32[]{:S(2)}, u32[]{:S(2)}) collective-permute-start(bf16[1536,128]{1,0:T(8,128)(2,1)} %collective-permute-done.5), channel_id=1, source_target_pairs={{0,8},{1,12},{4,9},{5,13},{10,2},{11,6},{14,3},{15,7},{16,24},{17,... | collective-permute-start | bytes 1179656 | tf_op jit(solution)/shard_map/ppermute | solution.py:358
  24.0 18.1 %collective-permute-start.2 = (bf16[96,1536]{1,0:T(8,128)(2,1)}, bf16[96,1536]{1,0:T(8,128)(2,1)}, u32[]{:S(2)}, u32[]{:S(2)}) collective-permute-start(bf16[96,1536]{1,0:T(8,128)(2,1)} %collective-permute-done.1), channel_id=1, source_target_pairs={{0,8},{1,12},{4,9},{5,13},{10,2},{11,6},{14,3},{15,7},{16,24},{17,... | collective-permute-start | bytes 884744 | tf_op jit(solution)/shard_map/ppermute | solution.py:358
  26.9 18.2 %collective-permute-start = (bf16[96,1536]{1,0:T(8,128)(2,1)S(1)}, bf16[96,1536]{1,0:T(8,128)(2,1)S(1)}, u32[]{:S(2)}, u32[]{:S(2)}) collective-permute-start(bf16[96,1536]{1,0:T(8,128)(2,1)S(1)} %get-tuple-element.22.real_ref), channel_id=1, source_target_pairs={{0,0},{1,4},{2,8},{3,12},{4,1},{5,5},{6,9},{7,13},{8,2},{9,6},{10,... | collective-permute-start | bytes 884744 | tf_op jit(solution)/shard_map/ppermute | solution.py:358
  45.1 0.7 copy-start.1
  46.4 27.1 %collective-permute-start.9 = (bf16[1536,256]{1,0:T(8,128)(2,1)S(1)}, bf16[1536,256]{1,0:T(8,128)(2,1)S(1)}, u32[]{:S(2)}, u32[]{:S(2)}) collective-permute-start(bf16[1536,256]{1,0:T(8,128)(2,1)S(1)} %fill_window.1.refs_0_.refs_3_), channel_id=1, source_target_pairs={{0,4},{4,8},{8,12},{1,5},{5,9},{9,13},{2,6},{6,10},{10,14},{3,7},{... | collective-permute-start | bytes 2359304 | tf_op jit(solution)/shard_map/ppermute | solution.py:403
  57.5 21.6 %collective-permute-start.8 = (bf16[1536,256]{1,0:T(8,128)(2,1)S(1)}, bf16[1536,256]{1,0:T(8,128)(2,1)S(1)}, u32[]{:S(2)}, u32[]{:S(2)}) collective-permute-start(bf16[1536,256]{1,0:T(8,128)(2,1)S(1)} %fill_window.1.refs_0_.refs_3_), channel_id=1, source_target_pairs={{4,0},{8,4},{12,8},{5,1},{9,5},{13,9},{6,2},{10,6},{14,10},{7,3},{... | collective-permute-start | bytes 2359304 | tf_op jit(solution)/shard_map/ppermute | solution.py:404
  73.5 18.9 %collective-permute-start.12 = (bf16[1536,256]{1,0:T(8,128)(2,1)S(1)}, bf16[1536,256]{1,0:T(8,128)(2,1)S(1)}, u32[]{:S(2)}, u32[]{:S(2)}) collective-permute-start(bf16[1536,256]{1,0:T(8,128)(2,1)S(1)} %collective-permute-done.9.refs_2_.refs_5_.refs_7_), channel_id=1, source_target_pairs={{4,8},{8,12},{5,9},{9,13},{6,10},{10,14},{7,11},{11,15},{20,24},{2... | collective-permute-start | bytes 2359304 | tf_op jit(solution)/shard_map/ppermute | solution.py:403
  79.1 19.9 %collective-permute-start.11 = (bf16[1536,256]{1,0:T(8,128)(2,1)S(1)}, bf16[1536,256]{1,0:T(8,128)(2,1)}, u32[]{:S(2)}, u32[]{:S(2)}) collective-permute-start(bf16[1536,256]{1,0:T(8,128)(2,1)S(1)} %collective-permute-done.8.refs_1_.refs_4_.refs_6_), channel_id=1, source_target_pairs={{4,0},{8,4},{5,1},{9,5},{6,2},{10,6},{7,3},{11,7},{20,16},{24,20},... | collective-permute-start | bytes 2359304 | tf_op jit(solution)/shard_map/ppermute | solution.py:404
  90.1 1.1 copy-start
  91.2 23.7 %collective-permute-start.10 = (f32[1536,256]{1,0:T(8,128)}, f32[1536,256]{1,0:T(8,128)}, u32[]{:S(2)}, u32[]{:S(2)}) collective-permute-start(f32[1536,256]{1,0:T(8,128)} %get-tuple-element.27), channel_id=1, source_target_pairs={{0,1},{1,0},{2,3},{3,2},{4,5},{5,4},{6,7},{7,6},{8,9},{9,8},{10,11... | collective-permute-start | bytes 4718600 | tf_op jit(solution)/shard_map/ppermute | solution.py:432
  107.0 11.2 %collective-permute-start.13 = (f32[1536,256]{1,0:T(8,128)}, f32[1536,256]{1,0:T(8,128)}, u32[]{:S(2)}, u32[]{:S(2)}) collective-permute-start(f32[1536,256]{1,0:T(8,128)} %products.4), channel_id=1, source_target_pairs={{1,0},{3,2},{4,5},{6,7},{9,8},{11,10},{12,13},{14,15},{17,16},{19,... | collective-permute-start | bytes 4718600 | tf_op jit(solution)/shard_map/ppermute | solution.py:358
  112.1 9.4 %collective-permute-start.15 = (bf16[1536,256]{1,0:T(8,128)(2,1)S(1)}, bf16[1536,256]{1,0:T(8,128)(2,1)}, u32[]{:S(2)}, u32[]{:S(2)}) collective-permute-start(bf16[1536,256]{1,0:T(8,128)(2,1)S(1)} %collective-permute-done.12.refs_1_.refs_4_), channel_id=1, source_target_pairs={{8,12},{9,13},{10,14},{11,15},{24,28},{25,29},{26,30},{27,31}} | collective-permute-start | bytes 2359304 | tf_op jit(solution)/shard_map/ppermute | solution.py:403
  113.7 20.4 %collective-permute-start.14 = (bf16[1536,256]{1,0:T(8,128)(2,1)}, bf16[1536,256]{1,0:T(8,128)(2,1)}, u32[]{:S(2)}, u32[]{:S(2)}) collective-permute-start(bf16[1536,256]{1,0:T(8,128)(2,1)} %collective-permute-done.11.refs_0_.refs_3_), channel_id=1, source_target_pairs={{4,0},{5,1},{6,2},{7,3},{20,16},{21,17},{22,18},{23,19}} | collective-permute-start | bytes 2359304 | tf_op jit(solution)/shard_map/ppermute | solution.py:404
  142.3 16.3 %collective-permute-start.16 = (f32[1536,256]{1,0:T(8,128)}, f32[1536,256]{1,0:T(8,128)}, u32[]{:S(2)}, u32[]{:S(2)}) collective-permute-start(f32[1536,256]{1,0:T(8,128)} %products.5), channel_id=1, source_target_pairs={{0,1},{2,3},{5,4},{7,6},{8,9},{10,11},{13,12},{15,14},{16,17},{18,... | collective-permute-start | bytes 4718600 | tf_op jit(solution)/shard_map/ppermute | solution.py:358
  143.6 47.1 %collective-permute-start.17 = (f32[1536,256]{1,0:T(8,128)}, f32[1536,256]{1,0:T(8,128)}, u32[]{:S(2)}, u32[]{:S(2)}) collective-permute-start(f32[1536,256]{1,0:T(8,128)} %add.53), channel_id=1, source_target_pairs={{2,0},{3,1},{6,4},{7,5},{8,10},{9,11},{12,14},{13,15},{18,16},{19,... | collective-permute-start | bytes 4718600 | tf_op jit(solution)/shard_map/ppermute | solution.py:358
  144.9 45.8 %collective-permute-start.18 = (f32[1536,256]{1,0:T(8,128)}, f32[1536,256]{1,0:T(8,128)}, u32[]{:S(2)}, u32[]{:S(2)}) collective-permute-start(f32[1536,256]{1,0:T(8,128)} %add.54), channel_id=1, source_target_pairs={{0,2},{5,7},{10,8},{15,13},{16,18},{21,23},{26,24},{31,29}} | collective-permute-start | bytes 4718600 | tf_op jit(solution)/shard_map/ppermute | solution.py:358
  146.8 1.0 copy-start.2
  151.1 11.7 %copy-start.7 = (f32[2]{0:T(128)S(1)}, f32[2]{0:T(128)}, u32[]{:S(2)}) copy-start(f32[2]{0:T(128)} %param.7) | copy-start | bytes 28
  151.2 10.9 %collective-permute-start.20 = (f32[2,96,256]{2,1,0:T(8,128)S(1)}, f32[2,96,256]{2,1,0:T(8,128)S(1)}, u32[]{:S(2)}, u32[]{:S(2)}) collective-permute-start(f32[2,96,256]{2,1,0:T(8,128)S(1)} %slice.15), channel_id=1, source_target_pairs={{0,1},{1,0},{2,3},{3,2},{4,5},{5,4},{6,7},{7,6},{8,9},{9,8},{10,11... | collective-permute-start | bytes 589832 | tf_op jit(solution)/shard_map/ppermute | solution.py:456
  160.6 32.8 %collective-permute-start.19 = (f32[1536,256]{1,0:T(8,128)S(1)}, f32[1536,256]{1,0:T(8,128)S(1)}, u32[]{:S(2)}, u32[]{:S(2)}) collective-permute-start(f32[1536,256]{1,0:T(8,128)S(1)} %add.55.refs_0_), channel_id=1, source_target_pairs={{1,3},{4,6},{11,9},{14,12},{17,19},{20,22},{27,25},{30,28}} | collective-permute-start | bytes 4718600 | tf_op jit(solution)/shard_map/ppermute | solution.py:358
  162.1 0.7 copy-start.4
  162.8 26.9 %collective-permute-start.21 = (f32[1,96,256]{2,1,0:T(8,128)}, f32[1,96,256]{2,1,0:T(8,128)}, u32[]{:S(2)}, u32[]{:S(2)}) collective-permute-start(f32[1,96,256]{2,1,0:T(8,128)} %slice.19), channel_id=1, source_target_pairs={{0,2},{1,3},{2,0},{3,1},{4,6},{5,7},{6,4},{7,5},{8,10},{9,11},{10,... | collective-permute-start | bytes 294920 | tf_op jit(solution)/shard_map/ppermute | solution.py:456
  190.6 2.9 %copy-start.3 = (bf16[96,1536]{1,0:T(8,128)(2,1)S(1)}, bf16[96,1536]{1,0:T(8,128)(2,1)}, u32[]{:S(2)}) copy-start(bf16[96,1536]{1,0:T(8,128)(2,1)} %copy-done.1) | copy-start | bytes 884740

commit v5 on v4

--- a/solution.py
+++ b/solution.py
@@ -185,7 +185,8 @@
             out_ref[...] = ref[...]
 
 
-def product_kernel(counts, pick_ref, traces_ref, recv_ref, *refs):
+def product_kernel(counts, pick_ref, recv_ref, *refs):
+    tiles, refs = refs[:4], refs[4:]
     total, places = sum(counts), len(counts)
     out_refs, right_refs = refs[total:total + places], refs[total + places:]
 
@@ -197,9 +198,13 @@
             used += count
 
     recv = recv_ref[0:1, :]
-    real_rows, imag_rows = traces_ref[0] * recv, traces_ref[1] * recv
-    for out_ref, right_ref in zip(out_refs, right_refs):
-        out_ref[...] = complex_rows(real_rows, imag_rows, right_ref[...])
+    half = tiles[0].shape[1]
+    for side in range(2):
+        real_rows, imag_rows = (tiles[2 * part + side][0] * recv for part in range(2))
+        for out_ref, right_ref in zip(out_refs, right_refs):
+            out_ref[side * half:(side + 1) * half, :] = complex_rows(
+                real_rows, imag_rows, right_ref[...]
+            )
 
 
 def products(traces, recv8, groups):
@@ -208,15 +213,18 @@
     counts = tuple(len(sources) for _, sources in groups)
     flat = [source for _, sources in groups for source in sources]
     picks = jnp.stack([pick for pick, _ in groups]).astype(jnp.int32)
-    block = row_block(rows) // 2
+    block = row_block(rows)
+    quarter = lambda part, side: pl.BlockSpec(
+        (1, block // 2, cols), lambda i: (part, 2 * i + side, 0)
+    )
     return pl.pallas_call(
         functools.partial(product_kernel, counts),
         grid=(rows // block,),
         in_specs=[
             SMEM,
-            pl.BlockSpec((2, block, cols), lambda i: (0, i, 0)),
             pl.BlockSpec((8, cols), lambda i: (0, 0)),
         ]
+        + [quarter(part, side) for part in range(2) for side in range(2)]
         + [pl.BlockSpec((cols, lanes), lambda i: (0, 0))] * len(flat),
         out_specs=[pl.BlockSpec((block, lanes), lambda i: (i, 0))] * len(groups),
         out_shape=[jax.ShapeDtypeStruct((rows, lanes), jnp.float32)] * len(groups),
@@ -224,7 +232,7 @@
         compiler_params=params(),
         cost_estimate=cost(8 * rows * cols * lanes * len(groups), 4 * rows * lanes),
         name="products",
-    )(picks, traces, recv8, *flat)
+    )(picks, recv8, *[traces] * 4, *flat)
 
 
 def extra_kernel(counts, pick_ref, real_ref, imag_ref, *refs):
@@ -387,8 +395,8 @@
     recv_col8 = jnp.broadcast_to(recv_col[None], (8, tile))
 
     picked = pick_columns(traces, miss_col_lanes, recv_col8, live8, misses)
-    extra = [transpose(picked[0]), functools.reduce(jnp.add, transpose_round(picked[1]))]
-    picked, extra = lax.optimization_barrier((picked, extra))
+    extra = transpose(jnp.concatenate(picked))
+    extra = [extra[:misses], extra[misses:]]
     apart = row_index ^ col_index
     strides = [2**bit for bit in range(grid_size.bit_length() - 1)]
     terms, extra_terms = [], []
@@ -436,9 +444,9 @@
         mask = recv_col8
         for offset in range(2, grid_size):
             if offset == grid_size - 1:
-                totals = [total for *_, total in sums]
-                mask, totals = lax.optimization_barrier((mask, totals))
-                sums = [(*rest, total) for (*rest, _), total in zip(sums, totals)]
+                *rest, total = sums[0]
+                mask, total, extra = lax.optimization_barrier((mask, total, extra))
+                sums[0] = (*rest, total)
             (total,) = products(traces, mask, [options(offset)])
             total = add_up(total, offset, strides[:-1], 0)
             sums.append((offset, 0, apart == offset, total))

time: 197 us -> 197 us (level)
  Pallas kernels: 40.1 us -> 37.8 us
  waiting for transfers between devices: 81 us -> 83.3 us
    ppermute x3, waiting for transfers between devices: 24.3 us -> 49.5 us  [hop(): down.append(lax.ppermute(down[-1], 'row', back))]
    ppermute x3, waiting for transfers between devices: 14.7 us -> 0.86 us  [hop(): up.append(lax.ppermute(up[-1], 'row', ends))]
    ppermute x13 -> x10, waiting for transfers between devices: 15.2 us -> 6.21 us  [move(): return lax.ppermute(block, ('row', 'col'), route)]
    pallas_call x3, Pallas kernels: 25.7 us -> 23.5 us  [products(): pl.pallas_call(functools.partial(product_kernel, counts), grid=(rows // b...]
    ppermute x13 -> x10, starting transfers between devices: 31.8 us -> 31.9 us  [move(): return lax.ppermute(block, ('row', 'col'), route)]
  transfers between devices with their start and end apart: 22 -> 19, of which waited for: 7 -> 7; matrix products, arithmetic and copies ran while one was open for 7% -> 8% of each run, Pallas kernels for 14% -> 13%
where the time goes in v5:
time: 197 us; the launch traced here: 196 us
  waiting for transfers between devices  83.3 us (42%)
  starting transfers between devices  56.4 us (29%)
  Pallas kernels  37.8 us (19%)
  other arithmetic  13.5 us (7%)
  local copies, waits for them, and re-layouts  5 us (3%)
    ppermute x3, waiting for transfers between devices, hop(): down.append(lax.ppermute(down[-1], 'row', back))  49.5 us
    ppermute x10, starting transfers between devices, move(): return lax.ppermute(block, ('row', 'col'), route)  31.9 us
    ppermute x2, waiting for transfers between devices, local(): arrive = lax.ppermute(rest[1::2], 'col', pairs)  26.8 us
    pallas_call x3, Pallas kernels, products(): pl.pallas_call(functools.partial(product_kernel, counts), grid=(rows // b...  23.5 us
    ppermute x3, starting transfers between devices, hop(): up.append(lax.ppermute(up[-1], 'row', ends))  12.3 us
    ppermute x2, starting transfers between devices, local(): arrive = lax.ppermute(rest[1::2], 'col', pairs)  7.37 us
    pallas_call x1, Pallas kernels, pick_columns(): pl.pallas_call(pick_kernel, grid=(rows // block,), in_specs=[pl.BlockSpec...  6.28 us
    ppermute x10, waiting for transfers between devices, move(): return lax.ppermute(block, ('row', 'col'), route)  6.21 us
  transfers between devices with their start and end apart: 19, of which 7 were waited for; matrix products, arithmetic and copies ran while one was open for 8% of the time, Pallas kernels for 13%

profile of v5, /device:TPU:1, one launch (start us, length us, event | category | flops | bytes accessed | tf_op | source)
XLA Modules:
  0.0 196.5 jit_solution(477930599085138150)
XLA Ops:
  0.0 1.3 cut_window.1
  1.3 1.3 collective-permute-start.1
  2.6 4.6 %collective-permute-start.3 = (bf16[1536,128]{1,0:T(8,128)(2,1)S(1)}, bf16[1536,128]{1,0:T(8,128)(2,1)S(1)}, u32[]{:S(2)}, u32[]{:S(2)}) collective-permute-start(bf16[1536,128]{1,0:T(8,128)(2,1)S(1)} %get-tuple-element.18), channel_id=1, source_target_pairs={{0,0},{1,4},{4,1},{5,5},{10,10},{11,14},{14,11},{15,15},{16,16},{1... | collective-permute-start | bytes 1179656 | tf_op jit(solution)/shard_map/ppermute | solution.py:366
  7.2 1.9 collective-permute-start
  9.2 4.4 %collective-permute-done.1 = bf16[1536,128]{1,0:T(8,128)(2,1)S(1)} collective-permute-done((bf16[1536,128]{1,0:T(8,128)(2,1)S(1)}, bf16[1536,128]{1,0:T(8,128)(2,1)S(1)}, u32[]{:S(2)}, u32[]{:S(2)}) %collective-permute-start.1) | collective-permute-done | bytes 393248 | tf_op jit(solution)/shard_map/ppermute | solution.py:366
  13.5 6.1 %collective-permute-start.2 = (bf16[1536,128]{1,0:T(8,128)(2,1)S(1)}, bf16[1536,128]{1,0:T(8,128)(2,1)S(1)}, u32[]{:S(2)}, u32[]{:S(2)}) collective-permute-start(bf16[1536,128]{1,0:T(8,128)(2,1)S(1)} %collective-permute-done.1), channel_id=1, source_target_pairs={{0,8},{1,12},{4,9},{5,13},{10,2},{11,6},{14,3},{15,7},{16,24},{17,... | collective-permute-start | bytes 1179656 | tf_op jit(solution)/shard_map/ppermute | solution.py:366
  19.7 0.1 fusion
  19.9 0.1 dynamic_slice.14
  20.0 0.1 dynamic_slice.16
  20.1 6.3 %pick_columns.1 = (bf16[96,1536]{1,0:T(8,128)(2,1)S(1)}, bf16[96,1536]{1,0:T(8,128)(2,1)S(1)}) custom-call(bf16[2,1536,1536]{2,1,0:T(8,128)(2,1)} %tile_ref.1, s32[1,128]{1,0:T(1,128)S(1)} %pad_bitcast_fusion.miss_ref, bf16[8,1536]{1,0:T(8,128)(2,1)S(1)} %broadcast_in_dim.35.recv_ref, f32[8,1536]{1,0:T(8,128)S(1)} %broadcast_in_dim.37.live_ref), custom_call_target="tpu_custom_call" | custom-call | flops 37748736 | bytes 147456 | tf_op jit(solution)/shard_map/pick_columns/pallas_call | solution.py:103
  26.4 1.8 collective-permute-done.2.refs_1_
  28.2 0.4 fill_window.1.refs_4_.refs_7_.refs_0_
  28.7 1.3 collective-permute-start.4
  30.0 10.0 %collective-permute-start.5 = (bf16[1536,256]{1,0:T(8,128)(2,1)S(1)}, bf16[1536,256]{1,0:T(8,128)(2,1)S(1)}, u32[]{:S(2)}, u32[]{:S(2)}) collective-permute-start(bf16[1536,256]{1,0:T(8,128)(2,1)S(1)} %fill_window.1.refs_4_.refs_7_.refs_0_), channel_id=1, source_target_pairs={{0,4},{4,8},{8,12},{1,5},{5,9},{9,13},{2,6},{6,10},{10,14},{3,7},{... | collective-permute-start | bytes 2359304 | tf_op jit(solution)/shard_map/ppermute | solution.py:411
  40.0 0.1 pad_add_fusion.pick_ref
  40.1 15.7 %collective-permute-done.4.refs_5_.refs_8_.refs_1_.refs_6_ = bf16[1536,256]{1,0:T(8,128)(2,1)S(1)} collective-permute-done((bf16[1536,256]{1,0:T(8,128)(2,1)S(1)}, bf16[1536,256]{1,0:T(8,128)(2,1)S(1)}, u32[]{:S(2)}, u32[]{:S(2)}) %collective-permute-start.4) | collective-permute-done | bytes 786464 | tf_op jit(solution)/shard_map/ppermute | solution.py:412
  55.9 0.9 collective-permute-done.5.refs_6_.refs_9_.refs_2_.refs_7_
  56.7 8.5 %products.3 = (f32[1536,256]{1,0:T(8,128)S(1)}, f32[1536,256]{1,0:T(8,128)}) custom-call(s32[2]{0:T(128)S(1)} %pad_add_fusion.pick_ref, bf16[8,1536]{1,0:T(8,128)(2,1)S(1)} %broadcast_in_dim.35.recv_ref, bf16[2,1536,1536]{2,1,0:T(8,128)(2,1)} %tile_ref.1, bf16[2,1536,1536]{2,1,0:T(8,128)(2,1)} %tile_ref.1, bf16[2,1536,1536]{2,1,0:T(8,128)(2,1)} %tile_ref.1, ...), custom_call_target="tpu_custom_call" | custom-call | flops 150994944 | bytes 24576 | tf_op jit(solution)/shard_map/products/pallas_call | solution.py:220
  65.2 1.2 copy-done.2
  66.3 1.0 collective-permute-start.6
  67.3 0.7 collective-permute-start.10
  68.0 1.3 collective-permute-start.8
  69.3 0.9 pad_maximum_fusion
  70.2 8.1 %collective-permute-start.7 = (bf16[192,1536]{1,0:T(8,128)(2,1)}, bf16[192,1536]{1,0:T(8,128)(2,1)}, u32[]{:S(2)}, u32[]{:S(2)}) collective-permute-start(bf16[192,1536]{1,0:T(8,128)(2,1)} %pad_maximum_fusion), channel_id=1, source_target_pairs={{0,0},{1,4},{2,8},{3,12},{4,1},{5,5},{6,9},{7,13},{8,2},{9,6},{10,... | collective-permute-start | bytes 1769480 | tf_op jit(solution)/shard_map/ppermute | solution.py:366
  78.4 1.6 collective-permute-start.11
  80.0 19.6 %collective-permute-done.8.refs_4_.refs_3_ = bf16[1536,256]{1,0:T(8,128)(2,1)} collective-permute-done((bf16[1536,256]{1,0:T(8,128)(2,1)S(1)}, bf16[1536,256]{1,0:T(8,128)(2,1)}, u32[]{:S(2)}, u32[]{:S(2)}) %collective-permute-start.8) | collective-permute-done | bytes 786464 | tf_op jit(solution)/shard_map/ppermute | solution.py:412
  99.5 1.3 collective-permute-start.9
  100.8 7.4 %products.5 = f32[1536,256]{1,0:T(8,128)} custom-call(s32[1]{0:T(128)} %bitcast.7.pick_ref, bf16[8,1536]{1,0:T(8,128)(2,1)S(1)} %broadcast_in_dim.35.recv_ref, bf16[2,1536,1536]{2,1,0:T(8,128)(2,1)} %tile_ref.1, bf16[2,1536,1536]{2,1,0:T(8,128)(2,1)} %tile_ref.1, bf16[2,1536,1536]{2,1,0:T(8,128)(2,1)} %tile_ref.1, bf16[2,1536,1536]{2,1,0:T(8,128)(2,1)} %tile_ref.1, ...), custom_call_target="tpu_custom_call" | custom-call | flops 75497472 | bytes 24576 | tf_op jit(solution)/shard_map/products/pallas_call | solution.py:220
  108.2 3.9 %collective-permute-start.14 = (f32[1536,256]{1,0:T(8,128)}, f32[1536,256]{1,0:T(8,128)}, u32[]{:S(2)}, u32[]{:S(2)}) collective-permute-start(f32[1536,256]{1,0:T(8,128)} %products.5), channel_id=1, source_target_pairs={{1,0},{3,2},{4,5},{6,7},{9,8},{11,10},{12,13},{14,15},{17,16},{19,... | collective-permute-start | bytes 4718600 | tf_op jit(solution)/shard_map/ppermute | solution.py:366
  112.2 1.8 fusion.2
  114.0 3.2 %add.49 = f32[1536,256]{1,0:T(8,128)} add(f32[1536,256]{1,0:T(8,128)} %copy-done.2, f32[1536,256]{1,0:T(8,128)} %collective-permute-done.6) | non-fusion elementwise | flops 393216 | bytes 4718592 | tf_op jit(solution)/shard_map/add | solution.py:440
  117.2 14.2 %collective-permute-done.9.refs_4_.refs_5_ = bf16[1536,256]{1,0:T(8,128)(2,1)} collective-permute-done((bf16[1536,256]{1,0:T(8,128)(2,1)}, bf16[1536,256]{1,0:T(8,128)(2,1)}, u32[]{:S(2)}, u32[]{:S(2)}) %collective-permute-start.9) | collective-permute-done | bytes 786464 | tf_op jit(solution)/shard_map/ppermute | solution.py:412
  131.4 7.6 %products.4 = f32[1536,256]{1,0:T(8,128)} custom-call(s32[1]{0:T(128)} %bitcast.6.pick_ref, bf16[8,1536]{1,0:T(8,128)(2,1)S(1)} %broadcast_in_dim.35.recv_ref, bf16[2,1536,1536]{2,1,0:T(8,128)(2,1)} %tile_ref.1, bf16[2,1536,1536]{2,1,0:T(8,128)(2,1)} %tile_ref.1, bf16[2,1536,1536]{2,1,0:T(8,128)(2,1)} %tile_ref.1, bf16[2,1536,1536]{2,1,0:T(8,128)(2,1)} %tile_ref.1, ...), custom_call_target="tpu_custom_call" | custom-call | flops 75497472 | bytes 24576 | tf_op jit(solution)/shard_map/products/pallas_call | solution.py:220
  139.0 1.3 collective-permute-start.12
  140.3 1.3 collective-permute-start.13
  141.6 3.3 %add.52 = f32[1536,256]{1,0:T(8,128)} add(f32[1536,256]{1,0:T(8,128)} %products.5, f32[1536,256]{1,0:T(8,128)} %collective-permute-done.14) | non-fusion elementwise | flops 393216 | bytes 4718592 | tf_op jit(solution)/shard_map/add | solution.py:416
  144.9 1.9 collective-permute-start.15
  146.8 0.1 stack.46.pick_ref
  146.9 1.0 copy-done
  147.8 3.3 %extra_products.1 = f32[4,96,256]{2,1,0:T(8,128)S(1)} custom-call(s32[8]{0:T(128)S(1)} %stack.46.pick_ref, bf16[96,1536]{1,0:T(8,128)(2,1)S(1)} %copy-done, bf16[96,1536]{1,0:T(8,128)(2,1)S(1)} %get-tuple-element.22.imag_ref, bf16[1536,256]{1,0:T(8,128)(2,1)S(1)} %fill_window.1.refs_4_.refs_7_.refs_0_, ...), custom_call_target="tpu_custom_call" | custom-call | flops 18874368 | bytes 24576 | tf_op jit(solution)/shard_map/extra_products/pallas_call | solution.py:253
  151.2 7.4 %collective-permute-start.17 = (f32[2,96,256]{2,1,0:T(8,128)S(1)}, f32[2,96,256]{2,1,0:T(8,128)S(1)}, u32[]{:S(2)}, u32[]{:S(2)}) collective-permute-start(f32[2,96,256]{2,1,0:T(8,128)S(1)} %slice.23), channel_id=1, source_target_pairs={{0,1},{1,0},{2,3},{3,2},{4,5},{5,4},{6,7},{7,6},{8,9},{9,8},{10,11... | collective-permute-start | bytes 589832 | tf_op jit(solution)/shard_map/ppermute | solution.py:464
  158.6 2.1 %add.50.refs_0_ = f32[1536,256]{1,0:T(8,128)S(1)} add(f32[1536,256]{1,0:T(8,128)} %products.4, f32[1536,256]{1,0:T(8,128)} %collective-permute-done.12) | non-fusion elementwise | flops 393216 | bytes 4718592 | tf_op jit(solution)/shard_map/add | solution.py:416
  160.7 1.4 collective-permute-start.16
  162.1 0.7 slice.29
  162.9 26.8 %collective-permute-done.18 = f32[1,96,256]{2,1,0:T(8,128)} collective-permute-done((f32[1,96,256]{2,1,0:T(8,128)}, f32[1,96,256]{2,1,0:T(8,128)}, u32[]{:S(2)}, u32[]{:S(2)}) %collective-permute-start.18) | collective-permute-done | bytes 98336 | tf_op jit(solution)/shard_map/ppermute | solution.py:464
  189.7 1.0 fusion.1.refs_3_
  190.7 2.8 %add_add_fusion.refs_1_ = f32[1536,256]{1,0:T(8,128)S(1)} fusion(f32[1536,256]{1,0:T(8,128)} %collective-permute-done.15, f32[1536,256]{1,0:T(8,128)} %add.52, f32[1536,256]{1,0:T(8,128)} %collective-permute-done.13, f32[1536,256]{1,0:T(8,128)} %add.49, pred[]{:T(512)S(6)} %eq.26, pred[]{:T(512)S(6)} %eq.25), kind=kLoop, calls=%fused_computation | loop fusion | flops 1966080 | bytes 7864322 | tf_op jit(solution)/shard_map/add | solution.py:456
  193.5 3.0 %finish.1 = f32[2,1536,128]{2,1,0:T(8,128)} custom-call(f32[2]{0:T(128)S(1)} %broadcast_multiply_fusion.wave_ref, f32[1]{0:T(128)} %bitcast.flag_ref, s32[96]{0:T(128)S(1)} %get-tuple-element.28.miss_ref, bf16[8,1536]{1,0:T(8,128)(2,1)S(1)} %broadcast_in_dim.35.recv_ref, bf16[2,1536,1536]{2,1,0:T(8,128)(2,1)} %tile_ref.1, bf16[96,1536]{1,0:T(8,128)(2,1)S(1)} %copy-done.1, ...), custom_call_target="tpu_custom_call" | custom-call | flops 61440 | bytes 122880 | tf_op jit(solution)/shard_map/finish/pallas_call | solution.py:303
  (39 shorter events, 0.2 us)
Async XLA Ops:
  0.0 9.1 %copy-start.7 = (s32[4,96]{1,0:T(4,128)S(1)}, s32[4,96]{1,0:T(4,128)}, u32[]{:S(2)}) copy-start(s32[4,96]{1,0:T(4,128)} %param.6) | copy-start | bytes 4612
  0.0 19.8 %copy-start.6 = (s32[6144]{0:T(1024)S(1)}, s32[6144]{0:T(1024)}, u32[]{:S(2)}) copy-start(s32[6144]{0:T(1024)} %param.5) | copy-start | bytes 73732
  1.3 12.2 %collective-permute-start.1 = (bf16[1536,128]{1,0:T(8,128)(2,1)S(1)}, bf16[1536,128]{1,0:T(8,128)(2,1)S(1)}, u32[]{:S(2)}, u32[]{:S(2)}) collective-permute-start(bf16[1536,128]{1,0:T(8,128)(2,1)S(1)} %get-tuple-element.18), channel_id=1, source_target_pairs={{2,0},{3,1},{6,4},{7,5},{8,10},{9,11},{12,14},{13,15},{18,16},{19,... | collective-permute-start | bytes 1179656 | tf_op jit(solution)/shard_map/ppermute | solution.py:366
  2.6 23.8 %collective-permute-start.3 = (bf16[1536,128]{1,0:T(8,128)(2,1)S(1)}, bf16[1536,128]{1,0:T(8,128)(2,1)S(1)}, u32[]{:S(2)}, u32[]{:S(2)}) collective-permute-start(bf16[1536,128]{1,0:T(8,128)(2,1)S(1)} %get-tuple-element.18), channel_id=1, source_target_pairs={{0,0},{1,4},{4,1},{5,5},{10,10},{11,14},{14,11},{15,15},{16,16},{1... | collective-permute-start | bytes 1179656 | tf_op jit(solution)/shard_map/ppermute | solution.py:366
  7.2 19.2 %collective-permute-start = (bf16[1536,128]{1,0:T(8,128)(2,1)S(1)}, bf16[1536,128]{1,0:T(8,128)(2,1)S(1)}, u32[]{:S(2)}, u32[]{:S(2)}) collective-permute-start(bf16[1536,128]{1,0:T(8,128)(2,1)S(1)} %get-tuple-element.17), channel_id=1, source_target_pairs={{0,0},{1,4},{2,8},{3,12},{4,1},{5,5},{6,9},{7,13},{8,2},{9,6},{10,... | collective-permute-start | bytes 1179656 | tf_op jit(solution)/shard_map/ppermute | solution.py:366
  13.5 14.7 %collective-permute-start.2 = (bf16[1536,128]{1,0:T(8,128)(2,1)S(1)}, bf16[1536,128]{1,0:T(8,128)(2,1)S(1)}, u32[]{:S(2)}, u32[]{:S(2)}) collective-permute-start(bf16[1536,128]{1,0:T(8,128)(2,1)S(1)} %collective-permute-done.1), channel_id=1, source_target_pairs={{0,8},{1,12},{4,9},{5,13},{10,2},{11,6},{14,3},{15,7},{16,24},{17,... | collective-permute-start | bytes 1179656 | tf_op jit(solution)/shard_map/ppermute | solution.py:366
  26.3 2.3 %copy-start.3 = (bf16[96,1536]{1,0:T(8,128)(2,1)}, bf16[96,1536]{1,0:T(8,128)(2,1)S(1)}, u32[]{:S(2)}) copy-start(bf16[96,1536]{1,0:T(8,128)(2,1)S(1)} %get-tuple-element.16.imag_ref) | copy-start | bytes 884740
  28.7 27.2 %collective-permute-start.4 = (bf16[1536,256]{1,0:T(8,128)(2,1)S(1)}, bf16[1536,256]{1,0:T(8,128)(2,1)S(1)}, u32[]{:S(2)}, u32[]{:S(2)}) collective-permute-start(bf16[1536,256]{1,0:T(8,128)(2,1)S(1)} %fill_window.1.refs_4_.refs_7_.refs_0_), channel_id=1, source_target_pairs={{4,0},{8,4},{12,8},{5,1},{9,5},{13,9},{6,2},{10,6},{14,10},{7,3},{... | collective-permute-start | bytes 2359304 | tf_op jit(solution)/shard_map/ppermute | solution.py:412
  30.0 26.8 %collective-permute-start.5 = (bf16[1536,256]{1,0:T(8,128)(2,1)S(1)}, bf16[1536,256]{1,0:T(8,128)(2,1)S(1)}, u32[]{:S(2)}, u32[]{:S(2)}) collective-permute-start(bf16[1536,256]{1,0:T(8,128)(2,1)S(1)} %fill_window.1.refs_4_.refs_7_.refs_0_), channel_id=1, source_target_pairs={{0,4},{4,8},{8,12},{1,5},{5,9},{9,13},{2,6},{6,10},{10,14},{3,7},{... | collective-permute-start | bytes 2359304 | tf_op jit(solution)/shard_map/ppermute | solution.py:411
  40.1 29.2 %copy-start.4 = (bf16[96,1536]{1,0:T(8,128)(2,1)S(1)}, bf16[96,1536]{1,0:T(8,128)(2,1)}, u32[]{:S(2)}) copy-start(bf16[96,1536]{1,0:T(8,128)(2,1)} %copy-done.3) | copy-start | bytes 884740
  65.2 1.2 copy-start.2
  66.3 47.7 %collective-permute-start.6 = (f32[1536,256]{1,0:T(8,128)}, f32[1536,256]{1,0:T(8,128)}, u32[]{:S(2)}, u32[]{:S(2)}) collective-permute-start(f32[1536,256]{1,0:T(8,128)} %get-tuple-element.20), channel_id=1, source_target_pairs={{0,1},{1,0},{2,3},{3,2},{4,5},{5,4},{6,7},{7,6},{8,9},{9,8},{10,11... | collective-permute-start | bytes 4718600 | tf_op jit(solution)/shard_map/ppermute | solution.py:440
  67.3 11.0 %collective-permute-start.10 = (bf16[1536,256]{1,0:T(8,128)(2,1)S(1)}, bf16[1536,256]{1,0:T(8,128)(2,1)S(1)}, u32[]{:S(2)}, u32[]{:S(2)}) collective-permute-start(bf16[1536,256]{1,0:T(8,128)(2,1)S(1)} %collective-permute-done.5.refs_6_.refs_9_.refs_2_.refs_7_), channel_id=1, source_target_pairs={{4,8},{8,12},{5,9},{9,13},{6,10},{10,14},{7,11},{11,15},{20,24},{2... | collective-permute-start | bytes 2359304 | tf_op jit(solution)/shard_map/ppermute | solution.py:411
  68.0 31.5 %collective-permute-start.8 = (bf16[1536,256]{1,0:T(8,128)(2,1)S(1)}, bf16[1536,256]{1,0:T(8,128)(2,1)}, u32[]{:S(2)}, u32[]{:S(2)}) collective-permute-start(bf16[1536,256]{1,0:T(8,128)(2,1)S(1)} %collective-permute-done.4.refs_5_.refs_8_.refs_1_.refs_6_), channel_id=1, source_target_pairs={{4,0},{8,4},{5,1},{9,5},{6,2},{10,6},{7,3},{11,7},{20,16},{24,20},... | collective-permute-start | bytes 2359304 | tf_op jit(solution)/shard_map/ppermute | solution.py:412
  70.2 42.0 %collective-permute-start.7 = (bf16[192,1536]{1,0:T(8,128)(2,1)}, bf16[192,1536]{1,0:T(8,128)(2,1)}, u32[]{:S(2)}, u32[]{:S(2)}) collective-permute-start(bf16[192,1536]{1,0:T(8,128)(2,1)} %pad_maximum_fusion), channel_id=1, source_target_pairs={{0,0},{1,4},{2,8},{3,12},{4,1},{5,5},{6,9},{7,13},{8,2},{9,6},{10,... | collective-permute-start | bytes 1769480 | tf_op jit(solution)/shard_map/ppermute | solution.py:366
  78.4 38.9 %collective-permute-start.11 = (bf16[1536,256]{1,0:T(8,128)(2,1)S(1)}, bf16[1536,256]{1,0:T(8,128)(2,1)}, u32[]{:S(2)}, u32[]{:S(2)}) collective-permute-start(bf16[1536,256]{1,0:T(8,128)(2,1)S(1)} %collective-permute-done.10.refs_5_.refs_4_), channel_id=1, source_target_pairs={{8,12},{9,13},{10,14},{11,15},{24,28},{25,29},{26,30},{27,31}} | collective-permute-start | bytes 2359304 | tf_op jit(solution)/shard_map/ppermute | solution.py:411
  99.5 31.9 %collective-permute-start.9 = (bf16[1536,256]{1,0:T(8,128)(2,1)}, bf16[1536,256]{1,0:T(8,128)(2,1)}, u32[]{:S(2)}, u32[]{:S(2)}) collective-permute-start(bf16[1536,256]{1,0:T(8,128)(2,1)} %collective-permute-done.8.refs_4_.refs_3_), channel_id=1, source_target_pairs={{4,0},{5,1},{6,2},{7,3},{20,16},{21,17},{22,18},{23,19}} | collective-permute-start | bytes 2359304 | tf_op jit(solution)/shard_map/ppermute | solution.py:412
  108.2 33.4 %collective-permute-start.14 = (f32[1536,256]{1,0:T(8,128)}, f32[1536,256]{1,0:T(8,128)}, u32[]{:S(2)}, u32[]{:S(2)}) collective-permute-start(f32[1536,256]{1,0:T(8,128)} %products.5), channel_id=1, source_target_pairs={{1,0},{3,2},{4,5},{6,7},{9,8},{11,10},{12,13},{14,15},{17,16},{19,... | collective-permute-start | bytes 4718600 | tf_op jit(solution)/shard_map/ppermute | solution.py:366
  139.0 19.6 %collective-permute-start.12 = (f32[1536,256]{1,0:T(8,128)}, f32[1536,256]{1,0:T(8,128)}, u32[]{:S(2)}, u32[]{:S(2)}) collective-permute-start(f32[1536,256]{1,0:T(8,128)} %products.4), channel_id=1, source_target_pairs={{0,1},{2,3},{5,4},{7,6},{8,9},{10,11},{13,12},{15,14},{16,17},{18,... | collective-permute-start | bytes 4718600 | tf_op jit(solution)/shard_map/ppermute | solution.py:366
  140.3 50.3 %collective-permute-start.13 = (f32[1536,256]{1,0:T(8,128)}, f32[1536,256]{1,0:T(8,128)}, u32[]{:S(2)}, u32[]{:S(2)}) collective-permute-start(f32[1536,256]{1,0:T(8,128)} %add.49), channel_id=1, source_target_pairs={{2,0},{3,1},{6,4},{7,5},{8,10},{9,11},{12,14},{13,15},{18,16},{19,... | collective-permute-start | bytes 4718600 | tf_op jit(solution)/shard_map/ppermute | solution.py:366
  144.9 45.7 %collective-permute-start.15 = (f32[1536,256]{1,0:T(8,128)}, f32[1536,256]{1,0:T(8,128)}, u32[]{:S(2)}, u32[]{:S(2)}) collective-permute-start(f32[1536,256]{1,0:T(8,128)} %add.52), channel_id=1, source_target_pairs={{0,2},{5,7},{10,8},{15,13},{16,18},{21,23},{26,24},{31,29}} | collective-permute-start | bytes 4718600 | tf_op jit(solution)/shard_map/ppermute | solution.py:366
  146.9 1.0 copy-start
  151.2 11.6 %copy-start.8 = (f32[2]{0:T(128)S(1)}, f32[2]{0:T(128)}, u32[]{:S(2)}) copy-start(f32[2]{0:T(128)} %param.7) | copy-start | bytes 28
  151.2 10.9 %collective-permute-start.17 = (f32[2,96,256]{2,1,0:T(8,128)S(1)}, f32[2,96,256]{2,1,0:T(8,128)S(1)}, u32[]{:S(2)}, u32[]{:S(2)}) collective-permute-start(f32[2,96,256]{2,1,0:T(8,128)S(1)} %slice.23), channel_id=1, source_target_pairs={{0,1},{1,0},{2,3},{3,2},{4,5},{5,4},{6,7},{7,6},{8,9},{9,8},{10,11... | collective-permute-start | bytes 589832 | tf_op jit(solution)/shard_map/ppermute | solution.py:464
  160.7 32.8 %collective-permute-start.16 = (f32[1536,256]{1,0:T(8,128)S(1)}, f32[1536,256]{1,0:T(8,128)S(1)}, u32[]{:S(2)}, u32[]{:S(2)}) collective-permute-start(f32[1536,256]{1,0:T(8,128)S(1)} %add.50.refs_0_), channel_id=1, source_target_pairs={{1,3},{4,6},{11,9},{14,12},{17,19},{20,22},{27,25},{30,28}} | collective-permute-start | bytes 4718600 | tf_op jit(solution)/shard_map/ppermute | solution.py:366
  162.1 0.7 copy-start.5
  162.8 26.8 %collective-permute-start.18 = (f32[1,96,256]{2,1,0:T(8,128)}, f32[1,96,256]{2,1,0:T(8,128)}, u32[]{:S(2)}, u32[]{:S(2)}) collective-permute-start(f32[1,96,256]{2,1,0:T(8,128)} %slice.29), channel_id=1, source_target_pairs={{0,2},{1,3},{2,0},{3,1},{4,6},{5,7},{6,4},{7,5},{8,10},{9,11},{10,... | collective-permute-start | bytes 294920 | tf_op jit(solution)/shard_map/ppermute | solution.py:464
  190.6 2.9 %copy-start.1 = (bf16[96,1536]{1,0:T(8,128)(2,1)S(1)}, bf16[96,1536]{1,0:T(8,128)(2,1)}, u32[]{:S(2)}) copy-start(bf16[96,1536]{1,0:T(8,128)(2,1)} %get-tuple-element.21.real_ref) | copy-start | bytes 884740

commit v6 on v5

--- a/solution.py
+++ b/solution.py
@@ -188,13 +188,21 @@
 def product_kernel(counts, pick_ref, recv_ref, *refs):
     tiles, refs = refs[:4], refs[4:]
     total, places = sum(counts), len(counts)
-    out_refs, right_refs = refs[total:total + places], refs[total + places:]
+    out_refs, right_refs = refs[total:total + places], refs[total + places:-1]
+    sem = refs[-1]
 
     @pl.when(pl.program_id(0) == 0)
     def _():
         used = 0
         for place, count in enumerate(counts):
-            choose(right_refs[place], pick_ref[place], refs[used:used + count])
+            for index, ref in enumerate(refs[used:used + count]):
+
+                @pl.when(pick_ref[place] == index)
+                def _():
+                    copy = pltpu.make_async_copy(ref, right_refs[place], sem.at[place])
+                    copy.start()
+                    copy.wait()
+
             used += count
 
     recv = recv_ref[0:1, :]
@@ -225,10 +233,11 @@
             pl.BlockSpec((8, cols), lambda i: (0, 0)),
         ]
         + [quarter(part, side) for part in range(2) for side in range(2)]
-        + [pl.BlockSpec((cols, lanes), lambda i: (0, 0))] * len(flat),
+        + [pl.BlockSpec(memory_space=pl.ANY)] * len(flat),
         out_specs=[pl.BlockSpec((block, lanes), lambda i: (i, 0))] * len(groups),
         out_shape=[jax.ShapeDtypeStruct((rows, lanes), jnp.float32)] * len(groups),
-        scratch_shapes=[pltpu.VMEM((cols, lanes), jnp.bfloat16)] * len(groups),
+        scratch_shapes=[pltpu.VMEM((cols, lanes), jnp.bfloat16)] * len(groups)
+        + [pltpu.SemaphoreType.DMA((len(groups),))],
         compiler_params=params(),
         cost_estimate=cost(8 * rows * cols * lanes * len(groups), 4 * rows * lanes),
         name="products",
@@ -270,8 +279,8 @@
         total = refs[used][...]
         if count > 1:
             total = total * flag_ref[0]
-        for ref in refs[used + 1:used + count]:
-            total = total + ref[...]
+        for index, ref in enumerate(refs[used + 1:used + count], 1):
+            total = total + (ref[...] * flag_ref[index] if index < count // 2 else ref[...])
         used += count
         totals.append(total)
 
@@ -395,8 +404,7 @@
     recv_col8 = jnp.broadcast_to(recv_col[None], (8, tile))
 
     picked = pick_columns(traces, miss_col_lanes, recv_col8, live8, misses)
-    extra = transpose(jnp.concatenate(picked))
-    extra = [extra[:misses], extra[misses:]]
+    extra = None
     apart = row_index ^ col_index
     strides = [2**bit for bit in range(grid_size.bit_length() - 1)]
     terms, extra_terms = [], []
@@ -424,6 +432,12 @@
 
         hop(1)
         hop(2)
+        if extra is None:
+            both, up[-1], down[-1] = lax.optimization_barrier(
+                (jnp.concatenate(picked), up[-1], down[-1])
+            )
+            both = transpose(both)
+            extra = [both[:misses], both[misses:]]
         _, (block0,) = options(0)
         pick1, sources1 = options(1)
         odd = apart & 1
@@ -441,21 +455,18 @@
         for distance in range(3, grid_size):
             hop(distance)
         sums = [(0, 1, apart // 2 == 0, total)]
+        first = last(total, 0, 1)
         mask = recv_col8
         for offset in range(2, grid_size):
             if offset == grid_size - 1:
-                *rest, total = sums[0]
-                mask, total, extra = lax.optimization_barrier((mask, total, extra))
-                sums[0] = (*rest, total)
+                mask, first, extra = lax.optimization_barrier((mask, first, extra))
             (total,) = products(traces, mask, [options(offset)])
             total = add_up(total, offset, strides[:-1], 0)
             sums.append((offset, 0, apart == offset, total))
-        early = None
-        for offset, skip, mine, total in sums[:-1]:
-            term = jnp.where(mine, total, 0.0) + last(total, offset, skip)
-            early = term if early is None else early + term
-        total = sums[-1][-1]
-        terms.append((total, early, last(total, grid_size - 1, 0)))
+        got = [first] + [last(total, offset, skip) for offset, skip, _, total in sums[1:]]
+        extra, _ = lax.optimization_barrier((extra, sums[-1][-1]))
+        terms.append([total for *_, total in sums] + got)
+        flags = [mine for _, _, mine, _ in sums]
         group = [(pick, apart ^ offset, sources) for offset in range(grid_size)
                  for pick, sources in [options(offset)]]
         rest = extra_products(extra, group)
@@ -465,7 +476,7 @@
             rest = rest[0::2] + arrive
         extra_terms.append((rest[0],))
     wave = wavelet * (1.0 / math.sqrt(order))
-    flag = (apart == grid_size - 1).astype(jnp.float32)[None]
+    flag = jnp.stack(flags).astype(jnp.float32)
     return finish(wave, flag, miss_row, recv_col8, traces, extra, terms + extra_terms)
 
 

time: 197 us -> 186 us (0.944)
  starting transfers between devices: 56.4 us -> 46.9 us
  other arithmetic: 13.5 us -> 5.37 us
  waiting for transfers between devices: 83.3 us -> 90.5 us
    ppermute x3, waiting for transfers between devices: 49.5 us -> 29.4 us  [hop(): down.append(lax.ppermute(down[-1], 'row', back))]
    ppermute x3, waiting for transfers between devices: 0.86 us -> 15.3 us  [hop(): up.append(lax.ppermute(up[-1], 'row', ends))]
    ppermute x10, waiting for transfers between devices: 6.21 us -> 17.2 us  [move(): return lax.ppermute(block, ('row', 'col'), route)]
    ppermute x2, starting transfers between devices: 7.37 us -> 0.57 us  [local(): arrive = lax.ppermute(rest[1::2], 'col', pairs)]
    pallas_call x1, Pallas kernels: 2.99 us -> 6.05 us  [finish(): pl.pallas_call(functools.partial(finish_kernel, counts), grid=(1,), in_sp...]
    add x1 -> x0, other arithmetic: 2.81 us -> none  [local(): early = term if early is None else early + term]
    add x2, other arithmetic: 5.36 us -> 2.78 us  [add_up(): total = total + move(total, sum_route(offset, grid_size, stride, skip))]
    ppermute x10, starting transfers between devices: 31.9 us -> 29.6 us  [move(): return lax.ppermute(block, ('row', 'col'), route)]
  transfers between devices with their start and end apart: 19 -> 19, of which waited for: 7 -> 11; matrix products, arithmetic and copies ran while one was open for 8% -> 4% of each run, Pallas kernels for 13% -> 13%
where the time goes in v6:
time: 186 us; the launch traced here: 185 us
  waiting for transfers between devices  90.5 us (49%)
  starting transfers between devices  46.9 us (25%)
  Pallas kernels  39.2 us (21%)
  other arithmetic  5.37 us (3%)
  local copies, waits for them, and re-layouts  3.09 us (2%)
    ppermute x10, starting transfers between devices, move(): return lax.ppermute(block, ('row', 'col'), route)  29.6 us
    ppermute x3, waiting for transfers between devices, hop(): down.append(lax.ppermute(down[-1], 'row', back))  29.4 us
    ppermute x2, waiting for transfers between devices, local(): arrive = lax.ppermute(rest[1::2], 'col', pairs)  27.5 us
    pallas_call x3, Pallas kernels, products(): pl.pallas_call(functools.partial(product_kernel, counts), grid=(rows // b...  21.8 us
    ppermute x10, waiting for transfers between devices, move(): return lax.ppermute(block, ('row', 'col'), route)  17.2 us
    ppermute x3, waiting for transfers between devices, hop(): up.append(lax.ppermute(up[-1], 'row', ends))  15.3 us
    ppermute x3, starting transfers between devices, hop(): up.append(lax.ppermute(up[-1], 'row', ends))  11.7 us
    pallas_call x1, Pallas kernels, pick_columns(): pl.pallas_call(pick_kernel, grid=(rows // block,), in_specs=[pl.BlockSpec...  6.28 us
  transfers between devices with their start and end apart: 19, of which 11 were waited for; matrix products, arithmetic and copies ran while one was open for 4% of the time, Pallas kernels for 13%

profile of v6, /device:TPU:1, one launch (start us, length us, event | category | flops | bytes accessed | tf_op | source)
XLA Modules:
  0.0 185.3 jit_solution(4848170964746915653)
XLA Ops:
  0.0 1.3 cut_window.1
  1.3 1.3 collective-permute-start.1
  2.6 4.6 %collective-permute-start.3 = (bf16[1536,128]{1,0:T(8,128)(2,1)S(1)}, bf16[1536,128]{1,0:T(8,128)(2,1)S(1)}, u32[]{:S(2)}, u32[]{:S(2)}) collective-permute-start(bf16[1536,128]{1,0:T(8,128)(2,1)S(1)} %get-tuple-element.23), channel_id=1, source_target_pairs={{0,0},{1,4},{4,1},{5,5},{10,10},{11,14},{14,11},{15,15},{16,16},{1... | collective-permute-start | bytes 1179656 | tf_op jit(solution)/shard_map/ppermute | solution.py:375
  7.2 1.9 %collective-permute-start = (bf16[1536,128]{1,0:T(8,128)(2,1)S(1)}, bf16[1536,128]{1,0:T(8,128)(2,1)S(1)}, u32[]{:S(2)}, u32[]{:S(2)}) collective-permute-start(bf16[1536,128]{1,0:T(8,128)(2,1)S(1)} %get-tuple-element.22), channel_id=1, source_target_pairs={{0,0},{1,4},{2,8},{3,12},{4,1},{5,5},{6,9},{7,13},{8,2},{9,6},{10,... | collective-permute-start | bytes 1179656 | tf_op jit(solution)/shard_map/ppermute | solution.py:375
  9.2 4.4 %collective-permute-done.1 = bf16[1536,128]{1,0:T(8,128)(2,1)S(1)} collective-permute-done((bf16[1536,128]{1,0:T(8,128)(2,1)S(1)}, bf16[1536,128]{1,0:T(8,128)(2,1)S(1)}, u32[]{:S(2)}, u32[]{:S(2)}) %collective-permute-start.1) | collective-permute-done | bytes 393248 | tf_op jit(solution)/shard_map/ppermute | solution.py:375
  13.5 6.1 %collective-permute-start.2 = (bf16[1536,128]{1,0:T(8,128)(2,1)S(1)}, bf16[1536,128]{1,0:T(8,128)(2,1)S(1)}, u32[]{:S(2)}, u32[]{:S(2)}) collective-permute-start(bf16[1536,128]{1,0:T(8,128)(2,1)S(1)} %collective-permute-done.1), channel_id=1, source_target_pairs={{0,8},{1,12},{4,9},{5,13},{10,2},{11,6},{14,3},{15,7},{16,24},{17,... | collective-permute-start | bytes 1179656 | tf_op jit(solution)/shard_map/ppermute | solution.py:375
  19.7 0.1 fusion
  19.9 0.1 dynamic_slice.14
  20.0 0.1 dynamic_slice.16
  20.1 6.3 %pick_columns.1 = (bf16[96,1536]{1,0:T(8,128)(2,1)S(1)}, bf16[96,1536]{1,0:T(8,128)(2,1)S(1)}) custom-call(bf16[2,1536,1536]{2,1,0:T(8,128)(2,1)} %tile_ref.1, s32[1,128]{1,0:T(1,128)S(1)} %pad_bitcast_fusion.miss_ref, bf16[8,1536]{1,0:T(8,128)(2,1)S(1)} %broadcast_in_dim.8.recv_ref, f32[8,1536]{1,0:T(8,128)S(1)} %broadcast_in_dim.10.live_ref), custom_call_target="tpu_custom_call" | custom-call | flops 37748736 | bytes 147456 | tf_op jit(solution)/shard_map/pick_columns/pallas_call | solution.py:103
  26.4 1.8 collective-permute-done.2.refs_1_
  28.2 0.4 fill_window.1.refs_4_.refs_7_.refs_0_
  28.7 9.4 %collective-permute-start.5 = (bf16[1536,256]{1,0:T(8,128)(2,1)S(1)}, bf16[1536,256]{1,0:T(8,128)(2,1)S(1)}, u32[]{:S(2)}, u32[]{:S(2)}) collective-permute-start(bf16[1536,256]{1,0:T(8,128)(2,1)S(1)} %fill_window.1.refs_4_.refs_7_.refs_0_), channel_id=1, source_target_pairs={{0,4},{4,8},{8,12},{1,5},{5,9},{9,13},{2,6},{6,10},{10,14},{3,7},{... | collective-permute-start | bytes 2359304 | tf_op jit(solution)/shard_map/ppermute | solution.py:419
  38.1 1.3 collective-permute-start.4
  39.5 15.3 %collective-permute-done.5.refs_6_.refs_9_.refs_2_.refs_7_ = bf16[1536,256]{1,0:T(8,128)(2,1)S(1)} collective-permute-done((bf16[1536,256]{1,0:T(8,128)(2,1)S(1)}, bf16[1536,256]{1,0:T(8,128)(2,1)S(1)}, u32[]{:S(2)}, u32[]{:S(2)}) %collective-permute-start.5) | collective-permute-done | bytes 786464 | tf_op jit(solution)/shard_map/ppermute | solution.py:419
  54.8 4.3 %collective-permute-done.4.refs_5_.refs_8_.refs_1_.refs_6_ = bf16[1536,256]{1,0:T(8,128)(2,1)S(1)} collective-permute-done((bf16[1536,256]{1,0:T(8,128)(2,1)S(1)}, bf16[1536,256]{1,0:T(8,128)(2,1)S(1)}, u32[]{:S(2)}, u32[]{:S(2)}) %collective-permute-start.4) | collective-permute-done | bytes 786464 | tf_op jit(solution)/shard_map/ppermute | solution.py:420
  59.0 7.6 %products.3 = (f32[1536,256]{1,0:T(8,128)S(1)}, f32[1536,256]{1,0:T(8,128)S(1)}) custom-call(s32[2]{0:T(128)S(1)} %pad_add_fusion.pick_ref, bf16[8,1536]{1,0:T(8,128)(2,1)S(1)} %broadcast_in_dim.8.recv_ref, bf16[2,1536,1536]{2,1,0:T(8,128)(2,1)} %tile_ref.1, bf16[2,1536,1536]{2,1,0:T(8,128)(2,1)} %tile_ref.1, bf16[2,1536,1536]{2,1,0:T(8,128)(2,1)} %tile_ref.1, ...), custom_call_target="tpu_custom_call" | custom-call | flops 150994944 | bytes 24576 | tf_op jit(solution)/shard_map/products/pallas_call | solution.py:228
  66.6 1.1 collective-permute-start.6
  67.8 0.7 collective-permute-start.8
  68.5 1.3 collective-permute-start.9
  69.8 1.0 collective-permute-done.6
  70.8 1.4 add.40.refs_0_
  72.2 1.3 collective-permute-start.7
  73.5 0.9 pad_maximum_fusion
  74.3 15.3 %collective-permute-done.9.refs_4_.refs_3_ = bf16[1536,256]{1,0:T(8,128)(2,1)} collective-permute-done((bf16[1536,256]{1,0:T(8,128)(2,1)S(1)}, bf16[1536,256]{1,0:T(8,128)(2,1)}, u32[]{:S(2)}, u32[]{:S(2)}) %collective-permute-start.9) | collective-permute-done | bytes 786464 | tf_op jit(solution)/shard_map/ppermute | solution.py:420
  89.6 3.2 %collective-permute-start.10 = (bf16[192,1536]{1,0:T(8,128)(2,1)}, bf16[192,1536]{1,0:T(8,128)(2,1)}, u32[]{:S(2)}, u32[]{:S(2)}) collective-permute-start(bf16[192,1536]{1,0:T(8,128)(2,1)} %pad_maximum_fusion), channel_id=1, source_target_pairs={{0,0},{1,4},{2,8},{3,12},{4,1},{5,5},{6,9},{7,13},{8,2},{9,6},{10,... | collective-permute-start | bytes 1769480 | tf_op jit(solution)/shard_map/ppermute | solution.py:375
  92.8 1.3 collective-permute-start.11
  94.1 1.5 collective-permute-start.12
  95.7 7.1 %products.5 = f32[1536,256]{1,0:T(8,128)S(1)} custom-call(s32[1]{0:T(128)} %bitcast.9.pick_ref, bf16[8,1536]{1,0:T(8,128)(2,1)S(1)} %broadcast_in_dim.8.recv_ref, bf16[2,1536,1536]{2,1,0:T(8,128)(2,1)} %tile_ref.1, bf16[2,1536,1536]{2,1,0:T(8,128)(2,1)} %tile_ref.1, bf16[2,1536,1536]{2,1,0:T(8,128)(2,1)} %tile_ref.1, bf16[2,1536,1536]{2,1,0:T(8,128)(2,1)} %tile_ref.1, ...), custom_call_target="tpu_custom_call" | custom-call | flops 75497472 | bytes 24576 | tf_op jit(solution)/shard_map/products/pallas_call | solution.py:228
  102.8 5.5 %collective-permute-start.14 = (f32[1536,256]{1,0:T(8,128)S(1)}, f32[1536,256]{1,0:T(8,128)S(1)}, u32[]{:S(2)}, u32[]{:S(2)}) collective-permute-start(f32[1536,256]{1,0:T(8,128)S(1)} %products.5), channel_id=1, source_target_pairs={{1,0},{3,2},{4,5},{6,7},{9,8},{11,10},{12,13},{14,15},{17,16},{19,... | collective-permute-start | bytes 4718600 | tf_op jit(solution)/shard_map/ppermute | solution.py:375
  108.3 6.8 %collective-permute-done.10 = bf16[192,1536]{1,0:T(8,128)(2,1)} collective-permute-done((bf16[192,1536]{1,0:T(8,128)(2,1)}, bf16[192,1536]{1,0:T(8,128)(2,1)}, u32[]{:S(2)}, u32[]{:S(2)}) %collective-permute-start.10) | collective-permute-done | bytes 589856 | tf_op jit(solution)/shard_map/ppermute | solution.py:375
  115.1 1.8 fusion.2
  116.9 9.8 %collective-permute-done.11.refs_4_.refs_5_ = bf16[1536,256]{1,0:T(8,128)(2,1)} collective-permute-done((bf16[1536,256]{1,0:T(8,128)(2,1)}, bf16[1536,256]{1,0:T(8,128)(2,1)}, u32[]{:S(2)}, u32[]{:S(2)}) %collective-permute-start.11) | collective-permute-done | bytes 786464 | tf_op jit(solution)/shard_map/ppermute | solution.py:420
  126.8 7.1 %products.4 = f32[1536,256]{1,0:T(8,128)S(1)} custom-call(s32[1]{0:T(128)} %bitcast.8.pick_ref, bf16[8,1536]{1,0:T(8,128)(2,1)S(1)} %broadcast_in_dim.8.recv_ref, bf16[2,1536,1536]{2,1,0:T(8,128)(2,1)} %tile_ref.1, bf16[2,1536,1536]{2,1,0:T(8,128)(2,1)} %tile_ref.1, bf16[2,1536,1536]{2,1,0:T(8,128)(2,1)} %tile_ref.1, bf16[2,1536,1536]{2,1,0:T(8,128)(2,1)} %tile_ref.1, ...), custom_call_target="tpu_custom_call" | custom-call | flops 75497472 | bytes 24576 | tf_op jit(solution)/shard_map/products/pallas_call | solution.py:228
  133.9 1.3 collective-permute-start.13
  135.2 1.4 add.42.refs_1_
  136.6 1.8 collective-permute-start.15
  138.4 4.2 %collective-permute-done.13 = f32[1536,256]{1,0:T(8,128)S(1)} collective-permute-done((f32[1536,256]{1,0:T(8,128)S(1)}, f32[1536,256]{1,0:T(8,128)S(1)}, u32[]{:S(2)}, u32[]{:S(2)}) %collective-permute-start.13) | collective-permute-done | bytes 1572896 | tf_op jit(solution)/shard_map/ppermute | solution.py:375
  142.6 1.4 add.41.refs_2_
  144.0 2.5 %collective-permute-start.16 = (f32[1536,256]{1,0:T(8,128)}, f32[1536,256]{1,0:T(8,128)}, u32[]{:S(2)}, u32[]{:S(2)}) collective-permute-start(f32[1536,256]{1,0:T(8,128)} %add.41.refs_2_), channel_id=1, source_target_pairs={{1,3},{4,6},{11,9},{14,12},{17,19},{20,22},{27,25},{30,28}} | collective-permute-start | bytes 4718600 | tf_op jit(solution)/shard_map/ppermute | solution.py:375
  146.5 0.1 stack.62.pick_ref
  146.6 1.0 copy-done
  147.6 3.3 %extra_products.1 = f32[4,96,256]{2,1,0:T(8,128)S(1)} custom-call(s32[8]{0:T(128)S(1)} %stack.62.pick_ref, bf16[96,1536]{1,0:T(8,128)(2,1)S(1)} %copy-done, bf16[96,1536]{1,0:T(8,128)(2,1)S(1)} %get-tuple-element.33.imag_ref, bf16[1536,256]{1,0:T(8,128)(2,1)S(1)} %fill_window.1.refs_4_.refs_7_.refs_0_, ...), custom_call_target="tpu_custom_call" | custom-call | flops 18874368 | bytes 24576 | tf_op jit(solution)/shard_map/extra_products/pallas_call | solution.py:262
  151.0 0.5 collective-permute-start.17
  151.5 1.1 collective-permute-done.17
  152.7 0.1 add_convert_fusion.flag_ref
  152.7 26.4 %collective-permute-done.18 = f32[1,96,256]{2,1,0:T(8,128)S(1)} collective-permute-done((f32[1,96,256]{2,1,0:T(8,128)S(1)}, f32[1,96,256]{2,1,0:T(8,128)S(1)}, u32[]{:S(2)}, u32[]{:S(2)}) %collective-permute-start.18) | collective-permute-done | bytes 98336 | tf_op jit(solution)/shard_map/ppermute | solution.py:475
  179.2 6.1 %finish.1 = f32[2,1536,128]{2,1,0:T(8,128)} custom-call(f32[2]{0:T(128)S(1)} %broadcast_multiply_fusion.wave_ref, f32[3]{0:T(128)S(1)} %add_convert_fusion.flag_ref, s32[96]{0:T(128)S(1)} %get-tuple-element.38.miss_ref, bf16[8,1536]{1,0:T(8,128)(2,1)S(1)} %broadcast_in_dim.8.recv_ref, bf16[2,1536,1536]{2,1,0:T(8,128)(2,1)} %tile_ref.1, ...), custom_call_target="tpu_custom_call" | custom-call | flops 61440 | bytes 122880 | tf_op jit(solution)/shard_map/finish/pallas_call | solution.py:312
  (35 shorter events, 0.3 us)
Async XLA Ops:
  0.0 9.1 %copy-start.5 = (s32[4,96]{1,0:T(4,128)S(1)}, s32[4,96]{1,0:T(4,128)}, u32[]{:S(2)}) copy-start(s32[4,96]{1,0:T(4,128)} %param.6) | copy-start | bytes 4612
  0.0 19.8 %copy-start.4 = (s32[6144]{0:T(1024)S(1)}, s32[6144]{0:T(1024)}, u32[]{:S(2)}) copy-start(s32[6144]{0:T(1024)} %param.5) | copy-start | bytes 73732
  1.3 12.2 %collective-permute-start.1 = (bf16[1536,128]{1,0:T(8,128)(2,1)S(1)}, bf16[1536,128]{1,0:T(8,128)(2,1)S(1)}, u32[]{:S(2)}, u32[]{:S(2)}) collective-permute-start(bf16[1536,128]{1,0:T(8,128)(2,1)S(1)} %get-tuple-element.23), channel_id=1, source_target_pairs={{2,0},{3,1},{6,4},{7,5},{8,10},{9,11},{12,14},{13,15},{18,16},{19,... | collective-permute-start | bytes 1179656 | tf_op jit(solution)/shard_map/ppermute | solution.py:375
  2.6 23.8 %collective-permute-start.3 = (bf16[1536,128]{1,0:T(8,128)(2,1)S(1)}, bf16[1536,128]{1,0:T(8,128)(2,1)S(1)}, u32[]{:S(2)}, u32[]{:S(2)}) collective-permute-start(bf16[1536,128]{1,0:T(8,128)(2,1)S(1)} %get-tuple-element.23), channel_id=1, source_target_pairs={{0,0},{1,4},{4,1},{5,5},{10,10},{11,14},{14,11},{15,15},{16,16},{1... | collective-permute-start | bytes 1179656 | tf_op jit(solution)/shard_map/ppermute | solution.py:375
  7.2 19.2 %collective-permute-start = (bf16[1536,128]{1,0:T(8,128)(2,1)S(1)}, bf16[1536,128]{1,0:T(8,128)(2,1)S(1)}, u32[]{:S(2)}, u32[]{:S(2)}) collective-permute-start(bf16[1536,128]{1,0:T(8,128)(2,1)S(1)} %get-tuple-element.22), channel_id=1, source_target_pairs={{0,0},{1,4},{2,8},{3,12},{4,1},{5,5},{6,9},{7,13},{8,2},{9,6},{10,... | collective-permute-start | bytes 1179656 | tf_op jit(solution)/shard_map/ppermute | solution.py:375
  13.5 14.7 %collective-permute-start.2 = (bf16[1536,128]{1,0:T(8,128)(2,1)S(1)}, bf16[1536,128]{1,0:T(8,128)(2,1)S(1)}, u32[]{:S(2)}, u32[]{:S(2)}) collective-permute-start(bf16[1536,128]{1,0:T(8,128)(2,1)S(1)} %collective-permute-done.1), channel_id=1, source_target_pairs={{0,8},{1,12},{4,9},{5,13},{10,2},{11,6},{14,3},{15,7},{16,24},{17,... | collective-permute-start | bytes 1179656 | tf_op jit(solution)/shard_map/ppermute | solution.py:375
  26.3 2.3 %copy-start.2 = (bf16[96,1536]{1,0:T(8,128)(2,1)}, bf16[96,1536]{1,0:T(8,128)(2,1)S(1)}, u32[]{:S(2)}) copy-start(bf16[96,1536]{1,0:T(8,128)(2,1)S(1)} %get-tuple-element.21.imag_ref) | copy-start | bytes 884740
  28.7 26.1 %collective-permute-start.5 = (bf16[1536,256]{1,0:T(8,128)(2,1)S(1)}, bf16[1536,256]{1,0:T(8,128)(2,1)S(1)}, u32[]{:S(2)}, u32[]{:S(2)}) collective-permute-start(bf16[1536,256]{1,0:T(8,128)(2,1)S(1)} %fill_window.1.refs_4_.refs_7_.refs_0_), channel_id=1, source_target_pairs={{0,4},{4,8},{8,12},{1,5},{5,9},{9,13},{2,6},{6,10},{10,14},{3,7},{... | collective-permute-start | bytes 2359304 | tf_op jit(solution)/shard_map/ppermute | solution.py:419
  38.1 21.0 %collective-permute-start.4 = (bf16[1536,256]{1,0:T(8,128)(2,1)S(1)}, bf16[1536,256]{1,0:T(8,128)(2,1)S(1)}, u32[]{:S(2)}, u32[]{:S(2)}) collective-permute-start(bf16[1536,256]{1,0:T(8,128)(2,1)S(1)} %fill_window.1.refs_4_.refs_7_.refs_0_), channel_id=1, source_target_pairs={{4,0},{8,4},{12,8},{5,1},{9,5},{13,9},{6,2},{10,6},{14,10},{7,3},{... | collective-permute-start | bytes 2359304 | tf_op jit(solution)/shard_map/ppermute | solution.py:420
  66.6 4.2 %collective-permute-start.6 = (f32[1536,256]{1,0:T(8,128)S(1)}, f32[1536,256]{1,0:T(8,128)S(1)}, u32[]{:S(2)}, u32[]{:S(2)}) collective-permute-start(f32[1536,256]{1,0:T(8,128)S(1)} %get-tuple-element.25), channel_id=1, source_target_pairs={{0,1},{1,0},{2,3},{3,2},{4,5},{5,4},{6,7},{7,6},{8,9},{9,8},{10,11... | collective-permute-start | bytes 4718600 | tf_op jit(solution)/shard_map/ppermute | solution.py:454
  67.8 6.6 %collective-permute-start.8 = (bf16[1536,256]{1,0:T(8,128)(2,1)S(1)}, bf16[1536,256]{1,0:T(8,128)(2,1)S(1)}, u32[]{:S(2)}, u32[]{:S(2)}) collective-permute-start(bf16[1536,256]{1,0:T(8,128)(2,1)S(1)} %collective-permute-done.5.refs_6_.refs_9_.refs_2_.refs_7_), channel_id=1, source_target_pairs={{4,8},{8,12},{5,9},{9,13},{6,10},{10,14},{7,11},{11,15},{20,24},{2... | collective-permute-start | bytes 2359304 | tf_op jit(solution)/shard_map/ppermute | solution.py:419
  68.5 21.2 %collective-permute-start.9 = (bf16[1536,256]{1,0:T(8,128)(2,1)S(1)}, bf16[1536,256]{1,0:T(8,128)(2,1)}, u32[]{:S(2)}, u32[]{:S(2)}) collective-permute-start(bf16[1536,256]{1,0:T(8,128)(2,1)S(1)} %collective-permute-done.4.refs_5_.refs_8_.refs_1_.refs_6_), channel_id=1, source_target_pairs={{4,0},{8,4},{5,1},{9,5},{6,2},{10,6},{7,3},{11,7},{20,16},{24,20},... | collective-permute-start | bytes 2359304 | tf_op jit(solution)/shard_map/ppermute | solution.py:420
  70.8 2.7 %copy-start.3 = (bf16[96,1536]{1,0:T(8,128)(2,1)S(1)}, bf16[96,1536]{1,0:T(8,128)(2,1)}, u32[]{:S(2)}) copy-start(bf16[96,1536]{1,0:T(8,128)(2,1)} %copy-done.2) | copy-start | bytes 884740
  72.2 44.8 %collective-permute-start.7 = (f32[1536,256]{1,0:T(8,128)}, f32[1536,256]{1,0:T(8,128)}, u32[]{:S(2)}, u32[]{:S(2)}) collective-permute-start(f32[1536,256]{1,0:T(8,128)} %add.40.refs_0_), channel_id=1, source_target_pairs={{2,0},{3,1},{6,4},{7,5},{8,10},{9,11},{12,14},{13,15},{18,16},{19,... | collective-permute-start | bytes 4718600 | tf_op jit(solution)/shard_map/ppermute | solution.py:375
  89.6 25.5 %collective-permute-start.10 = (bf16[192,1536]{1,0:T(8,128)(2,1)}, bf16[192,1536]{1,0:T(8,128)(2,1)}, u32[]{:S(2)}, u32[]{:S(2)}) collective-permute-start(bf16[192,1536]{1,0:T(8,128)(2,1)} %pad_maximum_fusion), channel_id=1, source_target_pairs={{0,0},{1,4},{2,8},{3,12},{4,1},{5,5},{6,9},{7,13},{8,2},{9,6},{10,... | collective-permute-start | bytes 1769480 | tf_op jit(solution)/shard_map/ppermute | solution.py:375
  92.8 34.0 %collective-permute-start.11 = (bf16[1536,256]{1,0:T(8,128)(2,1)}, bf16[1536,256]{1,0:T(8,128)(2,1)}, u32[]{:S(2)}, u32[]{:S(2)}) collective-permute-start(bf16[1536,256]{1,0:T(8,128)(2,1)} %collective-permute-done.9.refs_4_.refs_3_), channel_id=1, source_target_pairs={{4,0},{5,1},{6,2},{7,3},{20,16},{21,17},{22,18},{23,19}} | collective-permute-start | bytes 2359304 | tf_op jit(solution)/shard_map/ppermute | solution.py:420
  94.1 32.7 %collective-permute-start.12 = (bf16[1536,256]{1,0:T(8,128)(2,1)S(1)}, bf16[1536,256]{1,0:T(8,128)(2,1)}, u32[]{:S(2)}, u32[]{:S(2)}) collective-permute-start(bf16[1536,256]{1,0:T(8,128)(2,1)S(1)} %collective-permute-done.8.refs_5_.refs_4_), channel_id=1, source_target_pairs={{8,12},{9,13},{10,14},{11,15},{24,28},{25,29},{26,30},{27,31}} | collective-permute-start | bytes 2359304 | tf_op jit(solution)/shard_map/ppermute | solution.py:419
  102.8 32.4 %collective-permute-start.14 = (f32[1536,256]{1,0:T(8,128)S(1)}, f32[1536,256]{1,0:T(8,128)S(1)}, u32[]{:S(2)}, u32[]{:S(2)}) collective-permute-start(f32[1536,256]{1,0:T(8,128)S(1)} %products.5), channel_id=1, source_target_pairs={{1,0},{3,2},{4,5},{6,7},{9,8},{11,10},{12,13},{14,15},{17,16},{19,... | collective-permute-start | bytes 4718600 | tf_op jit(solution)/shard_map/ppermute | solution.py:375
  133.9 8.7 %collective-permute-start.13 = (f32[1536,256]{1,0:T(8,128)S(1)}, f32[1536,256]{1,0:T(8,128)S(1)}, u32[]{:S(2)}, u32[]{:S(2)}) collective-permute-start(f32[1536,256]{1,0:T(8,128)S(1)} %products.4), channel_id=1, source_target_pairs={{0,1},{2,3},{5,4},{7,6},{8,9},{10,11},{13,12},{15,14},{16,17},{18,... | collective-permute-start | bytes 4718600 | tf_op jit(solution)/shard_map/ppermute | solution.py:375
  136.6 42.6 %collective-permute-start.15 = (f32[1536,256]{1,0:T(8,128)}, f32[1536,256]{1,0:T(8,128)}, u32[]{:S(2)}, u32[]{:S(2)}) collective-permute-start(f32[1536,256]{1,0:T(8,128)} %add.42.refs_1_), channel_id=1, source_target_pairs={{0,2},{5,7},{10,8},{15,13},{16,18},{21,23},{26,24},{31,29}} | collective-permute-start | bytes 4718600 | tf_op jit(solution)/shard_map/ppermute | solution.py:375
  144.0 35.2 %collective-permute-start.16 = (f32[1536,256]{1,0:T(8,128)}, f32[1536,256]{1,0:T(8,128)}, u32[]{:S(2)}, u32[]{:S(2)}) collective-permute-start(f32[1536,256]{1,0:T(8,128)} %add.41.refs_2_), channel_id=1, source_target_pairs={{1,3},{4,6},{11,9},{14,12},{17,19},{20,22},{27,25},{30,28}} | collective-permute-start | bytes 4718600 | tf_op jit(solution)/shard_map/ppermute | solution.py:375
  146.6 1.0 copy-start
  147.6 3.9 %copy-start.6 = (f32[2]{0:T(128)S(1)}, f32[2]{0:T(128)}, u32[]{:S(2)}) copy-start(f32[2]{0:T(128)} %param.7) | copy-start | bytes 28
  150.9 28.3 %copy-start.1 = (bf16[96,1536]{1,0:T(8,128)(2,1)S(1)}, bf16[96,1536]{1,0:T(8,128)(2,1)}, u32[]{:S(2)}) copy-start(bf16[96,1536]{1,0:T(8,128)(2,1)} %get-tuple-element.32.real_ref) | copy-start | bytes 884740
  151.0 1.6 collective-permute-start.17
  152.6 26.6 %collective-permute-start.18 = (f32[1,96,256]{2,1,0:T(8,128)S(1)}, f32[1,96,256]{2,1,0:T(8,128)S(1)}, u32[]{:S(2)}, u32[]{:S(2)}) collective-permute-start(f32[1,96,256]{2,1,0:T(8,128)S(1)} %slice.29), channel_id=1, source_target_pairs={{0,2},{1,3},{2,0},{3,1},{4,6},{5,7},{6,4},{7,5},{8,10},{9,11},{10,... | collective-permute-start | bytes 294920 | tf_op jit(solution)/shard_map/ppermute | solution.py:475

commit v7 on v6

--- a/solution.py
+++ b/solution.py
@@ -12,6 +12,8 @@
 LANES = 128
 CHUNKS = 1
 WIDTH = WIN // CHUNKS
+TINY = 1e-30
+HALF_TOP = 32768.0
 VMEM_LIMIT = 48 * 2**20
 VMEM = pl.BlockSpec(memory_space=pltpu.VMEM)
 SMEM = pl.BlockSpec(memory_space=pltpu.SMEM)
@@ -271,18 +273,9 @@
     )(picks, *rows, *flat)
 
 
-def finish_kernel(counts, wave_ref, flag_ref, miss_ref, recv_ref, tile_ref, real_ref, imag_ref, *refs):
+def finish_kernel(wave_ref, miss_ref, recv_ref, tile_ref, real_ref, imag_ref, *refs):
     out_ref, row_ref = refs[-2:]
-    totals = []
-    used = 0
-    for count in counts:
-        total = refs[used][...]
-        if count > 1:
-            total = total * flag_ref[0]
-        for index, ref in enumerate(refs[used + 1:used + count], 1):
-            total = total + (ref[...] * flag_ref[index] if index < count // 2 else ref[...])
-        used += count
-        totals.append(total)
+    totals = [ref[...] for ref in refs[:-2]]
 
     def write(target, window, chunks):
         real_part, imag_part = unpack(chunks)
@@ -303,16 +296,15 @@
     lax.fori_loop(0, row_ref.shape[1], place, 0, unroll=8)
 
 
-def finish(wave, flag, miss, recv8, traces, extra, terms):
+def finish(wave, miss, recv8, traces, extra, terms):
     _, rows, _ = traces.shape
     misses = extra[0].shape[0]
-    counts = tuple(len(group) for group in terms)
     flat = [term for group in terms for term in group]
     window = lambda size: pl.BlockSpec((2, size, WIN), lambda i: (0, 0, 0))
     return pl.pallas_call(
-        functools.partial(finish_kernel, counts),
+        finish_kernel,
         grid=(1,),
-        in_specs=[SMEM, SMEM, SMEM, pl.BlockSpec((8, WIN), lambda i: (0, 0)), window(rows)]
+        in_specs=[SMEM, SMEM, pl.BlockSpec((8, WIN), lambda i: (0, 0)), window(rows)]
         + [pl.BlockSpec((misses, WIN), lambda i: (0, 0))] * 2
         + [VMEM] * len(flat),
         out_specs=window(rows),
@@ -321,7 +313,7 @@
         compiler_params=params(),
         cost_estimate=cost(20 * rows * WIN, 40 * rows * WIN),
         name="finish",
-    )(wave, flag, miss, recv8, traces, *extra, *flat)
+    )(wave, miss, recv8, traces, *extra, *flat)
 
 
 def mirror_routes(grid_size):
@@ -404,7 +396,8 @@
     recv_col8 = jnp.broadcast_to(recv_col[None], (8, tile))
 
     picked = pick_columns(traces, miss_col_lanes, recv_col8, live8, misses)
-    extra = None
+    both = transpose(jnp.concatenate(picked))
+    extra = [both[:misses], both[misses:]]
     apart = row_index ^ col_index
     strides = [2**bit for bit in range(grid_size.bit_length() - 1)]
     terms, extra_terms = [], []
@@ -424,20 +417,21 @@
                 total = total + move(total, sum_route(offset, grid_size, stride, skip))
             return total
 
-        def last(total, offset, skip):
-            return move(total, sum_route(offset, grid_size, strides[-1], skip))
+        def shrink(total):
+            unit = jnp.maximum(jnp.max(jnp.abs(total)), TINY) * (1.0 / HALF_TOP)
+            sent = (total * (1.0 / unit)).astype(jnp.float16)
+            return sent, jnp.broadcast_to(unit, (1, LANES))
+
+        def last(shrunk, offset, skip):
+            route = sum_route(offset, grid_size, strides[-1], skip)
+            return [move(part, route) for part in shrunk]
 
         def options(offset):
             return sources_of(up, down, offset, grid_size, row_index)
 
         hop(1)
+        extra, up[-1], down[-1] = lax.optimization_barrier((extra, up[-1], down[-1]))
         hop(2)
-        if extra is None:
-            both, up[-1], down[-1] = lax.optimization_barrier(
-                (jnp.concatenate(picked), up[-1], down[-1])
-            )
-            both = transpose(both)
-            extra = [both[:misses], both[misses:]]
         _, (block0,) = options(0)
         pick1, sources1 = options(1)
         odd = apart & 1
@@ -452,21 +446,25 @@
         )
         other_core = [(i, i ^ 1) for i in range(grid_size)]
         total = add_up(keep + lax.ppermute(sent, "col", other_core), 0, strides[1:-1], 1)
+        shrunk, up[-1], down[-1] = lax.optimization_barrier((shrink(total), up[-1], down[-1]))
         for distance in range(3, grid_size):
             hop(distance)
         sums = [(0, 1, apart // 2 == 0, total)]
-        first = last(total, 0, 1)
+        got = [last(shrunk, 0, 1)]
         mask = recv_col8
         for offset in range(2, grid_size):
             if offset == grid_size - 1:
-                mask, first, extra = lax.optimization_barrier((mask, first, extra))
+                mask, got[0] = lax.optimization_barrier((mask, got[0]))
             (total,) = products(traces, mask, [options(offset)])
             total = add_up(total, offset, strides[:-1], 0)
             sums.append((offset, 0, apart == offset, total))
-        got = [first] + [last(total, offset, skip) for offset, skip, _, total in sums[1:]]
-        extra, _ = lax.optimization_barrier((extra, sums[-1][-1]))
-        terms.append([total for *_, total in sums] + got)
-        flags = [mine for _, _, mine, _ in sums]
+            got.append(last(shrink(total), offset, 0))
+        extra, got[-1][1] = lax.optimization_barrier((extra, got[-1][1]))
+        whole_sum = None
+        for (*_, mine, part), (sent, units) in zip(sums, got):
+            term = jnp.where(mine, part, 0.0) + sent.astype(jnp.float32) * units[0, 0]
+            whole_sum = term if whole_sum is None else whole_sum + term
+        terms.append((whole_sum,))
         group = [(pick, apart ^ offset, sources) for offset in range(grid_size)
                  for pick, sources in [options(offset)]]
         rest = extra_products(extra, group)
@@ -476,8 +474,7 @@
             rest = rest[0::2] + arrive
         extra_terms.append((rest[0],))
     wave = wavelet * (1.0 / math.sqrt(order))
-    flag = jnp.stack(flags).astype(jnp.float32)
-    return finish(wave, flag, miss_row, recv_col8, traces, extra, terms + extra_terms)
+    return finish(wave, miss_row, recv_col8, traces, extra, terms + extra_terms)
 
 
 def solution(mesh):

time: 186 us -> 181 us (0.973)
  waiting for transfers between devices: 90.5 us -> 64.3 us
  other arithmetic: 5.37 us -> 20.4 us
  starting transfers between devices: 46.9 us -> 51.4 us
  between operations: 0.35 us -> 2.57 us
    ppermute x2, waiting for transfers between devices: 27.5 us -> 9.6 us  [local(): arrive = lax.ppermute(rest[1::2], 'col', pairs)]
    reduce_max x0 -> x3, other arithmetic: none -> 9.78 us  [shrink(): unit = jnp.maximum(jnp.max(jnp.abs(total)), TINY) * (1.0 / HALF_TOP)]
    ppermute x10 -> x13, waiting for transfers between devices: 17.2 us -> 10.6 us  [move(): return lax.ppermute(block, ('row', 'col'), route)]
    convert_element_type x1 -> x3, other arithmetic: 0.08 us -> 6.06 us  [shrink(): sent = (total * (1.0 / unit)).astype(jnp.float16)]
    pallas_call x1, Pallas kernels: 6.05 us -> 2.84 us  [finish(): pl.pallas_call(finish_kernel, grid=(1,), in_specs=[SMEM, SMEM, pl.BlockSp...]
    ppermute x2, starting transfers between devices: 0.57 us -> 3.08 us  [local(): arrive = lax.ppermute(rest[1::2], 'col', pairs)]
    ppermute x10 -> x13, starting transfers between devices: 29.6 us -> 32.1 us  [move(): return lax.ppermute(block, ('row', 'col'), route)]
    pallas_call x3, Pallas kernels: 21.8 us -> 24.1 us  [products(): pl.pallas_call(functools.partial(product_kernel, counts), grid=(rows // b...]
  transfers between devices with their start and end apart: 19 -> 22, of which waited for: 11 -> 7; matrix products, arithmetic and copies ran while one was open for 4% -> 9% of each run, Pallas kernels for 13% -> 15%
where the time goes in v7:
time: 181 us; the launch traced here: 180 us
  waiting for transfers between devices  64.3 us (36%)
  starting transfers between devices  51.4 us (28%)
  Pallas kernels  38.4 us (21%)
  other arithmetic  20.4 us (11%)
  local copies, waits for them, and re-layouts  2.74 us (2%)
  between operations  2.57 us (1%)
    ppermute x13, starting transfers between devices, move(): return lax.ppermute(block, ('row', 'col'), route)  32.1 us
    ppermute x3, waiting for transfers between devices, hop(): down.append(lax.ppermute(down[-1], 'row', back))  29.1 us
    pallas_call x3, Pallas kernels, products(): pl.pallas_call(functools.partial(product_kernel, counts), grid=(rows // b...  24.1 us
    ppermute x3, waiting for transfers between devices, hop(): up.append(lax.ppermute(up[-1], 'row', ends))  13.8 us
    ppermute x3, starting transfers between devices, hop(): up.append(lax.ppermute(up[-1], 'row', ends))  12.1 us
    ppermute x13, waiting for transfers between devices, move(): return lax.ppermute(block, ('row', 'col'), route)  10.6 us
    reduce_max x3, other arithmetic, shrink(): unit = jnp.maximum(jnp.max(jnp.abs(total)), TINY) * (1.0 / HALF_TOP)  9.78 us
    ppermute x2, waiting for transfers between devices, local(): arrive = lax.ppermute(rest[1::2], 'col', pairs)  9.6 us
  transfers between devices with their start and end apart: 22, of which 7 were waited for; matrix products, arithmetic and copies ran while one was open for 9% of the time, Pallas kernels for 15%

profile of v7, /device:TPU:1, one launch (start us, length us, event | category | flops | bytes accessed | tf_op | source)
XLA Modules:
  0.0 179.8 jit_solution(4981887757191982582)
XLA Ops:
  0.0 1.3 cut_window.1
  1.3 1.3 collective-permute-start.2
  2.6 4.6 %collective-permute-start.4 = (bf16[1536,128]{1,0:T(8,128)(2,1)S(1)}, bf16[1536,128]{1,0:T(8,128)(2,1)S(1)}, u32[]{:S(2)}, u32[]{:S(2)}) collective-permute-start(bf16[1536,128]{1,0:T(8,128)(2,1)S(1)} %get-tuple-element.28), channel_id=1, source_target_pairs={{0,0},{1,4},{4,1},{5,5},{10,10},{11,14},{14,11},{15,15},{16,16},{1... | collective-permute-start | bytes 1179656 | tf_op jit(solution)/shard_map/ppermute | solution.py:367
  7.2 1.9 %collective-permute-start.1 = (bf16[1536,128]{1,0:T(8,128)(2,1)S(1)}, bf16[1536,128]{1,0:T(8,128)(2,1)S(1)}, u32[]{:S(2)}, u32[]{:S(2)}) collective-permute-start(bf16[1536,128]{1,0:T(8,128)(2,1)S(1)} %get-tuple-element.27), channel_id=1, source_target_pairs={{0,0},{1,4},{2,8},{3,12},{4,1},{5,5},{6,9},{7,13},{8,2},{9,6},{10,... | collective-permute-start | bytes 1179656 | tf_op jit(solution)/shard_map/ppermute | solution.py:367
  9.5 6.3 %pick_columns.1 = (bf16[96,1536]{1,0:T(8,128)(2,1)S(1)}, bf16[96,1536]{1,0:T(8,128)(2,1)S(1)}) custom-call(bf16[2,1536,1536]{2,1,0:T(8,128)(2,1)} %tile_ref.1, s32[1,128]{1,0:T(1,128)S(1)} %pad_bitcast_fusion.miss_ref, bf16[8,1536]{1,0:T(8,128)(2,1)S(1)} %broadcast_in_dim.38.recv_ref, f32[8,1536]{1,0:T(8,128)S(1)} %broadcast_in_dim.40.live_ref), custom_call_target="tpu_custom_call" | custom-call | flops 37748736 | bytes 147456 | tf_op jit(solution)/shard_map/pick_columns/pallas_call | solution.py:105
  15.7 5.6 %collective-permute-start.3 = (bf16[1536,128]{1,0:T(8,128)(2,1)}, bf16[1536,128]{1,0:T(8,128)(2,1)S(1)}, u32[]{:S(2)}, u32[]{:S(2)}) collective-permute-start(bf16[1536,128]{1,0:T(8,128)(2,1)} %collective-permute-done.2), channel_id=1, source_target_pairs={{0,8},{1,12},{4,9},{5,13},{10,2},{11,6},{14,3},{15,7},{16,24},{17,... | collective-permute-start | bytes 1179656 | tf_op jit(solution)/shard_map/ppermute | solution.py:367
  21.3 0.9 pad_maximum_fusion
  22.2 1.9 %collective-permute-start = (bf16[192,1536]{1,0:T(8,128)(2,1)}, bf16[192,1536]{1,0:T(8,128)(2,1)S(1)}, u32[]{:S(2)}, u32[]{:S(2)}) collective-permute-start(bf16[192,1536]{1,0:T(8,128)(2,1)} %pad_maximum_fusion), channel_id=1, source_target_pairs={{0,0},{1,4},{2,8},{3,12},{4,1},{5,5},{6,9},{7,13},{8,2},{9,6},{10,... | collective-permute-start | bytes 1769480 | tf_op jit(solution)/shard_map/ppermute | solution.py:367
  24.2 6.0 %collective-permute-done.3.refs_1_ = bf16[1536,128]{1,0:T(8,128)(2,1)S(1)} collective-permute-done((bf16[1536,128]{1,0:T(8,128)(2,1)}, bf16[1536,128]{1,0:T(8,128)(2,1)S(1)}, u32[]{:S(2)}, u32[]{:S(2)}) %collective-permute-start.3) | collective-permute-done | bytes 393248 | tf_op jit(solution)/shard_map/ppermute | solution.py:367
  30.1 0.5 fill_window.1.refs_4_.refs_7_.refs_0_
  30.6 9.8 %collective-permute-start.5 = (bf16[1536,256]{1,0:T(8,128)(2,1)S(1)}, bf16[1536,256]{1,0:T(8,128)(2,1)S(1)}, u32[]{:S(2)}, u32[]{:S(2)}) collective-permute-start(bf16[1536,256]{1,0:T(8,128)(2,1)S(1)} %fill_window.1.refs_4_.refs_7_.refs_0_), channel_id=1, source_target_pairs={{0,4},{4,8},{8,12},{1,5},{5,9},{9,13},{2,6},{6,10},{10,14},{3,7},{... | collective-permute-start | bytes 2359304 | tf_op jit(solution)/shard_map/ppermute | solution.py:412
  40.4 1.3 collective-permute-start.6
  41.8 0.8 fusion.2
  42.6 13.8 %collective-permute-done.5.refs_6_.refs_9_.refs_2_.refs_7_ = bf16[1536,256]{1,0:T(8,128)(2,1)S(1)} collective-permute-done((bf16[1536,256]{1,0:T(8,128)(2,1)S(1)}, bf16[1536,256]{1,0:T(8,128)(2,1)S(1)}, u32[]{:S(2)}, u32[]{:S(2)}) %collective-permute-start.5) | collective-permute-done | bytes 786464 | tf_op jit(solution)/shard_map/ppermute | solution.py:412
  56.4 12.3 %collective-permute-done.6.refs_5_.refs_8_.refs_1_.refs_6_ = bf16[1536,256]{1,0:T(8,128)(2,1)S(1)} collective-permute-done((bf16[1536,256]{1,0:T(8,128)(2,1)S(1)}, bf16[1536,256]{1,0:T(8,128)(2,1)S(1)}, u32[]{:S(2)}, u32[]{:S(2)}) %collective-permute-start.6) | collective-permute-done | bytes 786464 | tf_op jit(solution)/shard_map/ppermute | solution.py:413
  68.6 7.6 %products.3 = (f32[1536,256]{1,0:T(8,128)S(1)}, f32[1536,256]{1,0:T(8,128)S(1)}) custom-call(s32[2]{0:T(128)S(1)} %pad_add_fusion.pick_ref, bf16[8,1536]{1,0:T(8,128)(2,1)S(1)} %broadcast_in_dim.38.recv_ref, bf16[2,1536,1536]{2,1,0:T(8,128)(2,1)} %tile_ref.1, bf16[2,1536,1536]{2,1,0:T(8,128)(2,1)} %tile_ref.1, bf16[2,1536,1536]{2,1,0:T(8,128)(2,1)} %tile_ref.1, ...), custom_call_target="tpu_custom_call" | custom-call | flops 150994944 | bytes 24576 | tf_op jit(solution)/shard_map/products/pallas_call | solution.py:230
  76.2 0.2 collective-permute-start.7
  76.5 0.7 collective-permute-start.8
  77.2 1.3 collective-permute-start.9
  78.5 1.2 collective-permute-done.7
  79.7 2.0 %abs_reduce_fusion.2 = (f32[]{:T(128)}, f32[1536,256]{1,0:T(8,128)}) fusion(f32[1536,256]{1,0:T(8,128)S(1)} %get-tuple-element.33, f32[1536,256]{1,0:T(8,128)S(1)} %collective-permute-done.7), kind=kLoop, calls=%fused_computation.6 | loop fusion | flops 1179647 | bytes 4718596 | tf_op jit(solution)/shard_map/reduce_max | solution.py:421
  82.4 2.5 %multiply_convert_fusion.2 = f16[1536,256]{1,0:T(8,128)(2,1)} fusion(f32[1536,256]{1,0:T(8,128)} %get-tuple-element.50, f32[]{:T(128)S(6)} %div.17), kind=kLoop, calls=%fused_computation.5 | loop fusion | flops 786432 | bytes 2359300 | tf_op jit(solution)/shard_map/convert_element_type | solution.py:422
  84.9 16.8 %collective-permute-done.9.refs_4_.refs_3_ = bf16[1536,256]{1,0:T(8,128)(2,1)} collective-permute-done((bf16[1536,256]{1,0:T(8,128)(2,1)S(1)}, bf16[1536,256]{1,0:T(8,128)(2,1)}, u32[]{:S(2)}, u32[]{:S(2)}) %collective-permute-start.9) | collective-permute-done | bytes 786464 | tf_op jit(solution)/shard_map/ppermute | solution.py:413
  101.6 1.3 collective-permute-start.10
  102.9 1.3 collective-permute-start.12
  104.2 1.6 collective-permute-start.13
  105.8 8.2 %products.5 = f32[1536,256]{1,0:T(8,128)} custom-call(s32[1]{0:T(128)} %bitcast.7.pick_ref, bf16[8,1536]{1,0:T(8,128)(2,1)S(1)} %broadcast_in_dim.38.recv_ref, bf16[2,1536,1536]{2,1,0:T(8,128)(2,1)} %tile_ref.1, bf16[2,1536,1536]{2,1,0:T(8,128)(2,1)} %tile_ref.1, bf16[2,1536,1536]{2,1,0:T(8,128)(2,1)} %tile_ref.1, bf16[2,1536,1536]{2,1,0:T(8,128)(2,1)} %tile_ref.1, ...), custom_call_target="tpu_custom_call" | custom-call | flops 75497472 | bytes 24576 | tf_op jit(solution)/shard_map/products/pallas_call | solution.py:230
  114.1 3.8 %collective-permute-start.16 = (f32[1536,256]{1,0:T(8,128)}, f32[1536,256]{1,0:T(8,128)}, u32[]{:S(2)}, u32[]{:S(2)}) collective-permute-start(f32[1536,256]{1,0:T(8,128)} %products.5), channel_id=1, source_target_pairs={{1,0},{3,2},{4,5},{6,7},{9,8},{11,10},{12,13},{14,15},{17,16},{19,... | collective-permute-start | bytes 4718600 | tf_op jit(solution)/shard_map/ppermute | solution.py:367
  117.8 1.3 collective-permute-start.11
  119.1 4.6 %collective-permute-done.11 = f32[1,128]{1,0:T(1,128)S(1)} collective-permute-done((f32[1,128]{1,0:T(1,128)S(1)}, f32[1,128]{1,0:T(1,128)S(1)}, u32[]{:S(2)}, u32[]{:S(2)}) %collective-permute-start.11) | collective-permute-done | bytes 544 | tf_op jit(solution)/shard_map/ppermute | solution.py:367
  123.8 8.3 %products.4 = f32[1536,256]{1,0:T(8,128)} custom-call(s32[1]{0:T(128)} %bitcast.3.pick_ref, bf16[8,1536]{1,0:T(8,128)(2,1)S(1)} %broadcast_in_dim.38.recv_ref, bf16[2,1536,1536]{2,1,0:T(8,128)(2,1)} %tile_ref.1, bf16[2,1536,1536]{2,1,0:T(8,128)(2,1)} %tile_ref.1, bf16[2,1536,1536]{2,1,0:T(8,128)(2,1)} %tile_ref.1, bf16[2,1536,1536]{2,1,0:T(8,128)(2,1)} %tile_ref.1, ...), custom_call_target="tpu_custom_call" | custom-call | flops 75497472 | bytes 24576 | tf_op jit(solution)/shard_map/products/pallas_call | solution.py:230
  132.0 1.3 collective-permute-start.14
  133.4 4.0 %abs_reduce_fusion = (f32[]{:T(128)}, f32[1536,256]{1,0:T(8,128)}) fusion(f32[1536,256]{1,0:T(8,128)} %products.5, f32[1536,256]{1,0:T(8,128)} %collective-permute-done.16), kind=kLoop, calls=%fused_computation.3 | loop fusion | flops 1179647 | bytes 4718596 | tf_op jit(solution)/shard_map/reduce_max | solution.py:421
  138.1 3.8 %abs_reduce_fusion.1 = (f32[]{:T(128)}, f32[1536,256]{1,0:T(8,128)}) fusion(f32[1536,256]{1,0:T(8,128)} %products.4, f32[1536,256]{1,0:T(8,128)} %collective-permute-done.14), kind=kLoop, calls=%fused_computation.4 | loop fusion | flops 1179647 | bytes 4718596 | tf_op jit(solution)/shard_map/reduce_max | solution.py:421
  142.6 4.7 %collective-permute-start.15 = (f32[1,128]{1,0:T(1,128)S(1)}, f32[1,128]{1,0:T(1,128)S(1)}, u32[]{:S(2)}, u32[]{:S(2)}) collective-permute-start(f32[1,128]{1,0:T(1,128)S(1)} %broadcast_in_dim.43), channel_id=1, source_target_pairs={{1,3},{4,6},{11,9},{14,12},{17,19},{20,22},{27,25},{30,28}} | collective-permute-start | bytes 1544 | tf_op jit(solution)/shard_map/ppermute | solution.py:367
  147.3 2.5 %multiply_convert_fusion.1 = f16[1536,256]{1,0:T(8,128)(2,1)} fusion(f32[1536,256]{1,0:T(8,128)} %get-tuple-element.46, f32[]{:T(128)S(6)} %div.21), kind=kLoop, calls=%fused_computation.2 | loop fusion | flops 786432 | bytes 2359300 | tf_op jit(solution)/shard_map/convert_element_type | solution.py:422
  149.8 1.6 collective-permute-start.17
  151.4 1.0 copy-done
  152.4 3.4 %extra_products.1 = f32[4,96,256]{2,1,0:T(8,128)S(1)} custom-call(s32[8]{0:T(128)S(1)} %stack.46.pick_ref, bf16[96,1536]{1,0:T(8,128)(2,1)S(1)} %copy-done, bf16[96,1536]{1,0:T(8,128)(2,1)S(1)} %get-tuple-element.41.imag_ref, bf16[1536,256]{1,0:T(8,128)(2,1)S(1)} %fill_window.1.refs_4_.refs_7_.refs_0_, ...), custom_call_target="tpu_custom_call" | custom-call | flops 18874368 | bytes 24576 | tf_op jit(solution)/shard_map/extra_products/pallas_call | solution.py:264
  155.8 3.1 %collective-permute-start.20 = (f32[2,96,256]{2,1,0:T(8,128)S(1)}, f32[2,96,256]{2,1,0:T(8,128)S(1)}, u32[]{:S(2)}, u32[]{:S(2)}) collective-permute-start(f32[2,96,256]{2,1,0:T(8,128)S(1)} %slice.35), channel_id=1, source_target_pairs={{0,1},{1,0},{2,3},{3,2},{4,5},{5,4},{6,7},{7,6},{8,9},{9,8},{10,11... | collective-permute-start | bytes 589832 | tf_op jit(solution)/shard_map/ppermute | solution.py:473
  158.9 1.1 multiply_convert_fusion
  160.0 2.3 %collective-permute-start.19 = (f16[1536,256]{1,0:T(8,128)(2,1)}, f16[1536,256]{1,0:T(8,128)(2,1)}, u32[]{:S(2)}, u32[]{:S(2)}) collective-permute-start(f16[1536,256]{1,0:T(8,128)(2,1)} %multiply_convert_fusion), channel_id=1, source_target_pairs={{1,3},{4,6},{11,9},{14,12},{17,19},{20,22},{27,25},{30,28}} | collective-permute-start | bytes 2359304 | tf_op jit(solution)/shard_map/ppermute | solution.py:367
  162.4 0.7 slice.41
  163.1 0.7 collective-permute-start.18
  163.8 9.6 %collective-permute-done.21 = f32[1,96,256]{2,1,0:T(8,128)} collective-permute-done((f32[1,96,256]{2,1,0:T(8,128)}, f32[1,96,256]{2,1,0:T(8,128)}, u32[]{:S(2)}, u32[]{:S(2)}) %collective-permute-start.21) | collective-permute-done | bytes 98336 | tf_op jit(solution)/shard_map/ppermute | solution.py:473
  173.4 1.0 fusion.1.refs_1_
  174.4 2.5 %add_add_fusion.refs_0_ = f32[1536,256]{1,0:T(8,128)S(1)} fusion(f16[1536,256]{1,0:T(8,128)(2,1)} %collective-permute-done.19, f32[1536,256]{1,0:T(8,128)} %get-tuple-element.48, f16[1536,256]{1,0:T(8,128)(2,1)} %collective-permute-done.17, f32[1536,256]{1,0:T(8,128)S(1)} %copy-done.3, f16[1536,256]{1,0:T(8,128)(2,1)} %collective-permute-done.10, ...), kind=kLoop, calls=%fused_computation | loop fusion | flops 5505024 | bytes 8650767 | tf_op jit(solution)/shard_map/add | solution.py:466
  176.9 2.8 %finish.1 = f32[2,1536,128]{2,1,0:T(8,128)} custom-call(f32[2]{0:T(128)S(1)} %broadcast_multiply_fusion.wave_ref, s32[96]{0:T(128)S(1)} %get-tuple-element.54.miss_ref, bf16[8,1536]{1,0:T(8,128)(2,1)S(1)} %broadcast_in_dim.38.recv_ref, bf16[2,1536,1536]{2,1,0:T(8,128)(2,1)} %tile_ref.1, bf16[96,1536]{1,0:T(8,128)(2,1)S(1)} %copy-done.1, ...), custom_call_target="tpu_custom_call" | custom-call | flops 61440 | bytes 122880 | tf_op jit(solution)/shard_map/finish/pallas_call | solution.py:304
  (51 shorter events, 0.7 us)
Async XLA Ops:
  0.0 9.1 %copy-start.7 = (s32[4,96]{1,0:T(4,128)S(1)}, s32[4,96]{1,0:T(4,128)}, u32[]{:S(2)}) copy-start(s32[4,96]{1,0:T(4,128)} %param.6) | copy-start | bytes 4612
  0.0 9.3 %copy-start.6 = (s32[6144]{0:T(1024)S(1)}, s32[6144]{0:T(1024)}, u32[]{:S(2)}) copy-start(s32[6144]{0:T(1024)} %param.5) | copy-start | bytes 73732
  1.3 14.4 %collective-permute-start.2 = (bf16[1536,128]{1,0:T(8,128)(2,1)S(1)}, bf16[1536,128]{1,0:T(8,128)(2,1)}, u32[]{:S(2)}, u32[]{:S(2)}) collective-permute-start(bf16[1536,128]{1,0:T(8,128)(2,1)S(1)} %get-tuple-element.28), channel_id=1, source_target_pairs={{2,0},{3,1},{6,4},{7,5},{8,10},{9,11},{12,14},{13,15},{18,16},{19,... | collective-permute-start | bytes 1179656 | tf_op jit(solution)/shard_map/ppermute | solution.py:367
  2.6 21.6 %collective-permute-start.4 = (bf16[1536,128]{1,0:T(8,128)(2,1)S(1)}, bf16[1536,128]{1,0:T(8,128)(2,1)S(1)}, u32[]{:S(2)}, u32[]{:S(2)}) collective-permute-start(bf16[1536,128]{1,0:T(8,128)(2,1)S(1)} %get-tuple-element.28), channel_id=1, source_target_pairs={{0,0},{1,4},{4,1},{5,5},{10,10},{11,14},{14,11},{15,15},{16,16},{1... | collective-permute-start | bytes 1179656 | tf_op jit(solution)/shard_map/ppermute | solution.py:367
  7.2 17.0 %collective-permute-start.1 = (bf16[1536,128]{1,0:T(8,128)(2,1)S(1)}, bf16[1536,128]{1,0:T(8,128)(2,1)S(1)}, u32[]{:S(2)}, u32[]{:S(2)}) collective-permute-start(bf16[1536,128]{1,0:T(8,128)(2,1)S(1)} %get-tuple-element.27), channel_id=1, source_target_pairs={{0,0},{1,4},{2,8},{3,12},{4,1},{5,5},{6,9},{7,13},{8,2},{9,6},{10,... | collective-permute-start | bytes 1179656 | tf_op jit(solution)/shard_map/ppermute | solution.py:367
  15.7 14.4 %collective-permute-start.3 = (bf16[1536,128]{1,0:T(8,128)(2,1)}, bf16[1536,128]{1,0:T(8,128)(2,1)S(1)}, u32[]{:S(2)}, u32[]{:S(2)}) collective-permute-start(bf16[1536,128]{1,0:T(8,128)(2,1)} %collective-permute-done.2), channel_id=1, source_target_pairs={{0,8},{1,12},{4,9},{5,13},{10,2},{11,6},{14,3},{15,7},{16,24},{17,... | collective-permute-start | bytes 1179656 | tf_op jit(solution)/shard_map/ppermute | solution.py:367
  22.2 19.6 %collective-permute-start = (bf16[192,1536]{1,0:T(8,128)(2,1)}, bf16[192,1536]{1,0:T(8,128)(2,1)S(1)}, u32[]{:S(2)}, u32[]{:S(2)}) collective-permute-start(bf16[192,1536]{1,0:T(8,128)(2,1)} %pad_maximum_fusion), channel_id=1, source_target_pairs={{0,0},{1,4},{2,8},{3,12},{4,1},{5,5},{6,9},{7,13},{8,2},{9,6},{10,... | collective-permute-start | bytes 1769480 | tf_op jit(solution)/shard_map/ppermute | solution.py:367
  30.6 25.7 %collective-permute-start.5 = (bf16[1536,256]{1,0:T(8,128)(2,1)S(1)}, bf16[1536,256]{1,0:T(8,128)(2,1)S(1)}, u32[]{:S(2)}, u32[]{:S(2)}) collective-permute-start(bf16[1536,256]{1,0:T(8,128)(2,1)S(1)} %fill_window.1.refs_4_.refs_7_.refs_0_), channel_id=1, source_target_pairs={{0,4},{4,8},{8,12},{1,5},{5,9},{9,13},{2,6},{6,10},{10,14},{3,7},{... | collective-permute-start | bytes 2359304 | tf_op jit(solution)/shard_map/ppermute | solution.py:412
  40.4 28.2 %collective-permute-start.6 = (bf16[1536,256]{1,0:T(8,128)(2,1)S(1)}, bf16[1536,256]{1,0:T(8,128)(2,1)S(1)}, u32[]{:S(2)}, u32[]{:S(2)}) collective-permute-start(bf16[1536,256]{1,0:T(8,128)(2,1)S(1)} %fill_window.1.refs_4_.refs_7_.refs_0_), channel_id=1, source_target_pairs={{4,0},{8,4},{12,8},{5,1},{9,5},{13,9},{6,2},{10,6},{14,10},{7,3},{... | collective-permute-start | bytes 2359304 | tf_op jit(solution)/shard_map/ppermute | solution.py:413
  76.2 3.5 %collective-permute-start.7 = (f32[1536,256]{1,0:T(8,128)S(1)}, f32[1536,256]{1,0:T(8,128)S(1)}, u32[]{:S(2)}, u32[]{:S(2)}) collective-permute-start(f32[1536,256]{1,0:T(8,128)S(1)} %get-tuple-element.34), channel_id=1, source_target_pairs={{0,1},{1,0},{2,3},{3,2},{4,5},{5,4},{6,7},{7,6},{8,9},{9,8},{10,11... | collective-permute-start | bytes 4718600 | tf_op jit(solution)/shard_map/ppermute | solution.py:448
  76.5 8.4 %collective-permute-start.8 = (bf16[1536,256]{1,0:T(8,128)(2,1)S(1)}, bf16[1536,256]{1,0:T(8,128)(2,1)S(1)}, u32[]{:S(2)}, u32[]{:S(2)}) collective-permute-start(bf16[1536,256]{1,0:T(8,128)(2,1)S(1)} %collective-permute-done.5.refs_6_.refs_9_.refs_2_.refs_7_), channel_id=1, source_target_pairs={{4,8},{8,12},{5,9},{9,13},{6,10},{10,14},{7,11},{11,15},{20,24},{2... | collective-permute-start | bytes 2359304 | tf_op jit(solution)/shard_map/ppermute | solution.py:412
  77.2 24.5 %collective-permute-start.9 = (bf16[1536,256]{1,0:T(8,128)(2,1)S(1)}, bf16[1536,256]{1,0:T(8,128)(2,1)}, u32[]{:S(2)}, u32[]{:S(2)}) collective-permute-start(bf16[1536,256]{1,0:T(8,128)(2,1)S(1)} %collective-permute-done.6.refs_5_.refs_8_.refs_1_.refs_6_), channel_id=1, source_target_pairs={{4,0},{8,4},{5,1},{9,5},{6,2},{10,6},{7,3},{11,7},{20,16},{24,20},... | collective-permute-start | bytes 2359304 | tf_op jit(solution)/shard_map/ppermute | solution.py:413
  101.6 22.1 %collective-permute-start.10 = (f16[1536,256]{1,0:T(8,128)(2,1)}, f16[1536,256]{1,0:T(8,128)(2,1)}, u32[]{:S(2)}, u32[]{:S(2)}) collective-permute-start(f16[1536,256]{1,0:T(8,128)(2,1)} %multiply_convert_fusion.2), channel_id=1, source_target_pairs={{2,0},{3,1},{6,4},{7,5},{8,10},{9,11},{12,14},{13,15},{18,16},{19,... | collective-permute-start | bytes 2359304 | tf_op jit(solution)/shard_map/ppermute | solution.py:367
  102.9 20.8 %collective-permute-start.12 = (bf16[1536,256]{1,0:T(8,128)(2,1)}, bf16[1536,256]{1,0:T(8,128)(2,1)}, u32[]{:S(2)}, u32[]{:S(2)}) collective-permute-start(bf16[1536,256]{1,0:T(8,128)(2,1)} %collective-permute-done.9.refs_4_.refs_3_), channel_id=1, source_target_pairs={{4,0},{5,1},{6,2},{7,3},{20,16},{21,17},{22,18},{23,19}} | collective-permute-start | bytes 2359304 | tf_op jit(solution)/shard_map/ppermute | solution.py:413
  104.2 19.5 %collective-permute-start.13 = (bf16[1536,256]{1,0:T(8,128)(2,1)S(1)}, bf16[1536,256]{1,0:T(8,128)(2,1)}, u32[]{:S(2)}, u32[]{:S(2)}) collective-permute-start(bf16[1536,256]{1,0:T(8,128)(2,1)S(1)} %collective-permute-done.8.refs_5_.refs_4_), channel_id=1, source_target_pairs={{8,12},{9,13},{10,14},{11,15},{24,28},{25,29},{26,30},{27,31}} | collective-permute-start | bytes 2359304 | tf_op jit(solution)/shard_map/ppermute | solution.py:412
  114.1 19.3 %collective-permute-start.16 = (f32[1536,256]{1,0:T(8,128)}, f32[1536,256]{1,0:T(8,128)}, u32[]{:S(2)}, u32[]{:S(2)}) collective-permute-start(f32[1536,256]{1,0:T(8,128)} %products.5), channel_id=1, source_target_pairs={{1,0},{3,2},{4,5},{6,7},{9,8},{11,10},{12,13},{14,15},{17,16},{19,... | collective-permute-start | bytes 4718600 | tf_op jit(solution)/shard_map/ppermute | solution.py:367
  117.8 5.9 %collective-permute-start.11 = (f32[1,128]{1,0:T(1,128)S(1)}, f32[1,128]{1,0:T(1,128)S(1)}, u32[]{:S(2)}, u32[]{:S(2)}) collective-permute-start(f32[1,128]{1,0:T(1,128)S(1)} %broadcast_in_dim.42), channel_id=1, source_target_pairs={{2,0},{3,1},{6,4},{7,5},{8,10},{9,11},{12,14},{13,15},{18,16},{19,... | collective-permute-start | bytes 1544 | tf_op jit(solution)/shard_map/ppermute | solution.py:367
  132.0 6.1 %collective-permute-start.14 = (f32[1536,256]{1,0:T(8,128)}, f32[1536,256]{1,0:T(8,128)}, u32[]{:S(2)}, u32[]{:S(2)}) collective-permute-start(f32[1536,256]{1,0:T(8,128)} %products.4), channel_id=1, source_target_pairs={{0,1},{2,3},{5,4},{7,6},{8,9},{10,11},{13,12},{15,14},{16,17},{18,... | collective-permute-start | bytes 4718600 | tf_op jit(solution)/shard_map/ppermute | solution.py:367
  142.6 8.8 %collective-permute-start.15 = (f32[1,128]{1,0:T(1,128)S(1)}, f32[1,128]{1,0:T(1,128)S(1)}, u32[]{:S(2)}, u32[]{:S(2)}) collective-permute-start(f32[1,128]{1,0:T(1,128)S(1)} %broadcast_in_dim.43), channel_id=1, source_target_pairs={{1,3},{4,6},{11,9},{14,12},{17,19},{20,22},{27,25},{30,28}} | collective-permute-start | bytes 1544 | tf_op jit(solution)/shard_map/ppermute | solution.py:367
  149.8 24.6 %collective-permute-start.17 = (f16[1536,256]{1,0:T(8,128)(2,1)}, f16[1536,256]{1,0:T(8,128)(2,1)}, u32[]{:S(2)}, u32[]{:S(2)}) collective-permute-start(f16[1536,256]{1,0:T(8,128)(2,1)} %multiply_convert_fusion.1), channel_id=1, source_target_pairs={{0,2},{5,7},{10,8},{15,13},{16,18},{21,23},{26,24},{31,29}} | collective-permute-start | bytes 2359304 | tf_op jit(solution)/shard_map/ppermute | solution.py:367
  151.4 1.0 copy-start
  152.4 6.6 %copy-start.4 = (f32[1536,256]{1,0:T(8,128)S(1)}, f32[1536,256]{1,0:T(8,128)}, u32[]{:S(2)}) copy-start(f32[1536,256]{1,0:T(8,128)} %get-tuple-element.48) | copy-start | bytes 4718596
  155.8 6.5 %collective-permute-start.20 = (f32[2,96,256]{2,1,0:T(8,128)S(1)}, f32[2,96,256]{2,1,0:T(8,128)S(1)}, u32[]{:S(2)}, u32[]{:S(2)}) collective-permute-start(f32[2,96,256]{2,1,0:T(8,128)S(1)} %slice.35), channel_id=1, source_target_pairs={{0,1},{1,0},{2,3},{3,2},{4,5},{5,4},{6,7},{7,6},{8,9},{9,8},{10,11... | collective-permute-start | bytes 589832 | tf_op jit(solution)/shard_map/ppermute | solution.py:473
  158.9 4.2 %copy-start.8 = (f32[2]{0:T(128)S(1)}, f32[2]{0:T(128)}, u32[]{:S(2)}) copy-start(f32[2]{0:T(128)} %param.7) | copy-start | bytes 28
  158.9 15.5 %copy-start.2 = (f32[1536,256]{1,0:T(8,128)S(1)}, f32[1536,256]{1,0:T(8,128)}, u32[]{:S(2)}) copy-start(f32[1536,256]{1,0:T(8,128)} %get-tuple-element.50) | copy-start | bytes 4718596
  158.9 15.5 %copy-start.3 = (f32[1536,256]{1,0:T(8,128)S(1)}, f32[1536,256]{1,0:T(8,128)}, u32[]{:S(2)}) copy-start(f32[1536,256]{1,0:T(8,128)} %get-tuple-element.46) | copy-start | bytes 4718596
  160.0 14.4 %collective-permute-start.19 = (f16[1536,256]{1,0:T(8,128)(2,1)}, f16[1536,256]{1,0:T(8,128)(2,1)}, u32[]{:S(2)}, u32[]{:S(2)}) collective-permute-start(f16[1536,256]{1,0:T(8,128)(2,1)} %multiply_convert_fusion), channel_id=1, source_target_pairs={{1,3},{4,6},{11,9},{14,12},{17,19},{20,22},{27,25},{30,28}} | collective-permute-start | bytes 2359304 | tf_op jit(solution)/shard_map/ppermute | solution.py:367
  162.4 0.7 copy-start.5
  163.1 10.3 %collective-permute-start.21 = (f32[1,96,256]{2,1,0:T(8,128)}, f32[1,96,256]{2,1,0:T(8,128)}, u32[]{:S(2)}, u32[]{:S(2)}) collective-permute-start(f32[1,96,256]{2,1,0:T(8,128)} %slice.41), channel_id=1, source_target_pairs={{0,2},{1,3},{2,0},{3,1},{4,6},{5,7},{6,4},{7,5},{8,10},{9,11},{10,... | collective-permute-start | bytes 294920 | tf_op jit(solution)/shard_map/ppermute | solution.py:473
  163.1 11.2 %collective-permute-start.18 = (f32[1,128]{1,0:T(1,128)S(1)}, f32[1,128]{1,0:T(1,128)S(1)}, u32[]{:S(2)}, u32[]{:S(2)}) collective-permute-start(f32[1,128]{1,0:T(1,128)S(1)} %broadcast_in_dim.45), channel_id=1, source_target_pairs={{0,2},{5,7},{10,8},{15,13},{16,18},{21,23},{26,24},{31,29}} | collective-permute-start | bytes 1544 | tf_op jit(solution)/shard_map/ppermute | solution.py:367
  174.4 2.5 %copy-start.1 = (bf16[96,1536]{1,0:T(8,128)(2,1)S(1)}, bf16[96,1536]{1,0:T(8,128)(2,1)}, u32[]{:S(2)}) copy-start(bf16[96,1536]{1,0:T(8,128)(2,1)} %get-tuple-element.40.real_ref) | copy-start | bytes 884740

commit v8 on v7

--- a/solution.py
+++ b/solution.py
@@ -432,42 +432,44 @@
         hop(1)
         extra, up[-1], down[-1] = lax.optimization_barrier((extra, up[-1], down[-1]))
         hop(2)
-        _, (block0,) = options(0)
-        pick1, sources1 = options(1)
+        other_core = [(i, i ^ 1) for i in range(grid_size)]
         odd = apart & 1
-        everything = [block0] + sources1
-        keep, sent = products(
-            traces,
-            recv_col8,
-            [
-                (jnp.where(odd == 1, 1 + pick1, 0), everything),
-                (jnp.where(odd == 1, 0, 1 + pick1), everything),
-            ],
-        )
-        other_core = [(i, i ^ 1) for i in range(grid_size)]
-        total = add_up(keep + lax.ppermute(sent, "col", other_core), 0, strides[1:-1], 1)
-        shrunk, up[-1], down[-1] = lax.optimization_barrier((shrink(total), up[-1], down[-1]))
+
+        def pair_sum(first, mask):
+            pick0, sources0 = options(first)
+            pick1, sources1 = options(first + 1)
+            pick1 = pick1 + len(sources0)
+            both_sources = sources0 + sources1
+            keep, sent = products(
+                traces,
+                mask,
+                [
+                    (jnp.where(odd == 1, pick1, pick0), both_sources),
+                    (jnp.where(odd == 1, pick0, pick1), both_sources),
+                ],
+            )
+            return add_up(keep + lax.ppermute(sent, "col", other_core), first, strides[1:-1], 1)
+
+        sums = [pair_sum(0, recv_col8)]
+        shrunk, up[-1], down[-1] = lax.optimization_barrier((shrink(sums[0]), up[-1], down[-1]))
         for distance in range(3, grid_size):
             hop(distance)
-        sums = [(0, 1, apart // 2 == 0, total)]
         got = [last(shrunk, 0, 1)]
         mask = recv_col8
-        for offset in range(2, grid_size):
-            if offset == grid_size - 1:
-                mask, got[0] = lax.optimization_barrier((mask, got[0]))
-            (total,) = products(traces, mask, [options(offset)])
-            total = add_up(total, offset, strides[:-1], 0)
-            sums.append((offset, 0, apart == offset, total))
-            got.append(last(shrink(total), offset, 0))
-        extra, got[-1][1] = lax.optimization_barrier((extra, got[-1][1]))
+        for first in range(2, grid_size, 2):
+            if first == grid_size - 2:
+                group = [(pick, apart ^ offset, sources) for offset in range(grid_size)
+                         for pick, sources in [options(offset)]]
+                rest = extra_products(extra, group)
+                mask, got[0], rest = lax.optimization_barrier((mask, got[0], rest))
+            sums.append(pair_sum(first, mask))
+            got.append(last(shrink(sums[-1]), first, 1))
         whole_sum = None
-        for (*_, mine, part), (sent, units) in zip(sums, got):
+        for index, (part, (sent, units)) in enumerate(zip(sums, got)):
+            mine = apart // 2 == index
             term = jnp.where(mine, part, 0.0) + sent.astype(jnp.float32) * units[0, 0]
             whole_sum = term if whole_sum is None else whole_sum + term
         terms.append((whole_sum,))
-        group = [(pick, apart ^ offset, sources) for offset in range(grid_size)
-                 for pick, sources in [options(offset)]]
-        rest = extra_products(extra, group)
         for stride in strides:
             pairs = [(i, i ^ stride) for i in range(grid_size)]
             arrive = lax.ppermute(rest[1::2], "col", pairs)

time: 181 us -> 178 us (0.983)
  waiting for transfers between devices: 64.3 us -> 81.6 us
  starting transfers between devices: 51.4 us -> 43.4 us
  other arithmetic: 20.4 us -> 12.6 us
  Pallas kernels: 38.4 us -> 32.7 us
    ppermute x3, waiting for transfers between devices: 29.1 us -> 44.4 us  [hop(): down.append(lax.ppermute(down[-1], 'row', back))]
    ppermute x13 -> x9, starting transfers between devices: 32.1 us -> 25.3 us  [move(): return lax.ppermute(block, ('row', 'col'), route)]
    pallas_call x3 -> x2, Pallas kernels: 24.1 us -> 18.6 us  [products(): pl.pallas_call(functools.partial(product_kernel, counts), grid=(rows // b...]
    ppermute x13 -> x9, waiting for transfers between devices: 10.6 us -> 5.69 us  [move(): return lax.ppermute(block, ('row', 'col'), route)]
    ppermute x2, waiting for transfers between devices: 9.6 us -> 14.3 us  [local(): arrive = lax.ppermute(rest[1::2], 'col', pairs)]
    reduce_max x3 -> x2, other arithmetic: 9.78 us -> 5.35 us  [shrink(): unit = jnp.maximum(jnp.max(jnp.abs(total)), TINY) * (1.0 / HALF_TOP)]
    ppermute x1 -> x2, waiting for transfers between devices: 1.22 us -> 4.58 us  [pair_sum(): lax.ppermute(sent, 'col', other_core)]
    ppermute x2, starting transfers between devices: 3.08 us -> 0.16 us  [local(): arrive = lax.ppermute(rest[1::2], 'col', pairs)]
  transfers between devices with their start and end apart: 22 -> 19, of which waited for: 7 -> 8; matrix products, arithmetic and copies ran while one was open for 9% -> 7% of each run, Pallas kernels for 15% -> 6%
where the time goes in v8:
time: 178 us; the launch traced here: 175 us
  waiting for transfers between devices  81.6 us (46%)
  starting transfers between devices  43.4 us (24%)
  Pallas kernels  32.7 us (18%)
  other arithmetic  12.6 us (7%)
  local copies, waits for them, and re-layouts  3.13 us (2%)
  between operations  1.84 us (1%)
    ppermute x3, waiting for transfers between devices, hop(): down.append(lax.ppermute(down[-1], 'row', back))  44.4 us
    ppermute x9, starting transfers between devices, move(): return lax.ppermute(block, ('row', 'col'), route)  25.3 us
    pallas_call x2, Pallas kernels, products(): pl.pallas_call(functools.partial(product_kernel, counts), grid=(rows // b...  18.6 us
    ppermute x2, waiting for transfers between devices, local(): arrive = lax.ppermute(rest[1::2], 'col', pairs)  14.3 us
    ppermute x3, waiting for transfers between devices, hop(): up.append(lax.ppermute(up[-1], 'row', ends))  12.7 us
    ppermute x3, starting transfers between devices, hop(): up.append(lax.ppermute(up[-1], 'row', ends))  12.1 us
    pallas_call x1, Pallas kernels, pick_columns(): pl.pallas_call(pick_kernel, grid=(rows // block,), in_specs=[pl.BlockSpec...  6.28 us
    ppermute x9, waiting for transfers between devices, move(): return lax.ppermute(block, ('row', 'col'), route)  5.69 us
  transfers between devices with their start and end apart: 19, of which 8 were waited for; matrix products, arithmetic and copies ran while one was open for 7% of the time, Pallas kernels for 6%

profile of v8, /device:TPU:1, one launch (start us, length us, event | category | flops | bytes accessed | tf_op | source)
XLA Modules:
  0.0 175.3 jit_solution(7993046645278029568)
XLA Ops:
  0.0 1.3 cut_window.1
  1.3 1.3 collective-permute-start.2
  2.6 4.6 %collective-permute-start.4 = (bf16[1536,128]{1,0:T(8,128)(2,1)S(1)}, bf16[1536,128]{1,0:T(8,128)(2,1)S(1)}, u32[]{:S(2)}, u32[]{:S(2)}) collective-permute-start(bf16[1536,128]{1,0:T(8,128)(2,1)S(1)} %get-tuple-element.28), channel_id=1, source_target_pairs={{0,0},{1,4},{4,1},{5,5},{10,10},{11,14},{14,11},{15,15},{16,16},{1... | collective-permute-start | bytes 1179656 | tf_op jit(solution)/shard_map/ppermute | solution.py:367
  7.2 1.9 %collective-permute-start.1 = (bf16[1536,128]{1,0:T(8,128)(2,1)S(1)}, bf16[1536,128]{1,0:T(8,128)(2,1)S(1)}, u32[]{:S(2)}, u32[]{:S(2)}) collective-permute-start(bf16[1536,128]{1,0:T(8,128)(2,1)S(1)} %get-tuple-element.27), channel_id=1, source_target_pairs={{0,0},{1,4},{2,8},{3,12},{4,1},{5,5},{6,9},{7,13},{8,2},{9,6},{10,... | collective-permute-start | bytes 1179656 | tf_op jit(solution)/shard_map/ppermute | solution.py:367
  9.2 0.1 fusion
  9.3 0.1 dynamic_slice.14
  9.5 6.3 %pick_columns.1 = (bf16[96,1536]{1,0:T(8,128)(2,1)S(1)}, bf16[96,1536]{1,0:T(8,128)(2,1)S(1)}) custom-call(bf16[2,1536,1536]{2,1,0:T(8,128)(2,1)} %tile_ref.1, s32[1,128]{1,0:T(1,128)S(1)} %pad_bitcast_fusion.miss_ref, bf16[8,1536]{1,0:T(8,128)(2,1)S(1)} %broadcast_in_dim.16.recv_ref, f32[8,1536]{1,0:T(8,128)S(1)} %broadcast_in_dim.36.live_ref), custom_call_target="tpu_custom_call" | custom-call | flops 37748736 | bytes 147456 | tf_op jit(solution)/shard_map/pick_columns/pallas_call | solution.py:105
  15.7 4.9 %collective-permute-start.3 = (bf16[1536,128]{1,0:T(8,128)(2,1)S(1)}, bf16[1536,128]{1,0:T(8,128)(2,1)S(1)}, u32[]{:S(2)}, u32[]{:S(2)}) collective-permute-start(bf16[1536,128]{1,0:T(8,128)(2,1)S(1)} %collective-permute-done.2), channel_id=1, source_target_pairs={{0,8},{1,12},{4,9},{5,13},{10,2},{11,6},{14,3},{15,7},{16,24},{17,... | collective-permute-start | bytes 1179656 | tf_op jit(solution)/shard_map/ppermute | solution.py:367
  20.6 0.9 pad_maximum_fusion
  21.5 1.9 %collective-permute-start = (bf16[192,1536]{1,0:T(8,128)(2,1)}, bf16[192,1536]{1,0:T(8,128)(2,1)}, u32[]{:S(2)}, u32[]{:S(2)}) collective-permute-start(bf16[192,1536]{1,0:T(8,128)(2,1)} %pad_maximum_fusion), channel_id=1, source_target_pairs={{0,0},{1,4},{2,8},{3,12},{4,1},{5,5},{6,9},{7,13},{8,2},{9,6},{10,... | collective-permute-start | bytes 1769480 | tf_op jit(solution)/shard_map/ppermute | solution.py:367
  23.4 0.1 dynamic_slice.16
  23.5 5.6 %collective-permute-done.3.refs_1_ = bf16[1536,128]{1,0:T(8,128)(2,1)S(1)} collective-permute-done((bf16[1536,128]{1,0:T(8,128)(2,1)S(1)}, bf16[1536,128]{1,0:T(8,128)(2,1)S(1)}, u32[]{:S(2)}, u32[]{:S(2)}) %collective-permute-start.3) | collective-permute-done | bytes 393248 | tf_op jit(solution)/shard_map/ppermute | solution.py:367
  29.1 0.4 fill_window.1.refs_4_.refs_7_.refs_0_
  29.6 9.8 %collective-permute-start.5 = (bf16[1536,256]{1,0:T(8,128)(2,1)S(1)}, bf16[1536,256]{1,0:T(8,128)(2,1)S(1)}, u32[]{:S(2)}, u32[]{:S(2)}) collective-permute-start(bf16[1536,256]{1,0:T(8,128)(2,1)S(1)} %fill_window.1.refs_4_.refs_7_.refs_0_), channel_id=1, source_target_pairs={{0,4},{4,8},{8,12},{1,5},{5,9},{9,13},{2,6},{6,10},{10,14},{3,7},{... | collective-permute-start | bytes 2359304 | tf_op jit(solution)/shard_map/ppermute | solution.py:412
  39.4 1.3 collective-permute-start.6
  40.7 0.1 pad_add_fusion.pick_ref
  40.8 1.8 %fusion.2 = (bf16[96,1536]{1,0:T(8,128)(2,1)S(1)}, bf16[96,1536]{1,0:T(8,128)(2,1)}) fusion(bf16[192,1536]{1,0:T(8,128)(2,1)} %collective-permute-done), kind=kLoop, calls=%fused_computation.18 | loop fusion | bytes 1179648 | tf_op jit(solution)/shard_map/slice | solution.py:400
  42.6 12.7 %collective-permute-done.5.refs_6_.refs_9_.refs_2_.refs_7_.refs_8_.refs_14_ = bf16[1536,256]{1,0:T(8,128)(2,1)S(1)} collective-permute-done((bf16[1536,256]{1,0:T(8,128)(2,1)S(1)}, bf16[1536,256]{1,0:T(8,128)(2,1)S(1)}, u32[]{:S(2)}, u32[]{:S(2)}) %collective-permute-start.5) | collective-permute-done | bytes 786464 | tf_op jit(solution)/shard_map/ppermute | solution.py:412
  55.3 12.7 %collective-permute-done.6.refs_5_.refs_8_.refs_1_.refs_6_.refs_7_.refs_13_ = bf16[1536,256]{1,0:T(8,128)(2,1)S(1)} collective-permute-done((bf16[1536,256]{1,0:T(8,128)(2,1)S(1)}, bf16[1536,256]{1,0:T(8,128)(2,1)S(1)}, u32[]{:S(2)}, u32[]{:S(2)}) %collective-permute-start.6) | collective-permute-done | bytes 786464 | tf_op jit(solution)/shard_map/ppermute | solution.py:413
  68.0 7.6 %products.2 = (f32[1536,256]{1,0:T(8,128)S(1)}, f32[1536,256]{1,0:T(8,128)S(1)}) custom-call(s32[2]{0:T(128)S(1)} %pad_add_fusion.pick_ref, bf16[8,1536]{1,0:T(8,128)(2,1)S(1)} %broadcast_in_dim.16.recv_ref, bf16[2,1536,1536]{2,1,0:T(8,128)(2,1)} %tile_ref.1, bf16[2,1536,1536]{2,1,0:T(8,128)(2,1)} %tile_ref.1, bf16[2,1536,1536]{2,1,0:T(8,128)(2,1)} %tile_ref.1, ...), custom_call_target="tpu_custom_call" | custom-call | flops 150994944 | bytes 24576 | tf_op jit(solution)/shard_map/products/pallas_call | solution.py:230
  75.6 0.3 collective-permute-start.7
  75.9 0.7 collective-permute-start.8
  76.6 1.3 collective-permute-start.9
  77.9 1.2 collective-permute-done.7
  79.0 2.0 %abs_reduce_fusion.1 = (f32[]{:T(128)}, f32[1536,256]{1,0:T(8,128)}) fusion(f32[1536,256]{1,0:T(8,128)S(1)} %get-tuple-element.33, f32[1536,256]{1,0:T(8,128)S(1)} %collective-permute-done.7), kind=kLoop, calls=%fused_computation.4 | loop fusion | flops 1179647 | bytes 4718596 | tf_op jit(solution)/shard_map/reduce_max | solution.py:421
  81.7 2.5 %multiply_convert_fusion.1 = f16[1536,256]{1,0:T(8,128)(2,1)} fusion(f32[1536,256]{1,0:T(8,128)} %get-tuple-element.48, f32[]{:T(128)S(6)} %div.18), kind=kLoop, calls=%fused_computation.3 | loop fusion | flops 786432 | bytes 2359300 | tf_op jit(solution)/shard_map/convert_element_type | solution.py:422
  84.2 16.8 %collective-permute-done.9.refs_3_.refs_4_.refs_10_ = bf16[1536,256]{1,0:T(8,128)(2,1)} collective-permute-done((bf16[1536,256]{1,0:T(8,128)(2,1)S(1)}, bf16[1536,256]{1,0:T(8,128)(2,1)}, u32[]{:S(2)}, u32[]{:S(2)}) %collective-permute-start.9) | collective-permute-done | bytes 786464 | tf_op jit(solution)/shard_map/ppermute | solution.py:413
  100.9 1.3 collective-permute-start.12
  102.2 1.6 collective-permute-start.13
  103.8 1.3 collective-permute-start.10
  105.1 0.1 stack.53.pick_ref
  105.2 0.1 pad_add_fusion.1.pick_ref
  105.3 1.3 collective-permute-start.11
  106.6 15.0 %collective-permute-done.12.refs_5_.refs_6_.refs_12_ = bf16[1536,256]{1,0:T(8,128)(2,1)} collective-permute-done((bf16[1536,256]{1,0:T(8,128)(2,1)}, bf16[1536,256]{1,0:T(8,128)(2,1)}, u32[]{:S(2)}, u32[]{:S(2)}) %collective-permute-start.12) | collective-permute-done | bytes 786464 | tf_op jit(solution)/shard_map/ppermute | solution.py:413
  121.5 1.0 copy-done
  122.5 3.3 %extra_products.1 = f32[4,96,256]{2,1,0:T(8,128)S(1)} custom-call(s32[8]{0:T(128)S(1)} %stack.53.pick_ref, bf16[96,1536]{1,0:T(8,128)(2,1)S(1)} %copy-done, bf16[96,1536]{1,0:T(8,128)(2,1)S(1)} %get-tuple-element.30.imag_ref, bf16[1536,256]{1,0:T(8,128)(2,1)S(1)} %fill_window.1.refs_4_.refs_7_.refs_0_, ...), custom_call_target="tpu_custom_call" | custom-call | flops 18874368 | bytes 24576 | tf_op jit(solution)/shard_map/extra_products/pallas_call | solution.py:264
  125.9 11.0 %products.3 = (f32[1536,256]{1,0:T(8,128)}, f32[1536,256]{1,0:T(8,128)}) custom-call(s32[2]{0:T(128)S(1)} %pad_add_fusion.1.pick_ref, bf16[8,1536]{1,0:T(8,128)(2,1)S(1)} %broadcast_in_dim.16.recv_ref, bf16[2,1536,1536]{2,1,0:T(8,128)(2,1)} %tile_ref.1, bf16[2,1536,1536]{2,1,0:T(8,128)(2,1)} %tile_ref.1, bf16[2,1536,1536]{2,1,0:T(8,128)(2,1)} %tile_ref.1, ...), custom_call_target="tpu_custom_call" | custom-call | flops 150994944 | bytes 24576 | tf_op jit(solution)/shard_map/products/pallas_call | solution.py:230
  136.9 1.6 collective-permute-start.14
  138.5 0.1 collective-permute-start.17
  138.6 3.4 %collective-permute-done.14 = f32[1536,256]{1,0:T(8,128)S(1)} collective-permute-done((f32[1536,256]{1,0:T(8,128)}, f32[1536,256]{1,0:T(8,128)S(1)}, u32[]{:S(2)}, u32[]{:S(2)}) %collective-permute-start.14) | collective-permute-done | bytes 1572896 | tf_op jit(solution)/shard_map/ppermute | solution.py:451
  142.0 3.4 %abs_reduce_fusion = (f32[]{:T(128)}, f32[1536,256]{1,0:T(8,128)}) fusion(f32[1536,256]{1,0:T(8,128)} %get-tuple-element.42, f32[1536,256]{1,0:T(8,128)S(1)} %collective-permute-done.14), kind=kLoop, calls=%fused_computation.2 | loop fusion | flops 1179647 | bytes 4718596 | tf_op jit(solution)/shard_map/reduce_max | solution.py:421
  146.2 1.7 multiply_convert_fusion
  147.9 4.9 %collective-permute-start.15 = (f16[1536,256]{1,0:T(8,128)(2,1)S(1)}, f16[1536,256]{1,0:T(8,128)(2,1)}, u32[]{:S(2)}, u32[]{:S(2)}) collective-permute-start(f16[1536,256]{1,0:T(8,128)(2,1)S(1)} %multiply_convert_fusion), channel_id=1, source_target_pairs={{0,2},{1,3},{4,6},{5,7},{10,8},{11,9},{14,12},{15,13},{16,18},{17,... | collective-permute-start | bytes 2359304 | tf_op jit(solution)/shard_map/ppermute | solution.py:367
  152.8 0.1 collective-permute-start.18
  153.0 3.3 %collective-permute-start.16 = (f32[1,128]{1,0:T(1,128)S(1)}, f32[1,128]{1,0:T(1,128)S(1)}, u32[]{:S(2)}, u32[]{:S(2)}) collective-permute-start(f32[1,128]{1,0:T(1,128)S(1)} %broadcast_in_dim.40), channel_id=1, source_target_pairs={{0,2},{1,3},{4,6},{5,7},{10,8},{11,9},{14,12},{15,13},{16,18},{17,... | collective-permute-start | bytes 1544 | tf_op jit(solution)/shard_map/ppermute | solution.py:367
  156.3 14.3 %collective-permute-done.18 = f32[1,96,256]{2,1,0:T(8,128)S(1)} collective-permute-done((f32[1,96,256]{2,1,0:T(8,128)S(1)}, f32[1,96,256]{2,1,0:T(8,128)S(1)}, u32[]{:S(2)}, u32[]{:S(2)}) %collective-permute-start.18) | collective-permute-done | bytes 98336 | tf_op jit(solution)/shard_map/ppermute | solution.py:475
  170.6 1.9 %add_add_fusion.refs_0_ = f32[1536,256]{1,0:T(8,128)S(1)} fusion(f16[1536,256]{1,0:T(8,128)(2,1)} %collective-permute-done.15, f32[1536,256]{1,0:T(8,128)} %get-tuple-element.46, f16[1536,256]{1,0:T(8,128)(2,1)} %collective-permute-done.10, f32[1536,256]{1,0:T(8,128)S(1)} %copy-done.4, f32[]{:T(128)S(1)} %bitcast.24, f32[]{:T(128)S(1)} %bitcast.23, ...), kind=kLoop, calls=%fused_computation | loop fusion | flops 3538944 | bytes 6291466 | tf_op jit(solution)/shard_map/add | solution.py:471
  172.5 2.8 %finish.1 = f32[2,1536,128]{2,1,0:T(8,128)} custom-call(f32[2]{0:T(128)S(1)} %broadcast_multiply_fusion.wave_ref, s32[96]{0:T(128)S(1)} %get-tuple-element.52.miss_ref, bf16[8,1536]{1,0:T(8,128)(2,1)S(1)} %broadcast_in_dim.16.recv_ref, bf16[2,1536,1536]{2,1,0:T(8,128)(2,1)} %tile_ref.1, bf16[96,1536]{1,0:T(8,128)(2,1)S(1)} %copy-done.1, ...), custom_call_target="tpu_custom_call" | custom-call | flops 61440 | bytes 122880 | tf_op jit(solution)/shard_map/finish/pallas_call | solution.py:304
  (40 shorter events, 0.2 us)
Async XLA Ops:
  0.0 9.1 %copy-start.6 = (s32[4,96]{1,0:T(4,128)S(1)}, s32[4,96]{1,0:T(4,128)}, u32[]{:S(2)}) copy-start(s32[4,96]{1,0:T(4,128)} %param.6) | copy-start | bytes 4612
  0.0 9.3 %copy-start.5 = (s32[6144]{0:T(1024)S(1)}, s32[6144]{0:T(1024)}, u32[]{:S(2)}) copy-start(s32[6144]{0:T(1024)} %param.5) | copy-start | bytes 73732
  1.3 14.4 %collective-permute-start.2 = (bf16[1536,128]{1,0:T(8,128)(2,1)S(1)}, bf16[1536,128]{1,0:T(8,128)(2,1)S(1)}, u32[]{:S(2)}, u32[]{:S(2)}) collective-permute-start(bf16[1536,128]{1,0:T(8,128)(2,1)S(1)} %get-tuple-element.28), channel_id=1, source_target_pairs={{2,0},{3,1},{6,4},{7,5},{8,10},{9,11},{12,14},{13,15},{18,16},{19,... | collective-permute-start | bytes 1179656 | tf_op jit(solution)/shard_map/ppermute | solution.py:367
  2.6 20.9 %collective-permute-start.4 = (bf16[1536,128]{1,0:T(8,128)(2,1)S(1)}, bf16[1536,128]{1,0:T(8,128)(2,1)S(1)}, u32[]{:S(2)}, u32[]{:S(2)}) collective-permute-start(bf16[1536,128]{1,0:T(8,128)(2,1)S(1)} %get-tuple-element.28), channel_id=1, source_target_pairs={{0,0},{1,4},{4,1},{5,5},{10,10},{11,14},{14,11},{15,15},{16,16},{1... | collective-permute-start | bytes 1179656 | tf_op jit(solution)/shard_map/ppermute | solution.py:367
  7.2 16.3 %collective-permute-start.1 = (bf16[1536,128]{1,0:T(8,128)(2,1)S(1)}, bf16[1536,128]{1,0:T(8,128)(2,1)S(1)}, u32[]{:S(2)}, u32[]{:S(2)}) collective-permute-start(bf16[1536,128]{1,0:T(8,128)(2,1)S(1)} %get-tuple-element.27), channel_id=1, source_target_pairs={{0,0},{1,4},{2,8},{3,12},{4,1},{5,5},{6,9},{7,13},{8,2},{9,6},{10,... | collective-permute-start | bytes 1179656 | tf_op jit(solution)/shard_map/ppermute | solution.py:367
  15.7 13.4 %collective-permute-start.3 = (bf16[1536,128]{1,0:T(8,128)(2,1)S(1)}, bf16[1536,128]{1,0:T(8,128)(2,1)S(1)}, u32[]{:S(2)}, u32[]{:S(2)}) collective-permute-start(bf16[1536,128]{1,0:T(8,128)(2,1)S(1)} %collective-permute-done.2), channel_id=1, source_target_pairs={{0,8},{1,12},{4,9},{5,13},{10,2},{11,6},{14,3},{15,7},{16,24},{17,... | collective-permute-start | bytes 1179656 | tf_op jit(solution)/shard_map/ppermute | solution.py:367
  21.5 19.3 %collective-permute-start = (bf16[192,1536]{1,0:T(8,128)(2,1)}, bf16[192,1536]{1,0:T(8,128)(2,1)}, u32[]{:S(2)}, u32[]{:S(2)}) collective-permute-start(bf16[192,1536]{1,0:T(8,128)(2,1)} %pad_maximum_fusion), channel_id=1, source_target_pairs={{0,0},{1,4},{2,8},{3,12},{4,1},{5,5},{6,9},{7,13},{8,2},{9,6},{10,... | collective-permute-start | bytes 1769480 | tf_op jit(solution)/shard_map/ppermute | solution.py:367
  29.6 25.7 %collective-permute-start.5 = (bf16[1536,256]{1,0:T(8,128)(2,1)S(1)}, bf16[1536,256]{1,0:T(8,128)(2,1)S(1)}, u32[]{:S(2)}, u32[]{:S(2)}) collective-permute-start(bf16[1536,256]{1,0:T(8,128)(2,1)S(1)} %fill_window.1.refs_4_.refs_7_.refs_0_), channel_id=1, source_target_pairs={{0,4},{4,8},{8,12},{1,5},{5,9},{9,13},{2,6},{6,10},{10,14},{3,7},{... | collective-permute-start | bytes 2359304 | tf_op jit(solution)/shard_map/ppermute | solution.py:412
  39.4 28.6 %collective-permute-start.6 = (bf16[1536,256]{1,0:T(8,128)(2,1)S(1)}, bf16[1536,256]{1,0:T(8,128)(2,1)S(1)}, u32[]{:S(2)}, u32[]{:S(2)}) collective-permute-start(bf16[1536,256]{1,0:T(8,128)(2,1)S(1)} %fill_window.1.refs_4_.refs_7_.refs_0_), channel_id=1, source_target_pairs={{4,0},{8,4},{12,8},{5,1},{9,5},{13,9},{6,2},{10,6},{14,10},{7,3},{... | collective-permute-start | bytes 2359304 | tf_op jit(solution)/shard_map/ppermute | solution.py:413
  75.6 3.5 %collective-permute-start.7 = (f32[1536,256]{1,0:T(8,128)S(1)}, f32[1536,256]{1,0:T(8,128)S(1)}, u32[]{:S(2)}, u32[]{:S(2)}) collective-permute-start(f32[1536,256]{1,0:T(8,128)S(1)} %get-tuple-element.34), channel_id=1, source_target_pairs={{0,1},{1,0},{2,3},{3,2},{4,5},{5,4},{6,7},{7,6},{8,9},{9,8},{10,11... | collective-permute-start | bytes 4718600 | tf_op jit(solution)/shard_map/ppermute | solution.py:451
  75.9 8.3 %collective-permute-start.8 = (bf16[1536,256]{1,0:T(8,128)(2,1)S(1)}, bf16[1536,256]{1,0:T(8,128)(2,1)S(1)}, u32[]{:S(2)}, u32[]{:S(2)}) collective-permute-start(bf16[1536,256]{1,0:T(8,128)(2,1)S(1)} %collective-permute-done.5.refs_6_.refs_9_.refs_2_.refs_7_.refs_8_.refs_14_), channel_id=1, source_target_pairs={{4,8},{8,12},{5,9},{9,13},{6,10},{10,14},{7,11},{11,15},{20,24},{2... | collective-permute-start | bytes 2359304 | tf_op jit(solution)/shard_map/ppermute | solution.py:412
  76.6 24.4 %collective-permute-start.9 = (bf16[1536,256]{1,0:T(8,128)(2,1)S(1)}, bf16[1536,256]{1,0:T(8,128)(2,1)}, u32[]{:S(2)}, u32[]{:S(2)}) collective-permute-start(bf16[1536,256]{1,0:T(8,128)(2,1)S(1)} %collective-permute-done.6.refs_5_.refs_8_.refs_1_.refs_6_.refs_7_.refs_13_), channel_id=1, source_target_pairs={{4,0},{8,4},{5,1},{9,5},{6,2},{10,6},{7,3},{11,7},{20,16},{24,20},... | collective-permute-start | bytes 2359304 | tf_op jit(solution)/shard_map/ppermute | solution.py:413
  100.9 20.6 %collective-permute-start.12 = (bf16[1536,256]{1,0:T(8,128)(2,1)}, bf16[1536,256]{1,0:T(8,128)(2,1)}, u32[]{:S(2)}, u32[]{:S(2)}) collective-permute-start(bf16[1536,256]{1,0:T(8,128)(2,1)} %collective-permute-done.9.refs_3_.refs_4_.refs_10_), channel_id=1, source_target_pairs={{4,0},{5,1},{6,2},{7,3},{20,16},{21,17},{22,18},{23,19}} | collective-permute-start | bytes 2359304 | tf_op jit(solution)/shard_map/ppermute | solution.py:413
  102.2 19.3 %collective-permute-start.13 = (bf16[1536,256]{1,0:T(8,128)(2,1)S(1)}, bf16[1536,256]{1,0:T(8,128)(2,1)}, u32[]{:S(2)}, u32[]{:S(2)}) collective-permute-start(bf16[1536,256]{1,0:T(8,128)(2,1)S(1)} %collective-permute-done.8.refs_4_.refs_5_.refs_11_), channel_id=1, source_target_pairs={{8,12},{9,13},{10,14},{11,15},{24,28},{25,29},{26,30},{27,31}} | collective-permute-start | bytes 2359304 | tf_op jit(solution)/shard_map/ppermute | solution.py:412
  103.8 22.1 %collective-permute-start.10 = (f16[1536,256]{1,0:T(8,128)(2,1)}, f16[1536,256]{1,0:T(8,128)(2,1)}, u32[]{:S(2)}, u32[]{:S(2)}) collective-permute-start(f16[1536,256]{1,0:T(8,128)(2,1)} %multiply_convert_fusion.1), channel_id=1, source_target_pairs={{2,0},{3,1},{6,4},{7,5},{8,10},{9,11},{12,14},{13,15},{18,16},{19,... | collective-permute-start | bytes 2359304 | tf_op jit(solution)/shard_map/ppermute | solution.py:367
  105.3 20.6 %collective-permute-start.11 = (f32[1,128]{1,0:T(1,128)S(1)}, f32[1,128]{1,0:T(1,128)S(1)}, u32[]{:S(2)}, u32[]{:S(2)}) collective-permute-start(f32[1,128]{1,0:T(1,128)S(1)} %broadcast_in_dim.39), channel_id=1, source_target_pairs={{2,0},{3,1},{6,4},{7,5},{8,10},{9,11},{12,14},{13,15},{18,16},{19,... | collective-permute-start | bytes 1544 | tf_op jit(solution)/shard_map/ppermute | solution.py:367
  121.5 1.0 copy-start
  125.8 12.7 %copy-start.2 = (f32[4,96,256]{2,1,0:T(8,128)}, f32[4,96,256]{2,1,0:T(8,128)S(1)}, u32[]{:S(2)}) copy-start(f32[4,96,256]{2,1,0:T(8,128)S(1)} %extra_products.1) | copy-start | bytes 1179652
  136.9 5.2 %collective-permute-start.14 = (f32[1536,256]{1,0:T(8,128)}, f32[1536,256]{1,0:T(8,128)S(1)}, u32[]{:S(2)}, u32[]{:S(2)}) collective-permute-start(f32[1536,256]{1,0:T(8,128)} %get-tuple-element.43), channel_id=1, source_target_pairs={{0,1},{1,0},{2,3},{3,2},{4,5},{5,4},{6,7},{7,6},{8,9},{9,8},{10,11... | collective-permute-start | bytes 4718600 | tf_op jit(solution)/shard_map/ppermute | solution.py:451
  138.5 14.2 %collective-permute-start.17 = (f32[2,96,256]{2,1,0:T(8,128)S(1)}, f32[2,96,256]{2,1,0:T(8,128)S(1)}, u32[]{:S(2)}, u32[]{:S(2)}) collective-permute-start(f32[2,96,256]{2,1,0:T(8,128)S(1)} %slice.31), channel_id=1, source_target_pairs={{0,1},{1,0},{2,3},{3,2},{4,5},{5,4},{6,7},{7,6},{8,9},{9,8},{10,11... | collective-permute-start | bytes 589832 | tf_op jit(solution)/shard_map/ppermute | solution.py:475
  145.4 7.4 %copy-start.3 = (f32[4,96,256]{2,1,0:T(8,128)S(1)}, f32[4,96,256]{2,1,0:T(8,128)}, u32[]{:S(2)}) copy-start(f32[4,96,256]{2,1,0:T(8,128)} %copy-done.2) | copy-start | bytes 1179652
  146.1 6.8 %copy-start.7 = (f32[2]{0:T(128)S(1)}, f32[2]{0:T(128)}, u32[]{:S(2)}) copy-start(f32[2]{0:T(128)} %param.7) | copy-start | bytes 28
  146.1 24.4 %copy-start.4 = (f32[1536,256]{1,0:T(8,128)S(1)}, f32[1536,256]{1,0:T(8,128)}, u32[]{:S(2)}) copy-start(f32[1536,256]{1,0:T(8,128)} %get-tuple-element.48) | copy-start | bytes 4718596
  147.9 22.7 %collective-permute-start.15 = (f16[1536,256]{1,0:T(8,128)(2,1)S(1)}, f16[1536,256]{1,0:T(8,128)(2,1)}, u32[]{:S(2)}, u32[]{:S(2)}) collective-permute-start(f16[1536,256]{1,0:T(8,128)(2,1)S(1)} %multiply_convert_fusion), channel_id=1, source_target_pairs={{0,2},{1,3},{4,6},{5,7},{10,8},{11,9},{14,12},{15,13},{16,18},{17,... | collective-permute-start | bytes 2359304 | tf_op jit(solution)/shard_map/ppermute | solution.py:367
  152.8 17.7 %collective-permute-start.18 = (f32[1,96,256]{2,1,0:T(8,128)S(1)}, f32[1,96,256]{2,1,0:T(8,128)S(1)}, u32[]{:S(2)}, u32[]{:S(2)}) collective-permute-start(f32[1,96,256]{2,1,0:T(8,128)S(1)} %slice.37), channel_id=1, source_target_pairs={{0,2},{1,3},{2,0},{3,1},{4,6},{5,7},{6,4},{7,5},{8,10},{9,11},{10,... | collective-permute-start | bytes 294920 | tf_op jit(solution)/shard_map/ppermute | solution.py:475
  153.0 17.6 %collective-permute-start.16 = (f32[1,128]{1,0:T(1,128)S(1)}, f32[1,128]{1,0:T(1,128)S(1)}, u32[]{:S(2)}, u32[]{:S(2)}) collective-permute-start(f32[1,128]{1,0:T(1,128)S(1)} %broadcast_in_dim.40), channel_id=1, source_target_pairs={{0,2},{1,3},{4,6},{5,7},{10,8},{11,9},{14,12},{15,13},{16,18},{17,... | collective-permute-start | bytes 1544 | tf_op jit(solution)/shard_map/ppermute | solution.py:367
  170.6 1.9 %copy-start.1 = (bf16[96,1536]{1,0:T(8,128)(2,1)S(1)}, bf16[96,1536]{1,0:T(8,128)(2,1)}, u32[]{:S(2)}) copy-start(bf16[96,1536]{1,0:T(8,128)(2,1)} %get-tuple-element.29.real_ref) | copy-start | bytes 884740

commit v9 on v8

--- a/solution.py
+++ b/solution.py
@@ -369,19 +369,17 @@
     def transpose(block):
         return move(block, whole)
 
-    def transpose_round(block):
+    def rounds(block):
         if hops is None:
-            return [move(block, whole)]
-        near, first, second = hops
-        return [move(move(block, first), second), move(block, near)]
+            return [move(block, whole)], None
+        return [move(block, hops[0])], move(block, hops[1])
+
+    def arrive_round(near, half_way):
+        return near if half_way is None else near + [move(half_way, hops[2])]
 
     direct, round_about = cut_window(traces)
-    arrived = [[transpose(direct)], transpose_round(round_about)]
-    if CHUNKS == 1:
-        arrived = [arrived]
-    else:
-        arrived = [arrived[:1], arrived[1:]]
-
+    first_arrival = transpose(direct)
+    near, half_way = rounds(round_about)
     miss_row = lax.dynamic_index_in_dim(missing, row_index, 0, keepdims=False)
     miss_col = lax.dynamic_index_in_dim(missing, col_index, 0, keepdims=False)
     as_lanes = lambda m: jnp.pad(m, (0, LANES - misses), constant_values=-1)[None]
@@ -396,8 +394,11 @@
     recv_col8 = jnp.broadcast_to(recv_col[None], (8, tile))
 
     picked = pick_columns(traces, miss_col_lanes, recv_col8, live8, misses)
-    both = transpose(jnp.concatenate(picked))
-    extra = [both[:misses], both[misses:]]
+    if half_way is not None:
+        picked, half_way = lax.optimization_barrier((picked, half_way))
+    arrived = [[first_arrival], arrive_round(near, half_way)]
+    arrived = [arrived] if CHUNKS == 1 else [arrived[:1], arrived[1:]]
+    extra = [transpose(picked[0]), functools.reduce(jnp.add, arrive_round(*rounds(picked[1])))]
     apart = row_index ^ col_index
     strides = [2**bit for bit in range(grid_size.bit_length() - 1)]
     terms, extra_terms = [], []

time: 178 us -> 181 us (1.017)
  starting transfers between devices: 43.4 us -> 57.2 us
  waiting for transfers between devices: 81.6 us -> 70.6 us
    ppermute x9 -> x12, waiting for transfers between devices: 5.69 us -> 24.5 us  [move(): return lax.ppermute(block, ('row', 'col'), route)]
    ppermute x3, waiting for transfers between devices: 44.4 us -> 27.1 us  [hop(): down.append(lax.ppermute(down[-1], 'row', back))]
    ppermute x9 -> x12, starting transfers between devices: 25.3 us -> 38.7 us  [move(): return lax.ppermute(block, ('row', 'col'), route)]
    ppermute x3, waiting for transfers between devices: 12.7 us -> 0.01 us  [hop(): up.append(lax.ppermute(up[-1], 'row', ends))]
    slice x1 -> x0, local copies, waits for them, and re-layouts: 1.83 us -> none  [local(): extra = [both[:misses], both[misses:]]]
  transfers between devices with their start and end apart: 19 -> 22, of which waited for: 8 -> 10; matrix products, arithmetic and copies ran while one was open for 7% -> 6% of each run, Pallas kernels for 6% -> 6%
where the time goes in v9:
time: 181 us; the launch traced here: 179 us
  waiting for transfers between devices  70.6 us (39%)
  starting transfers between devices  57.2 us (32%)
  Pallas kernels  34.2 us (19%)
  other arithmetic  13.1 us (7%)
  local copies, waits for them, and re-layouts  2.01 us (1%)
    ppermute x12, starting transfers between devices, move(): return lax.ppermute(block, ('row', 'col'), route)  38.7 us
    ppermute x3, waiting for transfers between devices, hop(): down.append(lax.ppermute(down[-1], 'row', back))  27.1 us
    ppermute x12, waiting for transfers between devices, move(): return lax.ppermute(block, ('row', 'col'), route)  24.5 us
    pallas_call x2, Pallas kernels, products(): pl.pallas_call(functools.partial(product_kernel, counts), grid=(rows // b...  18.7 us
    ppermute x2, waiting for transfers between devices, local(): arrive = lax.ppermute(rest[1::2], 'col', pairs)  14.3 us
    ppermute x3, starting transfers between devices, hop(): up.append(lax.ppermute(up[-1], 'row', ends))  12.1 us
    pallas_call x1, Pallas kernels, pick_columns(): pl.pallas_call(pick_kernel, grid=(rows // block,), in_specs=[pl.BlockSpec...  6.86 us
    reduce_max x2, other arithmetic, shrink(): unit = jnp.maximum(jnp.max(jnp.abs(total)), TINY) * (1.0 / HALF_TOP)  5.54 us
  transfers between devices with their start and end apart: 22, of which 10 were waited for; matrix products, arithmetic and copies ran while one was open for 6% of the time, Pallas kernels for 6%

profile of v9, /device:TPU:1, one launch (start us, length us, event | category | flops | bytes accessed | tf_op | source)
XLA Modules:
  0.0 179.0 jit_solution(16142289441231029659)
XLA Ops:
  0.0 1.3 cut_window.1
  1.3 1.3 collective-permute-start
  2.6 4.6 %collective-permute-start.6 = (bf16[1536,128]{1,0:T(8,128)(2,1)S(1)}, bf16[1536,128]{1,0:T(8,128)(2,1)S(1)}, u32[]{:S(2)}, u32[]{:S(2)}) collective-permute-start(bf16[1536,128]{1,0:T(8,128)(2,1)S(1)} %get-tuple-element.30), channel_id=1, source_target_pairs={{0,0},{1,4},{4,1},{5,5},{10,10},{11,14},{14,11},{15,15},{16,16},{1... | collective-permute-start | bytes 1179656 | tf_op jit(solution)/shard_map/ppermute | solution.py:367
  7.2 1.9 %collective-permute-start.5 = (bf16[1536,128]{1,0:T(8,128)(2,1)S(1)}, bf16[1536,128]{1,0:T(8,128)(2,1)S(1)}, u32[]{:S(2)}, u32[]{:S(2)}) collective-permute-start(bf16[1536,128]{1,0:T(8,128)(2,1)S(1)} %get-tuple-element.33), channel_id=1, source_target_pairs={{0,0},{1,4},{2,8},{3,12},{4,1},{5,5},{6,9},{7,13},{8,2},{9,6},{10,... | collective-permute-start | bytes 1179656 | tf_op jit(solution)/shard_map/ppermute | solution.py:367
  9.2 0.1 fusion
  9.3 0.1 dynamic_slice.14
  9.5 6.9 %pick_columns.1 = (bf16[96,1536]{1,0:T(8,128)(2,1)}, bf16[96,1536]{1,0:T(8,128)(2,1)S(1)}) custom-call(bf16[2,1536,1536]{2,1,0:T(8,128)(2,1)} %tile_ref.1, s32[1,128]{1,0:T(1,128)S(1)} %pad_bitcast_fusion.miss_ref, bf16[8,1536]{1,0:T(8,128)(2,1)S(1)} %broadcast_in_dim.16.recv_ref, f32[8,1536]{1,0:T(8,128)S(1)} %broadcast_in_dim.36.live_ref), custom_call_target="tpu_custom_call" | custom-call | flops 37748736 | bytes 147456 | tf_op jit(solution)/shard_map/pick_columns/pallas_call | solution.py:105
  16.3 4.8 %collective-permute-start.7 = (bf16[1536,128]{1,0:T(8,128)(2,1)S(1)}, bf16[1536,128]{1,0:T(8,128)(2,1)S(1)}, u32[]{:S(2)}, u32[]{:S(2)}) collective-permute-start(bf16[1536,128]{1,0:T(8,128)(2,1)S(1)} %collective-permute-done), channel_id=1, source_target_pairs={{0,8},{1,12},{4,9},{5,13},{10,2},{11,6},{14,3},{15,7},{16,24},{17,... | collective-permute-start | bytes 1179656 | tf_op jit(solution)/shard_map/ppermute | solution.py:367
  21.3 0.2 collective-permute-done.5.refs_0_
  21.4 8.3 %collective-permute-done.7.refs_2_ = bf16[1536,128]{1,0:T(8,128)(2,1)S(1)} collective-permute-done((bf16[1536,128]{1,0:T(8,128)(2,1)S(1)}, bf16[1536,128]{1,0:T(8,128)(2,1)S(1)}, u32[]{:S(2)}, u32[]{:S(2)}) %collective-permute-start.7) | collective-permute-done | bytes 393248 | tf_op jit(solution)/shard_map/ppermute | solution.py:367
  29.7 1.2 fill_window.1.refs_4_.refs_7_.refs_0_
  30.9 9.8 %collective-permute-start.8 = (bf16[1536,256]{1,0:T(8,128)(2,1)S(1)}, bf16[1536,256]{1,0:T(8,128)(2,1)S(1)}, u32[]{:S(2)}, u32[]{:S(2)}) collective-permute-start(bf16[1536,256]{1,0:T(8,128)(2,1)S(1)} %fill_window.1.refs_4_.refs_7_.refs_0_), channel_id=1, source_target_pairs={{0,4},{4,8},{8,12},{1,5},{5,9},{9,13},{2,6},{6,10},{10,14},{3,7},{... | collective-permute-start | bytes 2359304 | tf_op jit(solution)/shard_map/ppermute | solution.py:413
  40.7 1.3 collective-permute-start.9
  42.0 1.3 collective-permute-start.3
  43.3 5.3 %collective-permute-start.2 = (bf16[96,1536]{1,0:T(8,128)(2,1)S(1)}, bf16[96,1536]{1,0:T(8,128)(2,1)S(1)}, u32[]{:S(2)}, u32[]{:S(2)}) collective-permute-start(bf16[96,1536]{1,0:T(8,128)(2,1)S(1)} %get-tuple-element.32.imag_ref), channel_id=1, source_target_pairs={{0,0},{1,4},{4,1},{5,5},{10,10},{11,14},{14,11},{15,15},{16,16},{1... | collective-permute-start | bytes 884744 | tf_op jit(solution)/shard_map/ppermute | solution.py:367
  48.5 2.8 %collective-permute-done.3 = bf16[96,1536]{1,0:T(8,128)(2,1)} collective-permute-done((bf16[96,1536]{1,0:T(8,128)(2,1)S(1)}, bf16[96,1536]{1,0:T(8,128)(2,1)}, u32[]{:S(2)}, u32[]{:S(2)}) %collective-permute-start.3) | collective-permute-done | bytes 294944 | tf_op jit(solution)/shard_map/ppermute | solution.py:367
  51.3 6.2 %collective-permute-start.4 = (bf16[96,1536]{1,0:T(8,128)(2,1)}, bf16[96,1536]{1,0:T(8,128)(2,1)}, u32[]{:S(2)}, u32[]{:S(2)}) collective-permute-start(bf16[96,1536]{1,0:T(8,128)(2,1)} %collective-permute-done.3), channel_id=1, source_target_pairs={{0,8},{1,12},{4,9},{5,13},{10,2},{11,6},{14,3},{15,7},{16,24},{17,... | collective-permute-start | bytes 884744 | tf_op jit(solution)/shard_map/ppermute | solution.py:367
  57.6 2.5 %collective-permute-start.1 = (bf16[96,1536]{1,0:T(8,128)(2,1)}, bf16[96,1536]{1,0:T(8,128)(2,1)S(1)}, u32[]{:S(2)}, u32[]{:S(2)}) collective-permute-start(bf16[96,1536]{1,0:T(8,128)(2,1)} %get-tuple-element.31.real_ref), channel_id=1, source_target_pairs={{0,0},{1,4},{2,8},{3,12},{4,1},{5,5},{6,9},{7,13},{8,2},{9,6},{10,... | collective-permute-start | bytes 884744 | tf_op jit(solution)/shard_map/ppermute | solution.py:367
  60.2 9.7 %collective-permute-done.2 = bf16[96,1536]{1,0:T(8,128)(2,1)S(1)} collective-permute-done((bf16[96,1536]{1,0:T(8,128)(2,1)S(1)}, bf16[96,1536]{1,0:T(8,128)(2,1)S(1)}, u32[]{:S(2)}, u32[]{:S(2)}) %collective-permute-start.2) | collective-permute-done | bytes 294944 | tf_op jit(solution)/shard_map/ppermute | solution.py:367
  69.9 0.7 copy-done.6
  70.6 1.1 add.49.imag_ref
  71.7 3.6 %collective-permute-done.1.real_ref = bf16[96,1536]{1,0:T(8,128)(2,1)S(1)} collective-permute-done((bf16[96,1536]{1,0:T(8,128)(2,1)}, bf16[96,1536]{1,0:T(8,128)(2,1)S(1)}, u32[]{:S(2)}, u32[]{:S(2)}) %collective-permute-start.1) | collective-permute-done | bytes 294944 | tf_op jit(solution)/shard_map/ppermute | solution.py:367
  75.3 7.7 %products.2 = (f32[1536,256]{1,0:T(8,128)S(1)}, f32[1536,256]{1,0:T(8,128)S(1)}) custom-call(s32[2]{0:T(128)S(1)} %pad_add_fusion.pick_ref, bf16[8,1536]{1,0:T(8,128)(2,1)S(1)} %broadcast_in_dim.16.recv_ref, bf16[2,1536,1536]{2,1,0:T(8,128)(2,1)} %tile_ref.1, bf16[2,1536,1536]{2,1,0:T(8,128)(2,1)} %tile_ref.1, bf16[2,1536,1536]{2,1,0:T(8,128)(2,1)} %tile_ref.1, ...), custom_call_target="tpu_custom_call" | custom-call | flops 150994944 | bytes 24576 | tf_op jit(solution)/shard_map/products/pallas_call | solution.py:230
  83.1 0.7 collective-permute-start.11
  83.8 1.3 collective-permute-start.12
  85.1 1.4 collective-permute-done.10
  86.5 2.0 %abs_reduce_fusion.1 = (f32[]{:T(128)}, f32[1536,256]{1,0:T(8,128)}) fusion(f32[1536,256]{1,0:T(8,128)S(1)} %get-tuple-element.39, f32[1536,256]{1,0:T(8,128)S(1)} %collective-permute-done.10), kind=kLoop, calls=%fused_computation.4 | loop fusion | flops 1179647 | bytes 4718596 | tf_op jit(solution)/shard_map/reduce_max | solution.py:422
  89.2 2.5 %multiply_convert_fusion.1 = f16[1536,256]{1,0:T(8,128)(2,1)} fusion(f32[1536,256]{1,0:T(8,128)} %get-tuple-element.54, f32[]{:T(128)S(6)} %div.18), kind=kLoop, calls=%fused_computation.3 | loop fusion | flops 786432 | bytes 2359300 | tf_op jit(solution)/shard_map/convert_element_type | solution.py:423
  91.7 12.8 %collective-permute-done.12.refs_3_.refs_4_.refs_10_ = bf16[1536,256]{1,0:T(8,128)(2,1)} collective-permute-done((bf16[1536,256]{1,0:T(8,128)(2,1)S(1)}, bf16[1536,256]{1,0:T(8,128)(2,1)}, u32[]{:S(2)}, u32[]{:S(2)}) %collective-permute-start.12) | collective-permute-done | bytes 786464 | tf_op jit(solution)/shard_map/ppermute | solution.py:414
  104.5 1.3 collective-permute-start.15
  105.7 1.6 collective-permute-start.16
  107.3 1.3 collective-permute-start.13
  108.6 0.1 stack.53.pick_ref
  108.8 1.3 collective-permute-start.14
  110.1 14.3 %collective-permute-done.15.refs_5_.refs_6_.refs_12_ = bf16[1536,256]{1,0:T(8,128)(2,1)} collective-permute-done((bf16[1536,256]{1,0:T(8,128)(2,1)}, bf16[1536,256]{1,0:T(8,128)(2,1)}, u32[]{:S(2)}, u32[]{:S(2)}) %collective-permute-start.15) | collective-permute-done | bytes 786464 | tf_op jit(solution)/shard_map/ppermute | solution.py:414
  124.4 1.0 copy-done.3
  125.3 3.3 %extra_products.1 = f32[4,96,256]{2,1,0:T(8,128)S(1)} custom-call(s32[8]{0:T(128)S(1)} %stack.53.pick_ref, bf16[96,1536]{1,0:T(8,128)(2,1)S(1)} %copy-done.3, bf16[96,1536]{1,0:T(8,128)(2,1)S(1)} %add.49.imag_ref, bf16[1536,256]{1,0:T(8,128)(2,1)S(1)} %fill_window.1.refs_4_.refs_7_.refs_0_, ...), custom_call_target="tpu_custom_call" | custom-call | flops 18874368 | bytes 24576 | tf_op jit(solution)/shard_map/extra_products/pallas_call | solution.py:264
  128.7 11.0 %products.3 = (f32[1536,256]{1,0:T(8,128)}, f32[1536,256]{1,0:T(8,128)}) custom-call(s32[2]{0:T(128)S(1)} %pad_add_fusion.1.pick_ref, bf16[8,1536]{1,0:T(8,128)(2,1)S(1)} %broadcast_in_dim.16.recv_ref, bf16[2,1536,1536]{2,1,0:T(8,128)(2,1)} %tile_ref.1, bf16[2,1536,1536]{2,1,0:T(8,128)(2,1)} %tile_ref.1, bf16[2,1536,1536]{2,1,0:T(8,128)(2,1)} %tile_ref.1, ...), custom_call_target="tpu_custom_call" | custom-call | flops 150994944 | bytes 24576 | tf_op jit(solution)/shard_map/products/pallas_call | solution.py:230
  139.7 2.3 %collective-permute-start.17 = (f32[1536,256]{1,0:T(8,128)}, f32[1536,256]{1,0:T(8,128)S(1)}, u32[]{:S(2)}, u32[]{:S(2)}) collective-permute-start(f32[1536,256]{1,0:T(8,128)} %get-tuple-element.49), channel_id=1, source_target_pairs={{0,1},{1,0},{2,3},{3,2},{4,5},{5,4},{6,7},{7,6},{8,9},{9,8},{10,11... | collective-permute-start | bytes 4718600 | tf_op jit(solution)/shard_map/ppermute | solution.py:452
  142.0 0.1 collective-permute-start.20
  142.1 3.4 %collective-permute-done.17 = f32[1536,256]{1,0:T(8,128)S(1)} collective-permute-done((f32[1536,256]{1,0:T(8,128)}, f32[1536,256]{1,0:T(8,128)S(1)}, u32[]{:S(2)}, u32[]{:S(2)}) %collective-permute-start.17) | collective-permute-done | bytes 1572896 | tf_op jit(solution)/shard_map/ppermute | solution.py:452
  145.6 3.5 %abs_reduce_fusion = (f32[]{:T(128)}, f32[1536,256]{1,0:T(8,128)}) fusion(f32[1536,256]{1,0:T(8,128)} %get-tuple-element.48, f32[1536,256]{1,0:T(8,128)S(1)} %collective-permute-done.17), kind=kLoop, calls=%fused_computation.2 | loop fusion | flops 1179647 | bytes 4718596 | tf_op jit(solution)/shard_map/reduce_max | solution.py:422
  149.8 1.7 multiply_convert_fusion
  151.5 4.9 %collective-permute-start.18 = (f16[1536,256]{1,0:T(8,128)(2,1)S(1)}, f16[1536,256]{1,0:T(8,128)(2,1)}, u32[]{:S(2)}, u32[]{:S(2)}) collective-permute-start(f16[1536,256]{1,0:T(8,128)(2,1)S(1)} %multiply_convert_fusion), channel_id=1, source_target_pairs={{0,2},{1,3},{4,6},{5,7},{10,8},{11,9},{14,12},{15,13},{16,18},{17,... | collective-permute-start | bytes 2359304 | tf_op jit(solution)/shard_map/ppermute | solution.py:367
  156.5 3.3 %collective-permute-start.19 = (f32[1,128]{1,0:T(1,128)S(1)}, f32[1,128]{1,0:T(1,128)S(1)}, u32[]{:S(2)}, u32[]{:S(2)}) collective-permute-start(f32[1,128]{1,0:T(1,128)S(1)} %broadcast_in_dim.40), channel_id=1, source_target_pairs={{0,2},{1,3},{4,6},{5,7},{10,8},{11,9},{14,12},{15,13},{16,18},{17,... | collective-permute-start | bytes 1544 | tf_op jit(solution)/shard_map/ppermute | solution.py:367
  159.8 14.3 %collective-permute-done.21 = f32[1,96,256]{2,1,0:T(8,128)S(1)} collective-permute-done((f32[1,96,256]{2,1,0:T(8,128)S(1)}, f32[1,96,256]{2,1,0:T(8,128)S(1)}, u32[]{:S(2)}, u32[]{:S(2)}) %collective-permute-start.21) | collective-permute-done | bytes 98336 | tf_op jit(solution)/shard_map/ppermute | solution.py:476
  174.2 2.0 %add_add_fusion.refs_0_ = f32[1536,256]{1,0:T(8,128)S(1)} fusion(f16[1536,256]{1,0:T(8,128)(2,1)} %collective-permute-done.18, f32[1536,256]{1,0:T(8,128)} %get-tuple-element.52, f16[1536,256]{1,0:T(8,128)(2,1)} %collective-permute-done.13, f32[1536,256]{1,0:T(8,128)S(1)} %copy-done.5, f32[]{:T(128)S(1)} %bitcast.24, f32[]{:T(128)S(1)} %bitcast.23, ...), kind=kLoop, calls=%fused_computation | loop fusion | flops 3538944 | bytes 6291466 | tf_op jit(solution)/shard_map/add | solution.py:472
  176.1 2.8 %finish.1 = f32[2,1536,128]{2,1,0:T(8,128)} custom-call(f32[2]{0:T(128)S(1)} %broadcast_multiply_fusion.wave_ref, s32[96]{0:T(128)S(1)} %get-tuple-element.56.miss_ref, bf16[8,1536]{1,0:T(8,128)(2,1)S(1)} %broadcast_in_dim.16.recv_ref, bf16[2,1536,1536]{2,1,0:T(8,128)(2,1)} %tile_ref.1, bf16[96,1536]{1,0:T(8,128)(2,1)S(1)} %copy-done.4, ...), custom_call_target="tpu_custom_call" | custom-call | flops 61440 | bytes 122880 | tf_op jit(solution)/shard_map/finish/pallas_call | solution.py:304
  (49 shorter events, 0.6 us)
Async XLA Ops:
  0.0 9.1 %copy-start.8 = (s32[4,96]{1,0:T(4,128)S(1)}, s32[4,96]{1,0:T(4,128)}, u32[]{:S(2)}) copy-start(s32[4,96]{1,0:T(4,128)} %param.6) | copy-start | bytes 4612
  0.0 9.3 %copy-start.7 = (s32[6144]{0:T(1024)S(1)}, s32[6144]{0:T(1024)}, u32[]{:S(2)}) copy-start(s32[6144]{0:T(1024)} %param.5) | copy-start | bytes 73732
  1.3 15.0 %collective-permute-start = (bf16[1536,128]{1,0:T(8,128)(2,1)S(1)}, bf16[1536,128]{1,0:T(8,128)(2,1)S(1)}, u32[]{:S(2)}, u32[]{:S(2)}) collective-permute-start(bf16[1536,128]{1,0:T(8,128)(2,1)S(1)} %get-tuple-element.30), channel_id=1, source_target_pairs={{2,0},{3,1},{6,4},{7,5},{8,10},{9,11},{12,14},{13,15},{18,16},{19,... | collective-permute-start | bytes 1179656 | tf_op jit(solution)/shard_map/ppermute | solution.py:367
  2.6 18.7 %collective-permute-start.6 = (bf16[1536,128]{1,0:T(8,128)(2,1)S(1)}, bf16[1536,128]{1,0:T(8,128)(2,1)S(1)}, u32[]{:S(2)}, u32[]{:S(2)}) collective-permute-start(bf16[1536,128]{1,0:T(8,128)(2,1)S(1)} %get-tuple-element.30), channel_id=1, source_target_pairs={{0,0},{1,4},{4,1},{5,5},{10,10},{11,14},{14,11},{15,15},{16,16},{1... | collective-permute-start | bytes 1179656 | tf_op jit(solution)/shard_map/ppermute | solution.py:367
  7.2 14.2 %collective-permute-start.5 = (bf16[1536,128]{1,0:T(8,128)(2,1)S(1)}, bf16[1536,128]{1,0:T(8,128)(2,1)S(1)}, u32[]{:S(2)}, u32[]{:S(2)}) collective-permute-start(bf16[1536,128]{1,0:T(8,128)(2,1)S(1)} %get-tuple-element.33), channel_id=1, source_target_pairs={{0,0},{1,4},{2,8},{3,12},{4,1},{5,5},{6,9},{7,13},{8,2},{9,6},{10,... | collective-permute-start | bytes 1179656 | tf_op jit(solution)/shard_map/ppermute | solution.py:367
  16.3 13.4 %collective-permute-start.7 = (bf16[1536,128]{1,0:T(8,128)(2,1)S(1)}, bf16[1536,128]{1,0:T(8,128)(2,1)S(1)}, u32[]{:S(2)}, u32[]{:S(2)}) collective-permute-start(bf16[1536,128]{1,0:T(8,128)(2,1)S(1)} %collective-permute-done), channel_id=1, source_target_pairs={{0,8},{1,12},{4,9},{5,13},{10,2},{11,6},{14,3},{15,7},{16,24},{17,... | collective-permute-start | bytes 1179656 | tf_op jit(solution)/shard_map/ppermute | solution.py:367
  30.9 44.5 %collective-permute-start.8 = (bf16[1536,256]{1,0:T(8,128)(2,1)S(1)}, bf16[1536,256]{1,0:T(8,128)(2,1)S(1)}, u32[]{:S(2)}, u32[]{:S(2)}) collective-permute-start(bf16[1536,256]{1,0:T(8,128)(2,1)S(1)} %fill_window.1.refs_4_.refs_7_.refs_0_), channel_id=1, source_target_pairs={{0,4},{4,8},{8,12},{1,5},{5,9},{9,13},{2,6},{6,10},{10,14},{3,7},{... | collective-permute-start | bytes 2359304 | tf_op jit(solution)/shard_map/ppermute | solution.py:413
  40.7 34.7 %collective-permute-start.9 = (bf16[1536,256]{1,0:T(8,128)(2,1)S(1)}, bf16[1536,256]{1,0:T(8,128)(2,1)S(1)}, u32[]{:S(2)}, u32[]{:S(2)}) collective-permute-start(bf16[1536,256]{1,0:T(8,128)(2,1)S(1)} %fill_window.1.refs_4_.refs_7_.refs_0_), channel_id=1, source_target_pairs={{4,0},{8,4},{12,8},{5,1},{9,5},{13,9},{6,2},{10,6},{14,10},{7,3},{... | collective-permute-start | bytes 2359304 | tf_op jit(solution)/shard_map/ppermute | solution.py:414
  42.0 9.4 %collective-permute-start.3 = (bf16[96,1536]{1,0:T(8,128)(2,1)S(1)}, bf16[96,1536]{1,0:T(8,128)(2,1)}, u32[]{:S(2)}, u32[]{:S(2)}) collective-permute-start(bf16[96,1536]{1,0:T(8,128)(2,1)S(1)} %get-tuple-element.32.imag_ref), channel_id=1, source_target_pairs={{2,0},{3,1},{6,4},{7,5},{8,10},{9,11},{12,14},{13,15},{18,16},{19,... | collective-permute-start | bytes 884744 | tf_op jit(solution)/shard_map/ppermute | solution.py:367
  43.3 26.6 %collective-permute-start.2 = (bf16[96,1536]{1,0:T(8,128)(2,1)S(1)}, bf16[96,1536]{1,0:T(8,128)(2,1)S(1)}, u32[]{:S(2)}, u32[]{:S(2)}) collective-permute-start(bf16[96,1536]{1,0:T(8,128)(2,1)S(1)} %get-tuple-element.32.imag_ref), channel_id=1, source_target_pairs={{0,0},{1,4},{4,1},{5,5},{10,10},{11,14},{14,11},{15,15},{16,16},{1... | collective-permute-start | bytes 884744 | tf_op jit(solution)/shard_map/ppermute | solution.py:367
  51.3 19.3 %collective-permute-start.4 = (bf16[96,1536]{1,0:T(8,128)(2,1)}, bf16[96,1536]{1,0:T(8,128)(2,1)}, u32[]{:S(2)}, u32[]{:S(2)}) collective-permute-start(bf16[96,1536]{1,0:T(8,128)(2,1)} %collective-permute-done.3), channel_id=1, source_target_pairs={{0,8},{1,12},{4,9},{5,13},{10,2},{11,6},{14,3},{15,7},{16,24},{17,... | collective-permute-start | bytes 884744 | tf_op jit(solution)/shard_map/ppermute | solution.py:367
  57.6 17.8 %collective-permute-start.1 = (bf16[96,1536]{1,0:T(8,128)(2,1)}, bf16[96,1536]{1,0:T(8,128)(2,1)S(1)}, u32[]{:S(2)}, u32[]{:S(2)}) collective-permute-start(bf16[96,1536]{1,0:T(8,128)(2,1)} %get-tuple-element.31.real_ref), channel_id=1, source_target_pairs={{0,0},{1,4},{2,8},{3,12},{4,1},{5,5},{6,9},{7,13},{8,2},{9,6},{10,... | collective-permute-start | bytes 884744 | tf_op jit(solution)/shard_map/ppermute | solution.py:367
  69.9 0.7 copy-start.6
  75.3 7.7 %copy-start.2 = (bf16[96,1536]{1,0:T(8,128)(2,1)}, bf16[96,1536]{1,0:T(8,128)(2,1)S(1)}, u32[]{:S(2)}) copy-start(bf16[96,1536]{1,0:T(8,128)(2,1)S(1)} %collective-permute-done.1.real_ref) | copy-start | bytes 884740
  83.0 3.5 %collective-permute-start.10 = (f32[1536,256]{1,0:T(8,128)S(1)}, f32[1536,256]{1,0:T(8,128)S(1)}, u32[]{:S(2)}, u32[]{:S(2)}) collective-permute-start(f32[1536,256]{1,0:T(8,128)S(1)} %get-tuple-element.40), channel_id=1, source_target_pairs={{0,1},{1,0},{2,3},{3,2},{4,5},{5,4},{6,7},{7,6},{8,9},{9,8},{10,11... | collective-permute-start | bytes 4718600 | tf_op jit(solution)/shard_map/ppermute | solution.py:452
  83.1 8.6 %collective-permute-start.11 = (bf16[1536,256]{1,0:T(8,128)(2,1)S(1)}, bf16[1536,256]{1,0:T(8,128)(2,1)S(1)}, u32[]{:S(2)}, u32[]{:S(2)}) collective-permute-start(bf16[1536,256]{1,0:T(8,128)(2,1)S(1)} %collective-permute-done.8.refs_6_.refs_9_.refs_2_.refs_7_.refs_8_.refs_14_), channel_id=1, source_target_pairs={{4,8},{8,12},{5,9},{9,13},{6,10},{10,14},{7,11},{11,15},{20,24},{2... | collective-permute-start | bytes 2359304 | tf_op jit(solution)/shard_map/ppermute | solution.py:413
  83.8 20.6 %collective-permute-start.12 = (bf16[1536,256]{1,0:T(8,128)(2,1)S(1)}, bf16[1536,256]{1,0:T(8,128)(2,1)}, u32[]{:S(2)}, u32[]{:S(2)}) collective-permute-start(bf16[1536,256]{1,0:T(8,128)(2,1)S(1)} %collective-permute-done.9.refs_5_.refs_8_.refs_1_.refs_6_.refs_7_.refs_13_), channel_id=1, source_target_pairs={{4,0},{8,4},{5,1},{9,5},{6,2},{10,6},{7,3},{11,7},{20,16},{24,20},... | collective-permute-start | bytes 2359304 | tf_op jit(solution)/shard_map/ppermute | solution.py:414
  104.5 19.9 %collective-permute-start.15 = (bf16[1536,256]{1,0:T(8,128)(2,1)}, bf16[1536,256]{1,0:T(8,128)(2,1)}, u32[]{:S(2)}, u32[]{:S(2)}) collective-permute-start(bf16[1536,256]{1,0:T(8,128)(2,1)} %collective-permute-done.12.refs_3_.refs_4_.refs_10_), channel_id=1, source_target_pairs={{4,0},{5,1},{6,2},{7,3},{20,16},{21,17},{22,18},{23,19}} | collective-permute-start | bytes 2359304 | tf_op jit(solution)/shard_map/ppermute | solution.py:414
  105.7 18.6 %collective-permute-start.16 = (bf16[1536,256]{1,0:T(8,128)(2,1)S(1)}, bf16[1536,256]{1,0:T(8,128)(2,1)}, u32[]{:S(2)}, u32[]{:S(2)}) collective-permute-start(bf16[1536,256]{1,0:T(8,128)(2,1)S(1)} %collective-permute-done.11.refs_4_.refs_5_.refs_11_), channel_id=1, source_target_pairs={{8,12},{9,13},{10,14},{11,15},{24,28},{25,29},{26,30},{27,31}} | collective-permute-start | bytes 2359304 | tf_op jit(solution)/shard_map/ppermute | solution.py:413
  107.3 21.4 %collective-permute-start.13 = (f16[1536,256]{1,0:T(8,128)(2,1)}, f16[1536,256]{1,0:T(8,128)(2,1)}, u32[]{:S(2)}, u32[]{:S(2)}) collective-permute-start(f16[1536,256]{1,0:T(8,128)(2,1)} %multiply_convert_fusion.1), channel_id=1, source_target_pairs={{2,0},{3,1},{6,4},{7,5},{8,10},{9,11},{12,14},{13,15},{18,16},{19,... | collective-permute-start | bytes 2359304 | tf_op jit(solution)/shard_map/ppermute | solution.py:367
  108.8 19.9 %collective-permute-start.14 = (f32[1,128]{1,0:T(1,128)S(1)}, f32[1,128]{1,0:T(1,128)S(1)}, u32[]{:S(2)}, u32[]{:S(2)}) collective-permute-start(f32[1,128]{1,0:T(1,128)S(1)} %broadcast_in_dim.39), channel_id=1, source_target_pairs={{2,0},{3,1},{6,4},{7,5},{8,10},{9,11},{12,14},{13,15},{18,16},{19,... | collective-permute-start | bytes 1544 | tf_op jit(solution)/shard_map/ppermute | solution.py:367
  124.4 1.0 copy-start.3
  128.7 13.4 %copy-start = (f32[4,96,256]{2,1,0:T(8,128)}, f32[4,96,256]{2,1,0:T(8,128)S(1)}, u32[]{:S(2)}) copy-start(f32[4,96,256]{2,1,0:T(8,128)S(1)} %extra_products.1) | copy-start | bytes 1179652
  139.7 5.9 %collective-permute-start.17 = (f32[1536,256]{1,0:T(8,128)}, f32[1536,256]{1,0:T(8,128)S(1)}, u32[]{:S(2)}, u32[]{:S(2)}) collective-permute-start(f32[1536,256]{1,0:T(8,128)} %get-tuple-element.49), channel_id=1, source_target_pairs={{0,1},{1,0},{2,3},{3,2},{4,5},{5,4},{6,7},{7,6},{8,9},{9,8},{10,11... | collective-permute-start | bytes 4718600 | tf_op jit(solution)/shard_map/ppermute | solution.py:452
  142.0 14.3 %collective-permute-start.20 = (f32[2,96,256]{2,1,0:T(8,128)S(1)}, f32[2,96,256]{2,1,0:T(8,128)S(1)}, u32[]{:S(2)}, u32[]{:S(2)}) collective-permute-start(f32[2,96,256]{2,1,0:T(8,128)S(1)} %slice.23), channel_id=1, source_target_pairs={{0,1},{1,0},{2,3},{3,2},{4,5},{5,4},{6,7},{7,6},{8,9},{9,8},{10,11... | collective-permute-start | bytes 589832 | tf_op jit(solution)/shard_map/ppermute | solution.py:476
  149.1 7.3 %copy-start.1 = (f32[4,96,256]{2,1,0:T(8,128)S(1)}, f32[4,96,256]{2,1,0:T(8,128)}, u32[]{:S(2)}) copy-start(f32[4,96,256]{2,1,0:T(8,128)} %copy-done) | copy-start | bytes 1179652
  149.8 6.7 %copy-start.9 = (f32[2]{0:T(128)S(1)}, f32[2]{0:T(128)}, u32[]{:S(2)}) copy-start(f32[2]{0:T(128)} %param.7) | copy-start | bytes 28
  149.8 24.4 %copy-start.5 = (f32[1536,256]{1,0:T(8,128)S(1)}, f32[1536,256]{1,0:T(8,128)}, u32[]{:S(2)}) copy-start(f32[1536,256]{1,0:T(8,128)} %get-tuple-element.54) | copy-start | bytes 4718596
  151.5 22.7 %collective-permute-start.18 = (f16[1536,256]{1,0:T(8,128)(2,1)S(1)}, f16[1536,256]{1,0:T(8,128)(2,1)}, u32[]{:S(2)}, u32[]{:S(2)}) collective-permute-start(f16[1536,256]{1,0:T(8,128)(2,1)S(1)} %multiply_convert_fusion), channel_id=1, source_target_pairs={{0,2},{1,3},{4,6},{5,7},{10,8},{11,9},{14,12},{15,13},{16,18},{17,... | collective-permute-start | bytes 2359304 | tf_op jit(solution)/shard_map/ppermute | solution.py:367
  156.4 17.7 %collective-permute-start.21 = (f32[1,96,256]{2,1,0:T(8,128)S(1)}, f32[1,96,256]{2,1,0:T(8,128)S(1)}, u32[]{:S(2)}, u32[]{:S(2)}) collective-permute-start(f32[1,96,256]{2,1,0:T(8,128)S(1)} %slice.27), channel_id=1, source_target_pairs={{0,2},{1,3},{2,0},{3,1},{4,6},{5,7},{6,4},{7,5},{8,10},{9,11},{10,... | collective-permute-start | bytes 294920 | tf_op jit(solution)/shard_map/ppermute | solution.py:476
  156.5 17.6 %collective-permute-start.19 = (f32[1,128]{1,0:T(1,128)S(1)}, f32[1,128]{1,0:T(1,128)S(1)}, u32[]{:S(2)}, u32[]{:S(2)}) collective-permute-start(f32[1,128]{1,0:T(1,128)S(1)} %broadcast_in_dim.40), channel_id=1, source_target_pairs={{0,2},{1,3},{4,6},{5,7},{10,8},{11,9},{14,12},{15,13},{16,18},{17,... | collective-permute-start | bytes 1544 | tf_op jit(solution)/shard_map/ppermute | solution.py:367
  174.2 2.0 %copy-start.4 = (bf16[96,1536]{1,0:T(8,128)(2,1)S(1)}, bf16[96,1536]{1,0:T(8,128)(2,1)}, u32[]{:S(2)}) copy-start(bf16[96,1536]{1,0:T(8,128)(2,1)} %copy-done.2) | copy-start | bytes 884740

commit v10 on v8

--- a/solution.py
+++ b/solution.py
@@ -61,24 +61,24 @@
     return real_part, imag_part
 
 
-def halves(real_part, imag_part):
-    return [real_part, imag_part] if CHUNKS == 1 else pack(real_part, imag_part)
-
-
-def cut_kernel(traces_ref, *out_refs):
-    parts = halves(traces_ref[0].astype(jnp.float32), traces_ref[1].astype(jnp.float32))
-    for out_ref, part in zip(out_refs, parts):
-        out_ref[...] = part.astype(jnp.bfloat16)
+def cut_kernel(traces_ref, direct_ref, rest_ref):
+    rows = traces_ref.shape[1]
+    top = rows - rest_ref.shape[0]
+    direct_ref[:rows] = traces_ref[0]
+    direct_ref[rows:] = traces_ref[1, :top]
+    rest_ref[...] = traces_ref[1, top:]
 
 
 def cut_window(traces):
     rows = traces.shape[1]
+    rest = rows // 3 * 2
+    sizes = (2 * rows - rest, rest)
     return pl.pallas_call(
         cut_kernel,
         grid=(1,),
         in_specs=[pl.BlockSpec((2, rows, WIN), lambda i: (0, 0, 0))],
-        out_specs=[pl.BlockSpec((rows, WIN), lambda i: (0, 0))] * 2,
-        out_shape=[jax.ShapeDtypeStruct((rows, WIN), jnp.bfloat16)] * 2,
+        out_specs=[pl.BlockSpec((size, WIN), lambda i: (0, 0)) for size in sizes],
+        out_shape=[jax.ShapeDtypeStruct((size, WIN), jnp.bfloat16) for size in sizes],
         compiler_params=params(),
         cost_estimate=cost(rows * WIN, 8 * rows * WIN),
         name="cut_window",
@@ -120,51 +120,40 @@
     )(traces, miss_lanes, recv8, live8)
 
 
-def fill_kernel(counts, first_half, real_ref, imag_ref, miss_ref, recv_ref, *refs):
-    out_ref = refs[-1]
+def fill_kernel(real_ref, imag_ref, miss_ref, recv_ref, direct_ref, *refs):
+    rest_refs, out_ref = refs[:-1], refs[-1]
     rows = out_ref.shape[0]
     misses = real_ref.shape[0]
     hot = one_hot(miss_ref[...], rows, jnp.float32)
-    dead = jnp.max(hot, axis=1, keepdims=True)
+    keep = (1.0 - jnp.max(hot, axis=1, keepdims=True)) * recv_ref[0:1, :].astype(jnp.float32)
     hot = hot[:, :misses].astype(jnp.bfloat16)
-    patches = halves(real_ref[...].astype(jnp.float32), imag_ref[...].astype(jnp.float32))
-    mask = recv_ref[...].astype(jnp.float32)
-    mask = halves(mask, mask)[0][0:1, :]
-    used = 0
-    for index, count in enumerate(counts):
-        arrived = refs[used][...].astype(jnp.float32)
-        for more in refs[used + 1:used + count]:
-            arrived = arrived + more[...].astype(jnp.float32)
-        used += count
-        patch = patches[first_half + index].astype(jnp.bfloat16)
-        moved = jnp.dot(hot, patch, preferred_element_type=jnp.float32)
-        filled = arrived * ((1.0 - dead) * mask) + moved
-        out_ref[:, index * WIN:(index + 1) * WIN] = filled.astype(jnp.bfloat16)
-
-
-def fill_window(first_half, arrived, picked, miss_lanes, recv8):
-    rows = arrived[0][0].shape[0]
+    rest = rest_refs[0][...].astype(jnp.float32)
+    for more in rest_refs[1:]:
+        rest = rest + more[...].astype(jnp.float32)
+    direct = direct_ref[...].astype(jnp.float32)
+    arrived = [direct[:rows], jnp.concatenate([direct[rows:], rest], axis=0)]
+    for part, patch_ref in enumerate((real_ref, imag_ref)):
+        moved = jnp.dot(hot, patch_ref[...], preferred_element_type=jnp.float32)
+        filled = arrived[part] * keep + moved
+        out_ref[:, part * WIN:(part + 1) * WIN] = filled.astype(jnp.bfloat16)
+
+
+def fill_window(direct, rest, picked, miss_lanes, recv8):
     misses = picked[0].shape[0]
-    counts = tuple(len(group) for group in arrived)
-    flat = [part for group in arrived for part in group]
-    lanes = len(counts) * WIN
-    whole = pl.BlockSpec((rows, WIN), lambda i: (0, 0))
-    return pl.pallas_call(
-        functools.partial(fill_kernel, counts, first_half),
+    whole = lambda array: pl.BlockSpec(array.shape, lambda i: (0, 0))
+    patch = pl.BlockSpec((misses, WIN), lambda i: (0, 0))
+    rows = (direct.shape[0] + rest[0].shape[0]) // 2
+    return pl.pallas_call(
+        fill_kernel,
         grid=(1,),
-        in_specs=[
-            pl.BlockSpec((misses, WIN), lambda i: (0, 0)),
-            pl.BlockSpec((misses, WIN), lambda i: (0, 0)),
-            pl.BlockSpec((1, LANES), lambda i: (0, 0)),
-            pl.BlockSpec((8, WIN), lambda i: (0, 0)),
-        ]
-        + [whole] * len(flat),
-        out_specs=pl.BlockSpec((rows, lanes), lambda i: (0, 0)),
-        out_shape=jax.ShapeDtypeStruct((rows, lanes), jnp.bfloat16),
-        compiler_params=params(),
-        cost_estimate=cost(4 * rows * LANES * lanes, 8 * rows * lanes),
+        in_specs=[patch, patch, whole(miss_lanes), whole(recv8), whole(direct)]
+        + [whole(piece) for piece in rest],
+        out_specs=pl.BlockSpec((rows, 2 * WIN), lambda i: (0, 0)),
+        out_shape=jax.ShapeDtypeStruct((rows, 2 * WIN), jnp.bfloat16),
+        compiler_params=params(),
+        cost_estimate=cost(8 * rows * LANES * WIN, 16 * rows * WIN),
         name="fill_window",
-    )(*picked, miss_lanes, recv8, *flat)
+    )(*picked, miss_lanes, recv8, direct, *rest)
 
 
 def complex_rows(real_rows, imag_rows, right):
@@ -369,18 +358,13 @@
     def transpose(block):
         return move(block, whole)
 
-    def transpose_round(block):
-        if hops is None:
-            return [move(block, whole)]
+    direct, rest = cut_window(traces)
+    direct = transpose(direct)
+    if hops is None:
+        rest = [move(rest, whole)]
+    else:
         near, first, second = hops
-        return [move(move(block, first), second), move(block, near)]
-
-    direct, round_about = cut_window(traces)
-    arrived = [[transpose(direct)], transpose_round(round_about)]
-    if CHUNKS == 1:
-        arrived = [arrived]
-    else:
-        arrived = [arrived[:1], arrived[1:]]
+        rest = [move(move(rest, first), second), move(rest, near)]
 
     miss_row = lax.dynamic_index_in_dim(missing, row_index, 0, keepdims=False)
     miss_col = lax.dynamic_index_in_dim(missing, col_index, 0, keepdims=False)
@@ -402,7 +386,7 @@
     strides = [2**bit for bit in range(grid_size.bit_length() - 1)]
     terms, extra_terms = [], []
     for chunk in range(CHUNKS):
-        window = fill_window(chunk, arrived[chunk], picked, miss_col_lanes, recv_row8)
+        window = fill_window(direct, rest, picked, miss_col_lanes, recv_row8)
         up, down = [window], [window]
         sums = []
 

time: 178 us -> 183 us (1.028)
  waiting for transfers between devices: 81.6 us -> 90.6 us
  starting transfers between devices: 43.4 us -> 39.3 us
    ppermute x3, starting transfers between devices: 12.1 us -> 3.61 us  [hop(): up.append(lax.ppermute(up[-1], 'row', ends))]
    ppermute x9, waiting for transfers between devices: 5.69 us -> 11.2 us  [move(): return lax.ppermute(block, ('row', 'col'), route)]
    ppermute x9, starting transfers between devices: 25.3 us -> 29.7 us  [move(): return lax.ppermute(block, ('row', 'col'), route)]
    ppermute x3, waiting for transfers between devices: 44.4 us -> 47.4 us  [hop(): down.append(lax.ppermute(down[-1], 'row', back))]
where the time goes in v10:
time: 183 us; the launch traced here: 180 us
  waiting for transfers between devices  90.6 us (50%)
  starting transfers between devices  39.3 us (21%)
  Pallas kernels  32.7 us (18%)
  other arithmetic  12.8 us (7%)
  local copies, waits for them, and re-layouts  3.13 us (2%)
  between operations  1.85 us (1%)
    ppermute x3, waiting for transfers between devices, hop(): down.append(lax.ppermute(down[-1], 'row', back))  47.4 us
    ppermute x9, starting transfers between devices, move(): return lax.ppermute(block, ('row', 'col'), route)  29.7 us
    pallas_call x2, Pallas kernels, products(): pl.pallas_call(functools.partial(product_kernel, counts), grid=(rows // b...  18.6 us
    ppermute x2, waiting for transfers between devices, local(): arrive = lax.ppermute(rest[1::2], 'col', pairs)  14.3 us
    ppermute x3, waiting for transfers between devices, hop(): up.append(lax.ppermute(up[-1], 'row', ends))  13.2 us
    ppermute x9, waiting for transfers between devices, move(): return lax.ppermute(block, ('row', 'col'), route)  11.2 us
    pallas_call x1, Pallas kernels, pick_columns(): pl.pallas_call(pick_kernel, grid=(rows // block,), in_specs=[pl.BlockSpec...  6.28 us
    reduce_max x2, other arithmetic, shrink(): unit = jnp.maximum(jnp.max(jnp.abs(total)), TINY) * (1.0 / HALF_TOP)  5.4 us
  transfers between devices with their start and end apart: 19, of which 8 were waited for; matrix products, arithmetic and copies ran while one was open for 7% of the time, Pallas kernels for 6%

profile of v10, /device:TPU:1, one launch (start us, length us, event | category | flops | bytes accessed | tf_op | source)
XLA Modules:
  0.0 180.4 jit_solution(10648324975623047854)
XLA Ops:
  0.0 1.2 cut_window.1
  1.2 1.3 collective-permute-start.2
  2.5 4.6 %collective-permute-start.1 = (bf16[2048,128]{1,0:T(8,128)(2,1)S(1)}, bf16[2048,128]{1,0:T(8,128)(2,1)S(1)}, u32[]{:S(2)}, u32[]{:S(2)}) collective-permute-start(bf16[2048,128]{1,0:T(8,128)(2,1)S(1)} %get-tuple-element.27), channel_id=1, source_target_pairs={{0,0},{1,4},{2,8},{3,12},{4,1},{5,5},{6,9},{7,13},{8,2},{9,6},{10,... | collective-permute-start | bytes 1572872 | tf_op jit(solution)/shard_map/ppermute | solution.py:356
  7.1 0.1 fusion
  7.3 0.1 dynamic_slice.14
  7.4 6.3 %pick_columns.1 = (bf16[96,1536]{1,0:T(8,128)(2,1)S(1)}, bf16[96,1536]{1,0:T(8,128)(2,1)S(1)}) custom-call(bf16[2,1536,1536]{2,1,0:T(8,128)(2,1)} %tile_ref.1, s32[1,128]{1,0:T(1,128)S(1)} %pad_bitcast_fusion.miss_ref, bf16[8,1536]{1,0:T(8,128)(2,1)S(1)} %broadcast_in_dim.16.recv_ref, f32[8,1536]{1,0:T(8,128)S(1)} %broadcast_in_dim.36.live_ref), custom_call_target="tpu_custom_call" | custom-call | flops 37748736 | bytes 147456 | tf_op jit(solution)/shard_map/pick_columns/pallas_call | solution.py:105
  13.7 0.9 pad_maximum_fusion
  14.6 1.9 %collective-permute-start = (bf16[192,1536]{1,0:T(8,128)(2,1)}, bf16[192,1536]{1,0:T(8,128)(2,1)}, u32[]{:S(2)}, u32[]{:S(2)}) collective-permute-start(bf16[192,1536]{1,0:T(8,128)(2,1)} %pad_maximum_fusion), channel_id=1, source_target_pairs={{0,0},{1,4},{2,8},{3,12},{4,1},{5,5},{6,9},{7,13},{8,2},{9,6},{10,... | collective-permute-start | bytes 1769480 | tf_op jit(solution)/shard_map/ppermute | solution.py:356
  16.5 3.6 %collective-permute-start.4 = (bf16[1024,128]{1,0:T(8,128)(2,1)S(1)}, bf16[1024,128]{1,0:T(8,128)(2,1)S(1)}, u32[]{:S(2)}, u32[]{:S(2)}) collective-permute-start(bf16[1024,128]{1,0:T(8,128)(2,1)S(1)} %get-tuple-element.28), channel_id=1, source_target_pairs={{0,0},{1,4},{4,1},{5,5},{10,10},{11,14},{14,11},{15,15},{16,16},{1... | collective-permute-start | bytes 786440 | tf_op jit(solution)/shard_map/ppermute | solution.py:356
  20.2 7.5 %collective-permute-start.3 = (bf16[1024,128]{1,0:T(8,128)(2,1)S(1)}, bf16[1024,128]{1,0:T(8,128)(2,1)S(1)}, u32[]{:S(2)}, u32[]{:S(2)}) collective-permute-start(bf16[1024,128]{1,0:T(8,128)(2,1)S(1)} %collective-permute-done.2), channel_id=1, source_target_pairs={{0,8},{1,12},{4,9},{5,13},{10,2},{11,6},{14,3},{15,7},{16,24},{17,... | collective-permute-start | bytes 786440 | tf_op jit(solution)/shard_map/ppermute | solution.py:356
  27.7 0.1 dynamic_slice.16
  27.8 11.1 %collective-permute-done.4.refs_1_ = bf16[1024,128]{1,0:T(8,128)(2,1)S(1)} collective-permute-done((bf16[1024,128]{1,0:T(8,128)(2,1)S(1)}, bf16[1024,128]{1,0:T(8,128)(2,1)S(1)}, u32[]{:S(2)}, u32[]{:S(2)}) %collective-permute-start.4) | collective-permute-done | bytes 262176 | tf_op jit(solution)/shard_map/ppermute | solution.py:356
  38.9 0.5 fill_window.1.refs_4_.refs_7_.refs_0_
  39.4 1.3 collective-permute-start.5
  40.8 1.3 collective-permute-start.6
  42.1 0.1 pad_add_fusion.pick_ref
  42.2 1.8 %fusion.2 = (bf16[96,1536]{1,0:T(8,128)(2,1)S(1)}, bf16[96,1536]{1,0:T(8,128)(2,1)}) fusion(bf16[192,1536]{1,0:T(8,128)(2,1)} %collective-permute-done), kind=kLoop, calls=%fused_computation.18 | loop fusion | bytes 1179648 | tf_op jit(solution)/shard_map/slice | solution.py:384
  44.0 13.2 %collective-permute-done.5.refs_6_.refs_9_.refs_2_.refs_7_.refs_8_.refs_14_ = bf16[1536,256]{1,0:T(8,128)(2,1)S(1)} collective-permute-done((bf16[1536,256]{1,0:T(8,128)(2,1)S(1)}, bf16[1536,256]{1,0:T(8,128)(2,1)S(1)}, u32[]{:S(2)}, u32[]{:S(2)}) %collective-permute-start.5) | collective-permute-done | bytes 786464 | tf_op jit(solution)/shard_map/ppermute | solution.py:396
  57.2 15.6 %collective-permute-done.6.refs_5_.refs_8_.refs_1_.refs_6_.refs_7_.refs_13_ = bf16[1536,256]{1,0:T(8,128)(2,1)S(1)} collective-permute-done((bf16[1536,256]{1,0:T(8,128)(2,1)S(1)}, bf16[1536,256]{1,0:T(8,128)(2,1)S(1)}, u32[]{:S(2)}, u32[]{:S(2)}) %collective-permute-start.6) | collective-permute-done | bytes 786464 | tf_op jit(solution)/shard_map/ppermute | solution.py:397
  72.8 7.6 %products.2 = (f32[1536,256]{1,0:T(8,128)S(1)}, f32[1536,256]{1,0:T(8,128)S(1)}) custom-call(s32[2]{0:T(128)S(1)} %pad_add_fusion.pick_ref, bf16[8,1536]{1,0:T(8,128)(2,1)S(1)} %broadcast_in_dim.16.recv_ref, bf16[2,1536,1536]{2,1,0:T(8,128)(2,1)} %tile_ref.1, bf16[2,1536,1536]{2,1,0:T(8,128)(2,1)} %tile_ref.1, bf16[2,1536,1536]{2,1,0:T(8,128)(2,1)} %tile_ref.1, ...), custom_call_target="tpu_custom_call" | custom-call | flops 150994944 | bytes 24576 | tf_op jit(solution)/shard_map/products/pallas_call | solution.py:219
  80.4 0.3 collective-permute-start.7
  80.7 0.7 collective-permute-start.8
  81.4 1.3 collective-permute-start.9
  82.7 1.2 collective-permute-done.7
  83.9 2.0 %abs_reduce_fusion.1 = (f32[]{:T(128)}, f32[1536,256]{1,0:T(8,128)}) fusion(f32[1536,256]{1,0:T(8,128)S(1)} %get-tuple-element.33, f32[1536,256]{1,0:T(8,128)S(1)} %collective-permute-done.7), kind=kLoop, calls=%fused_computation.4 | loop fusion | flops 1179647 | bytes 4718596 | tf_op jit(solution)/shard_map/reduce_max | solution.py:405
  86.5 2.5 %multiply_convert_fusion.1 = f16[1536,256]{1,0:T(8,128)(2,1)} fusion(f32[1536,256]{1,0:T(8,128)} %get-tuple-element.48, f32[]{:T(128)S(6)} %div.18), kind=kLoop, calls=%fused_computation.3 | loop fusion | flops 786432 | bytes 2359300 | tf_op jit(solution)/shard_map/convert_element_type | solution.py:406
  89.0 16.8 %collective-permute-done.9.refs_3_.refs_4_.refs_10_ = bf16[1536,256]{1,0:T(8,128)(2,1)} collective-permute-done((bf16[1536,256]{1,0:T(8,128)(2,1)S(1)}, bf16[1536,256]{1,0:T(8,128)(2,1)}, u32[]{:S(2)}, u32[]{:S(2)}) %collective-permute-start.9) | collective-permute-done | bytes 786464 | tf_op jit(solution)/shard_map/ppermute | solution.py:397
  105.8 1.3 collective-permute-start.12
  107.1 1.6 collective-permute-start.13
  108.7 1.3 collective-permute-start.10
  110.0 0.1 stack.53.pick_ref
  110.1 0.1 pad_add_fusion.1.pick_ref
  110.1 1.3 collective-permute-start.11
  111.4 15.0 %collective-permute-done.12.refs_5_.refs_6_.refs_12_ = bf16[1536,256]{1,0:T(8,128)(2,1)} collective-permute-done((bf16[1536,256]{1,0:T(8,128)(2,1)}, bf16[1536,256]{1,0:T(8,128)(2,1)}, u32[]{:S(2)}, u32[]{:S(2)}) %collective-permute-start.12) | collective-permute-done | bytes 786464 | tf_op jit(solution)/shard_map/ppermute | solution.py:397
  126.4 1.0 copy-done
  127.4 3.3 %extra_products.1 = f32[4,96,256]{2,1,0:T(8,128)S(1)} custom-call(s32[8]{0:T(128)S(1)} %stack.53.pick_ref, bf16[96,1536]{1,0:T(8,128)(2,1)S(1)} %copy-done, bf16[96,1536]{1,0:T(8,128)(2,1)S(1)} %get-tuple-element.30.imag_ref, bf16[1536,256]{1,0:T(8,128)(2,1)S(1)} %fill_window.1.refs_4_.refs_7_.refs_0_, ...), custom_call_target="tpu_custom_call" | custom-call | flops 18874368 | bytes 24576 | tf_op jit(solution)/shard_map/extra_products/pallas_call | solution.py:253
  130.7 11.0 %products.3 = (f32[1536,256]{1,0:T(8,128)}, f32[1536,256]{1,0:T(8,128)}) custom-call(s32[2]{0:T(128)S(1)} %pad_add_fusion.1.pick_ref, bf16[8,1536]{1,0:T(8,128)(2,1)S(1)} %broadcast_in_dim.16.recv_ref, bf16[2,1536,1536]{2,1,0:T(8,128)(2,1)} %tile_ref.1, bf16[2,1536,1536]{2,1,0:T(8,128)(2,1)} %tile_ref.1, bf16[2,1536,1536]{2,1,0:T(8,128)(2,1)} %tile_ref.1, ...), custom_call_target="tpu_custom_call" | custom-call | flops 150994944 | bytes 24576 | tf_op jit(solution)/shard_map/products/pallas_call | solution.py:219
  141.8 1.6 collective-permute-start.14
  143.4 0.1 collective-permute-start.17
  143.5 3.4 %collective-permute-done.14 = f32[1536,256]{1,0:T(8,128)S(1)} collective-permute-done((f32[1536,256]{1,0:T(8,128)}, f32[1536,256]{1,0:T(8,128)S(1)}, u32[]{:S(2)}, u32[]{:S(2)}) %collective-permute-start.14) | collective-permute-done | bytes 1572896 | tf_op jit(solution)/shard_map/ppermute | solution.py:435
  146.9 3.4 %abs_reduce_fusion = (f32[]{:T(128)}, f32[1536,256]{1,0:T(8,128)}) fusion(f32[1536,256]{1,0:T(8,128)} %get-tuple-element.42, f32[1536,256]{1,0:T(8,128)S(1)} %collective-permute-done.14), kind=kLoop, calls=%fused_computation.2 | loop fusion | flops 1179647 | bytes 4718596 | tf_op jit(solution)/shard_map/reduce_max | solution.py:405
  151.1 1.7 multiply_convert_fusion
  152.8 4.9 %collective-permute-start.15 = (f16[1536,256]{1,0:T(8,128)(2,1)S(1)}, f16[1536,256]{1,0:T(8,128)(2,1)}, u32[]{:S(2)}, u32[]{:S(2)}) collective-permute-start(f16[1536,256]{1,0:T(8,128)(2,1)S(1)} %multiply_convert_fusion), channel_id=1, source_target_pairs={{0,2},{1,3},{4,6},{5,7},{10,8},{11,9},{14,12},{15,13},{16,18},{17,... | collective-permute-start | bytes 2359304 | tf_op jit(solution)/shard_map/ppermute | solution.py:356
  157.7 0.1 collective-permute-start.18
  157.9 3.3 %collective-permute-start.16 = (f32[1,128]{1,0:T(1,128)S(1)}, f32[1,128]{1,0:T(1,128)S(1)}, u32[]{:S(2)}, u32[]{:S(2)}) collective-permute-start(f32[1,128]{1,0:T(1,128)S(1)} %broadcast_in_dim.40), channel_id=1, source_target_pairs={{0,2},{1,3},{4,6},{5,7},{10,8},{11,9},{14,12},{15,13},{16,18},{17,... | collective-permute-start | bytes 1544 | tf_op jit(solution)/shard_map/ppermute | solution.py:356
  161.2 14.3 %collective-permute-done.18 = f32[1,96,256]{2,1,0:T(8,128)S(1)} collective-permute-done((f32[1,96,256]{2,1,0:T(8,128)S(1)}, f32[1,96,256]{2,1,0:T(8,128)S(1)}, u32[]{:S(2)}, u32[]{:S(2)}) %collective-permute-start.18) | collective-permute-done | bytes 98336 | tf_op jit(solution)/shard_map/ppermute | solution.py:459
  175.5 2.1 %add_add_fusion.refs_0_ = f32[1536,256]{1,0:T(8,128)S(1)} fusion(f16[1536,256]{1,0:T(8,128)(2,1)} %collective-permute-done.15, f32[1536,256]{1,0:T(8,128)} %get-tuple-element.46, f16[1536,256]{1,0:T(8,128)(2,1)} %collective-permute-done.10, f32[1536,256]{1,0:T(8,128)S(1)} %copy-done.4, f32[]{:T(128)S(1)} %bitcast.24, f32[]{:T(128)S(1)} %bitcast.23, ...), kind=kLoop, calls=%fused_computation | loop fusion | flops 3538944 | bytes 6291466 | tf_op jit(solution)/shard_map/add | solution.py:455
  177.6 2.8 %finish.1 = f32[2,1536,128]{2,1,0:T(8,128)} custom-call(f32[2]{0:T(128)S(1)} %broadcast_multiply_fusion.wave_ref, s32[96]{0:T(128)S(1)} %get-tuple-element.52.miss_ref, bf16[8,1536]{1,0:T(8,128)(2,1)S(1)} %broadcast_in_dim.16.recv_ref, bf16[2,1536,1536]{2,1,0:T(8,128)(2,1)} %tile_ref.1, bf16[96,1536]{1,0:T(8,128)(2,1)S(1)} %copy-done.1, ...), custom_call_target="tpu_custom_call" | custom-call | flops 61440 | bytes 122880 | tf_op jit(solution)/shard_map/finish/pallas_call | solution.py:293
  (40 shorter events, 0.2 us)
Async XLA Ops:
  0.0 7.1 %copy-start.6 = (s32[4,96]{1,0:T(4,128)S(1)}, s32[4,96]{1,0:T(4,128)}, u32[]{:S(2)}) copy-start(s32[4,96]{1,0:T(4,128)} %param.6) | copy-start | bytes 4612
  0.0 7.3 %copy-start.5 = (s32[6144]{0:T(1024)S(1)}, s32[6144]{0:T(1024)}, u32[]{:S(2)}) copy-start(s32[6144]{0:T(1024)} %param.5) | copy-start | bytes 73732
  1.2 18.9 %collective-permute-start.2 = (bf16[1024,128]{1,0:T(8,128)(2,1)S(1)}, bf16[1024,128]{1,0:T(8,128)(2,1)S(1)}, u32[]{:S(2)}, u32[]{:S(2)}) collective-permute-start(bf16[1024,128]{1,0:T(8,128)(2,1)S(1)} %get-tuple-element.28), channel_id=1, source_target_pairs={{2,0},{3,1},{6,4},{7,5},{8,10},{9,11},{12,14},{13,15},{18,16},{19,... | collective-permute-start | bytes 786440 | tf_op jit(solution)/shard_map/ppermute | solution.py:356
  2.5 36.4 %collective-permute-start.1 = (bf16[2048,128]{1,0:T(8,128)(2,1)S(1)}, bf16[2048,128]{1,0:T(8,128)(2,1)S(1)}, u32[]{:S(2)}, u32[]{:S(2)}) collective-permute-start(bf16[2048,128]{1,0:T(8,128)(2,1)S(1)} %get-tuple-element.27), channel_id=1, source_target_pairs={{0,0},{1,4},{2,8},{3,12},{4,1},{5,5},{6,9},{7,13},{8,2},{9,6},{10,... | collective-permute-start | bytes 1572872 | tf_op jit(solution)/shard_map/ppermute | solution.py:356
  14.6 27.6 %collective-permute-start = (bf16[192,1536]{1,0:T(8,128)(2,1)}, bf16[192,1536]{1,0:T(8,128)(2,1)}, u32[]{:S(2)}, u32[]{:S(2)}) collective-permute-start(bf16[192,1536]{1,0:T(8,128)(2,1)} %pad_maximum_fusion), channel_id=1, source_target_pairs={{0,0},{1,4},{2,8},{3,12},{4,1},{5,5},{6,9},{7,13},{8,2},{9,6},{10,... | collective-permute-start | bytes 1769480 | tf_op jit(solution)/shard_map/ppermute | solution.py:356
  16.5 22.4 %collective-permute-start.4 = (bf16[1024,128]{1,0:T(8,128)(2,1)S(1)}, bf16[1024,128]{1,0:T(8,128)(2,1)S(1)}, u32[]{:S(2)}, u32[]{:S(2)}) collective-permute-start(bf16[1024,128]{1,0:T(8,128)(2,1)S(1)} %get-tuple-element.28), channel_id=1, source_target_pairs={{0,0},{1,4},{4,1},{5,5},{10,10},{11,14},{14,11},{15,15},{16,16},{1... | collective-permute-start | bytes 786440 | tf_op jit(solution)/shard_map/ppermute | solution.py:356
  20.2 18.8 %collective-permute-start.3 = (bf16[1024,128]{1,0:T(8,128)(2,1)S(1)}, bf16[1024,128]{1,0:T(8,128)(2,1)S(1)}, u32[]{:S(2)}, u32[]{:S(2)}) collective-permute-start(bf16[1024,128]{1,0:T(8,128)(2,1)S(1)} %collective-permute-done.2), channel_id=1, source_target_pairs={{0,8},{1,12},{4,9},{5,13},{10,2},{11,6},{14,3},{15,7},{16,24},{17,... | collective-permute-start | bytes 786440 | tf_op jit(solution)/shard_map/ppermute | solution.py:356
  39.4 17.8 %collective-permute-start.5 = (bf16[1536,256]{1,0:T(8,128)(2,1)S(1)}, bf16[1536,256]{1,0:T(8,128)(2,1)S(1)}, u32[]{:S(2)}, u32[]{:S(2)}) collective-permute-start(bf16[1536,256]{1,0:T(8,128)(2,1)S(1)} %fill_window.1.refs_4_.refs_7_.refs_0_), channel_id=1, source_target_pairs={{0,4},{4,8},{8,12},{1,5},{5,9},{9,13},{2,6},{6,10},{10,14},{3,7},{... | collective-permute-start | bytes 2359304 | tf_op jit(solution)/shard_map/ppermute | solution.py:396
  40.8 32.0 %collective-permute-start.6 = (bf16[1536,256]{1,0:T(8,128)(2,1)S(1)}, bf16[1536,256]{1,0:T(8,128)(2,1)S(1)}, u32[]{:S(2)}, u32[]{:S(2)}) collective-permute-start(bf16[1536,256]{1,0:T(8,128)(2,1)S(1)} %fill_window.1.refs_4_.refs_7_.refs_0_), channel_id=1, source_target_pairs={{4,0},{8,4},{12,8},{5,1},{9,5},{13,9},{6,2},{10,6},{14,10},{7,3},{... | collective-permute-start | bytes 2359304 | tf_op jit(solution)/shard_map/ppermute | solution.py:397
  80.4 3.5 %collective-permute-start.7 = (f32[1536,256]{1,0:T(8,128)S(1)}, f32[1536,256]{1,0:T(8,128)S(1)}, u32[]{:S(2)}, u32[]{:S(2)}) collective-permute-start(f32[1536,256]{1,0:T(8,128)S(1)} %get-tuple-element.34), channel_id=1, source_target_pairs={{0,1},{1,0},{2,3},{3,2},{4,5},{5,4},{6,7},{7,6},{8,9},{9,8},{10,11... | collective-permute-start | bytes 4718600 | tf_op jit(solution)/shard_map/ppermute | solution.py:435
  80.7 8.3 %collective-permute-start.8 = (bf16[1536,256]{1,0:T(8,128)(2,1)S(1)}, bf16[1536,256]{1,0:T(8,128)(2,1)S(1)}, u32[]{:S(2)}, u32[]{:S(2)}) collective-permute-start(bf16[1536,256]{1,0:T(8,128)(2,1)S(1)} %collective-permute-done.5.refs_6_.refs_9_.refs_2_.refs_7_.refs_8_.refs_14_), channel_id=1, source_target_pairs={{4,8},{8,12},{5,9},{9,13},{6,10},{10,14},{7,11},{11,15},{20,24},{2... | collective-permute-start | bytes 2359304 | tf_op jit(solution)/shard_map/ppermute | solution.py:396
  81.4 24.4 %collective-permute-start.9 = (bf16[1536,256]{1,0:T(8,128)(2,1)S(1)}, bf16[1536,256]{1,0:T(8,128)(2,1)}, u32[]{:S(2)}, u32[]{:S(2)}) collective-permute-start(bf16[1536,256]{1,0:T(8,128)(2,1)S(1)} %collective-permute-done.6.refs_5_.refs_8_.refs_1_.refs_6_.refs_7_.refs_13_), channel_id=1, source_target_pairs={{4,0},{8,4},{5,1},{9,5},{6,2},{10,6},{7,3},{11,7},{20,16},{24,20},... | collective-permute-start | bytes 2359304 | tf_op jit(solution)/shard_map/ppermute | solution.py:397
  105.8 20.6 %collective-permute-start.12 = (bf16[1536,256]{1,0:T(8,128)(2,1)}, bf16[1536,256]{1,0:T(8,128)(2,1)}, u32[]{:S(2)}, u32[]{:S(2)}) collective-permute-start(bf16[1536,256]{1,0:T(8,128)(2,1)} %collective-permute-done.9.refs_3_.refs_4_.refs_10_), channel_id=1, source_target_pairs={{4,0},{5,1},{6,2},{7,3},{20,16},{21,17},{22,18},{23,19}} | collective-permute-start | bytes 2359304 | tf_op jit(solution)/shard_map/ppermute | solution.py:397
  107.1 19.3 %collective-permute-start.13 = (bf16[1536,256]{1,0:T(8,128)(2,1)S(1)}, bf16[1536,256]{1,0:T(8,128)(2,1)}, u32[]{:S(2)}, u32[]{:S(2)}) collective-permute-start(bf16[1536,256]{1,0:T(8,128)(2,1)S(1)} %collective-permute-done.8.refs_4_.refs_5_.refs_11_), channel_id=1, source_target_pairs={{8,12},{9,13},{10,14},{11,15},{24,28},{25,29},{26,30},{27,31}} | collective-permute-start | bytes 2359304 | tf_op jit(solution)/shard_map/ppermute | solution.py:396
  108.7 22.1 %collective-permute-start.10 = (f16[1536,256]{1,0:T(8,128)(2,1)}, f16[1536,256]{1,0:T(8,128)(2,1)}, u32[]{:S(2)}, u32[]{:S(2)}) collective-permute-start(f16[1536,256]{1,0:T(8,128)(2,1)} %multiply_convert_fusion.1), channel_id=1, source_target_pairs={{2,0},{3,1},{6,4},{7,5},{8,10},{9,11},{12,14},{13,15},{18,16},{19,... | collective-permute-start | bytes 2359304 | tf_op jit(solution)/shard_map/ppermute | solution.py:356
  110.1 20.6 %collective-permute-start.11 = (f32[1,128]{1,0:T(1,128)S(1)}, f32[1,128]{1,0:T(1,128)S(1)}, u32[]{:S(2)}, u32[]{:S(2)}) collective-permute-start(f32[1,128]{1,0:T(1,128)S(1)} %broadcast_in_dim.39), channel_id=1, source_target_pairs={{2,0},{3,1},{6,4},{7,5},{8,10},{9,11},{12,14},{13,15},{18,16},{19,... | collective-permute-start | bytes 1544 | tf_op jit(solution)/shard_map/ppermute | solution.py:356
  126.4 1.0 copy-start
  130.7 12.7 %copy-start.2 = (f32[4,96,256]{2,1,0:T(8,128)}, f32[4,96,256]{2,1,0:T(8,128)S(1)}, u32[]{:S(2)}) copy-start(f32[4,96,256]{2,1,0:T(8,128)S(1)} %extra_products.1) | copy-start | bytes 1179652
  141.8 5.1 %collective-permute-start.14 = (f32[1536,256]{1,0:T(8,128)}, f32[1536,256]{1,0:T(8,128)S(1)}, u32[]{:S(2)}, u32[]{:S(2)}) collective-permute-start(f32[1536,256]{1,0:T(8,128)} %get-tuple-element.43), channel_id=1, source_target_pairs={{0,1},{1,0},{2,3},{3,2},{4,5},{5,4},{6,7},{7,6},{8,9},{9,8},{10,11... | collective-permute-start | bytes 4718600 | tf_op jit(solution)/shard_map/ppermute | solution.py:435
  143.4 14.3 %collective-permute-start.17 = (f32[2,96,256]{2,1,0:T(8,128)S(1)}, f32[2,96,256]{2,1,0:T(8,128)S(1)}, u32[]{:S(2)}, u32[]{:S(2)}) collective-permute-start(f32[2,96,256]{2,1,0:T(8,128)S(1)} %slice.31), channel_id=1, source_target_pairs={{0,1},{1,0},{2,3},{3,2},{4,5},{5,4},{6,7},{7,6},{8,9},{9,8},{10,11... | collective-permute-start | bytes 589832 | tf_op jit(solution)/shard_map/ppermute | solution.py:459
  150.3 7.4 %copy-start.3 = (f32[4,96,256]{2,1,0:T(8,128)S(1)}, f32[4,96,256]{2,1,0:T(8,128)}, u32[]{:S(2)}) copy-start(f32[4,96,256]{2,1,0:T(8,128)} %copy-done.2) | copy-start | bytes 1179652
  151.0 6.8 %copy-start.7 = (f32[2]{0:T(128)S(1)}, f32[2]{0:T(128)}, u32[]{:S(2)}) copy-start(f32[2]{0:T(128)} %param.7) | copy-start | bytes 28
  151.0 24.4 %copy-start.4 = (f32[1536,256]{1,0:T(8,128)S(1)}, f32[1536,256]{1,0:T(8,128)}, u32[]{:S(2)}) copy-start(f32[1536,256]{1,0:T(8,128)} %get-tuple-element.48) | copy-start | bytes 4718596
  152.8 22.7 %collective-permute-start.15 = (f16[1536,256]{1,0:T(8,128)(2,1)S(1)}, f16[1536,256]{1,0:T(8,128)(2,1)}, u32[]{:S(2)}, u32[]{:S(2)}) collective-permute-start(f16[1536,256]{1,0:T(8,128)(2,1)S(1)} %multiply_convert_fusion), channel_id=1, source_target_pairs={{0,2},{1,3},{4,6},{5,7},{10,8},{11,9},{14,12},{15,13},{16,18},{17,... | collective-permute-start | bytes 2359304 | tf_op jit(solution)/shard_map/ppermute | solution.py:356
  157.7 17.7 %collective-permute-start.18 = (f32[1,96,256]{2,1,0:T(8,128)S(1)}, f32[1,96,256]{2,1,0:T(8,128)S(1)}, u32[]{:S(2)}, u32[]{:S(2)}) collective-permute-start(f32[1,96,256]{2,1,0:T(8,128)S(1)} %slice.37), channel_id=1, source_target_pairs={{0,2},{1,3},{2,0},{3,1},{4,6},{5,7},{6,4},{7,5},{8,10},{9,11},{10,... | collective-permute-start | bytes 294920 | tf_op jit(solution)/shard_map/ppermute | solution.py:459
  157.9 17.6 %collective-permute-start.16 = (f32[1,128]{1,0:T(1,128)S(1)}, f32[1,128]{1,0:T(1,128)S(1)}, u32[]{:S(2)}, u32[]{:S(2)}) collective-permute-start(f32[1,128]{1,0:T(1,128)S(1)} %broadcast_in_dim.40), channel_id=1, source_target_pairs={{0,2},{1,3},{4,6},{5,7},{10,8},{11,9},{14,12},{15,13},{16,18},{17,... | collective-permute-start | bytes 1544 | tf_op jit(solution)/shard_map/ppermute | solution.py:356
  175.5 2.1 %copy-start.1 = (bf16[96,1536]{1,0:T(8,128)(2,1)S(1)}, bf16[96,1536]{1,0:T(8,128)(2,1)}, u32[]{:S(2)}) copy-start(bf16[96,1536]{1,0:T(8,128)(2,1)} %get-tuple-element.29.real_ref) | copy-start | bytes 884740

commit v11 on v8

--- a/solution.py
+++ b/solution.py
@@ -396,8 +396,7 @@
     recv_col8 = jnp.broadcast_to(recv_col[None], (8, tile))
 
     picked = pick_columns(traces, miss_col_lanes, recv_col8, live8, misses)
-    both = transpose(jnp.concatenate(picked))
-    extra = [both[:misses], both[misses:]]
+    both = jnp.concatenate(picked)
     apart = row_index ^ col_index
     strides = [2**bit for bit in range(grid_size.bit_length() - 1)]
     terms, extra_terms = [], []
@@ -430,7 +429,9 @@
             return sources_of(up, down, offset, grid_size, row_index)
 
         hop(1)
-        extra, up[-1], down[-1] = lax.optimization_barrier((extra, up[-1], down[-1]))
+        both, up[-1], down[-1] = lax.optimization_barrier((both, up[-1], down[-1]))
+        both = transpose(both)
+        extra = [both[:misses], both[misses:]]
         hop(2)
         other_core = [(i, i ^ 1) for i in range(grid_size)]
         odd = apart & 1
@@ -450,18 +451,20 @@
             )
             return add_up(keep + lax.ppermute(sent, "col", other_core), first, strides[1:-1], 1)
 
-        sums = [pair_sum(0, recv_col8)]
-        shrunk, up[-1], down[-1] = lax.optimization_barrier((shrink(sums[0]), up[-1], down[-1]))
+        extra, mask = lax.optimization_barrier((extra, recv_col8))
+        sums = [pair_sum(0, mask)]
+        shrunk = shrink(sums[0])
         for distance in range(3, grid_size):
             hop(distance)
-        got = [last(shrunk, 0, 1)]
+        got = []
         mask = recv_col8
         for first in range(2, grid_size, 2):
             if first == grid_size - 2:
                 group = [(pick, apart ^ offset, sources) for offset in range(grid_size)
                          for pick, sources in [options(offset)]]
                 rest = extra_products(extra, group)
-                mask, got[0], rest = lax.optimization_barrier((mask, got[0], rest))
+                mask, shrunk, rest = lax.optimization_barrier((mask, shrunk, rest))
+                got.insert(0, last(shrunk, 0, 1))
             sums.append(pair_sum(first, mask))
             got.append(last(shrink(sums[-1]), first, 1))
         whole_sum = None

time: 178 us -> 181 us (1.017)
    ppermute x9, waiting for transfers between devices: 5.69 us -> 25.8 us  [move(): return lax.ppermute(block, ('row', 'col'), route)]
    ppermute x3, waiting for transfers between devices: 44.4 us -> 29 us  [hop(): down.append(lax.ppermute(down[-1], 'row', back))]
    ppermute x2, waiting for transfers between devices: 14.3 us -> 11.8 us  [local(): arrive = lax.ppermute(rest[1::2], 'col', pairs)]
    ppermute x2, waiting for transfers between devices: 4.58 us -> 2.13 us  [pair_sum(): lax.ppermute(sent, 'col', other_core)]
    ppermute x3, waiting for transfers between devices: 12.7 us -> 14.5 us  [hop(): up.append(lax.ppermute(up[-1], 'row', ends))]
  transfers between devices with their start and end apart: 19 -> 19, of which waited for: 8 -> 8; matrix products, arithmetic and copies ran while one was open for 7% -> 3% of each run, Pallas kernels for 6% -> 10%
where the time goes in v11:
time: 181 us; the launch traced here: 178 us
  waiting for transfers between devices  83.2 us (46%)
  starting transfers between devices  43.9 us (24%)
  Pallas kernels  32.7 us (18%)
  other arithmetic  12.1 us (7%)
  local copies, waits for them, and re-layouts  4.26 us (2%)
  between operations  1.84 us (1%)
    ppermute x3, waiting for transfers between devices, hop(): down.append(lax.ppermute(down[-1], 'row', back))  29 us
    ppermute x9, starting transfers between devices, move(): return lax.ppermute(block, ('row', 'col'), route)  26.3 us
    ppermute x9, waiting for transfers between devices, move(): return lax.ppermute(block, ('row', 'col'), route)  25.8 us
    pallas_call x2, Pallas kernels, products(): pl.pallas_call(functools.partial(product_kernel, counts), grid=(rows // b...  18.3 us
    ppermute x3, waiting for transfers between devices, hop(): up.append(lax.ppermute(up[-1], 'row', ends))  14.5 us
    ppermute x3, starting transfers between devices, hop(): up.append(lax.ppermute(up[-1], 'row', ends))  12.6 us
    ppermute x2, waiting for transfers between devices, local(): arrive = lax.ppermute(rest[1::2], 'col', pairs)  11.8 us
    pallas_call x1, Pallas kernels, pick_columns(): pl.pallas_call(pick_kernel, grid=(rows // block,), in_specs=[pl.BlockSpec...  6.28 us
  transfers between devices with their start and end apart: 19, of which 8 were waited for; matrix products, arithmetic and copies ran while one was open for 3% of the time, Pallas kernels for 10%

profile of v11, /device:TPU:1, one launch (start us, length us, event | category | flops | bytes accessed | tf_op | source)
XLA Modules:
  0.0 178.0 jit_solution(12598101631935741073)
XLA Ops:
  0.0 1.3 cut_window.1
  1.3 1.3 collective-permute-start.1
  2.6 4.6 %collective-permute-start.3 = (bf16[1536,128]{1,0:T(8,128)(2,1)S(1)}, bf16[1536,128]{1,0:T(8,128)(2,1)S(1)}, u32[]{:S(2)}, u32[]{:S(2)}) collective-permute-start(bf16[1536,128]{1,0:T(8,128)(2,1)S(1)} %get-tuple-element.26), channel_id=1, source_target_pairs={{0,0},{1,4},{4,1},{5,5},{10,10},{11,14},{14,11},{15,15},{16,16},{1... | collective-permute-start | bytes 1179656 | tf_op jit(solution)/shard_map/ppermute | solution.py:367
  7.2 1.9 %collective-permute-start = (bf16[1536,128]{1,0:T(8,128)(2,1)S(1)}, bf16[1536,128]{1,0:T(8,128)(2,1)S(1)}, u32[]{:S(2)}, u32[]{:S(2)}) collective-permute-start(bf16[1536,128]{1,0:T(8,128)(2,1)S(1)} %get-tuple-element.25), channel_id=1, source_target_pairs={{0,0},{1,4},{2,8},{3,12},{4,1},{5,5},{6,9},{7,13},{8,2},{9,6},{10,... | collective-permute-start | bytes 1179656 | tf_op jit(solution)/shard_map/ppermute | solution.py:367
  9.2 4.4 %collective-permute-done.1 = bf16[1536,128]{1,0:T(8,128)(2,1)S(1)} collective-permute-done((bf16[1536,128]{1,0:T(8,128)(2,1)S(1)}, bf16[1536,128]{1,0:T(8,128)(2,1)S(1)}, u32[]{:S(2)}, u32[]{:S(2)}) %collective-permute-start.1) | collective-permute-done | bytes 393248 | tf_op jit(solution)/shard_map/ppermute | solution.py:367
  13.5 6.1 %collective-permute-start.2 = (bf16[1536,128]{1,0:T(8,128)(2,1)S(1)}, bf16[1536,128]{1,0:T(8,128)(2,1)S(1)}, u32[]{:S(2)}, u32[]{:S(2)}) collective-permute-start(bf16[1536,128]{1,0:T(8,128)(2,1)S(1)} %collective-permute-done.1), channel_id=1, source_target_pairs={{0,8},{1,12},{4,9},{5,13},{10,2},{11,6},{14,3},{15,7},{16,24},{17,... | collective-permute-start | bytes 1179656 | tf_op jit(solution)/shard_map/ppermute | solution.py:367
  19.7 0.1 fusion
  19.9 0.1 dynamic_slice.14
  20.0 0.1 dynamic_slice.16
  20.1 6.3 %pick_columns.1 = (bf16[96,1536]{1,0:T(8,128)(2,1)S(1)}, bf16[96,1536]{1,0:T(8,128)(2,1)S(1)}) custom-call(bf16[2,1536,1536]{2,1,0:T(8,128)(2,1)} %tile_ref.1, s32[1,128]{1,0:T(1,128)S(1)} %pad_bitcast_fusion.miss_ref, bf16[8,1536]{1,0:T(8,128)(2,1)S(1)} %broadcast_in_dim.16.recv_ref, f32[8,1536]{1,0:T(8,128)S(1)} %broadcast_in_dim.36.live_ref), custom_call_target="tpu_custom_call" | custom-call | flops 37748736 | bytes 147456 | tf_op jit(solution)/shard_map/pick_columns/pallas_call | solution.py:105
  26.4 1.8 %collective-permute-done.2.refs_1_ = bf16[1536,128]{1,0:T(8,128)(2,1)S(1)} collective-permute-done((bf16[1536,128]{1,0:T(8,128)(2,1)S(1)}, bf16[1536,128]{1,0:T(8,128)(2,1)S(1)}, u32[]{:S(2)}, u32[]{:S(2)}) %collective-permute-start.2) | collective-permute-done | bytes 393248 | tf_op jit(solution)/shard_map/ppermute | solution.py:367
  28.2 0.5 fill_window.1.refs_4_.refs_7_.refs_0_
  28.7 9.4 %collective-permute-start.4 = (bf16[1536,256]{1,0:T(8,128)(2,1)S(1)}, bf16[1536,256]{1,0:T(8,128)(2,1)S(1)}, u32[]{:S(2)}, u32[]{:S(2)}) collective-permute-start(bf16[1536,256]{1,0:T(8,128)(2,1)S(1)} %fill_window.1.refs_4_.refs_7_.refs_0_), channel_id=1, source_target_pairs={{0,4},{4,8},{8,12},{1,5},{5,9},{9,13},{2,6},{6,10},{10,14},{3,7},{... | collective-permute-start | bytes 2359304 | tf_op jit(solution)/shard_map/ppermute | solution.py:411
  38.1 1.3 collective-permute-start.5
  39.4 0.9 pad_maximum_fusion
  40.3 14.5 %collective-permute-done.4.refs_6_.refs_9_.refs_2_.refs_7_.refs_8_.refs_14_ = bf16[1536,256]{1,0:T(8,128)(2,1)S(1)} collective-permute-done((bf16[1536,256]{1,0:T(8,128)(2,1)S(1)}, bf16[1536,256]{1,0:T(8,128)(2,1)S(1)}, u32[]{:S(2)}, u32[]{:S(2)}) %collective-permute-start.4) | collective-permute-done | bytes 786464 | tf_op jit(solution)/shard_map/ppermute | solution.py:411
  54.8 4.3 %collective-permute-done.5.refs_5_.refs_8_.refs_1_.refs_6_.refs_7_.refs_13_ = bf16[1536,256]{1,0:T(8,128)(2,1)S(1)} collective-permute-done((bf16[1536,256]{1,0:T(8,128)(2,1)S(1)}, bf16[1536,256]{1,0:T(8,128)(2,1)S(1)}, u32[]{:S(2)}, u32[]{:S(2)}) %collective-permute-start.5) | collective-permute-done | bytes 786464 | tf_op jit(solution)/shard_map/ppermute | solution.py:412
  59.1 2.2 %collective-permute-start.6 = (bf16[192,1536]{1,0:T(8,128)(2,1)}, bf16[192,1536]{1,0:T(8,128)(2,1)}, u32[]{:S(2)}, u32[]{:S(2)}) collective-permute-start(bf16[192,1536]{1,0:T(8,128)(2,1)} %pad_maximum_fusion), channel_id=1, source_target_pairs={{0,0},{1,4},{2,8},{3,12},{4,1},{5,5},{6,9},{7,13},{8,2},{9,6},{10,... | collective-permute-start | bytes 1769480 | tf_op jit(solution)/shard_map/ppermute | solution.py:367
  61.3 0.1 pad_add_fusion.pick_ref
  61.4 1.3 collective-permute-start.8
  62.6 1.6 collective-permute-start.9
  64.2 19.5 %collective-permute-done.6 = bf16[192,1536]{1,0:T(8,128)(2,1)} collective-permute-done((bf16[192,1536]{1,0:T(8,128)(2,1)}, bf16[192,1536]{1,0:T(8,128)(2,1)}, u32[]{:S(2)}, u32[]{:S(2)}) %collective-permute-start.6) | collective-permute-done | bytes 589856 | tf_op jit(solution)/shard_map/ppermute | solution.py:367
  83.7 1.8 %fusion.2 = (bf16[96,1536]{1,0:T(8,128)(2,1)S(1)}, bf16[96,1536]{1,0:T(8,128)(2,1)}) fusion(bf16[192,1536]{1,0:T(8,128)(2,1)} %collective-permute-done.6), kind=kLoop, calls=%fused_computation.18 | loop fusion | bytes 1179648 | tf_op jit(solution)/shard_map/slice | solution.py:434
  85.6 8.5 %products.2 = (f32[1536,256]{1,0:T(8,128)S(1)}, f32[1536,256]{1,0:T(8,128)}) custom-call(s32[2]{0:T(128)S(1)} %pad_add_fusion.pick_ref, bf16[8,1536]{1,0:T(8,128)(2,1)S(1)} %broadcast_in_dim.16.recv_ref, bf16[2,1536,1536]{2,1,0:T(8,128)(2,1)} %tile_ref.1, bf16[2,1536,1536]{2,1,0:T(8,128)(2,1)} %tile_ref.1, bf16[2,1536,1536]{2,1,0:T(8,128)(2,1)} %tile_ref.1, ...), custom_call_target="tpu_custom_call" | custom-call | flops 150994944 | bytes 24576 | tf_op jit(solution)/shard_map/products/pallas_call | solution.py:230
  94.1 1.1 copy-done.4
  95.2 1.3 collective-permute-start.10
  96.5 1.6 collective-permute-start.11
  98.1 0.1 stack.53.pick_ref
  98.2 0.1 pad_add_fusion.1.pick_ref
  98.3 24.7 %collective-permute-done.10.refs_5_.refs_6_.refs_12_ = bf16[1536,256]{1,0:T(8,128)(2,1)} collective-permute-done((bf16[1536,256]{1,0:T(8,128)(2,1)S(1)}, bf16[1536,256]{1,0:T(8,128)(2,1)}, u32[]{:S(2)}, u32[]{:S(2)}) %collective-permute-start.10) | collective-permute-done | bytes 786464 | tf_op jit(solution)/shard_map/ppermute | solution.py:412
  123.0 1.0 copy-done
  123.9 3.5 %extra_products.1 = f32[4,96,256]{2,1,0:T(8,128)S(1)} custom-call(s32[8]{0:T(128)S(1)} %stack.53.pick_ref, bf16[96,1536]{1,0:T(8,128)(2,1)S(1)} %copy-done, bf16[96,1536]{1,0:T(8,128)(2,1)S(1)} %get-tuple-element.29.imag_ref, bf16[1536,256]{1,0:T(8,128)(2,1)S(1)} %fill_window.1.refs_4_.refs_7_.refs_0_, ...), custom_call_target="tpu_custom_call" | custom-call | flops 18874368 | bytes 24576 | tf_op jit(solution)/shard_map/extra_products/pallas_call | solution.py:264
  127.4 3.5 %abs_reduce_fusion.1 = (f32[]{:T(128)}, f32[1536,256]{1,0:T(8,128)}) fusion(f32[1536,256]{1,0:T(8,128)S(1)} %copy-done.5, f32[1536,256]{1,0:T(8,128)} %collective-permute-done.7), kind=kLoop, calls=%fused_computation.4 | loop fusion | flops 1179647 | bytes 4718596 | tf_op jit(solution)/shard_map/reduce_max | solution.py:420
  131.6 2.5 %multiply_convert_fusion.1 = f16[1536,256]{1,0:T(8,128)(2,1)} fusion(f32[1536,256]{1,0:T(8,128)} %get-tuple-element.44, f32[]{:T(128)S(6)} %div.18), kind=kLoop, calls=%fused_computation.3 | loop fusion | flops 786432 | bytes 2359300 | tf_op jit(solution)/shard_map/convert_element_type | solution.py:421
  134.1 9.9 %products.3 = (f32[1536,256]{1,0:T(8,128)}, f32[1536,256]{1,0:T(8,128)}) custom-call(s32[2]{0:T(128)S(1)} %pad_add_fusion.1.pick_ref, bf16[8,1536]{1,0:T(8,128)(2,1)S(1)} %broadcast_in_dim.16.recv_ref, bf16[2,1536,1536]{2,1,0:T(8,128)(2,1)} %tile_ref.1, bf16[2,1536,1536]{2,1,0:T(8,128)(2,1)} %tile_ref.1, bf16[2,1536,1536]{2,1,0:T(8,128)(2,1)} %tile_ref.1, ...), custom_call_target="tpu_custom_call" | custom-call | flops 150994944 | bytes 24576 | tf_op jit(solution)/shard_map/products/pallas_call | solution.py:230
  144.0 1.0 collective-permute-start.14
  145.0 0.1 collective-permute-start.17
  145.1 1.3 collective-permute-start.12
  146.4 2.1 %collective-permute-done.14 = f32[1536,256]{1,0:T(8,128)S(1)} collective-permute-done((f32[1536,256]{1,0:T(8,128)}, f32[1536,256]{1,0:T(8,128)S(1)}, u32[]{:S(2)}, u32[]{:S(2)}) %collective-permute-start.14) | collective-permute-done | bytes 1572896 | tf_op jit(solution)/shard_map/ppermute | solution.py:452
  148.5 2.3 %abs_reduce_fusion = (f32[]{:T(128)}, f32[1536,256]{1,0:T(8,128)S(1)}) fusion(f32[1536,256]{1,0:T(8,128)} %get-tuple-element.38, f32[1536,256]{1,0:T(8,128)S(1)} %collective-permute-done.14), kind=kLoop, calls=%fused_computation.2 | loop fusion | flops 1179647 | bytes 4718596 | tf_op jit(solution)/shard_map/reduce_max | solution.py:420
  151.5 0.2 multiply_convert_fusion
  151.7 3.7 %collective-permute-start.15 = (f16[1536,256]{1,0:T(8,128)(2,1)S(1)}, f16[1536,256]{1,0:T(8,128)(2,1)}, u32[]{:S(2)}, u32[]{:S(2)}) collective-permute-start(f16[1536,256]{1,0:T(8,128)(2,1)S(1)} %multiply_convert_fusion), channel_id=1, source_target_pairs={{0,2},{1,3},{4,6},{5,7},{10,8},{11,9},{14,12},{15,13},{16,18},{17,... | collective-permute-start | bytes 2359304 | tf_op jit(solution)/shard_map/ppermute | solution.py:367
  155.4 0.1 collective-permute-start.18
  155.5 1.3 collective-permute-start.13
  156.8 4.0 %collective-permute-start.16 = (f32[1,128]{1,0:T(1,128)S(1)}, f32[1,128]{1,0:T(1,128)S(1)}, u32[]{:S(2)}, u32[]{:S(2)}) collective-permute-start(f32[1,128]{1,0:T(1,128)S(1)} %broadcast_in_dim.40), channel_id=1, source_target_pairs={{0,2},{1,3},{4,6},{5,7},{10,8},{11,9},{14,12},{15,13},{16,18},{17,... | collective-permute-start | bytes 1544 | tf_op jit(solution)/shard_map/ppermute | solution.py:367
  160.8 11.8 %collective-permute-done.18 = f32[1,96,256]{2,1,0:T(8,128)S(1)} collective-permute-done((f32[1,96,256]{2,1,0:T(8,128)S(1)}, f32[1,96,256]{2,1,0:T(8,128)S(1)}, u32[]{:S(2)}, u32[]{:S(2)}) %collective-permute-start.18) | collective-permute-done | bytes 98336 | tf_op jit(solution)/shard_map/ppermute | solution.py:478
  172.7 2.4 %add_add_fusion.refs_0_ = f32[1536,256]{1,0:T(8,128)S(1)} fusion(f16[1536,256]{1,0:T(8,128)(2,1)} %collective-permute-done.15, f32[1536,256]{1,0:T(8,128)} %copy-done.6, f16[1536,256]{1,0:T(8,128)(2,1)} %collective-permute-done.12, f32[1536,256]{1,0:T(8,128)} %get-tuple-element.44, f32[]{:T(128)S(1)} %bitcast.24, f32[]{:T(128)S(1)} %bitcast.23, pred[]{:T(512)S(6)} %eq.23, ...), kind=kLoop, calls=%fused_computation | loop fusion | flops 3538944 | bytes 6291466 | tf_op jit(solution)/shard_map/add | solution.py:474
  175.1 2.8 %finish.1 = f32[2,1536,128]{2,1,0:T(8,128)} custom-call(f32[2]{0:T(128)S(1)} %broadcast_multiply_fusion.wave_ref, s32[96]{0:T(128)S(1)} %get-tuple-element.48.miss_ref, bf16[8,1536]{1,0:T(8,128)(2,1)S(1)} %broadcast_in_dim.16.recv_ref, bf16[2,1536,1536]{2,1,0:T(8,128)(2,1)} %tile_ref.1, bf16[96,1536]{1,0:T(8,128)(2,1)S(1)} %copy-done.1, ...), custom_call_target="tpu_custom_call" | custom-call | flops 61440 | bytes 122880 | tf_op jit(solution)/shard_map/finish/pallas_call | solution.py:304
  (44 shorter events, 0.2 us)
Async XLA Ops:
  0.0 9.1 %copy-start.8 = (s32[4,96]{1,0:T(4,128)S(1)}, s32[4,96]{1,0:T(4,128)}, u32[]{:S(2)}) copy-start(s32[4,96]{1,0:T(4,128)} %param.6) | copy-start | bytes 4612
  0.0 19.8 %copy-start.7 = (s32[6144]{0:T(1024)S(1)}, s32[6144]{0:T(1024)}, u32[]{:S(2)}) copy-start(s32[6144]{0:T(1024)} %param.5) | copy-start | bytes 73732
  1.3 12.2 %collective-permute-start.1 = (bf16[1536,128]{1,0:T(8,128)(2,1)S(1)}, bf16[1536,128]{1,0:T(8,128)(2,1)S(1)}, u32[]{:S(2)}, u32[]{:S(2)}) collective-permute-start(bf16[1536,128]{1,0:T(8,128)(2,1)S(1)} %get-tuple-element.26), channel_id=1, source_target_pairs={{2,0},{3,1},{6,4},{7,5},{8,10},{9,11},{12,14},{13,15},{18,16},{19,... | collective-permute-start | bytes 1179656 | tf_op jit(solution)/shard_map/ppermute | solution.py:367
  2.6 23.8 %collective-permute-start.3 = (bf16[1536,128]{1,0:T(8,128)(2,1)S(1)}, bf16[1536,128]{1,0:T(8,128)(2,1)S(1)}, u32[]{:S(2)}, u32[]{:S(2)}) collective-permute-start(bf16[1536,128]{1,0:T(8,128)(2,1)S(1)} %get-tuple-element.26), channel_id=1, source_target_pairs={{0,0},{1,4},{4,1},{5,5},{10,10},{11,14},{14,11},{15,15},{16,16},{1... | collective-permute-start | bytes 1179656 | tf_op jit(solution)/shard_map/ppermute | solution.py:367
  7.2 19.2 %collective-permute-start = (bf16[1536,128]{1,0:T(8,128)(2,1)S(1)}, bf16[1536,128]{1,0:T(8,128)(2,1)S(1)}, u32[]{:S(2)}, u32[]{:S(2)}) collective-permute-start(bf16[1536,128]{1,0:T(8,128)(2,1)S(1)} %get-tuple-element.25), channel_id=1, source_target_pairs={{0,0},{1,4},{2,8},{3,12},{4,1},{5,5},{6,9},{7,13},{8,2},{9,6},{10,... | collective-permute-start | bytes 1179656 | tf_op jit(solution)/shard_map/ppermute | solution.py:367
  13.5 14.7 %collective-permute-start.2 = (bf16[1536,128]{1,0:T(8,128)(2,1)S(1)}, bf16[1536,128]{1,0:T(8,128)(2,1)S(1)}, u32[]{:S(2)}, u32[]{:S(2)}) collective-permute-start(bf16[1536,128]{1,0:T(8,128)(2,1)S(1)} %collective-permute-done.1), channel_id=1, source_target_pairs={{0,8},{1,12},{4,9},{5,13},{10,2},{11,6},{14,3},{15,7},{16,24},{17,... | collective-permute-start | bytes 1179656 | tf_op jit(solution)/shard_map/ppermute | solution.py:367
  28.7 26.1 %collective-permute-start.4 = (bf16[1536,256]{1,0:T(8,128)(2,1)S(1)}, bf16[1536,256]{1,0:T(8,128)(2,1)S(1)}, u32[]{:S(2)}, u32[]{:S(2)}) collective-permute-start(bf16[1536,256]{1,0:T(8,128)(2,1)S(1)} %fill_window.1.refs_4_.refs_7_.refs_0_), channel_id=1, source_target_pairs={{0,4},{4,8},{8,12},{1,5},{5,9},{9,13},{2,6},{6,10},{10,14},{3,7},{... | collective-permute-start | bytes 2359304 | tf_op jit(solution)/shard_map/ppermute | solution.py:411
  38.1 21.0 %collective-permute-start.5 = (bf16[1536,256]{1,0:T(8,128)(2,1)S(1)}, bf16[1536,256]{1,0:T(8,128)(2,1)S(1)}, u32[]{:S(2)}, u32[]{:S(2)}) collective-permute-start(bf16[1536,256]{1,0:T(8,128)(2,1)S(1)} %fill_window.1.refs_4_.refs_7_.refs_0_), channel_id=1, source_target_pairs={{4,0},{8,4},{12,8},{5,1},{9,5},{13,9},{6,2},{10,6},{14,10},{7,3},{... | collective-permute-start | bytes 2359304 | tf_op jit(solution)/shard_map/ppermute | solution.py:412
  59.1 24.7 %collective-permute-start.6 = (bf16[192,1536]{1,0:T(8,128)(2,1)}, bf16[192,1536]{1,0:T(8,128)(2,1)}, u32[]{:S(2)}, u32[]{:S(2)}) collective-permute-start(bf16[192,1536]{1,0:T(8,128)(2,1)} %pad_maximum_fusion), channel_id=1, source_target_pairs={{0,0},{1,4},{2,8},{3,12},{4,1},{5,5},{6,9},{7,13},{8,2},{9,6},{10,... | collective-permute-start | bytes 1769480 | tf_op jit(solution)/shard_map/ppermute | solution.py:367
  61.4 33.9 %collective-permute-start.8 = (bf16[1536,256]{1,0:T(8,128)(2,1)S(1)}, bf16[1536,256]{1,0:T(8,128)(2,1)S(1)}, u32[]{:S(2)}, u32[]{:S(2)}) collective-permute-start(bf16[1536,256]{1,0:T(8,128)(2,1)S(1)} %collective-permute-done.5.refs_5_.refs_8_.refs_1_.refs_6_.refs_7_.refs_13_), channel_id=1, source_target_pairs={{4,0},{8,4},{5,1},{9,5},{6,2},{10,6},{7,3},{11,7},{20,16},{24,20},... | collective-permute-start | bytes 2359304 | tf_op jit(solution)/shard_map/ppermute | solution.py:412
  62.6 33.9 %collective-permute-start.9 = (bf16[1536,256]{1,0:T(8,128)(2,1)S(1)}, bf16[1536,256]{1,0:T(8,128)(2,1)}, u32[]{:S(2)}, u32[]{:S(2)}) collective-permute-start(bf16[1536,256]{1,0:T(8,128)(2,1)S(1)} %collective-permute-done.4.refs_6_.refs_9_.refs_2_.refs_7_.refs_8_.refs_14_), channel_id=1, source_target_pairs={{4,8},{8,12},{5,9},{9,13},{6,10},{10,14},{7,11},{11,15},{20,24},{2... | collective-permute-start | bytes 2359304 | tf_op jit(solution)/shard_map/ppermute | solution.py:411
  94.1 1.1 copy-start.4
  95.2 32.2 %collective-permute-start.7 = (f32[1536,256]{1,0:T(8,128)}, f32[1536,256]{1,0:T(8,128)}, u32[]{:S(2)}, u32[]{:S(2)}) collective-permute-start(f32[1536,256]{1,0:T(8,128)} %get-tuple-element.34), channel_id=1, source_target_pairs={{0,1},{1,0},{2,3},{3,2},{4,5},{5,4},{6,7},{7,6},{8,9},{9,8},{10,11... | collective-permute-start | bytes 4718600 | tf_op jit(solution)/shard_map/ppermute | solution.py:452
  95.2 27.8 %collective-permute-start.10 = (bf16[1536,256]{1,0:T(8,128)(2,1)S(1)}, bf16[1536,256]{1,0:T(8,128)(2,1)}, u32[]{:S(2)}, u32[]{:S(2)}) collective-permute-start(bf16[1536,256]{1,0:T(8,128)(2,1)S(1)} %collective-permute-done.8.refs_3_.refs_4_.refs_10_), channel_id=1, source_target_pairs={{4,0},{5,1},{6,2},{7,3},{20,16},{21,17},{22,18},{23,19}} | collective-permute-start | bytes 2359304 | tf_op jit(solution)/shard_map/ppermute | solution.py:412
  96.5 26.5 %collective-permute-start.11 = (bf16[1536,256]{1,0:T(8,128)(2,1)}, bf16[1536,256]{1,0:T(8,128)(2,1)}, u32[]{:S(2)}, u32[]{:S(2)}) collective-permute-start(bf16[1536,256]{1,0:T(8,128)(2,1)} %collective-permute-done.9.refs_4_.refs_5_.refs_11_), channel_id=1, source_target_pairs={{8,12},{9,13},{10,14},{11,15},{24,28},{25,29},{26,30},{27,31}} | collective-permute-start | bytes 2359304 | tf_op jit(solution)/shard_map/ppermute | solution.py:411
  123.0 1.0 copy-start
  123.9 3.5 %copy-start.5 = (f32[1536,256]{1,0:T(8,128)S(1)}, f32[1536,256]{1,0:T(8,128)}, u32[]{:S(2)}) copy-start(f32[1536,256]{1,0:T(8,128)} %copy-done.4) | copy-start | bytes 4718596
  127.4 3.5 %copy-start.2 = (f32[4,96,256]{2,1,0:T(8,128)}, f32[4,96,256]{2,1,0:T(8,128)S(1)}, u32[]{:S(2)}) copy-start(f32[4,96,256]{2,1,0:T(8,128)S(1)} %extra_products.1) | copy-start | bytes 1179652
  134.1 10.9 %copy-start.3 = (f32[4,96,256]{2,1,0:T(8,128)S(1)}, f32[4,96,256]{2,1,0:T(8,128)}, u32[]{:S(2)}) copy-start(f32[4,96,256]{2,1,0:T(8,128)} %copy-done.2) | copy-start | bytes 1179652
  144.0 4.5 %collective-permute-start.14 = (f32[1536,256]{1,0:T(8,128)}, f32[1536,256]{1,0:T(8,128)S(1)}, u32[]{:S(2)}, u32[]{:S(2)}) collective-permute-start(f32[1536,256]{1,0:T(8,128)} %get-tuple-element.39), channel_id=1, source_target_pairs={{0,1},{1,0},{2,3},{3,2},{4,5},{5,4},{6,7},{7,6},{8,9},{9,8},{10,11... | collective-permute-start | bytes 4718600 | tf_op jit(solution)/shard_map/ppermute | solution.py:452
  145.0 10.4 %collective-permute-start.17 = (f32[2,96,256]{2,1,0:T(8,128)S(1)}, f32[2,96,256]{2,1,0:T(8,128)S(1)}, u32[]{:S(2)}, u32[]{:S(2)}) collective-permute-start(f32[2,96,256]{2,1,0:T(8,128)S(1)} %slice.31), channel_id=1, source_target_pairs={{0,1},{1,0},{2,3},{3,2},{4,5},{5,4},{6,7},{7,6},{8,9},{9,8},{10,11... | collective-permute-start | bytes 589832 | tf_op jit(solution)/shard_map/ppermute | solution.py:478
  145.1 27.6 %collective-permute-start.12 = (f16[1536,256]{1,0:T(8,128)(2,1)}, f16[1536,256]{1,0:T(8,128)(2,1)}, u32[]{:S(2)}, u32[]{:S(2)}) collective-permute-start(f16[1536,256]{1,0:T(8,128)(2,1)} %multiply_convert_fusion.1), channel_id=1, source_target_pairs={{2,0},{3,1},{6,4},{7,5},{8,10},{9,11},{12,14},{13,15},{18,16},{19,... | collective-permute-start | bytes 2359304 | tf_op jit(solution)/shard_map/ppermute | solution.py:367
  150.8 4.6 %copy-start.6 = (f32[1536,256]{1,0:T(8,128)}, f32[1536,256]{1,0:T(8,128)S(1)}, u32[]{:S(2)}) copy-start(f32[1536,256]{1,0:T(8,128)S(1)} %get-tuple-element.42) | copy-start | bytes 4718596
  151.5 4.0 %copy-start.9 = (f32[2]{0:T(128)S(1)}, f32[2]{0:T(128)}, u32[]{:S(2)}) copy-start(f32[2]{0:T(128)} %param.7) | copy-start | bytes 28
  151.7 21.0 %collective-permute-start.15 = (f16[1536,256]{1,0:T(8,128)(2,1)S(1)}, f16[1536,256]{1,0:T(8,128)(2,1)}, u32[]{:S(2)}, u32[]{:S(2)}) collective-permute-start(f16[1536,256]{1,0:T(8,128)(2,1)S(1)} %multiply_convert_fusion), channel_id=1, source_target_pairs={{0,2},{1,3},{4,6},{5,7},{10,8},{11,9},{14,12},{15,13},{16,18},{17,... | collective-permute-start | bytes 2359304 | tf_op jit(solution)/shard_map/ppermute | solution.py:367
  155.4 17.2 %collective-permute-start.18 = (f32[1,96,256]{2,1,0:T(8,128)S(1)}, f32[1,96,256]{2,1,0:T(8,128)S(1)}, u32[]{:S(2)}, u32[]{:S(2)}) collective-permute-start(f32[1,96,256]{2,1,0:T(8,128)S(1)} %slice.37), channel_id=1, source_target_pairs={{0,2},{1,3},{2,0},{3,1},{4,6},{5,7},{6,4},{7,5},{8,10},{9,11},{10,... | collective-permute-start | bytes 294920 | tf_op jit(solution)/shard_map/ppermute | solution.py:478
  155.5 17.1 %collective-permute-start.13 = (f32[1,128]{1,0:T(1,128)S(1)}, f32[1,128]{1,0:T(1,128)S(1)}, u32[]{:S(2)}, u32[]{:S(2)}) collective-permute-start(f32[1,128]{1,0:T(1,128)S(1)} %broadcast_in_dim.39), channel_id=1, source_target_pairs={{2,0},{3,1},{6,4},{7,5},{8,10},{9,11},{12,14},{13,15},{18,16},{19,... | collective-permute-start | bytes 1544 | tf_op jit(solution)/shard_map/ppermute | solution.py:367
  156.8 15.8 %collective-permute-start.16 = (f32[1,128]{1,0:T(1,128)S(1)}, f32[1,128]{1,0:T(1,128)S(1)}, u32[]{:S(2)}, u32[]{:S(2)}) collective-permute-start(f32[1,128]{1,0:T(1,128)S(1)} %broadcast_in_dim.40), channel_id=1, source_target_pairs={{0,2},{1,3},{4,6},{5,7},{10,8},{11,9},{14,12},{15,13},{16,18},{17,... | collective-permute-start | bytes 1544 | tf_op jit(solution)/shard_map/ppermute | solution.py:367
  172.7 2.4 %copy-start.1 = (bf16[96,1536]{1,0:T(8,128)(2,1)S(1)}, bf16[96,1536]{1,0:T(8,128)(2,1)}, u32[]{:S(2)}) copy-start(bf16[96,1536]{1,0:T(8,128)(2,1)} %get-tuple-element.28.real_ref) | copy-start | bytes 884740

commit v12 on v8

--- a/solution.py
+++ b/solution.py
@@ -461,7 +461,7 @@
                 group = [(pick, apart ^ offset, sources) for offset in range(grid_size)
                          for pick, sources in [options(offset)]]
                 rest = extra_products(extra, group)
-                mask, got[0], rest = lax.optimization_barrier((mask, got[0], rest))
+                mask, rest = lax.optimization_barrier((mask, rest))
             sums.append(pair_sum(first, mask))
             got.append(last(shrink(sums[-1]), first, 1))
         whole_sum = None

time: 178 us -> 178 us (level)
    ppermute x3, waiting for transfers between devices: 44.4 us -> 47 us  [hop(): down.append(lax.ppermute(down[-1], 'row', back))]
    ppermute x2, waiting for transfers between devices: 14.3 us -> 12.3 us  [local(): arrive = lax.ppermute(rest[1::2], 'col', pairs)]
  transfers between devices with their start and end apart: 19 -> 19, of which waited for: 8 -> 8; matrix products, arithmetic and copies ran while one was open for 7% -> 7% of each run, Pallas kernels for 6% -> 4%
where the time goes in v12:
time: 178 us; the launch traced here: 175 us
  waiting for transfers between devices  80.7 us (45%)
  starting transfers between devices  44 us (25%)
  Pallas kernels  32.8 us (18%)
  other arithmetic  12.8 us (7%)
  local copies, waits for them, and re-layouts  3.13 us (2%)
  between operations  1.85 us (1%)
    ppermute x3, waiting for transfers between devices, hop(): down.append(lax.ppermute(down[-1], 'row', back))  47 us
    ppermute x9, starting transfers between devices, move(): return lax.ppermute(block, ('row', 'col'), route)  26 us
    pallas_call x2, Pallas kernels, products(): pl.pallas_call(functools.partial(product_kernel, counts), grid=(rows // b...  18.6 us
    ppermute x3, waiting for transfers between devices, hop(): up.append(lax.ppermute(up[-1], 'row', ends))  12.7 us
    ppermute x2, waiting for transfers between devices, local(): arrive = lax.ppermute(rest[1::2], 'col', pairs)  12.3 us
    ppermute x3, starting transfers between devices, hop(): up.append(lax.ppermute(up[-1], 'row', ends))  12.1 us
    pallas_call x1, Pallas kernels, pick_columns(): pl.pallas_call(pick_kernel, grid=(rows // block,), in_specs=[pl.BlockSpec...  6.28 us
    ppermute x9, waiting for transfers between devices, move(): return lax.ppermute(block, ('row', 'col'), route)  5.66 us
  transfers between devices with their start and end apart: 19, of which 8 were waited for; matrix products, arithmetic and copies ran while one was open for 7% of the time, Pallas kernels for 4%

profile of v12, /device:TPU:1, one launch (start us, length us, event | category | flops | bytes accessed | tf_op | source)
XLA Modules:
  0.0 175.3 jit_solution(4096688286602985723)
XLA Ops:
  0.0 1.3 cut_window.1
  1.3 1.3 collective-permute-start.2
  2.6 4.6 %collective-permute-start.4 = (bf16[1536,128]{1,0:T(8,128)(2,1)S(1)}, bf16[1536,128]{1,0:T(8,128)(2,1)S(1)}, u32[]{:S(2)}, u32[]{:S(2)}) collective-permute-start(bf16[1536,128]{1,0:T(8,128)(2,1)S(1)} %get-tuple-element.26), channel_id=1, source_target_pairs={{0,0},{1,4},{4,1},{5,5},{10,10},{11,14},{14,11},{15,15},{16,16},{1... | collective-permute-start | bytes 1179656 | tf_op jit(solution)/shard_map/ppermute | solution.py:367
  7.2 1.9 %collective-permute-start.1 = (bf16[1536,128]{1,0:T(8,128)(2,1)S(1)}, bf16[1536,128]{1,0:T(8,128)(2,1)S(1)}, u32[]{:S(2)}, u32[]{:S(2)}) collective-permute-start(bf16[1536,128]{1,0:T(8,128)(2,1)S(1)} %get-tuple-element.25), channel_id=1, source_target_pairs={{0,0},{1,4},{2,8},{3,12},{4,1},{5,5},{6,9},{7,13},{8,2},{9,6},{10,... | collective-permute-start | bytes 1179656 | tf_op jit(solution)/shard_map/ppermute | solution.py:367
  9.2 0.1 fusion
  9.3 0.1 dynamic_slice.14
  9.5 6.3 %pick_columns.1 = (bf16[96,1536]{1,0:T(8,128)(2,1)S(1)}, bf16[96,1536]{1,0:T(8,128)(2,1)S(1)}) custom-call(bf16[2,1536,1536]{2,1,0:T(8,128)(2,1)} %tile_ref.1, s32[1,128]{1,0:T(1,128)S(1)} %pad_bitcast_fusion.miss_ref, bf16[8,1536]{1,0:T(8,128)(2,1)S(1)} %broadcast_in_dim.16.recv_ref, f32[8,1536]{1,0:T(8,128)S(1)} %broadcast_in_dim.36.live_ref), custom_call_target="tpu_custom_call" | custom-call | flops 37748736 | bytes 147456 | tf_op jit(solution)/shard_map/pick_columns/pallas_call | solution.py:105
  15.7 4.9 %collective-permute-start.3 = (bf16[1536,128]{1,0:T(8,128)(2,1)S(1)}, bf16[1536,128]{1,0:T(8,128)(2,1)S(1)}, u32[]{:S(2)}, u32[]{:S(2)}) collective-permute-start(bf16[1536,128]{1,0:T(8,128)(2,1)S(1)} %collective-permute-done.2), channel_id=1, source_target_pairs={{0,8},{1,12},{4,9},{5,13},{10,2},{11,6},{14,3},{15,7},{16,24},{17,... | collective-permute-start | bytes 1179656 | tf_op jit(solution)/shard_map/ppermute | solution.py:367
  20.6 0.9 pad_maximum_fusion
  21.5 1.9 %collective-permute-start = (bf16[192,1536]{1,0:T(8,128)(2,1)}, bf16[192,1536]{1,0:T(8,128)(2,1)}, u32[]{:S(2)}, u32[]{:S(2)}) collective-permute-start(bf16[192,1536]{1,0:T(8,128)(2,1)} %pad_maximum_fusion), channel_id=1, source_target_pairs={{0,0},{1,4},{2,8},{3,12},{4,1},{5,5},{6,9},{7,13},{8,2},{9,6},{10,... | collective-permute-start | bytes 1769480 | tf_op jit(solution)/shard_map/ppermute | solution.py:367
  23.4 0.1 dynamic_slice.16
  23.5 5.6 %collective-permute-done.3.refs_1_ = bf16[1536,128]{1,0:T(8,128)(2,1)S(1)} collective-permute-done((bf16[1536,128]{1,0:T(8,128)(2,1)S(1)}, bf16[1536,128]{1,0:T(8,128)(2,1)S(1)}, u32[]{:S(2)}, u32[]{:S(2)}) %collective-permute-start.3) | collective-permute-done | bytes 393248 | tf_op jit(solution)/shard_map/ppermute | solution.py:367
  29.1 0.5 fill_window.1.refs_4_.refs_7_.refs_0_
  29.6 9.8 %collective-permute-start.5 = (bf16[1536,256]{1,0:T(8,128)(2,1)S(1)}, bf16[1536,256]{1,0:T(8,128)(2,1)S(1)}, u32[]{:S(2)}, u32[]{:S(2)}) collective-permute-start(bf16[1536,256]{1,0:T(8,128)(2,1)S(1)} %fill_window.1.refs_4_.refs_7_.refs_0_), channel_id=1, source_target_pairs={{0,4},{4,8},{8,12},{1,5},{5,9},{9,13},{2,6},{6,10},{10,14},{3,7},{... | collective-permute-start | bytes 2359304 | tf_op jit(solution)/shard_map/ppermute | solution.py:412
  39.4 1.3 collective-permute-start.6
  40.7 0.1 pad_add_fusion.pick_ref
  40.8 1.8 %fusion.2 = (bf16[96,1536]{1,0:T(8,128)(2,1)S(1)}, bf16[96,1536]{1,0:T(8,128)(2,1)}) fusion(bf16[192,1536]{1,0:T(8,128)(2,1)} %collective-permute-done), kind=kLoop, calls=%fused_computation.18 | loop fusion | bytes 1179648 | tf_op jit(solution)/shard_map/slice | solution.py:400
  42.6 12.7 %collective-permute-done.5.refs_6_.refs_9_.refs_2_.refs_7_.refs_8_.refs_14_ = bf16[1536,256]{1,0:T(8,128)(2,1)S(1)} collective-permute-done((bf16[1536,256]{1,0:T(8,128)(2,1)S(1)}, bf16[1536,256]{1,0:T(8,128)(2,1)S(1)}, u32[]{:S(2)}, u32[]{:S(2)}) %collective-permute-start.5) | collective-permute-done | bytes 786464 | tf_op jit(solution)/shard_map/ppermute | solution.py:412
  55.3 12.6 %collective-permute-done.6.refs_5_.refs_8_.refs_1_.refs_6_.refs_7_.refs_13_ = bf16[1536,256]{1,0:T(8,128)(2,1)S(1)} collective-permute-done((bf16[1536,256]{1,0:T(8,128)(2,1)S(1)}, bf16[1536,256]{1,0:T(8,128)(2,1)S(1)}, u32[]{:S(2)}, u32[]{:S(2)}) %collective-permute-start.6) | collective-permute-done | bytes 786464 | tf_op jit(solution)/shard_map/ppermute | solution.py:413
  68.0 7.6 %products.2 = (f32[1536,256]{1,0:T(8,128)S(1)}, f32[1536,256]{1,0:T(8,128)S(1)}) custom-call(s32[2]{0:T(128)S(1)} %pad_add_fusion.pick_ref, bf16[8,1536]{1,0:T(8,128)(2,1)S(1)} %broadcast_in_dim.16.recv_ref, bf16[2,1536,1536]{2,1,0:T(8,128)(2,1)} %tile_ref.1, bf16[2,1536,1536]{2,1,0:T(8,128)(2,1)} %tile_ref.1, bf16[2,1536,1536]{2,1,0:T(8,128)(2,1)} %tile_ref.1, ...), custom_call_target="tpu_custom_call" | custom-call | flops 150994944 | bytes 24576 | tf_op jit(solution)/shard_map/products/pallas_call | solution.py:230
  75.6 0.3 collective-permute-start.7
  75.8 0.7 collective-permute-start.8
  76.6 1.3 collective-permute-start.9
  77.9 1.2 collective-permute-done.7
  79.0 2.0 %abs_reduce_fusion.1 = (f32[]{:T(128)}, f32[1536,256]{1,0:T(8,128)}) fusion(f32[1536,256]{1,0:T(8,128)S(1)} %get-tuple-element.31, f32[1536,256]{1,0:T(8,128)S(1)} %collective-permute-done.7), kind=kLoop, calls=%fused_computation.4 | loop fusion | flops 1179647 | bytes 4718596 | tf_op jit(solution)/shard_map/reduce_max | solution.py:421
  81.7 2.5 %multiply_convert_fusion.1 = f16[1536,256]{1,0:T(8,128)(2,1)} fusion(f32[1536,256]{1,0:T(8,128)} %get-tuple-element.44, f32[]{:T(128)S(6)} %div.18), kind=kLoop, calls=%fused_computation.3 | loop fusion | flops 786432 | bytes 2359300 | tf_op jit(solution)/shard_map/convert_element_type | solution.py:422
  84.2 16.8 %collective-permute-done.9.refs_3_.refs_4_.refs_10_ = bf16[1536,256]{1,0:T(8,128)(2,1)} collective-permute-done((bf16[1536,256]{1,0:T(8,128)(2,1)S(1)}, bf16[1536,256]{1,0:T(8,128)(2,1)}, u32[]{:S(2)}, u32[]{:S(2)}) %collective-permute-start.9) | collective-permute-done | bytes 786464 | tf_op jit(solution)/shard_map/ppermute | solution.py:413
  101.0 1.3 collective-permute-start.12
  102.3 1.6 collective-permute-start.13
  103.8 0.1 stack.56.pick_ref
  103.9 0.1 pad_add_fusion.1.pick_ref
  104.0 17.6 %collective-permute-done.12.refs_5_.refs_6_.refs_12_ = bf16[1536,256]{1,0:T(8,128)(2,1)} collective-permute-done((bf16[1536,256]{1,0:T(8,128)(2,1)}, bf16[1536,256]{1,0:T(8,128)(2,1)}, u32[]{:S(2)}, u32[]{:S(2)}) %collective-permute-start.12) | collective-permute-done | bytes 786464 | tf_op jit(solution)/shard_map/ppermute | solution.py:413
  121.6 1.0 copy-done
  122.6 3.3 %extra_products.1 = f32[4,96,256]{2,1,0:T(8,128)S(1)} custom-call(s32[8]{0:T(128)S(1)} %stack.56.pick_ref, bf16[96,1536]{1,0:T(8,128)(2,1)S(1)} %copy-done, bf16[96,1536]{1,0:T(8,128)(2,1)S(1)} %get-tuple-element.28.imag_ref, bf16[1536,256]{1,0:T(8,128)(2,1)S(1)} %fill_window.1.refs_4_.refs_7_.refs_0_, ...), custom_call_target="tpu_custom_call" | custom-call | flops 18874368 | bytes 24576 | tf_op jit(solution)/shard_map/extra_products/pallas_call | solution.py:264
  125.9 11.0 %products.3 = (f32[1536,256]{1,0:T(8,128)}, f32[1536,256]{1,0:T(8,128)}) custom-call(s32[2]{0:T(128)S(1)} %pad_add_fusion.1.pick_ref, bf16[8,1536]{1,0:T(8,128)(2,1)S(1)} %broadcast_in_dim.16.recv_ref, bf16[2,1536,1536]{2,1,0:T(8,128)(2,1)} %tile_ref.1, bf16[2,1536,1536]{2,1,0:T(8,128)(2,1)} %tile_ref.1, bf16[2,1536,1536]{2,1,0:T(8,128)(2,1)} %tile_ref.1, ...), custom_call_target="tpu_custom_call" | custom-call | flops 150994944 | bytes 24576 | tf_op jit(solution)/shard_map/products/pallas_call | solution.py:230
  136.9 1.6 collective-permute-start.14
  138.5 1.3 collective-permute-start.10
  139.8 0.1 collective-permute-start.17
  139.9 1.8 %collective-permute-done.14 = f32[1536,256]{1,0:T(8,128)S(1)} collective-permute-done((f32[1536,256]{1,0:T(8,128)}, f32[1536,256]{1,0:T(8,128)S(1)}, u32[]{:S(2)}, u32[]{:S(2)}) %collective-permute-start.14) | collective-permute-done | bytes 1572896 | tf_op jit(solution)/shard_map/ppermute | solution.py:451
  141.8 3.4 %abs_reduce_fusion = (f32[]{:T(128)}, f32[1536,256]{1,0:T(8,128)}) fusion(f32[1536,256]{1,0:T(8,128)} %get-tuple-element.38, f32[1536,256]{1,0:T(8,128)S(1)} %collective-permute-done.14), kind=kLoop, calls=%fused_computation.2 | loop fusion | flops 1179647 | bytes 4718596 | tf_op jit(solution)/shard_map/reduce_max | solution.py:421
  145.9 1.7 multiply_convert_fusion
  147.7 4.9 %collective-permute-start.15 = (f16[1536,256]{1,0:T(8,128)(2,1)S(1)}, f16[1536,256]{1,0:T(8,128)(2,1)}, u32[]{:S(2)}, u32[]{:S(2)}) collective-permute-start(f16[1536,256]{1,0:T(8,128)(2,1)S(1)} %multiply_convert_fusion), channel_id=1, source_target_pairs={{0,2},{1,3},{4,6},{5,7},{10,8},{11,9},{14,12},{15,13},{16,18},{17,... | collective-permute-start | bytes 2359304 | tf_op jit(solution)/shard_map/ppermute | solution.py:367
  152.6 0.1 collective-permute-start.18
  152.7 1.3 collective-permute-start.11
  154.0 4.0 %collective-permute-start.16 = (f32[1,128]{1,0:T(1,128)S(1)}, f32[1,128]{1,0:T(1,128)S(1)}, u32[]{:S(2)}, u32[]{:S(2)}) collective-permute-start(f32[1,128]{1,0:T(1,128)S(1)} %broadcast_in_dim.40), channel_id=1, source_target_pairs={{0,2},{1,3},{4,6},{5,7},{10,8},{11,9},{14,12},{15,13},{16,18},{17,... | collective-permute-start | bytes 1544 | tf_op jit(solution)/shard_map/ppermute | solution.py:367
  158.0 12.3 %collective-permute-done.18 = f32[1,96,256]{2,1,0:T(8,128)S(1)} collective-permute-done((f32[1,96,256]{2,1,0:T(8,128)S(1)}, f32[1,96,256]{2,1,0:T(8,128)S(1)}, u32[]{:S(2)}, u32[]{:S(2)}) %collective-permute-start.18) | collective-permute-done | bytes 98336 | tf_op jit(solution)/shard_map/ppermute | solution.py:475
  170.4 2.1 %add_add_fusion.refs_0_ = f32[1536,256]{1,0:T(8,128)S(1)} fusion(f16[1536,256]{1,0:T(8,128)(2,1)} %collective-permute-done.15, f32[1536,256]{1,0:T(8,128)} %get-tuple-element.42, f16[1536,256]{1,0:T(8,128)(2,1)} %collective-permute-done.10, f32[1536,256]{1,0:T(8,128)S(1)} %copy-done.4, f32[]{:T(128)S(1)} %bitcast.24, f32[]{:T(128)S(1)} %bitcast.23, ...), kind=kLoop, calls=%fused_computation | loop fusion | flops 3538944 | bytes 6291466 | tf_op jit(solution)/shard_map/add | solution.py:471
  172.4 2.8 %finish.1 = f32[2,1536,128]{2,1,0:T(8,128)} custom-call(f32[2]{0:T(128)S(1)} %broadcast_multiply_fusion.wave_ref, s32[96]{0:T(128)S(1)} %get-tuple-element.48.miss_ref, bf16[8,1536]{1,0:T(8,128)(2,1)S(1)} %broadcast_in_dim.16.recv_ref, bf16[2,1536,1536]{2,1,0:T(8,128)(2,1)} %tile_ref.1, bf16[96,1536]{1,0:T(8,128)(2,1)S(1)} %copy-done.1, ...), custom_call_target="tpu_custom_call" | custom-call | flops 61440 | bytes 122880 | tf_op jit(solution)/shard_map/finish/pallas_call | solution.py:304
  (40 shorter events, 0.2 us)
Async XLA Ops:
  0.0 9.1 %copy-start.6 = (s32[4,96]{1,0:T(4,128)S(1)}, s32[4,96]{1,0:T(4,128)}, u32[]{:S(2)}) copy-start(s32[4,96]{1,0:T(4,128)} %param.6) | copy-start | bytes 4612
  0.0 9.3 %copy-start.5 = (s32[6144]{0:T(1024)S(1)}, s32[6144]{0:T(1024)}, u32[]{:S(2)}) copy-start(s32[6144]{0:T(1024)} %param.5) | copy-start | bytes 73732
  1.3 14.4 %collective-permute-start.2 = (bf16[1536,128]{1,0:T(8,128)(2,1)S(1)}, bf16[1536,128]{1,0:T(8,128)(2,1)S(1)}, u32[]{:S(2)}, u32[]{:S(2)}) collective-permute-start(bf16[1536,128]{1,0:T(8,128)(2,1)S(1)} %get-tuple-element.26), channel_id=1, source_target_pairs={{2,0},{3,1},{6,4},{7,5},{8,10},{9,11},{12,14},{13,15},{18,16},{19,... | collective-permute-start | bytes 1179656 | tf_op jit(solution)/shard_map/ppermute | solution.py:367
  2.6 20.9 %collective-permute-start.4 = (bf16[1536,128]{1,0:T(8,128)(2,1)S(1)}, bf16[1536,128]{1,0:T(8,128)(2,1)S(1)}, u32[]{:S(2)}, u32[]{:S(2)}) collective-permute-start(bf16[1536,128]{1,0:T(8,128)(2,1)S(1)} %get-tuple-element.26), channel_id=1, source_target_pairs={{0,0},{1,4},{4,1},{5,5},{10,10},{11,14},{14,11},{15,15},{16,16},{1... | collective-permute-start | bytes 1179656 | tf_op jit(solution)/shard_map/ppermute | solution.py:367
  7.2 16.3 %collective-permute-start.1 = (bf16[1536,128]{1,0:T(8,128)(2,1)S(1)}, bf16[1536,128]{1,0:T(8,128)(2,1)S(1)}, u32[]{:S(2)}, u32[]{:S(2)}) collective-permute-start(bf16[1536,128]{1,0:T(8,128)(2,1)S(1)} %get-tuple-element.25), channel_id=1, source_target_pairs={{0,0},{1,4},{2,8},{3,12},{4,1},{5,5},{6,9},{7,13},{8,2},{9,6},{10,... | collective-permute-start | bytes 1179656 | tf_op jit(solution)/shard_map/ppermute | solution.py:367
  15.7 13.4 %collective-permute-start.3 = (bf16[1536,128]{1,0:T(8,128)(2,1)S(1)}, bf16[1536,128]{1,0:T(8,128)(2,1)S(1)}, u32[]{:S(2)}, u32[]{:S(2)}) collective-permute-start(bf16[1536,128]{1,0:T(8,128)(2,1)S(1)} %collective-permute-done.2), channel_id=1, source_target_pairs={{0,8},{1,12},{4,9},{5,13},{10,2},{11,6},{14,3},{15,7},{16,24},{17,... | collective-permute-start | bytes 1179656 | tf_op jit(solution)/shard_map/ppermute | solution.py:367
  21.5 19.3 %collective-permute-start = (bf16[192,1536]{1,0:T(8,128)(2,1)}, bf16[192,1536]{1,0:T(8,128)(2,1)}, u32[]{:S(2)}, u32[]{:S(2)}) collective-permute-start(bf16[192,1536]{1,0:T(8,128)(2,1)} %pad_maximum_fusion), channel_id=1, source_target_pairs={{0,0},{1,4},{2,8},{3,12},{4,1},{5,5},{6,9},{7,13},{8,2},{9,6},{10,... | collective-permute-start | bytes 1769480 | tf_op jit(solution)/shard_map/ppermute | solution.py:367
  29.6 25.7 %collective-permute-start.5 = (bf16[1536,256]{1,0:T(8,128)(2,1)S(1)}, bf16[1536,256]{1,0:T(8,128)(2,1)S(1)}, u32[]{:S(2)}, u32[]{:S(2)}) collective-permute-start(bf16[1536,256]{1,0:T(8,128)(2,1)S(1)} %fill_window.1.refs_4_.refs_7_.refs_0_), channel_id=1, source_target_pairs={{0,4},{4,8},{8,12},{1,5},{5,9},{9,13},{2,6},{6,10},{10,14},{3,7},{... | collective-permute-start | bytes 2359304 | tf_op jit(solution)/shard_map/ppermute | solution.py:412
  39.4 28.6 %collective-permute-start.6 = (bf16[1536,256]{1,0:T(8,128)(2,1)S(1)}, bf16[1536,256]{1,0:T(8,128)(2,1)S(1)}, u32[]{:S(2)}, u32[]{:S(2)}) collective-permute-start(bf16[1536,256]{1,0:T(8,128)(2,1)S(1)} %fill_window.1.refs_4_.refs_7_.refs_0_), channel_id=1, source_target_pairs={{4,0},{8,4},{12,8},{5,1},{9,5},{13,9},{6,2},{10,6},{14,10},{7,3},{... | collective-permute-start | bytes 2359304 | tf_op jit(solution)/shard_map/ppermute | solution.py:413
  75.6 3.5 %collective-permute-start.7 = (f32[1536,256]{1,0:T(8,128)S(1)}, f32[1536,256]{1,0:T(8,128)S(1)}, u32[]{:S(2)}, u32[]{:S(2)}) collective-permute-start(f32[1536,256]{1,0:T(8,128)S(1)} %get-tuple-element.32), channel_id=1, source_target_pairs={{0,1},{1,0},{2,3},{3,2},{4,5},{5,4},{6,7},{7,6},{8,9},{9,8},{10,11... | collective-permute-start | bytes 4718600 | tf_op jit(solution)/shard_map/ppermute | solution.py:451
  75.8 8.4 %collective-permute-start.8 = (bf16[1536,256]{1,0:T(8,128)(2,1)S(1)}, bf16[1536,256]{1,0:T(8,128)(2,1)S(1)}, u32[]{:S(2)}, u32[]{:S(2)}) collective-permute-start(bf16[1536,256]{1,0:T(8,128)(2,1)S(1)} %collective-permute-done.5.refs_6_.refs_9_.refs_2_.refs_7_.refs_8_.refs_14_), channel_id=1, source_target_pairs={{4,8},{8,12},{5,9},{9,13},{6,10},{10,14},{7,11},{11,15},{20,24},{2... | collective-permute-start | bytes 2359304 | tf_op jit(solution)/shard_map/ppermute | solution.py:412
  76.6 24.4 %collective-permute-start.9 = (bf16[1536,256]{1,0:T(8,128)(2,1)S(1)}, bf16[1536,256]{1,0:T(8,128)(2,1)}, u32[]{:S(2)}, u32[]{:S(2)}) collective-permute-start(bf16[1536,256]{1,0:T(8,128)(2,1)S(1)} %collective-permute-done.6.refs_5_.refs_8_.refs_1_.refs_6_.refs_7_.refs_13_), channel_id=1, source_target_pairs={{4,0},{8,4},{5,1},{9,5},{6,2},{10,6},{7,3},{11,7},{20,16},{24,20},... | collective-permute-start | bytes 2359304 | tf_op jit(solution)/shard_map/ppermute | solution.py:413
  101.0 20.6 %collective-permute-start.12 = (bf16[1536,256]{1,0:T(8,128)(2,1)}, bf16[1536,256]{1,0:T(8,128)(2,1)}, u32[]{:S(2)}, u32[]{:S(2)}) collective-permute-start(bf16[1536,256]{1,0:T(8,128)(2,1)} %collective-permute-done.9.refs_3_.refs_4_.refs_10_), channel_id=1, source_target_pairs={{4,0},{5,1},{6,2},{7,3},{20,16},{21,17},{22,18},{23,19}} | collective-permute-start | bytes 2359304 | tf_op jit(solution)/shard_map/ppermute | solution.py:413
  102.3 19.3 %collective-permute-start.13 = (bf16[1536,256]{1,0:T(8,128)(2,1)S(1)}, bf16[1536,256]{1,0:T(8,128)(2,1)}, u32[]{:S(2)}, u32[]{:S(2)}) collective-permute-start(bf16[1536,256]{1,0:T(8,128)(2,1)S(1)} %collective-permute-done.8.refs_4_.refs_5_.refs_11_), channel_id=1, source_target_pairs={{8,12},{9,13},{10,14},{11,15},{24,28},{25,29},{26,30},{27,31}} | collective-permute-start | bytes 2359304 | tf_op jit(solution)/shard_map/ppermute | solution.py:412
  121.6 1.0 copy-start
  125.9 13.9 %copy-start.2 = (f32[4,96,256]{2,1,0:T(8,128)}, f32[4,96,256]{2,1,0:T(8,128)S(1)}, u32[]{:S(2)}) copy-start(f32[4,96,256]{2,1,0:T(8,128)S(1)} %extra_products.1) | copy-start | bytes 1179652
  136.9 4.8 %collective-permute-start.14 = (f32[1536,256]{1,0:T(8,128)}, f32[1536,256]{1,0:T(8,128)S(1)}, u32[]{:S(2)}, u32[]{:S(2)}) collective-permute-start(f32[1536,256]{1,0:T(8,128)} %get-tuple-element.39), channel_id=1, source_target_pairs={{0,1},{1,0},{2,3},{3,2},{4,5},{5,4},{6,7},{7,6},{8,9},{9,8},{10,11... | collective-permute-start | bytes 4718600 | tf_op jit(solution)/shard_map/ppermute | solution.py:451
  138.5 31.8 %collective-permute-start.10 = (f16[1536,256]{1,0:T(8,128)(2,1)}, f16[1536,256]{1,0:T(8,128)(2,1)}, u32[]{:S(2)}, u32[]{:S(2)}) collective-permute-start(f16[1536,256]{1,0:T(8,128)(2,1)} %multiply_convert_fusion.1), channel_id=1, source_target_pairs={{2,0},{3,1},{6,4},{7,5},{8,10},{9,11},{12,14},{13,15},{18,16},{19,... | collective-permute-start | bytes 2359304 | tf_op jit(solution)/shard_map/ppermute | solution.py:367
  139.8 12.7 %collective-permute-start.17 = (f32[2,96,256]{2,1,0:T(8,128)S(1)}, f32[2,96,256]{2,1,0:T(8,128)S(1)}, u32[]{:S(2)}, u32[]{:S(2)}) collective-permute-start(f32[2,96,256]{2,1,0:T(8,128)S(1)} %slice.31), channel_id=1, source_target_pairs={{0,1},{1,0},{2,3},{3,2},{4,5},{5,4},{6,7},{7,6},{8,9},{9,8},{10,11... | collective-permute-start | bytes 589832 | tf_op jit(solution)/shard_map/ppermute | solution.py:475
  145.2 7.4 %copy-start.3 = (f32[4,96,256]{2,1,0:T(8,128)S(1)}, f32[4,96,256]{2,1,0:T(8,128)}, u32[]{:S(2)}) copy-start(f32[4,96,256]{2,1,0:T(8,128)} %copy-done.2) | copy-start | bytes 1179652
  145.9 6.7 %copy-start.7 = (f32[2]{0:T(128)S(1)}, f32[2]{0:T(128)}, u32[]{:S(2)}) copy-start(f32[2]{0:T(128)} %param.7) | copy-start | bytes 28
  145.9 24.4 %copy-start.4 = (f32[1536,256]{1,0:T(8,128)S(1)}, f32[1536,256]{1,0:T(8,128)}, u32[]{:S(2)}) copy-start(f32[1536,256]{1,0:T(8,128)} %get-tuple-element.44) | copy-start | bytes 4718596
  147.7 22.7 %collective-permute-start.15 = (f16[1536,256]{1,0:T(8,128)(2,1)S(1)}, f16[1536,256]{1,0:T(8,128)(2,1)}, u32[]{:S(2)}, u32[]{:S(2)}) collective-permute-start(f16[1536,256]{1,0:T(8,128)(2,1)S(1)} %multiply_convert_fusion), channel_id=1, source_target_pairs={{0,2},{1,3},{4,6},{5,7},{10,8},{11,9},{14,12},{15,13},{16,18},{17,... | collective-permute-start | bytes 2359304 | tf_op jit(solution)/shard_map/ppermute | solution.py:367
  152.6 17.7 %collective-permute-start.18 = (f32[1,96,256]{2,1,0:T(8,128)S(1)}, f32[1,96,256]{2,1,0:T(8,128)S(1)}, u32[]{:S(2)}, u32[]{:S(2)}) collective-permute-start(f32[1,96,256]{2,1,0:T(8,128)S(1)} %slice.37), channel_id=1, source_target_pairs={{0,2},{1,3},{2,0},{3,1},{4,6},{5,7},{6,4},{7,5},{8,10},{9,11},{10,... | collective-permute-start | bytes 294920 | tf_op jit(solution)/shard_map/ppermute | solution.py:475
  152.7 17.6 %collective-permute-start.11 = (f32[1,128]{1,0:T(1,128)S(1)}, f32[1,128]{1,0:T(1,128)S(1)}, u32[]{:S(2)}, u32[]{:S(2)}) collective-permute-start(f32[1,128]{1,0:T(1,128)S(1)} %broadcast_in_dim.39), channel_id=1, source_target_pairs={{2,0},{3,1},{6,4},{7,5},{8,10},{9,11},{12,14},{13,15},{18,16},{19,... | collective-permute-start | bytes 1544 | tf_op jit(solution)/shard_map/ppermute | solution.py:367
  154.0 16.3 %collective-permute-start.16 = (f32[1,128]{1,0:T(1,128)S(1)}, f32[1,128]{1,0:T(1,128)S(1)}, u32[]{:S(2)}, u32[]{:S(2)}) collective-permute-start(f32[1,128]{1,0:T(1,128)S(1)} %broadcast_in_dim.40), channel_id=1, source_target_pairs={{0,2},{1,3},{4,6},{5,7},{10,8},{11,9},{14,12},{15,13},{16,18},{17,... | collective-permute-start | bytes 1544 | tf_op jit(solution)/shard_map/ppermute | solution.py:367
  170.4 2.1 %copy-start.1 = (bf16[96,1536]{1,0:T(8,128)(2,1)S(1)}, bf16[96,1536]{1,0:T(8,128)(2,1)}, u32[]{:S(2)}) copy-start(bf16[96,1536]{1,0:T(8,128)(2,1)} %get-tuple-element.27.real_ref) | copy-start | bytes 884740

commit v13 on v12

--- a/solution.py
+++ b/solution.py
@@ -396,13 +396,17 @@
     recv_col8 = jnp.broadcast_to(recv_col[None], (8, tile))
 
     picked = pick_columns(traces, miss_col_lanes, recv_col8, live8, misses)
-    both = transpose(jnp.concatenate(picked))
-    extra = [both[:misses], both[misses:]]
+    both = jnp.concatenate(picked)
+    extra = None
     apart = row_index ^ col_index
     strides = [2**bit for bit in range(grid_size.bit_length() - 1)]
     terms, extra_terms = [], []
     for chunk in range(CHUNKS):
         window = fill_window(chunk, arrived[chunk], picked, miss_col_lanes, recv_row8)
+        if extra is None:
+            both, window = lax.optimization_barrier((both, window))
+            both = transpose(both)
+            extra = [both[:misses], both[misses:]]
         up, down = [window], [window]
         sums = []
 

time: 178 us -> 186 us (1.045)
  starting transfers between devices: 44 us -> 49.7 us
  waiting for transfers between devices: 80.7 us -> 84.3 us
    ppermute x9, waiting for transfers between devices: 5.66 us -> 21.8 us  [move(): return lax.ppermute(block, ('row', 'col'), route)]
    ppermute x9, starting transfers between devices: 26 us -> 36.1 us  [move(): return lax.ppermute(block, ('row', 'col'), route)]
    ppermute x3, waiting for transfers between devices: 12.7 us -> 3.33 us  [hop(): up.append(lax.ppermute(up[-1], 'row', ends))]
    ppermute x3, starting transfers between devices: 12.1 us -> 3.74 us  [hop(): up.append(lax.ppermute(up[-1], 'row', ends))]
    ppermute x2, starting transfers between devices: 1.87 us -> 5.89 us  [pair_sum(): lax.ppermute(sent, 'col', other_core)]
    ppermute x3, waiting for transfers between devices: 47 us -> 44.1 us  [hop(): down.append(lax.ppermute(down[-1], 'row', back))]
  transfers between devices with their start and end apart: 19 -> 19, of which waited for: 8 -> 10; matrix products, arithmetic and copies ran while one was open for 7% -> 7% of each run, Pallas kernels for 4% -> 3%
where the time goes in v13:
time: 186 us; the launch traced here: 184 us
  waiting for transfers between devices  84.3 us (45%)
  starting transfers between devices  49.7 us (27%)
  Pallas kernels  32.8 us (18%)
  other arithmetic  12 us (6%)
  local copies, waits for them, and re-layouts  3.12 us (2%)
  between operations  1.86 us (1%)
    ppermute x3, waiting for transfers between devices, hop(): down.append(lax.ppermute(down[-1], 'row', back))  44.1 us
    ppermute x9, starting transfers between devices, move(): return lax.ppermute(block, ('row', 'col'), route)  36.1 us
    ppermute x9, waiting for transfers between devices, move(): return lax.ppermute(block, ('row', 'col'), route)  21.8 us
    pallas_call x2, Pallas kernels, products(): pl.pallas_call(functools.partial(product_kernel, counts), grid=(rows // b...  18.6 us
    ppermute x2, waiting for transfers between devices, local(): arrive = lax.ppermute(rest[1::2], 'col', pairs)  12.3 us
    pallas_call x1, Pallas kernels, pick_columns(): pl.pallas_call(pick_kernel, grid=(rows // block,), in_specs=[pl.BlockSpec...  6.28 us
    ppermute x2, starting transfers between devices, pair_sum(): lax.ppermute(sent, 'col', other_core)  5.89 us
    reduce_max x2, other arithmetic, shrink(): unit = jnp.maximum(jnp.max(jnp.abs(total)), TINY) * (1.0 / HALF_TOP)  5.4 us
  transfers between devices with their start and end apart: 19, of which 10 were waited for; matrix products, arithmetic and copies ran while one was open for 7% of the time, Pallas kernels for 3%

profile of v13, /device:TPU:1, one launch (start us, length us, event | category | flops | bytes accessed | tf_op | source)
XLA Modules:
  0.0 183.9 jit_solution(2852248044717803602)
XLA Ops:
  0.0 1.3 cut_window.1
  1.3 1.3 collective-permute-start.1
  2.6 4.6 %collective-permute-start.3 = (bf16[1536,128]{1,0:T(8,128)(2,1)S(1)}, bf16[1536,128]{1,0:T(8,128)(2,1)S(1)}, u32[]{:S(2)}, u32[]{:S(2)}) collective-permute-start(bf16[1536,128]{1,0:T(8,128)(2,1)S(1)} %get-tuple-element.28), channel_id=1, source_target_pairs={{0,0},{1,4},{4,1},{5,5},{10,10},{11,14},{14,11},{15,15},{16,16},{1... | collective-permute-start | bytes 1179656 | tf_op jit(solution)/shard_map/ppermute | solution.py:367
  7.2 1.9 %collective-permute-start = (bf16[1536,128]{1,0:T(8,128)(2,1)S(1)}, bf16[1536,128]{1,0:T(8,128)(2,1)S(1)}, u32[]{:S(2)}, u32[]{:S(2)}) collective-permute-start(bf16[1536,128]{1,0:T(8,128)(2,1)S(1)} %get-tuple-element.27), channel_id=1, source_target_pairs={{0,0},{1,4},{2,8},{3,12},{4,1},{5,5},{6,9},{7,13},{8,2},{9,6},{10,... | collective-permute-start | bytes 1179656 | tf_op jit(solution)/shard_map/ppermute | solution.py:367
  9.2 4.4 %collective-permute-done.1 = bf16[1536,128]{1,0:T(8,128)(2,1)S(1)} collective-permute-done((bf16[1536,128]{1,0:T(8,128)(2,1)S(1)}, bf16[1536,128]{1,0:T(8,128)(2,1)S(1)}, u32[]{:S(2)}, u32[]{:S(2)}) %collective-permute-start.1) | collective-permute-done | bytes 393248 | tf_op jit(solution)/shard_map/ppermute | solution.py:367
  13.5 6.1 %collective-permute-start.2 = (bf16[1536,128]{1,0:T(8,128)(2,1)S(1)}, bf16[1536,128]{1,0:T(8,128)(2,1)S(1)}, u32[]{:S(2)}, u32[]{:S(2)}) collective-permute-start(bf16[1536,128]{1,0:T(8,128)(2,1)S(1)} %collective-permute-done.1), channel_id=1, source_target_pairs={{0,8},{1,12},{4,9},{5,13},{10,2},{11,6},{14,3},{15,7},{16,24},{17,... | collective-permute-start | bytes 1179656 | tf_op jit(solution)/shard_map/ppermute | solution.py:367
  19.7 0.1 fusion
  19.8 0.1 dynamic_slice.14
  19.9 0.1 dynamic_slice.16
  20.0 6.3 %pick_columns.1 = (bf16[96,1536]{1,0:T(8,128)(2,1)S(1)}, bf16[96,1536]{1,0:T(8,128)(2,1)S(1)}) custom-call(bf16[2,1536,1536]{2,1,0:T(8,128)(2,1)} %tile_ref.1, s32[1,128]{1,0:T(1,128)S(1)} %pad_bitcast_fusion.miss_ref, bf16[8,1536]{1,0:T(8,128)(2,1)S(1)} %broadcast_in_dim.16.recv_ref, f32[8,1536]{1,0:T(8,128)S(1)} %broadcast_in_dim.36.live_ref), custom_call_target="tpu_custom_call" | custom-call | flops 37748736 | bytes 147456 | tf_op jit(solution)/shard_map/pick_columns/pallas_call | solution.py:105
  26.4 1.8 collective-permute-done.2.refs_1_
  28.2 0.5 fill_window.1.refs_4_.refs_7_.refs_0_
  28.7 9.4 %collective-permute-start.4 = (bf16[192,1536]{1,0:T(8,128)(2,1)S(1)}, bf16[192,1536]{1,0:T(8,128)(2,1)}, u32[]{:S(2)}, u32[]{:S(2)}) collective-permute-start(bf16[192,1536]{1,0:T(8,128)(2,1)S(1)} %pad_maximum_fusion), channel_id=1, source_target_pairs={{0,0},{1,4},{2,8},{3,12},{4,1},{5,5},{6,9},{7,13},{8,2},{9,6},{10,... | collective-permute-start | bytes 1769480 | tf_op jit(solution)/shard_map/ppermute | solution.py:367
  38.1 1.5 collective-permute-start.5
  39.6 1.3 collective-permute-start.6
  40.9 0.1 pad_add_fusion.pick_ref
  41.0 15.6 %collective-permute-done.4 = bf16[192,1536]{1,0:T(8,128)(2,1)} collective-permute-done((bf16[192,1536]{1,0:T(8,128)(2,1)S(1)}, bf16[192,1536]{1,0:T(8,128)(2,1)}, u32[]{:S(2)}, u32[]{:S(2)}) %collective-permute-start.4) | collective-permute-done | bytes 589856 | tf_op jit(solution)/shard_map/ppermute | solution.py:367
  56.6 1.8 fusion.2
  58.4 3.3 %collective-permute-done.5.refs_6_.refs_9_.refs_2_.refs_7_.refs_8_.refs_14_ = bf16[1536,256]{1,0:T(8,128)(2,1)S(1)} collective-permute-done((bf16[1536,256]{1,0:T(8,128)(2,1)S(1)}, bf16[1536,256]{1,0:T(8,128)(2,1)S(1)}, u32[]{:S(2)}, u32[]{:S(2)}) %collective-permute-start.5) | collective-permute-done | bytes 786464 | tf_op jit(solution)/shard_map/ppermute | solution.py:416
  61.8 6.9 %collective-permute-done.6.refs_5_.refs_8_.refs_1_.refs_6_.refs_7_.refs_13_ = bf16[1536,256]{1,0:T(8,128)(2,1)S(1)} collective-permute-done((bf16[1536,256]{1,0:T(8,128)(2,1)S(1)}, bf16[1536,256]{1,0:T(8,128)(2,1)S(1)}, u32[]{:S(2)}, u32[]{:S(2)}) %collective-permute-start.6) | collective-permute-done | bytes 786464 | tf_op jit(solution)/shard_map/ppermute | solution.py:417
  68.7 7.6 %products.2 = (f32[1536,256]{1,0:T(8,128)S(1)}, f32[1536,256]{1,0:T(8,128)S(1)}) custom-call(s32[2]{0:T(128)S(1)} %pad_add_fusion.pick_ref, bf16[8,1536]{1,0:T(8,128)(2,1)S(1)} %broadcast_in_dim.16.recv_ref, bf16[2,1536,1536]{2,1,0:T(8,128)(2,1)} %tile_ref.1, bf16[2,1536,1536]{2,1,0:T(8,128)(2,1)} %tile_ref.1, bf16[2,1536,1536]{2,1,0:T(8,128)(2,1)} %tile_ref.1, ...), custom_call_target="tpu_custom_call" | custom-call | flops 150994944 | bytes 24576 | tf_op jit(solution)/shard_map/products/pallas_call | solution.py:230
  76.3 4.3 %collective-permute-start.7 = (f32[1536,256]{1,0:T(8,128)S(1)}, f32[1536,256]{1,0:T(8,128)S(1)}, u32[]{:S(2)}, u32[]{:S(2)}) collective-permute-start(f32[1536,256]{1,0:T(8,128)S(1)} %get-tuple-element.36), channel_id=1, source_target_pairs={{0,1},{1,0},{2,3},{3,2},{4,5},{5,4},{6,7},{7,6},{8,9},{9,8},{10,11... | collective-permute-start | bytes 4718600 | tf_op jit(solution)/shard_map/ppermute | solution.py:455
  80.6 0.7 collective-permute-start.8
  81.3 1.3 collective-permute-start.9
  82.6 1.0 collective-permute-done.7
  83.6 2.0 %abs_reduce_fusion.1 = (f32[]{:T(128)}, f32[1536,256]{1,0:T(8,128)}) fusion(f32[1536,256]{1,0:T(8,128)S(1)} %get-tuple-element.35, f32[1536,256]{1,0:T(8,128)S(1)} %collective-permute-done.7), kind=kLoop, calls=%fused_computation.4 | loop fusion | flops 1179647 | bytes 4718596 | tf_op jit(solution)/shard_map/reduce_max | solution.py:425
  86.3 2.5 %multiply_convert_fusion.1 = f16[1536,256]{1,0:T(8,128)(2,1)} fusion(f32[1536,256]{1,0:T(8,128)} %get-tuple-element.48, f32[]{:T(128)S(6)} %div.18), kind=kLoop, calls=%fused_computation.3 | loop fusion | flops 786432 | bytes 2359300 | tf_op jit(solution)/shard_map/convert_element_type | solution.py:426
  88.7 19.6 %collective-permute-done.9.refs_3_.refs_4_.refs_10_ = bf16[1536,256]{1,0:T(8,128)(2,1)} collective-permute-done((bf16[1536,256]{1,0:T(8,128)(2,1)S(1)}, bf16[1536,256]{1,0:T(8,128)(2,1)}, u32[]{:S(2)}, u32[]{:S(2)}) %collective-permute-start.9) | collective-permute-done | bytes 786464 | tf_op jit(solution)/shard_map/ppermute | solution.py:417
  108.3 1.3 collective-permute-start.12
  109.6 1.6 collective-permute-start.13
  111.2 0.1 stack.56.pick_ref
  111.3 0.1 pad_add_fusion.1.pick_ref
  111.3 17.6 %collective-permute-done.12.refs_5_.refs_6_.refs_12_ = bf16[1536,256]{1,0:T(8,128)(2,1)} collective-permute-done((bf16[1536,256]{1,0:T(8,128)(2,1)}, bf16[1536,256]{1,0:T(8,128)(2,1)}, u32[]{:S(2)}, u32[]{:S(2)}) %collective-permute-start.12) | collective-permute-done | bytes 786464 | tf_op jit(solution)/shard_map/ppermute | solution.py:417
  128.9 1.0 copy-done
  129.9 3.3 %extra_products.1 = f32[4,96,256]{2,1,0:T(8,128)S(1)} custom-call(s32[8]{0:T(128)S(1)} %stack.56.pick_ref, bf16[96,1536]{1,0:T(8,128)(2,1)S(1)} %copy-done, bf16[96,1536]{1,0:T(8,128)(2,1)S(1)} %get-tuple-element.32.imag_ref, bf16[1536,256]{1,0:T(8,128)(2,1)S(1)} %fill_window.1.refs_4_.refs_7_.refs_0_, ...), custom_call_target="tpu_custom_call" | custom-call | flops 18874368 | bytes 24576 | tf_op jit(solution)/shard_map/extra_products/pallas_call | solution.py:264
  133.2 11.0 %products.3 = (f32[1536,256]{1,0:T(8,128)}, f32[1536,256]{1,0:T(8,128)}) custom-call(s32[2]{0:T(128)S(1)} %pad_add_fusion.1.pick_ref, bf16[8,1536]{1,0:T(8,128)(2,1)S(1)} %broadcast_in_dim.16.recv_ref, bf16[2,1536,1536]{2,1,0:T(8,128)(2,1)} %tile_ref.1, bf16[2,1536,1536]{2,1,0:T(8,128)(2,1)} %tile_ref.1, bf16[2,1536,1536]{2,1,0:T(8,128)(2,1)} %tile_ref.1, ...), custom_call_target="tpu_custom_call" | custom-call | flops 150994944 | bytes 24576 | tf_op jit(solution)/shard_map/products/pallas_call | solution.py:230
  144.2 1.6 collective-permute-start.14
  145.9 1.3 collective-permute-start.10
  147.2 0.1 collective-permute-start.17
  147.3 1.8 collective-permute-done.14
  149.1 3.4 %abs_reduce_fusion = (f32[]{:T(128)}, f32[1536,256]{1,0:T(8,128)}) fusion(f32[1536,256]{1,0:T(8,128)} %get-tuple-element.42, f32[1536,256]{1,0:T(8,128)S(1)} %collective-permute-done.14), kind=kLoop, calls=%fused_computation.2 | loop fusion | flops 1179647 | bytes 4718596 | tf_op jit(solution)/shard_map/reduce_max | solution.py:425
  153.3 1.7 multiply_convert_fusion
  155.0 6.1 %collective-permute-start.15 = (f16[1536,256]{1,0:T(8,128)(2,1)S(1)}, f16[1536,256]{1,0:T(8,128)(2,1)}, u32[]{:S(2)}, u32[]{:S(2)}) collective-permute-start(f16[1536,256]{1,0:T(8,128)(2,1)S(1)} %multiply_convert_fusion), channel_id=1, source_target_pairs={{0,2},{1,3},{4,6},{5,7},{10,8},{11,9},{14,12},{15,13},{16,18},{17,... | collective-permute-start | bytes 2359304 | tf_op jit(solution)/shard_map/ppermute | solution.py:367
  161.3 1.3 collective-permute-start.11
  162.6 4.0 %collective-permute-start.16 = (f32[1,128]{1,0:T(1,128)S(1)}, f32[1,128]{1,0:T(1,128)S(1)}, u32[]{:S(2)}, u32[]{:S(2)}) collective-permute-start(f32[1,128]{1,0:T(1,128)S(1)} %broadcast_in_dim.40), channel_id=1, source_target_pairs={{0,2},{1,3},{4,6},{5,7},{10,8},{11,9},{14,12},{15,13},{16,18},{17,... | collective-permute-start | bytes 1544 | tf_op jit(solution)/shard_map/ppermute | solution.py:367
  166.6 12.3 %collective-permute-done.18 = f32[1,96,256]{2,1,0:T(8,128)S(1)} collective-permute-done((f32[1,96,256]{2,1,0:T(8,128)S(1)}, f32[1,96,256]{2,1,0:T(8,128)S(1)}, u32[]{:S(2)}, u32[]{:S(2)}) %collective-permute-start.18) | collective-permute-done | bytes 98336 | tf_op jit(solution)/shard_map/ppermute | solution.py:479
  179.0 2.1 %add_add_fusion.refs_0_ = f32[1536,256]{1,0:T(8,128)S(1)} fusion(f16[1536,256]{1,0:T(8,128)(2,1)} %collective-permute-done.15, f32[1536,256]{1,0:T(8,128)} %get-tuple-element.46, f16[1536,256]{1,0:T(8,128)(2,1)} %collective-permute-done.10, f32[1536,256]{1,0:T(8,128)S(1)} %copy-done.4, f32[]{:T(128)S(1)} %bitcast.24, f32[]{:T(128)S(1)} %bitcast.23, ...), kind=kLoop, calls=%fused_computation | loop fusion | flops 3538944 | bytes 6291466 | tf_op jit(solution)/shard_map/add | solution.py:475
  181.0 2.8 %finish.1 = f32[2,1536,128]{2,1,0:T(8,128)} custom-call(f32[2]{0:T(128)S(1)} %broadcast_multiply_fusion.wave_ref, s32[96]{0:T(128)S(1)} %get-tuple-element.52.miss_ref, bf16[8,1536]{1,0:T(8,128)(2,1)S(1)} %broadcast_in_dim.16.recv_ref, bf16[2,1536,1536]{2,1,0:T(8,128)(2,1)} %tile_ref.1, bf16[96,1536]{1,0:T(8,128)(2,1)S(1)} %copy-done.1, ...), custom_call_target="tpu_custom_call" | custom-call | flops 61440 | bytes 122880 | tf_op jit(solution)/shard_map/finish/pallas_call | solution.py:304
  (40 shorter events, 0.3 us)
Async XLA Ops:
  0.0 9.1 %copy-start.6 = (s32[4,96]{1,0:T(4,128)S(1)}, s32[4,96]{1,0:T(4,128)}, u32[]{:S(2)}) copy-start(s32[4,96]{1,0:T(4,128)} %param.6) | copy-start | bytes 4612
  0.0 9.2 %copy-start.5 = (s32[6144]{0:T(1024)S(1)}, s32[6144]{0:T(1024)}, u32[]{:S(2)}) copy-start(s32[6144]{0:T(1024)} %param.5) | copy-start | bytes 73732
  1.3 12.2 %collective-permute-start.1 = (bf16[1536,128]{1,0:T(8,128)(2,1)S(1)}, bf16[1536,128]{1,0:T(8,128)(2,1)S(1)}, u32[]{:S(2)}, u32[]{:S(2)}) collective-permute-start(bf16[1536,128]{1,0:T(8,128)(2,1)S(1)} %get-tuple-element.28), channel_id=1, source_target_pairs={{2,0},{3,1},{6,4},{7,5},{8,10},{9,11},{12,14},{13,15},{18,16},{19,... | collective-permute-start | bytes 1179656 | tf_op jit(solution)/shard_map/ppermute | solution.py:367
  2.6 23.8 %collective-permute-start.3 = (bf16[1536,128]{1,0:T(8,128)(2,1)S(1)}, bf16[1536,128]{1,0:T(8,128)(2,1)S(1)}, u32[]{:S(2)}, u32[]{:S(2)}) collective-permute-start(bf16[1536,128]{1,0:T(8,128)(2,1)S(1)} %get-tuple-element.28), channel_id=1, source_target_pairs={{0,0},{1,4},{4,1},{5,5},{10,10},{11,14},{14,11},{15,15},{16,16},{1... | collective-permute-start | bytes 1179656 | tf_op jit(solution)/shard_map/ppermute | solution.py:367
  7.2 19.2 %collective-permute-start = (bf16[1536,128]{1,0:T(8,128)(2,1)S(1)}, bf16[1536,128]{1,0:T(8,128)(2,1)S(1)}, u32[]{:S(2)}, u32[]{:S(2)}) collective-permute-start(bf16[1536,128]{1,0:T(8,128)(2,1)S(1)} %get-tuple-element.27), channel_id=1, source_target_pairs={{0,0},{1,4},{2,8},{3,12},{4,1},{5,5},{6,9},{7,13},{8,2},{9,6},{10,... | collective-permute-start | bytes 1179656 | tf_op jit(solution)/shard_map/ppermute | solution.py:367
  13.5 14.7 %collective-permute-start.2 = (bf16[1536,128]{1,0:T(8,128)(2,1)S(1)}, bf16[1536,128]{1,0:T(8,128)(2,1)S(1)}, u32[]{:S(2)}, u32[]{:S(2)}) collective-permute-start(bf16[1536,128]{1,0:T(8,128)(2,1)S(1)} %collective-permute-done.1), channel_id=1, source_target_pairs={{0,8},{1,12},{4,9},{5,13},{10,2},{11,6},{14,3},{15,7},{16,24},{17,... | collective-permute-start | bytes 1179656 | tf_op jit(solution)/shard_map/ppermute | solution.py:367
  28.7 28.0 %collective-permute-start.4 = (bf16[192,1536]{1,0:T(8,128)(2,1)S(1)}, bf16[192,1536]{1,0:T(8,128)(2,1)}, u32[]{:S(2)}, u32[]{:S(2)}) collective-permute-start(bf16[192,1536]{1,0:T(8,128)(2,1)S(1)} %pad_maximum_fusion), channel_id=1, source_target_pairs={{0,0},{1,4},{2,8},{3,12},{4,1},{5,5},{6,9},{7,13},{8,2},{9,6},{10,... | collective-permute-start | bytes 1769480 | tf_op jit(solution)/shard_map/ppermute | solution.py:367
  38.1 23.7 %collective-permute-start.5 = (bf16[1536,256]{1,0:T(8,128)(2,1)S(1)}, bf16[1536,256]{1,0:T(8,128)(2,1)S(1)}, u32[]{:S(2)}, u32[]{:S(2)}) collective-permute-start(bf16[1536,256]{1,0:T(8,128)(2,1)S(1)} %fill_window.1.refs_4_.refs_7_.refs_0_), channel_id=1, source_target_pairs={{0,4},{4,8},{8,12},{1,5},{5,9},{9,13},{2,6},{6,10},{10,14},{3,7},{... | collective-permute-start | bytes 2359304 | tf_op jit(solution)/shard_map/ppermute | solution.py:416
  39.6 29.1 %collective-permute-start.6 = (bf16[1536,256]{1,0:T(8,128)(2,1)S(1)}, bf16[1536,256]{1,0:T(8,128)(2,1)S(1)}, u32[]{:S(2)}, u32[]{:S(2)}) collective-permute-start(bf16[1536,256]{1,0:T(8,128)(2,1)S(1)} %fill_window.1.refs_4_.refs_7_.refs_0_), channel_id=1, source_target_pairs={{4,0},{8,4},{12,8},{5,1},{9,5},{13,9},{6,2},{10,6},{14,10},{7,3},{... | collective-permute-start | bytes 2359304 | tf_op jit(solution)/shard_map/ppermute | solution.py:417
  76.3 7.3 %collective-permute-start.7 = (f32[1536,256]{1,0:T(8,128)S(1)}, f32[1536,256]{1,0:T(8,128)S(1)}, u32[]{:S(2)}, u32[]{:S(2)}) collective-permute-start(f32[1536,256]{1,0:T(8,128)S(1)} %get-tuple-element.36), channel_id=1, source_target_pairs={{0,1},{1,0},{2,3},{3,2},{4,5},{5,4},{6,7},{7,6},{8,9},{9,8},{10,11... | collective-permute-start | bytes 4718600 | tf_op jit(solution)/shard_map/ppermute | solution.py:455
  80.6 8.2 %collective-permute-start.8 = (bf16[1536,256]{1,0:T(8,128)(2,1)S(1)}, bf16[1536,256]{1,0:T(8,128)(2,1)S(1)}, u32[]{:S(2)}, u32[]{:S(2)}) collective-permute-start(bf16[1536,256]{1,0:T(8,128)(2,1)S(1)} %collective-permute-done.5.refs_6_.refs_9_.refs_2_.refs_7_.refs_8_.refs_14_), channel_id=1, source_target_pairs={{4,8},{8,12},{5,9},{9,13},{6,10},{10,14},{7,11},{11,15},{20,24},{2... | collective-permute-start | bytes 2359304 | tf_op jit(solution)/shard_map/ppermute | solution.py:416
  81.3 27.1 %collective-permute-start.9 = (bf16[1536,256]{1,0:T(8,128)(2,1)S(1)}, bf16[1536,256]{1,0:T(8,128)(2,1)}, u32[]{:S(2)}, u32[]{:S(2)}) collective-permute-start(bf16[1536,256]{1,0:T(8,128)(2,1)S(1)} %collective-permute-done.6.refs_5_.refs_8_.refs_1_.refs_6_.refs_7_.refs_13_), channel_id=1, source_target_pairs={{4,0},{8,4},{5,1},{9,5},{6,2},{10,6},{7,3},{11,7},{20,16},{24,20},... | collective-permute-start | bytes 2359304 | tf_op jit(solution)/shard_map/ppermute | solution.py:417
  108.3 20.6 %collective-permute-start.12 = (bf16[1536,256]{1,0:T(8,128)(2,1)}, bf16[1536,256]{1,0:T(8,128)(2,1)}, u32[]{:S(2)}, u32[]{:S(2)}) collective-permute-start(bf16[1536,256]{1,0:T(8,128)(2,1)} %collective-permute-done.9.refs_3_.refs_4_.refs_10_), channel_id=1, source_target_pairs={{4,0},{5,1},{6,2},{7,3},{20,16},{21,17},{22,18},{23,19}} | collective-permute-start | bytes 2359304 | tf_op jit(solution)/shard_map/ppermute | solution.py:417
  109.6 19.3 %collective-permute-start.13 = (bf16[1536,256]{1,0:T(8,128)(2,1)S(1)}, bf16[1536,256]{1,0:T(8,128)(2,1)}, u32[]{:S(2)}, u32[]{:S(2)}) collective-permute-start(bf16[1536,256]{1,0:T(8,128)(2,1)S(1)} %collective-permute-done.8.refs_4_.refs_5_.refs_11_), channel_id=1, source_target_pairs={{8,12},{9,13},{10,14},{11,15},{24,28},{25,29},{26,30},{27,31}} | collective-permute-start | bytes 2359304 | tf_op jit(solution)/shard_map/ppermute | solution.py:416
  128.9 1.0 copy-start
  133.2 13.9 %copy-start.2 = (f32[4,96,256]{2,1,0:T(8,128)}, f32[4,96,256]{2,1,0:T(8,128)S(1)}, u32[]{:S(2)}) copy-start(f32[4,96,256]{2,1,0:T(8,128)S(1)} %extra_products.1) | copy-start | bytes 1179652
  144.2 4.9 %collective-permute-start.14 = (f32[1536,256]{1,0:T(8,128)}, f32[1536,256]{1,0:T(8,128)S(1)}, u32[]{:S(2)}, u32[]{:S(2)}) collective-permute-start(f32[1536,256]{1,0:T(8,128)} %get-tuple-element.43), channel_id=1, source_target_pairs={{0,1},{1,0},{2,3},{3,2},{4,5},{5,4},{6,7},{7,6},{8,9},{9,8},{10,11... | collective-permute-start | bytes 4718600 | tf_op jit(solution)/shard_map/ppermute | solution.py:455
  145.9 33.0 %collective-permute-start.10 = (f16[1536,256]{1,0:T(8,128)(2,1)}, f16[1536,256]{1,0:T(8,128)(2,1)}, u32[]{:S(2)}, u32[]{:S(2)}) collective-permute-start(f16[1536,256]{1,0:T(8,128)(2,1)} %multiply_convert_fusion.1), channel_id=1, source_target_pairs={{2,0},{3,1},{6,4},{7,5},{8,10},{9,11},{12,14},{13,15},{18,16},{19,... | collective-permute-start | bytes 2359304 | tf_op jit(solution)/shard_map/ppermute | solution.py:367
  147.2 13.9 %collective-permute-start.17 = (f32[2,96,256]{2,1,0:T(8,128)S(1)}, f32[2,96,256]{2,1,0:T(8,128)S(1)}, u32[]{:S(2)}, u32[]{:S(2)}) collective-permute-start(f32[2,96,256]{2,1,0:T(8,128)S(1)} %slice.31), channel_id=1, source_target_pairs={{0,1},{1,0},{2,3},{3,2},{4,5},{5,4},{6,7},{7,6},{8,9},{9,8},{10,11... | collective-permute-start | bytes 589832 | tf_op jit(solution)/shard_map/ppermute | solution.py:479
  152.5 8.6 %copy-start.3 = (f32[4,96,256]{2,1,0:T(8,128)S(1)}, f32[4,96,256]{2,1,0:T(8,128)}, u32[]{:S(2)}) copy-start(f32[4,96,256]{2,1,0:T(8,128)} %copy-done.2) | copy-start | bytes 1179652
  153.3 8.0 %copy-start.7 = (f32[2]{0:T(128)S(1)}, f32[2]{0:T(128)}, u32[]{:S(2)}) copy-start(f32[2]{0:T(128)} %param.7) | copy-start | bytes 28
  153.3 25.7 %copy-start.4 = (f32[1536,256]{1,0:T(8,128)S(1)}, f32[1536,256]{1,0:T(8,128)}, u32[]{:S(2)}) copy-start(f32[1536,256]{1,0:T(8,128)} %get-tuple-element.48) | copy-start | bytes 4718596
  155.0 23.9 %collective-permute-start.15 = (f16[1536,256]{1,0:T(8,128)(2,1)S(1)}, f16[1536,256]{1,0:T(8,128)(2,1)}, u32[]{:S(2)}, u32[]{:S(2)}) collective-permute-start(f16[1536,256]{1,0:T(8,128)(2,1)S(1)} %multiply_convert_fusion), channel_id=1, source_target_pairs={{0,2},{1,3},{4,6},{5,7},{10,8},{11,9},{14,12},{15,13},{16,18},{17,... | collective-permute-start | bytes 2359304 | tf_op jit(solution)/shard_map/ppermute | solution.py:367
  161.2 17.7 %collective-permute-start.18 = (f32[1,96,256]{2,1,0:T(8,128)S(1)}, f32[1,96,256]{2,1,0:T(8,128)S(1)}, u32[]{:S(2)}, u32[]{:S(2)}) collective-permute-start(f32[1,96,256]{2,1,0:T(8,128)S(1)} %slice.37), channel_id=1, source_target_pairs={{0,2},{1,3},{2,0},{3,1},{4,6},{5,7},{6,4},{7,5},{8,10},{9,11},{10,... | collective-permute-start | bytes 294920 | tf_op jit(solution)/shard_map/ppermute | solution.py:479
  161.3 17.6 %collective-permute-start.11 = (f32[1,128]{1,0:T(1,128)S(1)}, f32[1,128]{1,0:T(1,128)S(1)}, u32[]{:S(2)}, u32[]{:S(2)}) collective-permute-start(f32[1,128]{1,0:T(1,128)S(1)} %broadcast_in_dim.39), channel_id=1, source_target_pairs={{2,0},{3,1},{6,4},{7,5},{8,10},{9,11},{12,14},{13,15},{18,16},{19,... | collective-permute-start | bytes 1544 | tf_op jit(solution)/shard_map/ppermute | solution.py:367
  162.6 16.3 %collective-permute-start.16 = (f32[1,128]{1,0:T(1,128)S(1)}, f32[1,128]{1,0:T(1,128)S(1)}, u32[]{:S(2)}, u32[]{:S(2)}) collective-permute-start(f32[1,128]{1,0:T(1,128)S(1)} %broadcast_in_dim.40), channel_id=1, source_target_pairs={{0,2},{1,3},{4,6},{5,7},{10,8},{11,9},{14,12},{15,13},{16,18},{17,... | collective-permute-start | bytes 1544 | tf_op jit(solution)/shard_map/ppermute | solution.py:367
  178.9 2.1 %copy-start.1 = (bf16[96,1536]{1,0:T(8,128)(2,1)S(1)}, bf16[96,1536]{1,0:T(8,128)(2,1)}, u32[]{:S(2)}) copy-start(bf16[96,1536]{1,0:T(8,128)(2,1)} %get-tuple-element.31.real_ref) | copy-start | bytes 884740

commit v14 on v12

--- a/solution.py
+++ b/solution.py
@@ -223,7 +223,7 @@
     counts = tuple(len(sources) for _, sources in groups)
     flat = [source for _, sources in groups for source in sources]
     picks = jnp.stack([pick for pick, _ in groups]).astype(jnp.int32)
-    block = row_block(rows)
+    block = rows // 4 if rows % 128 == 0 else rows
     quarter = lambda part, side: pl.BlockSpec(
         (1, block // 2, cols), lambda i: (part, 2 * i + side, 0)
     )

time: 178 us -> 178 us (level)
  no operation moved by 1% of the time
where the time goes in v14:
time: 178 us; the launch traced here: 175 us
  waiting for transfers between devices  80.7 us (45%)
  starting transfers between devices  44 us (25%)
  Pallas kernels  33 us (19%)
  other arithmetic  12.8 us (7%)
  local copies, waits for them, and re-layouts  3.13 us (2%)
  between operations  1.84 us (1%)
    ppermute x3, waiting for transfers between devices, hop(): down.append(lax.ppermute(down[-1], 'row', back))  47 us
    ppermute x9, starting transfers between devices, move(): return lax.ppermute(block, ('row', 'col'), route)  26 us
    pallas_call x2, Pallas kernels, products(): pl.pallas_call(functools.partial(product_kernel, counts), grid=(rows // b...  18.8 us
    ppermute x3, waiting for transfers between devices, hop(): up.append(lax.ppermute(up[-1], 'row', ends))  12.7 us
    ppermute x2, waiting for transfers between devices, local(): arrive = lax.ppermute(rest[1::2], 'col', pairs)  12.3 us
    ppermute x3, starting transfers between devices, hop(): up.append(lax.ppermute(up[-1], 'row', ends))  12.1 us
    pallas_call x1, Pallas kernels, pick_columns(): pl.pallas_call(pick_kernel, grid=(rows // block,), in_specs=[pl.BlockSpec...  6.28 us
    ppermute x9, waiting for transfers between devices, move(): return lax.ppermute(block, ('row', 'col'), route)  5.66 us
  transfers between devices with their start and end apart: 19, of which 8 were waited for; matrix products, arithmetic and copies ran while one was open for 7% of the time, Pallas kernels for 4%

profile of v14, /device:TPU:1, one launch (start us, length us, event | category | flops | bytes accessed | tf_op | source)
XLA Modules:
  0.0 175.5 jit_solution(4439036214009100789)
XLA Ops:
  0.0 1.3 cut_window.1
  1.3 1.3 collective-permute-start.2
  2.6 4.6 %collective-permute-start.4 = (bf16[1536,128]{1,0:T(8,128)(2,1)S(1)}, bf16[1536,128]{1,0:T(8,128)(2,1)S(1)}, u32[]{:S(2)}, u32[]{:S(2)}) collective-permute-start(bf16[1536,128]{1,0:T(8,128)(2,1)S(1)} %get-tuple-element.26), channel_id=1, source_target_pairs={{0,0},{1,4},{4,1},{5,5},{10,10},{11,14},{14,11},{15,15},{16,16},{1... | collective-permute-start | bytes 1179656 | tf_op jit(solution)/shard_map/ppermute | solution.py:367
  7.2 1.9 %collective-permute-start.1 = (bf16[1536,128]{1,0:T(8,128)(2,1)S(1)}, bf16[1536,128]{1,0:T(8,128)(2,1)S(1)}, u32[]{:S(2)}, u32[]{:S(2)}) collective-permute-start(bf16[1536,128]{1,0:T(8,128)(2,1)S(1)} %get-tuple-element.25), channel_id=1, source_target_pairs={{0,0},{1,4},{2,8},{3,12},{4,1},{5,5},{6,9},{7,13},{8,2},{9,6},{10,... | collective-permute-start | bytes 1179656 | tf_op jit(solution)/shard_map/ppermute | solution.py:367
  9.2 0.1 fusion
  9.3 0.1 dynamic_slice.14
  9.5 6.3 %pick_columns.1 = (bf16[96,1536]{1,0:T(8,128)(2,1)S(1)}, bf16[96,1536]{1,0:T(8,128)(2,1)S(1)}) custom-call(bf16[2,1536,1536]{2,1,0:T(8,128)(2,1)} %tile_ref.1, s32[1,128]{1,0:T(1,128)S(1)} %pad_bitcast_fusion.miss_ref, bf16[8,1536]{1,0:T(8,128)(2,1)S(1)} %broadcast_in_dim.16.recv_ref, f32[8,1536]{1,0:T(8,128)S(1)} %broadcast_in_dim.36.live_ref), custom_call_target="tpu_custom_call" | custom-call | flops 37748736 | bytes 147456 | tf_op jit(solution)/shard_map/pick_columns/pallas_call | solution.py:105
  15.7 4.9 %collective-permute-start.3 = (bf16[1536,128]{1,0:T(8,128)(2,1)S(1)}, bf16[1536,128]{1,0:T(8,128)(2,1)S(1)}, u32[]{:S(2)}, u32[]{:S(2)}) collective-permute-start(bf16[1536,128]{1,0:T(8,128)(2,1)S(1)} %collective-permute-done.2), channel_id=1, source_target_pairs={{0,8},{1,12},{4,9},{5,13},{10,2},{11,6},{14,3},{15,7},{16,24},{17,... | collective-permute-start | bytes 1179656 | tf_op jit(solution)/shard_map/ppermute | solution.py:367
  20.6 0.9 pad_maximum_fusion
  21.5 1.9 %collective-permute-start = (bf16[192,1536]{1,0:T(8,128)(2,1)}, bf16[192,1536]{1,0:T(8,128)(2,1)}, u32[]{:S(2)}, u32[]{:S(2)}) collective-permute-start(bf16[192,1536]{1,0:T(8,128)(2,1)} %pad_maximum_fusion), channel_id=1, source_target_pairs={{0,0},{1,4},{2,8},{3,12},{4,1},{5,5},{6,9},{7,13},{8,2},{9,6},{10,... | collective-permute-start | bytes 1769480 | tf_op jit(solution)/shard_map/ppermute | solution.py:367
  23.4 0.1 dynamic_slice.16
  23.5 5.6 %collective-permute-done.3.refs_1_ = bf16[1536,128]{1,0:T(8,128)(2,1)S(1)} collective-permute-done((bf16[1536,128]{1,0:T(8,128)(2,1)S(1)}, bf16[1536,128]{1,0:T(8,128)(2,1)S(1)}, u32[]{:S(2)}, u32[]{:S(2)}) %collective-permute-start.3) | collective-permute-done | bytes 393248 | tf_op jit(solution)/shard_map/ppermute | solution.py:367
  29.1 0.5 fill_window.1.refs_4_.refs_7_.refs_0_
  29.6 9.8 %collective-permute-start.5 = (bf16[1536,256]{1,0:T(8,128)(2,1)S(1)}, bf16[1536,256]{1,0:T(8,128)(2,1)S(1)}, u32[]{:S(2)}, u32[]{:S(2)}) collective-permute-start(bf16[1536,256]{1,0:T(8,128)(2,1)S(1)} %fill_window.1.refs_4_.refs_7_.refs_0_), channel_id=1, source_target_pairs={{0,4},{4,8},{8,12},{1,5},{5,9},{9,13},{2,6},{6,10},{10,14},{3,7},{... | collective-permute-start | bytes 2359304 | tf_op jit(solution)/shard_map/ppermute | solution.py:412
  39.4 1.3 collective-permute-start.6
  40.7 0.1 pad_add_fusion.pick_ref
  40.8 1.8 %fusion.2 = (bf16[96,1536]{1,0:T(8,128)(2,1)S(1)}, bf16[96,1536]{1,0:T(8,128)(2,1)}) fusion(bf16[192,1536]{1,0:T(8,128)(2,1)} %collective-permute-done), kind=kLoop, calls=%fused_computation.18 | loop fusion | bytes 1179648 | tf_op jit(solution)/shard_map/slice | solution.py:400
  42.6 12.7 %collective-permute-done.5.refs_6_.refs_9_.refs_2_.refs_7_.refs_8_.refs_14_ = bf16[1536,256]{1,0:T(8,128)(2,1)S(1)} collective-permute-done((bf16[1536,256]{1,0:T(8,128)(2,1)S(1)}, bf16[1536,256]{1,0:T(8,128)(2,1)S(1)}, u32[]{:S(2)}, u32[]{:S(2)}) %collective-permute-start.5) | collective-permute-done | bytes 786464 | tf_op jit(solution)/shard_map/ppermute | solution.py:412
  55.3 12.6 %collective-permute-done.6.refs_5_.refs_8_.refs_1_.refs_6_.refs_7_.refs_13_ = bf16[1536,256]{1,0:T(8,128)(2,1)S(1)} collective-permute-done((bf16[1536,256]{1,0:T(8,128)(2,1)S(1)}, bf16[1536,256]{1,0:T(8,128)(2,1)S(1)}, u32[]{:S(2)}, u32[]{:S(2)}) %collective-permute-start.6) | collective-permute-done | bytes 786464 | tf_op jit(solution)/shard_map/ppermute | solution.py:413
  68.0 7.7 %products.2 = (f32[1536,256]{1,0:T(8,128)S(1)}, f32[1536,256]{1,0:T(8,128)S(1)}) custom-call(s32[2]{0:T(128)S(1)} %pad_add_fusion.pick_ref, bf16[8,1536]{1,0:T(8,128)(2,1)S(1)} %broadcast_in_dim.16.recv_ref, bf16[2,1536,1536]{2,1,0:T(8,128)(2,1)} %tile_ref.1, bf16[2,1536,1536]{2,1,0:T(8,128)(2,1)} %tile_ref.1, bf16[2,1536,1536]{2,1,0:T(8,128)(2,1)} %tile_ref.1, ...), custom_call_target="tpu_custom_call" | custom-call | flops 150994944 | bytes 24576 | tf_op jit(solution)/shard_map/products/pallas_call | solution.py:230
  75.7 0.3 collective-permute-start.7
  76.0 0.7 collective-permute-start.8
  76.7 1.3 collective-permute-start.9
  78.0 1.2 collective-permute-done.7
  79.2 2.0 %abs_reduce_fusion.1 = (f32[]{:T(128)}, f32[1536,256]{1,0:T(8,128)}) fusion(f32[1536,256]{1,0:T(8,128)S(1)} %get-tuple-element.31, f32[1536,256]{1,0:T(8,128)S(1)} %collective-permute-done.7), kind=kLoop, calls=%fused_computation.4 | loop fusion | flops 1179647 | bytes 4718596 | tf_op jit(solution)/shard_map/reduce_max | solution.py:421
  81.9 2.5 %multiply_convert_fusion.1 = f16[1536,256]{1,0:T(8,128)(2,1)} fusion(f32[1536,256]{1,0:T(8,128)} %get-tuple-element.44, f32[]{:T(128)S(6)} %div.18), kind=kLoop, calls=%fused_computation.3 | loop fusion | flops 786432 | bytes 2359300 | tf_op jit(solution)/shard_map/convert_element_type | solution.py:422
  84.3 16.8 %collective-permute-done.9.refs_3_.refs_4_.refs_10_ = bf16[1536,256]{1,0:T(8,128)(2,1)} collective-permute-done((bf16[1536,256]{1,0:T(8,128)(2,1)S(1)}, bf16[1536,256]{1,0:T(8,128)(2,1)}, u32[]{:S(2)}, u32[]{:S(2)}) %collective-permute-start.9) | collective-permute-done | bytes 786464 | tf_op jit(solution)/shard_map/ppermute | solution.py:413
  101.1 1.3 collective-permute-start.12
  102.4 1.6 collective-permute-start.13
  104.0 0.1 stack.56.pick_ref
  104.1 0.1 pad_add_fusion.1.pick_ref
  104.1 17.6 %collective-permute-done.12.refs_5_.refs_6_.refs_12_ = bf16[1536,256]{1,0:T(8,128)(2,1)} collective-permute-done((bf16[1536,256]{1,0:T(8,128)(2,1)}, bf16[1536,256]{1,0:T(8,128)(2,1)}, u32[]{:S(2)}, u32[]{:S(2)}) %collective-permute-start.12) | collective-permute-done | bytes 786464 | tf_op jit(solution)/shard_map/ppermute | solution.py:413
  121.8 1.0 copy-done
  122.7 3.3 %extra_products.1 = f32[4,96,256]{2,1,0:T(8,128)S(1)} custom-call(s32[8]{0:T(128)S(1)} %stack.56.pick_ref, bf16[96,1536]{1,0:T(8,128)(2,1)S(1)} %copy-done, bf16[96,1536]{1,0:T(8,128)(2,1)S(1)} %get-tuple-element.28.imag_ref, bf16[1536,256]{1,0:T(8,128)(2,1)S(1)} %fill_window.1.refs_4_.refs_7_.refs_0_, ...), custom_call_target="tpu_custom_call" | custom-call | flops 18874368 | bytes 24576 | tf_op jit(solution)/shard_map/extra_products/pallas_call | solution.py:264
  126.1 11.1 %products.3 = (f32[1536,256]{1,0:T(8,128)}, f32[1536,256]{1,0:T(8,128)}) custom-call(s32[2]{0:T(128)S(1)} %pad_add_fusion.1.pick_ref, bf16[8,1536]{1,0:T(8,128)(2,1)S(1)} %broadcast_in_dim.16.recv_ref, bf16[2,1536,1536]{2,1,0:T(8,128)(2,1)} %tile_ref.1, bf16[2,1536,1536]{2,1,0:T(8,128)(2,1)} %tile_ref.1, bf16[2,1536,1536]{2,1,0:T(8,128)(2,1)} %tile_ref.1, ...), custom_call_target="tpu_custom_call" | custom-call | flops 150994944 | bytes 24576 | tf_op jit(solution)/shard_map/products/pallas_call | solution.py:230
  137.1 1.6 collective-permute-start.14
  138.7 1.3 collective-permute-start.10
  140.0 0.1 collective-permute-start.17
  140.1 1.8 %collective-permute-done.14 = f32[1536,256]{1,0:T(8,128)S(1)} collective-permute-done((f32[1536,256]{1,0:T(8,128)}, f32[1536,256]{1,0:T(8,128)S(1)}, u32[]{:S(2)}, u32[]{:S(2)}) %collective-permute-start.14) | collective-permute-done | bytes 1572896 | tf_op jit(solution)/shard_map/ppermute | solution.py:451
  142.0 3.4 %abs_reduce_fusion = (f32[]{:T(128)}, f32[1536,256]{1,0:T(8,128)}) fusion(f32[1536,256]{1,0:T(8,128)} %get-tuple-element.38, f32[1536,256]{1,0:T(8,128)S(1)} %collective-permute-done.14), kind=kLoop, calls=%fused_computation.2 | loop fusion | flops 1179647 | bytes 4718596 | tf_op jit(solution)/shard_map/reduce_max | solution.py:421
  146.1 1.7 multiply_convert_fusion
  147.9 4.9 %collective-permute-start.15 = (f16[1536,256]{1,0:T(8,128)(2,1)S(1)}, f16[1536,256]{1,0:T(8,128)(2,1)}, u32[]{:S(2)}, u32[]{:S(2)}) collective-permute-start(f16[1536,256]{1,0:T(8,128)(2,1)S(1)} %multiply_convert_fusion), channel_id=1, source_target_pairs={{0,2},{1,3},{4,6},{5,7},{10,8},{11,9},{14,12},{15,13},{16,18},{17,... | collective-permute-start | bytes 2359304 | tf_op jit(solution)/shard_map/ppermute | solution.py:367
  152.8 0.1 collective-permute-start.18
  152.9 1.3 collective-permute-start.11
  154.2 4.0 %collective-permute-start.16 = (f32[1,128]{1,0:T(1,128)S(1)}, f32[1,128]{1,0:T(1,128)S(1)}, u32[]{:S(2)}, u32[]{:S(2)}) collective-permute-start(f32[1,128]{1,0:T(1,128)S(1)} %broadcast_in_dim.40), channel_id=1, source_target_pairs={{0,2},{1,3},{4,6},{5,7},{10,8},{11,9},{14,12},{15,13},{16,18},{17,... | collective-permute-start | bytes 1544 | tf_op jit(solution)/shard_map/ppermute | solution.py:367
  158.2 12.3 %collective-permute-done.18 = f32[1,96,256]{2,1,0:T(8,128)S(1)} collective-permute-done((f32[1,96,256]{2,1,0:T(8,128)S(1)}, f32[1,96,256]{2,1,0:T(8,128)S(1)}, u32[]{:S(2)}, u32[]{:S(2)}) %collective-permute-start.18) | collective-permute-done | bytes 98336 | tf_op jit(solution)/shard_map/ppermute | solution.py:475
  170.6 2.1 %add_add_fusion.refs_0_ = f32[1536,256]{1,0:T(8,128)S(1)} fusion(f16[1536,256]{1,0:T(8,128)(2,1)} %collective-permute-done.15, f32[1536,256]{1,0:T(8,128)} %get-tuple-element.42, f16[1536,256]{1,0:T(8,128)(2,1)} %collective-permute-done.10, f32[1536,256]{1,0:T(8,128)S(1)} %copy-done.4, f32[]{:T(128)S(1)} %bitcast.24, f32[]{:T(128)S(1)} %bitcast.23, ...), kind=kLoop, calls=%fused_computation | loop fusion | flops 3538944 | bytes 6291466 | tf_op jit(solution)/shard_map/add | solution.py:471
  172.6 2.8 %finish.1 = f32[2,1536,128]{2,1,0:T(8,128)} custom-call(f32[2]{0:T(128)S(1)} %broadcast_multiply_fusion.wave_ref, s32[96]{0:T(128)S(1)} %get-tuple-element.48.miss_ref, bf16[8,1536]{1,0:T(8,128)(2,1)S(1)} %broadcast_in_dim.16.recv_ref, bf16[2,1536,1536]{2,1,0:T(8,128)(2,1)} %tile_ref.1, bf16[96,1536]{1,0:T(8,128)(2,1)S(1)} %copy-done.1, ...), custom_call_target="tpu_custom_call" | custom-call | flops 61440 | bytes 122880 | tf_op jit(solution)/shard_map/finish/pallas_call | solution.py:304
  (40 shorter events, 0.2 us)
Async XLA Ops:
  0.0 9.1 %copy-start.6 = (s32[4,96]{1,0:T(4,128)S(1)}, s32[4,96]{1,0:T(4,128)}, u32[]{:S(2)}) copy-start(s32[4,96]{1,0:T(4,128)} %param.6) | copy-start | bytes 4612
  0.0 9.3 %copy-start.5 = (s32[6144]{0:T(1024)S(1)}, s32[6144]{0:T(1024)}, u32[]{:S(2)}) copy-start(s32[6144]{0:T(1024)} %param.5) | copy-start | bytes 73732
  1.3 14.4 %collective-permute-start.2 = (bf16[1536,128]{1,0:T(8,128)(2,1)S(1)}, bf16[1536,128]{1,0:T(8,128)(2,1)S(1)}, u32[]{:S(2)}, u32[]{:S(2)}) collective-permute-start(bf16[1536,128]{1,0:T(8,128)(2,1)S(1)} %get-tuple-element.26), channel_id=1, source_target_pairs={{2,0},{3,1},{6,4},{7,5},{8,10},{9,11},{12,14},{13,15},{18,16},{19,... | collective-permute-start | bytes 1179656 | tf_op jit(solution)/shard_map/ppermute | solution.py:367
  2.6 20.9 %collective-permute-start.4 = (bf16[1536,128]{1,0:T(8,128)(2,1)S(1)}, bf16[1536,128]{1,0:T(8,128)(2,1)S(1)}, u32[]{:S(2)}, u32[]{:S(2)}) collective-permute-start(bf16[1536,128]{1,0:T(8,128)(2,1)S(1)} %get-tuple-element.26), channel_id=1, source_target_pairs={{0,0},{1,4},{4,1},{5,5},{10,10},{11,14},{14,11},{15,15},{16,16},{1... | collective-permute-start | bytes 1179656 | tf_op jit(solution)/shard_map/ppermute | solution.py:367
  7.2 16.3 %collective-permute-start.1 = (bf16[1536,128]{1,0:T(8,128)(2,1)S(1)}, bf16[1536,128]{1,0:T(8,128)(2,1)S(1)}, u32[]{:S(2)}, u32[]{:S(2)}) collective-permute-start(bf16[1536,128]{1,0:T(8,128)(2,1)S(1)} %get-tuple-element.25), channel_id=1, source_target_pairs={{0,0},{1,4},{2,8},{3,12},{4,1},{5,5},{6,9},{7,13},{8,2},{9,6},{10,... | collective-permute-start | bytes 1179656 | tf_op jit(solution)/shard_map/ppermute | solution.py:367
  15.7 13.4 %collective-permute-start.3 = (bf16[1536,128]{1,0:T(8,128)(2,1)S(1)}, bf16[1536,128]{1,0:T(8,128)(2,1)S(1)}, u32[]{:S(2)}, u32[]{:S(2)}) collective-permute-start(bf16[1536,128]{1,0:T(8,128)(2,1)S(1)} %collective-permute-done.2), channel_id=1, source_target_pairs={{0,8},{1,12},{4,9},{5,13},{10,2},{11,6},{14,3},{15,7},{16,24},{17,... | collective-permute-start | bytes 1179656 | tf_op jit(solution)/shard_map/ppermute | solution.py:367
  21.5 19.3 %collective-permute-start = (bf16[192,1536]{1,0:T(8,128)(2,1)}, bf16[192,1536]{1,0:T(8,128)(2,1)}, u32[]{:S(2)}, u32[]{:S(2)}) collective-permute-start(bf16[192,1536]{1,0:T(8,128)(2,1)} %pad_maximum_fusion), channel_id=1, source_target_pairs={{0,0},{1,4},{2,8},{3,12},{4,1},{5,5},{6,9},{7,13},{8,2},{9,6},{10,... | collective-permute-start | bytes 1769480 | tf_op jit(solution)/shard_map/ppermute | solution.py:367
  29.6 25.7 %collective-permute-start.5 = (bf16[1536,256]{1,0:T(8,128)(2,1)S(1)}, bf16[1536,256]{1,0:T(8,128)(2,1)S(1)}, u32[]{:S(2)}, u32[]{:S(2)}) collective-permute-start(bf16[1536,256]{1,0:T(8,128)(2,1)S(1)} %fill_window.1.refs_4_.refs_7_.refs_0_), channel_id=1, source_target_pairs={{0,4},{4,8},{8,12},{1,5},{5,9},{9,13},{2,6},{6,10},{10,14},{3,7},{... | collective-permute-start | bytes 2359304 | tf_op jit(solution)/shard_map/ppermute | solution.py:412
  39.4 28.6 %collective-permute-start.6 = (bf16[1536,256]{1,0:T(8,128)(2,1)S(1)}, bf16[1536,256]{1,0:T(8,128)(2,1)S(1)}, u32[]{:S(2)}, u32[]{:S(2)}) collective-permute-start(bf16[1536,256]{1,0:T(8,128)(2,1)S(1)} %fill_window.1.refs_4_.refs_7_.refs_0_), channel_id=1, source_target_pairs={{4,0},{8,4},{12,8},{5,1},{9,5},{13,9},{6,2},{10,6},{14,10},{7,3},{... | collective-permute-start | bytes 2359304 | tf_op jit(solution)/shard_map/ppermute | solution.py:413
  75.7 3.5 %collective-permute-start.7 = (f32[1536,256]{1,0:T(8,128)S(1)}, f32[1536,256]{1,0:T(8,128)S(1)}, u32[]{:S(2)}, u32[]{:S(2)}) collective-permute-start(f32[1536,256]{1,0:T(8,128)S(1)} %get-tuple-element.32), channel_id=1, source_target_pairs={{0,1},{1,0},{2,3},{3,2},{4,5},{5,4},{6,7},{7,6},{8,9},{9,8},{10,11... | collective-permute-start | bytes 4718600 | tf_op jit(solution)/shard_map/ppermute | solution.py:451
  76.0 8.4 %collective-permute-start.8 = (bf16[1536,256]{1,0:T(8,128)(2,1)S(1)}, bf16[1536,256]{1,0:T(8,128)(2,1)S(1)}, u32[]{:S(2)}, u32[]{:S(2)}) collective-permute-start(bf16[1536,256]{1,0:T(8,128)(2,1)S(1)} %collective-permute-done.5.refs_6_.refs_9_.refs_2_.refs_7_.refs_8_.refs_14_), channel_id=1, source_target_pairs={{4,8},{8,12},{5,9},{9,13},{6,10},{10,14},{7,11},{11,15},{20,24},{2... | collective-permute-start | bytes 2359304 | tf_op jit(solution)/shard_map/ppermute | solution.py:412
  76.7 24.4 %collective-permute-start.9 = (bf16[1536,256]{1,0:T(8,128)(2,1)S(1)}, bf16[1536,256]{1,0:T(8,128)(2,1)}, u32[]{:S(2)}, u32[]{:S(2)}) collective-permute-start(bf16[1536,256]{1,0:T(8,128)(2,1)S(1)} %collective-permute-done.6.refs_5_.refs_8_.refs_1_.refs_6_.refs_7_.refs_13_), channel_id=1, source_target_pairs={{4,0},{8,4},{5,1},{9,5},{6,2},{10,6},{7,3},{11,7},{20,16},{24,20},... | collective-permute-start | bytes 2359304 | tf_op jit(solution)/shard_map/ppermute | solution.py:413
  101.1 20.6 %collective-permute-start.12 = (bf16[1536,256]{1,0:T(8,128)(2,1)}, bf16[1536,256]{1,0:T(8,128)(2,1)}, u32[]{:S(2)}, u32[]{:S(2)}) collective-permute-start(bf16[1536,256]{1,0:T(8,128)(2,1)} %collective-permute-done.9.refs_3_.refs_4_.refs_10_), channel_id=1, source_target_pairs={{4,0},{5,1},{6,2},{7,3},{20,16},{21,17},{22,18},{23,19}} | collective-permute-start | bytes 2359304 | tf_op jit(solution)/shard_map/ppermute | solution.py:413
  102.4 19.3 %collective-permute-start.13 = (bf16[1536,256]{1,0:T(8,128)(2,1)S(1)}, bf16[1536,256]{1,0:T(8,128)(2,1)}, u32[]{:S(2)}, u32[]{:S(2)}) collective-permute-start(bf16[1536,256]{1,0:T(8,128)(2,1)S(1)} %collective-permute-done.8.refs_4_.refs_5_.refs_11_), channel_id=1, source_target_pairs={{8,12},{9,13},{10,14},{11,15},{24,28},{25,29},{26,30},{27,31}} | collective-permute-start | bytes 2359304 | tf_op jit(solution)/shard_map/ppermute | solution.py:412
  121.8 1.0 copy-start
  126.0 14.0 %copy-start.2 = (f32[4,96,256]{2,1,0:T(8,128)}, f32[4,96,256]{2,1,0:T(8,128)S(1)}, u32[]{:S(2)}) copy-start(f32[4,96,256]{2,1,0:T(8,128)S(1)} %extra_products.1) | copy-start | bytes 1179652
  137.1 4.8 %collective-permute-start.14 = (f32[1536,256]{1,0:T(8,128)}, f32[1536,256]{1,0:T(8,128)S(1)}, u32[]{:S(2)}, u32[]{:S(2)}) collective-permute-start(f32[1536,256]{1,0:T(8,128)} %get-tuple-element.39), channel_id=1, source_target_pairs={{0,1},{1,0},{2,3},{3,2},{4,5},{5,4},{6,7},{7,6},{8,9},{9,8},{10,11... | collective-permute-start | bytes 4718600 | tf_op jit(solution)/shard_map/ppermute | solution.py:451
  138.7 31.8 %collective-permute-start.10 = (f16[1536,256]{1,0:T(8,128)(2,1)}, f16[1536,256]{1,0:T(8,128)(2,1)}, u32[]{:S(2)}, u32[]{:S(2)}) collective-permute-start(f16[1536,256]{1,0:T(8,128)(2,1)} %multiply_convert_fusion.1), channel_id=1, source_target_pairs={{2,0},{3,1},{6,4},{7,5},{8,10},{9,11},{12,14},{13,15},{18,16},{19,... | collective-permute-start | bytes 2359304 | tf_op jit(solution)/shard_map/ppermute | solution.py:367
  140.0 12.7 %collective-permute-start.17 = (f32[2,96,256]{2,1,0:T(8,128)S(1)}, f32[2,96,256]{2,1,0:T(8,128)S(1)}, u32[]{:S(2)}, u32[]{:S(2)}) collective-permute-start(f32[2,96,256]{2,1,0:T(8,128)S(1)} %slice.31), channel_id=1, source_target_pairs={{0,1},{1,0},{2,3},{3,2},{4,5},{5,4},{6,7},{7,6},{8,9},{9,8},{10,11... | collective-permute-start | bytes 589832 | tf_op jit(solution)/shard_map/ppermute | solution.py:475
  145.4 7.4 %copy-start.3 = (f32[4,96,256]{2,1,0:T(8,128)S(1)}, f32[4,96,256]{2,1,0:T(8,128)}, u32[]{:S(2)}) copy-start(f32[4,96,256]{2,1,0:T(8,128)} %copy-done.2) | copy-start | bytes 1179652
  146.1 6.8 %copy-start.7 = (f32[2]{0:T(128)S(1)}, f32[2]{0:T(128)}, u32[]{:S(2)}) copy-start(f32[2]{0:T(128)} %param.7) | copy-start | bytes 28
  146.1 24.4 %copy-start.4 = (f32[1536,256]{1,0:T(8,128)S(1)}, f32[1536,256]{1,0:T(8,128)}, u32[]{:S(2)}) copy-start(f32[1536,256]{1,0:T(8,128)} %get-tuple-element.44) | copy-start | bytes 4718596
  147.9 22.7 %collective-permute-start.15 = (f16[1536,256]{1,0:T(8,128)(2,1)S(1)}, f16[1536,256]{1,0:T(8,128)(2,1)}, u32[]{:S(2)}, u32[]{:S(2)}) collective-permute-start(f16[1536,256]{1,0:T(8,128)(2,1)S(1)} %multiply_convert_fusion), channel_id=1, source_target_pairs={{0,2},{1,3},{4,6},{5,7},{10,8},{11,9},{14,12},{15,13},{16,18},{17,... | collective-permute-start | bytes 2359304 | tf_op jit(solution)/shard_map/ppermute | solution.py:367
  152.8 17.7 %collective-permute-start.18 = (f32[1,96,256]{2,1,0:T(8,128)S(1)}, f32[1,96,256]{2,1,0:T(8,128)S(1)}, u32[]{:S(2)}, u32[]{:S(2)}) collective-permute-start(f32[1,96,256]{2,1,0:T(8,128)S(1)} %slice.37), channel_id=1, source_target_pairs={{0,2},{1,3},{2,0},{3,1},{4,6},{5,7},{6,4},{7,5},{8,10},{9,11},{10,... | collective-permute-start | bytes 294920 | tf_op jit(solution)/shard_map/ppermute | solution.py:475
  152.9 17.6 %collective-permute-start.11 = (f32[1,128]{1,0:T(1,128)S(1)}, f32[1,128]{1,0:T(1,128)S(1)}, u32[]{:S(2)}, u32[]{:S(2)}) collective-permute-start(f32[1,128]{1,0:T(1,128)S(1)} %broadcast_in_dim.39), channel_id=1, source_target_pairs={{2,0},{3,1},{6,4},{7,5},{8,10},{9,11},{12,14},{13,15},{18,16},{19,... | collective-permute-start | bytes 1544 | tf_op jit(solution)/shard_map/ppermute | solution.py:367
  154.2 16.3 %collective-permute-start.16 = (f32[1,128]{1,0:T(1,128)S(1)}, f32[1,128]{1,0:T(1,128)S(1)}, u32[]{:S(2)}, u32[]{:S(2)}) collective-permute-start(f32[1,128]{1,0:T(1,128)S(1)} %broadcast_in_dim.40), channel_id=1, source_target_pairs={{0,2},{1,3},{4,6},{5,7},{10,8},{11,9},{14,12},{15,13},{16,18},{17,... | collective-permute-start | bytes 1544 | tf_op jit(solution)/shard_map/ppermute | solution.py:367
  170.6 2.1 %copy-start.1 = (bf16[96,1536]{1,0:T(8,128)(2,1)S(1)}, bf16[96,1536]{1,0:T(8,128)(2,1)}, u32[]{:S(2)}) copy-start(bf16[96,1536]{1,0:T(8,128)(2,1)} %get-tuple-element.27.real_ref) | copy-start | bytes 884740
